TPU v7x, 32 devices: a whole 2x2x4 slice. The times are simulated.
32 devices in a mesh: replica: 2 (over y), tp: 16 (over z, x, core).
Axes of the slice: x: 2, y: 2, z: 4, core: 2. Of those that a mesh axis runs over, the one named last changes fastest.
Arguments:
- residual: bfloat16 [256, 16384], P('replica', 'tp'), parts along dimension 0, may hold values from -0.59765625 to 0.59765625
- attn_gain: bfloat16 [16384], replicated, may hold values from 0.25 to 1.75
- ffn_gain: bfloat16 [16384], replicated, may hold values from 0.099609375 to 1.8984375
- q_weight: bfloat16 [16384, 2048], P(None, 'tp'), may hold values from -0.046875 to 0.046875
- kv_weight: bfloat16 [16384, 2048], P(None, 'tp'), may hold values from -0.046875 to 0.046875
- o_weight: bfloat16 [2048, 16384], P('tp'), may hold values from -0.1875 to 0.1875
- key_cache: bfloat16 [4, 1024, 1024], P('replica', 'tp'), parts along dimension 0, may hold values from -260 to 260
- value_cache: bfloat16 [4, 1024, 1024], P('replica', 'tp'), parts along dimension 0, may hold values from -12 to 12
- prefix: int32 [4], P('replica'), parts along dimension 0, may hold values from 256 to 1024, as said below
Outputs:
- ffn_input: bfloat16 [256, 16384], P('replica'), parts along dimension 0
There are 2 independent parts, one for each index of `replica`. A program takes and returns all parts, laid end to end along the dimension named above; an argument that names none is the same for every part. Nothing has to cross between parts.
Inputs may be any that keep to these rules, and one draw needn't show every extreme that they name: `prefix`: the first sequence's cache is full, 1024; the others hold 256 to 1024 positions.
All inputs are finite; a program needn't handle non-finite values.
Results may differ from a plain program's by a relative error of at most 0.012.
The roundings to bfloat16 on the way count: a program that leaves them out, or rounds other values in their place, can miss the bound.
Values may be sent and summed in bfloat16 or wider, within the bound.
No kernel may reach another device: no remote copies, remote signals or barrier semaphores. Data moves between devices by JAX's collectives and lax.ppermute only.
A program may use at most 128 MiB of HBM per device.

v0:
```python
import jax
import jax.numpy as jnp
from jax import lax
from jax.sharding import PartitionSpec as P

HD = 128
KVH = 8
HQ_DEV = 1
SPAN = 64
SEQS = 2
CTX_DEV = 64


epsilon = 1e-05


def rms_rows(rows, gain):
    values_f = rows.astype(jnp.float32)
    factor = lax.rsqrt(jnp.mean(values_f * values_f, axis=-1, keepdims=True) + epsilon)
    return values_f * factor * gain.astype(jnp.float32)


def rotate(vectors, positions):
    half_width = vectors.shape[-1] // 2
    frequency = 500000.0 ** (-jnp.arange(half_width, dtype=jnp.float32) / half_width)
    angles = positions.astype(jnp.float32)[:, None] * frequency[None, :]
    cosine = jnp.cos(angles)[:, None, :]
    sine = jnp.sin(angles)[:, None, :]
    first_half = vectors[..., :half_width]
    second_half = vectors[..., half_width:]
    return jnp.concatenate(
        [first_half * cosine - second_half * sine, second_half * cosine + first_half * sine],
        axis=-1,
    )


def per_device(
    residual, attn_gain, ffn_gain, q_weight, kv_weight, o_weight, key_cache, value_cache, prefix
):
    tp_count = lax.axis_size("tp")
    tp_rank = lax.axis_index("tp")
    heads_all = HQ_DEV * tp_count
    group_size = heads_all // KVH
    token_count = SEQS * SPAN
    score_scale = HD ** (-0.5)
    whole_rows = lax.all_gather(residual, "tp", axis=1, tiled=True)
    normed = rms_rows(whole_rows, attn_gain).astype(jnp.bfloat16)
    positions = (prefix[:, None] + jnp.arange(SPAN, dtype=jnp.int32)[None, :]).reshape(-1)
    queries = jnp.dot(normed, q_weight, preferred_element_type=jnp.float32).reshape(
        token_count, HQ_DEV, HD
    )
    queries = rotate(queries, positions).astype(jnp.bfloat16)
    kv_part = jnp.dot(normed, kv_weight, preferred_element_type=jnp.float32)
    kv_whole = lax.all_gather(kv_part, "tp", axis=1, tiled=True)
    new_keys = rotate(kv_whole[:, : KVH * HD].reshape(token_count, KVH, HD), positions).astype(
        jnp.bfloat16
    )
    new_values = kv_whole[:, KVH * HD :].reshape(token_count, KVH, HD).astype(jnp.bfloat16)
    head_ids = tp_rank * HQ_DEV + jnp.arange(HQ_DEV, dtype=jnp.int32)
    own_kv = head_ids // group_size
    own_keys = jnp.take(new_keys, own_kv, axis=1).reshape(SEQS, SPAN, HQ_DEV, HD)
    own_values = jnp.take(new_values, own_kv, axis=1).reshape(SEQS, SPAN, HQ_DEV, HD)
    own_queries = queries.reshape(SEQS, SPAN, HQ_DEV, HD)
    causal = (jnp.arange(SPAN)[:, None] >= jnp.arange(SPAN)[None, :])[None, None]
    fresh_scores = (
        jnp.einsum("schd,skhd->shck", own_queries, own_keys, preferred_element_type=jnp.float32)
        * score_scale
    )
    fresh_scores = jnp.where(causal, fresh_scores, -1e30)
    fresh_max = fresh_scores.max(-1)
    gathered = lax.all_gather(queries.reshape(token_count, HQ_DEV * HD), "tp", axis=1, tiled=True)
    queries_all = gathered.reshape(SEQS, SPAN, KVH, group_size, HD)
    keys_local = key_cache.reshape(SEQS, CTX_DEV, KVH, HD)
    values_local = value_cache.reshape(SEQS, CTX_DEV, KVH, HD)
    local_scores = (
        jnp.einsum("sckgd,sjkd->skgcj", queries_all, keys_local, preferred_element_type=jnp.float32)
        * score_scale
    )
    first_slot = tp_rank * CTX_DEV
    is_valid = ((first_slot + jnp.arange(CTX_DEV, dtype=jnp.int32))[None, :] < prefix[:, None])[
        :, None, None, None, :
    ]
    local_scores = jnp.where(is_valid, local_scores, -1e30)
    local_max = local_scores.max(-1)
    local_weights = jnp.where(is_valid, jnp.exp(local_scores - local_max[..., None]), 0.0)
    local_total = local_weights.sum(-1)
    local_sum = jnp.einsum(
        "skgcj,sjkd->skgcd",
        local_weights.astype(jnp.bfloat16),
        values_local,
        preferred_element_type=jnp.float32,
    )
    sums_in, maxes_in, totals_in = (
        lax.all_to_all(
            local_sum.reshape(1, SEQS, heads_all, SPAN, HD),
            "tp",
            split_axis=2,
            concat_axis=0,
            tiled=True,
        ),
        lax.all_to_all(
            local_max.reshape(1, SEQS, heads_all, SPAN),
            "tp",
            split_axis=2,
            concat_axis=0,
            tiled=True,
        ),
        lax.all_to_all(
            local_total.reshape(1, SEQS, heads_all, SPAN),
            "tp",
            split_axis=2,
            concat_axis=0,
            tiled=True,
        ),
    )
    running_max = jnp.maximum(maxes_in.max(0), fresh_max)
    factors = jnp.exp(maxes_in - running_max[None])
    fresh_weights = jnp.where(causal, jnp.exp(fresh_scores - running_max[..., None]), 0.0)
    totals = (factors * totals_in).sum(0) + fresh_weights.sum(-1)
    summed = (factors[..., None] * sums_in).sum(0)
    summed = summed + jnp.einsum(
        "shck,skhd->shcd",
        fresh_weights.astype(jnp.bfloat16),
        own_values,
        preferred_element_type=jnp.float32,
    )
    attn = (summed / totals[..., None]).astype(jnp.bfloat16)
    attn = jnp.transpose(attn, (0, 2, 1, 3)).reshape(token_count, HQ_DEV * HD)
    share_part = lax.psum_scatter(
        lax.dot_general(
            o_weight, attn, (((0,), (1,)), ((), ())), preferred_element_type=jnp.float32
        ),
        "tp",
        scatter_dimension=0,
        tiled=True,
    )
    hidden = (residual.astype(jnp.float32) + share_part.T).astype(jnp.bfloat16)
    stream = lax.all_gather(hidden, "tp", axis=1, tiled=True)
    return rms_rows(stream, ffn_gain).astype(jnp.bfloat16)


def solution(mesh):
    return jax.shard_map(
        per_device,
        mesh=mesh,
        in_specs=(
            P("replica", "tp"),
            P(),
            P(),
            P(None, "tp"),
            P(None, "tp"),
            P("tp", None),
            P("replica", "tp", None),
            P("replica", "tp", None),
            P("replica"),
        ),
        out_specs=P("replica", None),
        check_vma=False,
    )
```

profile of v0, /device:TPU:0, one launch (start us, length us, event | category | flops | bytes accessed | tf_op | source)
XLA Modules:
  0.0 324.3 jit_solution(8186954011710646467)
XLA Ops:
  7.3 0.8 convert_element_type.59
  8.9 1.0 copy.70
  9.9 1.0 copy.72
  11.0 0.7 broadcast_compare_fusion
  12.0 50.8 %all-gather.4.cloned.1.call-done = bf16[128,16384]{1,0:T(8,128)(2,1)} async-done(((bf16[128,1024]{1,0:T(8,128)(2,1)}), bf16[128,16384]{1,0:T(8,128)(2,1)}) %all-gather.4.cloned.1.call-update) | async-done | bytes 4194320 | tf_op jit(solution)/shard_map/all_gather | solution.py:46
  62.9 3.2 fusion
  66.3 4.2 %fusion.8 = f32[128,128]{1,0:T(8,128)} fusion(bf16[16384,128]{1,0:T(8,128)(2,1)} %param.15, bf16[128,16384]{1,0:T(8,128)(2,1)S(1)} %copy-done.1, f32[16384]{0:T(1024)S(1)} %convert_element_type.59, f32[128]{0:T(128)S(1)} %add_rsqrt_fusion.1), kind=kOutput, calls=%fused_computation.14 | convolution fusion | flops 545259520 | bytes 8520192 | tf_op jit(solution)/shard_map/dot_general | solution.py:53
  70.6 5.5 %fusion.12 = f32[128,1,128]{0,2,1:T(8,128)S(1)} fusion(bf16[16384,128]{1,0:T(8,128)(2,1)} %param.14, bf16[128,16384]{1,0:T(8,128)(2,1)} %all-gather.4.cloned.1.call-done, f32[16384]{0:T(1024)S(1)} %convert_element_type.59, f32[128]{0:T(128)S(1)} %add_rsqrt_fusion.1), kind=kOutput, calls=%fused_computation.16 | convolution fusion | flops 545259520 | bytes 8520192 | tf_op jit(solution)/shard_map/dot_general | solution.py:49
  76.3 20.4 %all_gather.13 = bf16[128,2048]{0,1:T(8,128)(2,1)S(1)} all-gather(bf16[128,128]{0,1:T(8,128)(2,1)S(1)} %pad_maximum_fusion), channel_id=1, replica_groups=mesh['replica'=2,'tp'=16] {'tp'}, dimensions={1}, use_global_device_ids=true | all-gather | bytes 557056 | tf_op jit(solution)/shard_map/all_gather | solution.py:71
  98.2 3.5 %all-to-all-start = ((f32[16,1,128]{2,1,0:T(1,128)}), f32[16,1,128]{2,1,0:T(1,128)S(1)}, u32[]{:S(2)}, u32[]{:S(2)}) async-start(f32[16,1,128]{2,1,0:T(1,128)} %reshape.422), calls=%async_computation | async-start | bytes 16384 | tf_op jit(solution)/shard_map/all_to_all | solution.py:101
  102.7 5.3 %all-to-all-done = f32[16,1,128]{2,1,0:T(1,128)S(1)} async-done(((f32[16,1,128]{2,1,0:T(1,128)}), f32[16,1,128]{2,1,0:T(1,128)S(1)}, u32[]{:S(2)}, u32[]{:S(2)}) %all-to-all-start) | async-done | bytes 8224 | tf_op jit(solution)/shard_map/all_to_all | solution.py:101
  108.0 3.5 %all-to-all-start.2 = ((f32[16,1,128]{2,1,0:T(1,128)}), f32[16,1,128]{2,1,0:T(1,128)S(1)}, u32[]{:S(2)}, u32[]{:S(2)}) async-start(f32[16,1,128]{2,1,0:T(1,128)} %reshape.424), calls=%async_computation.2 | async-start | bytes 16384 | tf_op jit(solution)/shard_map/all_to_all | solution.py:108
  112.2 1.1 copy.51
  114.4 3.5 %all-to-all-done.2 = f32[16,1,128]{2,1,0:T(1,128)S(1)} async-done(((f32[16,1,128]{2,1,0:T(1,128)}), f32[16,1,128]{2,1,0:T(1,128)S(1)}, u32[]{:S(2)}, u32[]{:S(2)}) %all-to-all-start.2) | async-done | bytes 8224 | tf_op jit(solution)/shard_map/all_to_all | solution.py:108
  117.9 3.7 %all-to-all-start.1 = ((f32[1,2,16,64,128]{4,3,1,0,2:T(8,128)}), f32[1,2,16,64,128]{4,3,1,0,2:T(8,128)S(1)}, u32[]{:S(2)}, u32[]{:S(2)}) async-start(f32[1,2,16,64,128]{4,3,1,0,2:T(8,128)} %copy.51), calls=%async_computation.1 | async-start | bytes 2097152 | tf_op jit(solution)/shard_map/all_to_all | solution.py:94
  122.3 1.1 slice_bitcast_fusion
  123.5 1.1 fusion.28
  125.6 18.8 %all-to-all-done.1 = f32[1,2,16,64,128]{4,3,1,0,2:T(8,128)S(1)} async-done(((f32[1,2,16,64,128]{4,3,1,0,2:T(8,128)}), f32[1,2,16,64,128]{4,3,1,0,2:T(8,128)S(1)}, u32[]{:S(2)}, u32[]{:S(2)}) %all-to-all-start.1) | async-done | bytes 1048608 | tf_op jit(solution)/shard_map/all_to_all | solution.py:94
  145.0 6.7 %convolution_bitcast_fusion = f32[16384,128]{0,1:T(8,128)} fusion(bf16[128,128]{1,0:T(8,128)(2,1)S(1)} %bitcast.112, bf16[128,16384]{1,0:T(8,128)(2,1)} %param.16), kind=kOutput, calls=%fused_computation | convolution fusion | flops 536870912 | bytes 12615680 | tf_op jit(solution)/shard_map/dot_general | solution.py:130
  151.7 107.0 %reduce-scatter.2.cloned.1.call-done = f32[1024,128]{0,1:T(8,128)} async-done(((f32[16384,128]{0,1:T(8,128)}), f32[1024,128]{0,1:T(8,128)}) %reduce-scatter.2.cloned.1.call-update) | async-done | bytes 524304 | tf_op jit(solution)/shard_map/reduce_scatter | solution.py:129
  258.8 1.8 fusion.24
  260.6 50.6 %all-gather.8.cloned.1.call-done = bf16[128,16384]{1,0:T(8,128)(2,1)} async-done(((bf16[128,1024]{1,0:T(8,128)(2,1)}), bf16[128,16384]{1,0:T(8,128)(2,1)}) %all-gather.8.cloned.1.call-update) | async-done | bytes 4194320 | tf_op jit(solution)/shard_map/all_gather | solution.py:138
  311.2 3.2 fusion.3
  314.6 3.1 fusion.5
  (61 shorter events, 9.3 us)
Async XLA Ops:
  6.5 56.3 %all-gather.4.cloned.1.call-start = ((), (), s32[]{:S(2)}) async-start(), calls=%async_computation.4 | async-start | bytes 4456448 | tf_op jit(solution)/shard_map/all_gather | solution.py:46
  7.3 115.0 %all-gather.6.cloned.1.call-start = ((), (), s32[]{:S(2)}) async-start(), calls=%async_computation.5 | async-start | bytes 1114112 | tf_op jit(solution)/shard_map/all_gather | solution.py:54
  62.9 3.4 %copy-start.1 = (bf16[128,16384]{1,0:T(8,128)(2,1)S(1)}, bf16[128,16384]{1,0:T(8,128)(2,1)}, u32[]{:S(2)}) copy-start(bf16[128,16384]{1,0:T(8,128)(2,1)} %all-gather.4.cloned.1.call-done) | copy-start | bytes 12582916
  98.2 9.8 %all-to-all-start = ((f32[16,1,128]{2,1,0:T(1,128)}), f32[16,1,128]{2,1,0:T(1,128)S(1)}, u32[]{:S(2)}, u32[]{:S(2)}) async-start(f32[16,1,128]{2,1,0:T(1,128)} %reshape.422), calls=%async_computation | async-start | bytes 16384 | tf_op jit(solution)/shard_map/all_to_all | solution.py:101
  108.0 9.9 %all-to-all-start.2 = ((f32[16,1,128]{2,1,0:T(1,128)}), f32[16,1,128]{2,1,0:T(1,128)S(1)}, u32[]{:S(2)}, u32[]{:S(2)}) async-start(f32[16,1,128]{2,1,0:T(1,128)} %reshape.424), calls=%async_computation.2 | async-start | bytes 16384 | tf_op jit(solution)/shard_map/all_to_all | solution.py:108
  117.9 26.6 %all-to-all-start.1 = ((f32[1,2,16,64,128]{4,3,1,0,2:T(8,128)}), f32[1,2,16,64,128]{4,3,1,0,2:T(8,128)S(1)}, u32[]{:S(2)}, u32[]{:S(2)}) async-start(f32[1,2,16,64,128]{4,3,1,0,2:T(8,128)} %copy.51), calls=%async_computation.1 | async-start | bytes 2097152 | tf_op jit(solution)/shard_map/all_to_all | solution.py:94
  121.5 137.2 %reduce-scatter.2.cloned.1.call-start = ((), (), s32[]{:S(2)}) async-start(), calls=%async_computation.6 | async-start | bytes 8912896 | tf_op jit(solution)/shard_map/reduce_scatter | solution.py:129
  151.6 107.1 %copy-start.2 = (bf16[128,1024]{1,0:T(8,128)(2,1)S(1)}, bf16[128,1024]{1,0:T(8,128)(2,1)}, u32[]{:S(2)}) copy-start(bf16[128,1024]{1,0:T(8,128)(2,1)} %param.11) | copy-start | bytes 786436
  151.6 108.9 %copy-start.3 = (bf16[16384]{0:T(1024)(128)(2,1)S(1)}, bf16[16384]{0:T(1024)(128)(2,1)}, u32[]{:S(2)}) copy-start(bf16[16384]{0:T(1024)(128)(2,1)} %param.13) | copy-start | bytes 98308
  151.7 159.5 %all-gather.8.cloned.1.call-start = ((), (), s32[]{:S(2)}) async-start(), calls=%async_computation.7 | async-start | bytes 4456448 | tf_op jit(solution)/shard_map/all_gather | solution.py:138
  311.2 3.4 %copy-start = (bf16[128,16384]{1,0:T(8,128)(2,1)S(1)}, bf16[128,16384]{1,0:T(8,128)(2,1)}, u32[]{:S(2)}) copy-start(bf16[128,16384]{1,0:T(8,128)(2,1)} %all-gather.8.cloned.1.call-done) | copy-start | bytes 12582916
Sparse Core Ops, SparseCore 0:
  9.6 53.2 all-gather.3
  70.7 36.1 all-gather.5
  151.8 106.9 reduce-scatter.1
  260.8 50.3 all-gather.7
where the time goes:
time: 325 us; the launch traced here: 324 us
  waiting for transfers between devices  237 us (73%)
  blocking collectives  20.4 us (6%)
  matrix products  17.6 us (5%)
  other arithmetic  16.4 us (5%)
  between operations  13.4 us (4%)
  starting transfers between devices  10.7 us (3%)
  local copies, waits for them, and re-layouts  8.85 us (3%)
    reduce_scatter x1, waiting for transfers between devices, per_device(): lax.psum_scatter(lax.dot_general(o_weight, attn, (((0,), (1,)), ((), ()))...  107 us
    all_gather x1, waiting for transfers between devices, per_device(): whole_rows = lax.all_gather(residual, 'tp', axis=1, tiled=True)  50.8 us
    all_gather x1, waiting for transfers between devices, per_device(): stream = lax.all_gather(hidden, 'tp', axis=1, tiled=True)  50.6 us
    all_gather x1, blocking collectives, per_device(): lax.all_gather(queries.reshape(token_count, HQ_DEV * HD), 'tp', axis=1, t...  20.4 us
    all_to_all x1, waiting for transfers between devices, per_device(): lax.all_to_all(local_sum.reshape(1, SEQS, heads_all, SPAN, HD), 'tp', spl...  18.8 us
    dot_general x1, matrix products, per_device(): lax.dot_general(o_weight, attn, (((0,), (1,)), ((), ())), preferred_eleme...  6.65 us
  transfers between devices with their start and end apart: 7, of which 6 were waited for; matrix products, arithmetic and copies ran while one was open for 6% of the time, Pallas kernels for 0%

commit v1 on v0

--- a/solution.py
+++ b/solution.py
@@ -1,6 +1,8 @@
 import jax
 import jax.numpy as jnp
 from jax import lax
+from jax.experimental import pallas as pl
+from jax.experimental.pallas import tpu as pltpu
 from jax.sharding import PartitionSpec as P
 
 HD = 128
@@ -9,7 +11,8 @@
 SPAN = 64
 SEQS = 2
 CTX_DEV = 64
-
+TOKENS = SEQS * SPAN
+MIB = 1024 * 1024
 
 epsilon = 1e-05
 
@@ -20,18 +23,331 @@
     return values_f * factor * gain.astype(jnp.float32)
 
 
+def rope_tables(positions):
+    half_width = HD // 2
+    frequency = 500000.0 ** (-jnp.arange(half_width, dtype=jnp.float32) / half_width)
+    angles = positions.astype(jnp.float32)[:, None] * frequency[None, :]
+    return jnp.cos(angles), jnp.sin(angles)
+
+
 def rotate(vectors, positions):
     half_width = vectors.shape[-1] // 2
-    frequency = 500000.0 ** (-jnp.arange(half_width, dtype=jnp.float32) / half_width)
-    angles = positions.astype(jnp.float32)[:, None] * frequency[None, :]
-    cosine = jnp.cos(angles)[:, None, :]
-    sine = jnp.sin(angles)[:, None, :]
+    cosine, sine = rope_tables(positions)
+    cosine, sine = cosine[:, None, :], sine[:, None, :]
     first_half = vectors[..., :half_width]
     second_half = vectors[..., half_width:]
     return jnp.concatenate(
         [first_half * cosine - second_half * sine, second_half * cosine + first_half * sine],
         axis=-1,
     )
+
+
+CHIPS = 8
+RING = (0, 2, 4, 6, 7, 5, 3, 1)
+FORTH = [(2 * RING[i] + c, 2 * RING[(i + 1) % CHIPS] + c) for i in range(CHIPS) for c in range(2)]
+BACK = [(b, a) for a, b in FORTH]
+SWAP = [(t, t ^ 1) for t in range(2 * CHIPS)]
+STRAIGHT = [(k, 2 * k) for k in range(KVH)] + [(KVH + k, 2 * k + 1) for k in range(KVH)]
+CROSSED = [(k, 2 * k + 1) for k in range(KVH)] + [(KVH + k, 2 * k) for k in range(KVH)]
+
+
+def ring_place(rank):
+    chip = rank // 2
+    return jnp.where(chip % 2 == 0, chip // 2, CHIPS - 1 - chip // 2)
+
+
+def chip_at(place):
+    place = place % CHIPS
+    return jnp.where(place < CHIPS // 2, 2 * place, 2 * CHIPS - 1 - 2 * place)
+
+
+def send(array, pairs):
+    return lax.ppermute(array, "tp", pairs)
+
+
+OFFSETS = (0, -1, 1, -2, 2, -3, 3, 4)
+
+
+def ring_gather(halves):
+    forth, back = list(halves), list(halves)
+    got = [{0: halves[0]}, {0: halves[1]}]
+    for step in range(1, 5):
+        for h in range(2):
+            if step < 4 or h == 0:
+                forth[h] = send(forth[h], FORTH)
+                got[h][-step if step < 4 else 4] = forth[h]
+            if step < 4 or h == 1:
+                back[h] = send(back[h], BACK)
+                got[h][step] = back[h]
+    out = []
+    for offset in OFFSETS:
+        own = [got[h][offset] for h in range(2)]
+        other = [send(a, SWAP) for a in own]
+        out += [own, other]
+    return out
+
+
+def block_ids(rank):
+    place, core = ring_place(rank), rank % 2
+    ids = []
+    for offset in OFFSETS:
+        chip = chip_at(place + offset)
+        ids += [2 * chip + core, 2 * chip + 1 - core]
+    return jnp.stack(ids).astype(jnp.int32)
+
+
+def scatter_add(parts):
+    narrow = lambda a: a.astype(jnp.bfloat16)
+    totals = []
+    for h in range(2):
+        forth_len, back_len = (4, 3) if h == 0 else (3, 4)
+        sums = []
+        for length, pairs, sign in ((forth_len, FORTH, 1), (back_len, BACK, -1)):
+            running = send(narrow(parts[sign * length if length < 4 else 4][h]), pairs)
+            for distance in range(length - 1, 0, -1):
+                mine = parts[sign * distance][h]
+                running = send(narrow(running.astype(jnp.float32) + mine), pairs)
+            sums.append(running.astype(jnp.float32))
+        totals.append(sums[0] + sums[1])
+    return totals
+
+
+def project_kernel(ids, *refs):
+    blocks = refs[:32]
+    gain, cosine, sine, kv_cos, kv_sin, wq, wkv = refs[32:39]
+    q_out, kv_out = refs[39:41]
+    wq_buf, wkv_buf, sems = refs[41:]
+    width = blocks[0].shape[1]
+    copies = []
+    for i in range(16):
+        rows = pl.ds(pl.multiple_of(ids[i] * width, width), width)
+        pair = (
+            pltpu.make_async_copy(wq.at[rows, :], wq_buf.at[i], sems.at[0, i]),
+            pltpu.make_async_copy(wkv.at[rows, :], wkv_buf.at[i], sems.at[1, i]),
+        )
+        for copy in pair:
+            copy.start()
+        copies.append(pair)
+    factors = []
+    for h in range(2):
+        squares = jnp.zeros((SPAN, 128), jnp.float32)
+        for i in range(16):
+            for j in range(width // 128):
+                v = blocks[2 * i + h][:, j * 128 : (j + 1) * 128].astype(jnp.float32)
+                squares = squares + v * v
+        mean = jnp.sum(squares, axis=1, keepdims=True) * (1.0 / (16 * width))
+        factors.append(lax.rsqrt(mean + epsilon))
+    total = jnp.zeros((TOKENS, 2 * HD), jnp.float32)
+    for i in range(16):
+        gain_row = gain[ids[i]]
+        rows = [
+            (blocks[2 * i + h][...].astype(jnp.float32) * factors[h] * gain_row).astype(jnp.bfloat16)
+            for h in range(2)
+        ]
+        for copy in copies[i]:
+            copy.wait()
+        weights = jnp.concatenate([wq_buf[i], wkv_buf[i]], axis=1)
+        total = total + jnp.dot(
+            jnp.concatenate(rows, axis=0), weights, preferred_element_type=jnp.float32
+        )
+    q, kv = total[:, :HD], total[:, HD:]
+    q_out[...] = (q * cosine[...] + pltpu.roll(q, HD // 2, 1) * sine[...]).astype(jnp.bfloat16)
+    kv_out[...] = (kv * kv_cos[...] + pltpu.roll(kv, HD // 2, 1) * kv_sin[...]).astype(jnp.bfloat16)
+
+
+def project(ids, blocks, gain, tables, q_weight, kv_weight):
+    width = blocks[0].shape[1]
+    vmem = pl.BlockSpec(memory_space=pltpu.VMEM)
+    return pl.pallas_call(
+        project_kernel,
+        out_shape=[jax.ShapeDtypeStruct((TOKENS, HD), jnp.bfloat16)] * 2,
+        in_specs=[pl.BlockSpec(memory_space=pltpu.SMEM)]
+        + [vmem] * 37
+        + [pl.BlockSpec(memory_space=pl.ANY)] * 2,
+        out_specs=[vmem] * 2,
+        scratch_shapes=[
+            pltpu.VMEM((16, width, HD), jnp.bfloat16),
+            pltpu.VMEM((16, width, HD), jnp.bfloat16),
+            pltpu.SemaphoreType.DMA((2, 16)),
+        ],
+        compiler_params=pltpu.CompilerParams(vmem_limit_bytes=32 * MIB),
+        name="norm_project",
+    )(ids, *blocks, gain, *tables, q_weight, kv_weight)
+
+
+def attend_kernel(info, q, first, second, keys, values, out):
+    even = info[2] == 0
+    fresh_keys = jnp.where(even, first[...], second[...])
+    fresh_values = jnp.where(even, second[...], first[...])
+    scale = HD ** (-0.5)
+    context = keys.shape[0] * keys.shape[2]
+    contract = (((1,), (1,)), ((), ()))
+    for s in range(SEQS):
+        rows = slice(s * SPAN, (s + 1) * SPAN)
+        queries = q[rows, :]
+        old_keys = keys[:, s].reshape(context, HD)
+        old_values = values[:, s].reshape(context, HD)
+        old = lax.dot_general(queries, old_keys, contract, preferred_element_type=jnp.float32) * scale
+        fresh = (
+            lax.dot_general(queries, fresh_keys[rows], contract, preferred_element_type=jnp.float32)
+            * scale
+        )
+        valid = lax.broadcasted_iota(jnp.int32, old.shape, 1) < info[s]
+        causal = lax.broadcasted_iota(jnp.int32, fresh.shape, 0) >= lax.broadcasted_iota(
+            jnp.int32, fresh.shape, 1
+        )
+        old = jnp.where(valid, old, -1e30)
+        fresh = jnp.where(causal, fresh, -1e30)
+        most = jnp.maximum(
+            jnp.max(old, axis=1, keepdims=True), jnp.max(fresh, axis=1, keepdims=True)
+        )
+        old_weights = jnp.where(valid, jnp.exp(old - most), 0.0)
+        fresh_weights = jnp.where(causal, jnp.exp(fresh - most), 0.0)
+        totals = jnp.sum(old_weights, axis=1, keepdims=True) + jnp.sum(
+            fresh_weights, axis=1, keepdims=True
+        )
+        summed = jnp.dot(
+            old_weights.astype(jnp.bfloat16), old_values, preferred_element_type=jnp.float32
+        ) + jnp.dot(
+            fresh_weights.astype(jnp.bfloat16), fresh_values[rows], preferred_element_type=jnp.float32
+        )
+        out[rows, :] = (summed / totals).astype(jnp.bfloat16)
+
+
+def attend(info, q, first, second, keys, values):
+    vmem = pl.BlockSpec(memory_space=pltpu.VMEM)
+    return pl.pallas_call(
+        attend_kernel,
+        out_shape=jax.ShapeDtypeStruct((TOKENS, HD), jnp.bfloat16),
+        in_specs=[pl.BlockSpec(memory_space=pltpu.SMEM)] + [vmem] * 5,
+        out_specs=vmem,
+        compiler_params=pltpu.CompilerParams(vmem_limit_bytes=24 * MIB),
+        name="attend",
+    )(info, q, first, second, keys, values)
+
+
+def output_kernel(chips, attn, other, weight, other_weight, out):
+    left = jnp.concatenate([attn[...], other[...]], axis=1)
+    right = jnp.concatenate([weight[0], other_weight[0]], axis=0)
+    out[0] = jnp.dot(left, right, preferred_element_type=jnp.float32)
+
+
+def output_shares(chips, attn, other, weight, other_weight):
+    width = weight.shape[2]
+    whole = pl.BlockSpec((TOKENS, HD), lambda i, chips: (0, 0))
+    block = pl.BlockSpec((1, HD, width), lambda i, chips: (chips[i], 0, 0))
+    return pl.pallas_call(
+        output_kernel,
+        out_shape=jax.ShapeDtypeStruct((CHIPS, TOKENS, width), jnp.float32),
+        grid_spec=pltpu.PrefetchScalarGridSpec(
+            num_scalar_prefetch=1,
+            grid=(CHIPS,),
+            in_specs=[whole, whole, block, block],
+            out_specs=pl.BlockSpec((1, TOKENS, width), lambda i, chips: (i, 0, 0)),
+        ),
+        compiler_params=pltpu.CompilerParams(vmem_limit_bytes=24 * MIB),
+        name="output_shares",
+    )(chips, attn, other, weight, other_weight)
+
+
+def final_kernel(ids, *refs):
+    blocks, gain, out = refs[:32], refs[32], refs[33]
+    staged, sems = refs[34:]
+    width = blocks[0].shape[1]
+    factors = []
+    for h in range(2):
+        squares = jnp.zeros((SPAN, 128), jnp.float32)
+        for i in range(16):
+            for j in range(width // 128):
+                v = blocks[2 * i + h][:, j * 128 : (j + 1) * 128].astype(jnp.float32)
+                squares = squares + v * v
+        mean = jnp.sum(squares, axis=1, keepdims=True) * (1.0 / (16 * width))
+        factors.append(lax.rsqrt(mean + epsilon))
+    copies = []
+    for i in range(16):
+        gain_row = gain[ids[i]]
+        for h in range(2):
+            staged[i, h * SPAN : (h + 1) * SPAN, :] = (
+                blocks[2 * i + h][...].astype(jnp.float32) * factors[h] * gain_row
+            ).astype(jnp.bfloat16)
+        copy = pltpu.make_async_copy(
+            staged.at[i],
+            out.at[:, pl.ds(pl.multiple_of(ids[i] * width, width), width)],
+            sems.at[i],
+        )
+        copy.start()
+        copies.append(copy)
+    for copy in copies:
+        copy.wait()
+
+
+def final_norm(ids, blocks, gain):
+    width = blocks[0].shape[1]
+    vmem = pl.BlockSpec(memory_space=pltpu.VMEM)
+    return pl.pallas_call(
+        final_kernel,
+        out_shape=jax.ShapeDtypeStruct((TOKENS, 16 * width), jnp.bfloat16),
+        in_specs=[pl.BlockSpec(memory_space=pltpu.SMEM)] + [vmem] * 33,
+        out_specs=pl.BlockSpec(memory_space=pl.ANY),
+        scratch_shapes=[
+            pltpu.VMEM((16, TOKENS, width), jnp.bfloat16),
+            pltpu.SemaphoreType.DMA((16,)),
+        ],
+        compiler_params=pltpu.CompilerParams(vmem_limit_bytes=32 * MIB),
+        name="final_norm",
+    )(ids, *blocks, gain)
+
+
+def per_device_ring(
+    residual, attn_gain, ffn_gain, q_weight, kv_weight, o_weight, key_cache, value_cache, prefix
+):
+    rank = lax.axis_index("tp")
+    core = rank % 2
+    width = residual.shape[1]
+    ids = block_ids(rank)
+
+    by_head = lambda cache: jnp.transpose(cache.reshape(SEQS, CTX_DEV, KVH, HD), (2, 0, 1, 3))
+    pieces = jnp.stack([by_head(key_cache), by_head(value_cache)], axis=1)
+    pieces = pieces.reshape(2 * KVH, SEQS, CTX_DEV, HD)
+    mine = lax.all_to_all(pieces, "tp", split_axis=0, concat_axis=0, tiled=True)
+    theirs = send(mine, SWAP)
+    keys = jnp.where(core == 0, mine, theirs)
+    values = jnp.where(core == 0, theirs, mine)
+
+    columns = o_weight.reshape(HD, CHIPS, 2, width)
+    o_mine = jnp.transpose(lax.dynamic_index_in_dim(columns, core, 2, keepdims=False), (1, 0, 2))
+    o_sent = jnp.transpose(lax.dynamic_index_in_dim(columns, 1 - core, 2, keepdims=False), (1, 0, 2))
+    o_other = send(o_sent, SWAP)
+
+    positions = (prefix[:, None] + jnp.arange(SPAN, dtype=jnp.int32)[None, :]).reshape(-1)
+    cosine, sine = rope_tables(positions)
+    cosine = jnp.concatenate([cosine, cosine], axis=1)
+    sine = jnp.concatenate([-sine, sine], axis=1)
+    holds_keys = rank < KVH
+    tables = (cosine, sine, jnp.where(holds_keys, cosine, 1.0), jnp.where(holds_keys, sine, 0.0))
+
+    blocks = [a for pair in ring_gather([residual[:SPAN], residual[SPAN:]]) for a in pair]
+    queries, fresh = project(
+        ids, blocks, attn_gain.reshape(16, 1, width).astype(jnp.float32), tables, q_weight, kv_weight
+    )
+    first, second = send(fresh, STRAIGHT), send(fresh, CROSSED)
+    info = jnp.concatenate([prefix, core[None].astype(jnp.int32)])
+    attn = attend(info, queries, first, second, keys, values)
+
+    chips = jnp.stack([chip_at(ring_place(rank) + o) for o in OFFSETS]).astype(jnp.int32)
+    shares = output_shares(chips, attn, send(attn, SWAP), o_mine, o_other)
+    parts = {
+        o: [shares[i, :SPAN], shares[i, SPAN:]] for i, o in enumerate(OFFSETS)
+    }
+    others = scatter_add(parts)
+    hidden = [
+        (residual[h * SPAN : (h + 1) * SPAN].astype(jnp.float32) + (parts[0][h] + others[h])).astype(
+            jnp.bfloat16
+        )
+        for h in range(2)
+    ]
+    blocks = [a for pair in ring_gather(hidden) for a in pair]
+    return final_norm(ids, blocks, ffn_gain.reshape(16, 1, width).astype(jnp.float32))
 
 
 def per_device(
@@ -141,7 +457,7 @@
 
 def solution(mesh):
     return jax.shard_map(
-        per_device,
+        per_device_ring if mesh.shape["tp"] == 2 * CHIPS else per_device,
         mesh=mesh,
         in_specs=(
             P("replica", "tp"),

time: 325 us -> 185 us (0.57)
  waiting for transfers between devices: 237 us -> 60.1 us
  starting transfers between devices: 10.7 us -> 63.4 us
  local copies, waits for them, and re-layouts: 8.85 us -> 37.2 us
  blocking collectives: 20.4 us -> 0 us
  matrix products: 17.6 us -> 0 us
  Pallas kernels: 0 us -> 17.4 us
  between operations: 13.4 us -> 0.64 us
  other arithmetic: 16.4 us -> 5.86 us
    reduce_scatter x1 -> x0, waiting for transfers between devices: 107 us -> none  [per_device(): lax.psum_scatter(lax.dot_general(o_weight, attn, (((0,), (1,)), ((), ()))...]
    all_gather x3 -> x0, waiting for transfers between devices: 101 us -> none  [the longest x1 50.8 us: per_device(): whole_rows = lax.all_gather(residual, 'tp', axis=1, tiled=True)]
    ppermute x0 -> x79, waiting for transfers between devices: none -> 60.1 us  [send(): return lax.ppermute(array, 'tp', pairs)]
    ppermute x0 -> x79, starting transfers between devices: none -> 56.3 us  [send(): return lax.ppermute(array, 'tp', pairs)]
    all_to_all x3 -> x1, waiting for transfers between devices: 27.6 us -> 0.01 us  [per_device_ring(): mine = lax.all_to_all(pieces, 'tp', split_axis=0, concat_axis=0, tiled=True)]
    all_gather x1 -> x0, blocking collectives: 20.4 us -> none  [per_device(): lax.all_gather(queries.reshape(token_count, HQ_DEV * HD), 'tp', axis=1, t...]
    dot_general x7 -> x0, matrix products: 17.6 us -> none  [the longest x1 6.65 us: per_device(): lax.dot_general(o_weight, attn, (((0,), (1,)), ((), ())), preferred_eleme...]
    pallas_call x0 -> x4, Pallas kernels: none -> 17.4 us  [the longest x1 6.79 us: project(): pl.pallas_call(project_kernel, out_shape=[jax.ShapeDtypeStruct((TOKENS, H...]
  transfers between devices with their start and end apart: 7 -> 80, of which waited for: 6 -> 41; matrix products, arithmetic and copies ran while one was open for 6% -> 4% of each run, Pallas kernels for 0% -> 4%
where the time goes in v1:
time: 185 us
  starting transfers between devices  63.4 us (34%)
  waiting for transfers between devices  60.1 us (32%)
  local copies, waits for them, and re-layouts  37.2 us (20%)
  Pallas kernels  17.4 us (9%)
  other arithmetic  5.86 us (3%)
    ppermute x79, waiting for transfers between devices, send(): return lax.ppermute(array, 'tp', pairs)  60.1 us
    ppermute x79, starting transfers between devices, send(): return lax.ppermute(array, 'tp', pairs)  56.3 us
    unnamed x32, local copies, waits for them, and re-layouts  14.8 us
    dynamic_slice x1, local copies, waits for them, and re-layouts, per_device_ring(): lax.dynamic_index_in_dim(columns, 1 - core, 2, keepdims=False)  14.1 us
    reshape x1, local copies, waits for them, and re-layouts, per_device_ring(): columns = o_weight.reshape(HD, CHIPS, 2, width)  7.82 us
    all_to_all x1, starting transfers between devices, per_device_ring(): mine = lax.all_to_all(pieces, 'tp', split_axis=0, concat_axis=0, tiled=True)  7.07 us
    pallas_call x1, Pallas kernels, project(): pl.pallas_call(project_kernel, out_shape=[jax.ShapeDtypeStruct((TOKENS, H...  6.79 us
    pallas_call x1, Pallas kernels, output_shares(): pl.pallas_call(output_kernel, out_shape=jax.ShapeDtypeStruct((CHIPS, TOKE...  5.62 us
  transfers between devices with their start and end apart: 80, of which 41 were waited for; matrix products, arithmetic and copies ran while one was open for 4% of the time, Pallas kernels for 4%

profile of v1, /device:TPU:0, one launch (start us, length us, event | category | flops | bytes accessed | tf_op | source)
XLA Modules:
  0.0 184.6 jit_solution(2686479490684759524)
XLA Ops:
  0.0 7.8 %reshape.71 = bf16[128,8,2,1024]{3,2,1,0:T(2,128)(2,1)} reshape(bf16[128,16384]{1,0:T(8,128)(2,1)} %param.14) | data formatting | bytes 8388608 | tf_op jit(solution)/shard_map/reshape | solution.py:317
  7.8 14.1 %constant_dynamic-slice_fusion = (bf16[128,8,1,1024]{3,2,1,0:T(2,128)(2,1)S(1)}, bf16[128,8,1,1024]{3,2,1,0:T(2,128)(2,1)}) fusion(bf16[128,8,2,1024]{3,2,1,0:T(2,128)(2,1)} %reshape.71, s32[]{:T(128)S(6)} %select_n.211, s32[]{:T(128)S(6)} %select_n.210), kind=kLoop, calls=%fused_computation.59 | loop fusion | bytes 8388616 | tf_op jit(solution)/shard_map/jit(dynamic_index_in_dim)/dynamic_slice | solution.py:319
  21.9 3.6 %copy.22 = bf16[128,8,1,1024]{3,0,1,2:T(8,128)(2,1)} copy(bf16[128,8,1,1024]{3,2,1,0:T(2,128)(2,1)S(1)} %get-tuple-element.23) | data formatting | bytes 4194304
  27.0 7.1 %all-to-all-start = ((bf16[16,2,64,128]{3,2,1,0:T(8,128)(2,1)}), bf16[16,2,64,128]{3,2,1,0:T(8,128)(2,1)}, u32[]{:S(2)}, u32[]{:S(2)}) async-start(bf16[16,2,64,128]{3,2,1,0:T(8,128)(2,1)} %bitcast.30), calls=%async_computation | async-start | bytes 1048576 | tf_op jit(solution)/shard_map/all_to_all | solution.py:312
  38.2 8.3 %collective-permute-done.2.refs_4_ = bf16[64,1024]{1,0:T(8,128)(2,1)S(1)} collective-permute-done((bf16[64,1024]{1,0:T(8,128)(2,1)S(1)}, bf16[64,1024]{1,0:T(8,128)(2,1)S(1)}, u32[]{:S(2)}, u32[]{:S(2)}) %collective-permute-start.2) | collective-permute-done | bytes 131104 | tf_op jit(solution)/shard_map/ppermute | solution.py:65
  46.5 2.3 %collective-permute-done.7.refs_9_ = bf16[64,1024]{1,0:T(8,128)(2,1)S(1)} collective-permute-done((bf16[64,1024]{1,0:T(8,128)(2,1)S(1)}, bf16[64,1024]{1,0:T(8,128)(2,1)S(1)}, u32[]{:S(2)}, u32[]{:S(2)}) %collective-permute-start.7) | collective-permute-done | bytes 131104 | tf_op jit(solution)/shard_map/ppermute | solution.py:65
  49.1 4.5 %collective-permute-start.10 = (bf16[64,1024]{1,0:T(8,128)(2,1)S(1)}, bf16[64,1024]{1,0:T(8,128)(2,1)S(1)}, u32[]{:S(2)}, u32[]{:S(2)}) collective-permute-start(bf16[64,1024]{1,0:T(8,128)(2,1)S(1)} %collective-permute-done.2.refs_4_), channel_id=1, source_target_pairs={{0,4},{1,5},{4,8},{5,9},{8,12},{9,13},{12,14},{13,15},{14,10},{15,... | collective-permute-start | bytes 393224 | tf_op jit(solution)/shard_map/ppermute | solution.py:65
  53.6 2.5 %collective-permute-start.11 = (bf16[64,1024]{1,0:T(8,128)(2,1)S(1)}, bf16[64,1024]{1,0:T(8,128)(2,1)S(1)}, u32[]{:S(2)}, u32[]{:S(2)}) collective-permute-start(bf16[64,1024]{1,0:T(8,128)(2,1)S(1)} %collective-permute-done.3.refs_5_), channel_id=1, source_target_pairs={{0,4},{1,5},{4,8},{5,9},{8,12},{9,13},{12,14},{13,15},{14,10},{15,... | collective-permute-start | bytes 393224 | tf_op jit(solution)/shard_map/ppermute | solution.py:65
  57.5 2.9 %collective-permute-done.15.refs_17_ = bf16[64,1024]{1,0:T(8,128)(2,1)S(1)} collective-permute-done((bf16[64,1024]{1,0:T(8,128)(2,1)S(1)}, bf16[64,1024]{1,0:T(8,128)(2,1)S(1)}, u32[]{:S(2)}, u32[]{:S(2)}) %collective-permute-start.15) | collective-permute-done | bytes 131104 | tf_op jit(solution)/shard_map/ppermute | solution.py:65
  74.9 3.3 %collective-permute-done.26.refs_28_ = bf16[64,1024]{1,0:T(8,128)(2,1)} collective-permute-done((bf16[64,1024]{1,0:T(8,128)(2,1)S(1)}, bf16[64,1024]{1,0:T(8,128)(2,1)}, u32[]{:S(2)}, u32[]{:S(2)}) %collective-permute-start.26) | collective-permute-done | bytes 131104 | tf_op jit(solution)/shard_map/ppermute | solution.py:65
  91.6 6.8 %norm_project.1 = (bf16[128,128]{1,0:T(8,128)(2,1)S(1)}, bf16[128,128]{1,0:T(8,128)(2,1)S(1)}) custom-call(s32[16]{0:T(128)S(1)} %stack.103.ids, bf16[64,1024]{1,0:T(8,128)(2,1)S(1)} %get-tuple-element.32.refs_0_, bf16[64,1024]{1,0:T(8,128)(2,1)S(1)} %get-tuple-element.31.refs_1_, bf16[64,1024]{1,0:T(8,128)(2,1)S(1)} %collective-permute-done.refs_2_, ...), custom_call_target="tpu_custom_call" | custom-call | tf_op jit(solution)/shard_map/norm_project/pallas_call | solution.py:161
  99.0 2.8 %collective-permute-start.31 = (bf16[128,128]{1,0:T(8,128)(2,1)S(1)}, bf16[128,128]{1,0:T(8,128)(2,1)S(1)}, u32[]{:S(2)}, u32[]{:S(2)}) collective-permute-start(bf16[128,128]{1,0:T(8,128)(2,1)S(1)} %get-tuple-element.8), channel_id=1, source_target_pairs={{0,1},{1,3},{2,5},{3,7},{4,9},{5,11},{6,13},{7,15},{8,0},{9,2},{10... | collective-permute-start | bytes 98312 | tf_op jit(solution)/shard_map/ppermute | solution.py:65
  103.2 2.5 %collective-permute-done.31.second = bf16[128,128]{1,0:T(8,128)(2,1)S(1)} collective-permute-done((bf16[128,128]{1,0:T(8,128)(2,1)S(1)}, bf16[128,128]{1,0:T(8,128)(2,1)S(1)}, u32[]{:S(2)}, u32[]{:S(2)}) %collective-permute-start.31) | collective-permute-done | bytes 32800 | tf_op jit(solution)/shard_map/ppermute | solution.py:65
  107.1 2.2 %copy.23 = bf16[128,8,1,1024]{3,0,1,2:T(8,128)(2,1)S(1)} copy(bf16[128,8,1,1024]{3,2,1,0:T(2,128)(2,1)S(1)} %copy-done.9) | data formatting | bytes 4194304
  109.4 5.6 %output_shares.1 = f32[8,128,1024]{2,1,0:T(8,128)S(1)} custom-call(s32[8]{0:T(128)S(1)} %stack.112.chips, bf16[128,128]{1,0:T(8,128)(2,1)S(1)} %attend.1.attn, bf16[128,128]{1,0:T(8,128)(2,1)S(1)} %collective-permute-done.33.other, bf16[8,128,1024]{2,1,0:T(8,128)(2,1)S(1)} %bitcast.140, bf16[8,128,1024]{2,1,0:T(8,128)(2,1)} %collective-permute-done.34.other_weight), custom_call_target="tpu_custom_call" | custom-call | tf_op jit(solution)/shard_map/output_shares/pallas_call | solution.py:239
  115.5 2.3 %collective-permute-start.35 = (bf16[64,1024]{1,0:T(8,128)(2,1)S(1)}, bf16[64,1024]{1,0:T(8,128)(2,1)S(1)}, u32[]{:S(2)}, u32[]{:S(2)}) collective-permute-start(bf16[64,1024]{1,0:T(8,128)(2,1)S(1)} %get-tuple-element.28), channel_id=1, source_target_pairs={{0,4},{1,5},{4,8},{5,9},{8,12},{9,13},{12,14},{13,15},{14,10},{15,... | collective-permute-start | bytes 393224 | tf_op jit(solution)/shard_map/ppermute | solution.py:65
  121.8 2.3 %collective-permute-done.45 = bf16[64,1024]{1,0:T(8,128)(2,1)S(1)} collective-permute-done((bf16[64,1024]{1,0:T(8,128)(2,1)S(1)}, bf16[64,1024]{1,0:T(8,128)(2,1)S(1)}, u32[]{:S(2)}, u32[]{:S(2)}) %collective-permute-start.45) | collective-permute-done | bytes 131104 | tf_op jit(solution)/shard_map/ppermute | solution.py:65
  126.3 2.9 %collective-permute-done.36 = bf16[64,1024]{1,0:T(8,128)(2,1)S(1)} collective-permute-done((bf16[64,1024]{1,0:T(8,128)(2,1)S(1)}, bf16[64,1024]{1,0:T(8,128)(2,1)S(1)}, u32[]{:S(2)}, u32[]{:S(2)}) %collective-permute-start.36) | collective-permute-done | bytes 131104 | tf_op jit(solution)/shard_map/ppermute | solution.py:65
  137.6 2.8 %collective-permute-done.47 = bf16[64,1024]{1,0:T(8,128)(2,1)S(1)} collective-permute-done((bf16[64,1024]{1,0:T(8,128)(2,1)S(1)}, bf16[64,1024]{1,0:T(8,128)(2,1)S(1)}, u32[]{:S(2)}, u32[]{:S(2)}) %collective-permute-start.47) | collective-permute-done | bytes 131104 | tf_op jit(solution)/shard_map/ppermute | solution.py:65
  146.7 2.7 %collective-permute-done.44 = bf16[64,1024]{1,0:T(8,128)(2,1)S(1)} collective-permute-done((bf16[64,1024]{1,0:T(8,128)(2,1)S(1)}, bf16[64,1024]{1,0:T(8,128)(2,1)S(1)}, u32[]{:S(2)}, u32[]{:S(2)}) %collective-permute-start.44) | collective-permute-done | bytes 131104 | tf_op jit(solution)/shard_map/ppermute | solution.py:65
  149.8 2.2 %collective-permute-start.56 = (bf16[64,1024]{1,0:T(8,128)(2,1)S(1)}, bf16[64,1024]{1,0:T(8,128)(2,1)S(1)}, u32[]{:S(2)}, u32[]{:S(2)}) collective-permute-start(bf16[64,1024]{1,0:T(8,128)(2,1)S(1)} %get-tuple-element.11.refs_1_), channel_id=1, source_target_pairs={{4,0},{5,1},{8,4},{9,5},{12,8},{13,9},{14,12},{15,13},{10,14},{11,... | collective-permute-start | bytes 393224 | tf_op jit(solution)/shard_map/ppermute | solution.py:65
  168.2 2.2 %collective-permute-done.67.refs_20_ = bf16[64,1024]{1,0:T(8,128)(2,1)S(1)} collective-permute-done((bf16[64,1024]{1,0:T(8,128)(2,1)S(1)}, bf16[64,1024]{1,0:T(8,128)(2,1)S(1)}, u32[]{:S(2)}, u32[]{:S(2)}) %collective-permute-start.67) | collective-permute-done | bytes 131104 | tf_op jit(solution)/shard_map/ppermute | solution.py:65
  175.4 3.1 %collective-permute-done.75.refs_28_ = bf16[64,1024]{1,0:T(8,128)(2,1)S(1)} collective-permute-done((bf16[64,1024]{1,0:T(8,128)(2,1)S(1)}, bf16[64,1024]{1,0:T(8,128)(2,1)S(1)}, u32[]{:S(2)}, u32[]{:S(2)}) %collective-permute-start.75) | collective-permute-done | bytes 131104 | tf_op jit(solution)/shard_map/ppermute | solution.py:65
  180.8 3.6 %final_norm.1 = bf16[128,16384]{1,0:T(8,128)(2,1)} custom-call(s32[16]{0:T(128)S(1)} %stack.103.ids, bf16[64,1024]{1,0:T(8,128)(2,1)S(1)} %get-tuple-element.12.refs_0_, bf16[64,1024]{1,0:T(8,128)(2,1)S(1)} %get-tuple-element.11.refs_1_, bf16[64,1024]{1,0:T(8,128)(2,1)S(1)} %collective-permute-done.49.refs_2_, ...), custom_call_target="tpu_custom_call" | custom-call | tf_op jit(solution)/shard_map/final_norm/pallas_call | solution.py:287
  (194 shorter events, 83.5 us)
Async XLA Ops:
  25.5 84.0 %collective-permute-start.34 = (bf16[8,128,1024]{2,1,0:T(8,128)(2,1)}, bf16[8,128,1024]{2,1,0:T(8,128)(2,1)}, u32[]{:S(2)}, u32[]{:S(2)}) collective-permute-start(bf16[8,128,1024]{2,1,0:T(8,128)(2,1)} %bitcast.138), channel_id=1, source_target_pairs={{0,1},{1,0},{2,3},{3,2},{4,5},{5,4},{6,7},{7,6},{8,9},{9,8},{10,11... | collective-permute-start | bytes 6291464 | tf_op jit(solution)/shard_map/ppermute | solution.py:65
  27.0 47.3 %all-to-all-start = ((bf16[16,2,64,128]{3,2,1,0:T(8,128)(2,1)}), bf16[16,2,64,128]{3,2,1,0:T(8,128)(2,1)}, u32[]{:S(2)}, u32[]{:S(2)}) async-start(bf16[16,2,64,128]{3,2,1,0:T(8,128)(2,1)} %bitcast.30), calls=%async_computation | async-start | bytes 1048576 | tf_op jit(solution)/shard_map/all_to_all | solution.py:312
  34.1 12.4 %collective-permute-start.2 = (bf16[64,1024]{1,0:T(8,128)(2,1)S(1)}, bf16[64,1024]{1,0:T(8,128)(2,1)S(1)}, u32[]{:S(2)}, u32[]{:S(2)}) collective-permute-start(bf16[64,1024]{1,0:T(8,128)(2,1)S(1)} %get-tuple-element.32.refs_0_), channel_id=1, source_target_pairs={{0,4},{1,5},{4,8},{5,9},{8,12},{9,13},{12,14},{13,15},{14,10},{15,... | collective-permute-start | bytes 393224 | tf_op jit(solution)/shard_map/ppermute | solution.py:65
  36.0 12.8 %collective-permute-start.7 = (bf16[64,1024]{1,0:T(8,128)(2,1)S(1)}, bf16[64,1024]{1,0:T(8,128)(2,1)S(1)}, u32[]{:S(2)}, u32[]{:S(2)}) collective-permute-start(bf16[64,1024]{1,0:T(8,128)(2,1)S(1)} %get-tuple-element.31.refs_1_), channel_id=1, source_target_pairs={{4,0},{5,1},{8,4},{9,5},{12,8},{13,9},{14,12},{15,13},{10,14},{11,... | collective-permute-start | bytes 393224 | tf_op jit(solution)/shard_map/ppermute | solution.py:65
  36.1 13.0 %collective-permute-start.3 = (bf16[64,1024]{1,0:T(8,128)(2,1)S(1)}, bf16[64,1024]{1,0:T(8,128)(2,1)S(1)}, u32[]{:S(2)}, u32[]{:S(2)}) collective-permute-start(bf16[64,1024]{1,0:T(8,128)(2,1)S(1)} %get-tuple-element.31.refs_1_), channel_id=1, source_target_pairs={{0,4},{1,5},{4,8},{5,9},{8,12},{9,13},{12,14},{13,15},{14,10},{15,... | collective-permute-start | bytes 393224 | tf_op jit(solution)/shard_map/ppermute | solution.py:65
  38.0 15.6 %collective-permute-start.6 = (bf16[64,1024]{1,0:T(8,128)(2,1)S(1)}, bf16[64,1024]{1,0:T(8,128)(2,1)S(1)}, u32[]{:S(2)}, u32[]{:S(2)}) collective-permute-start(bf16[64,1024]{1,0:T(8,128)(2,1)S(1)} %get-tuple-element.32.refs_0_), channel_id=1, source_target_pairs={{4,0},{5,1},{8,4},{9,5},{12,8},{13,9},{14,12},{15,13},{10,14},{11,... | collective-permute-start | bytes 393224 | tf_op jit(solution)/shard_map/ppermute | solution.py:65
  46.5 7.1 %collective-permute-start = (bf16[64,1024]{1,0:T(8,128)(2,1)S(1)}, bf16[64,1024]{1,0:T(8,128)(2,1)S(1)}, u32[]{:S(2)}, u32[]{:S(2)}) collective-permute-start(bf16[64,1024]{1,0:T(8,128)(2,1)S(1)} %get-tuple-element.32.refs_0_), channel_id=1, source_target_pairs={{0,1},{1,0},{2,3},{3,2},{4,5},{5,4},{6,7},{7,6},{8,9},{9,8},{10,11... | collective-permute-start | bytes 393224 | tf_op jit(solution)/shard_map/ppermute | solution.py:65
  48.8 7.3 %collective-permute-start.1 = (bf16[64,1024]{1,0:T(8,128)(2,1)S(1)}, bf16[64,1024]{1,0:T(8,128)(2,1)S(1)}, u32[]{:S(2)}, u32[]{:S(2)}) collective-permute-start(bf16[64,1024]{1,0:T(8,128)(2,1)S(1)} %get-tuple-element.31.refs_1_), channel_id=1, source_target_pairs={{0,1},{1,0},{2,3},{3,2},{4,5},{5,4},{6,7},{7,6},{8,9},{9,8},{10,11... | collective-permute-start | bytes 393224 | tf_op jit(solution)/shard_map/ppermute | solution.py:65
  49.1 8.3 %collective-permute-start.10 = (bf16[64,1024]{1,0:T(8,128)(2,1)S(1)}, bf16[64,1024]{1,0:T(8,128)(2,1)S(1)}, u32[]{:S(2)}, u32[]{:S(2)}) collective-permute-start(bf16[64,1024]{1,0:T(8,128)(2,1)S(1)} %collective-permute-done.2.refs_4_), channel_id=1, source_target_pairs={{0,4},{1,5},{4,8},{5,9},{8,12},{9,13},{12,14},{13,15},{14,10},{15,... | collective-permute-start | bytes 393224 | tf_op jit(solution)/shard_map/ppermute | solution.py:65
  53.6 6.8 %collective-permute-start.15 = (bf16[64,1024]{1,0:T(8,128)(2,1)S(1)}, bf16[64,1024]{1,0:T(8,128)(2,1)S(1)}, u32[]{:S(2)}, u32[]{:S(2)}) collective-permute-start(bf16[64,1024]{1,0:T(8,128)(2,1)S(1)} %collective-permute-done.7.refs_9_), channel_id=1, source_target_pairs={{4,0},{5,1},{8,4},{9,5},{12,8},{13,9},{14,12},{15,13},{10,14},{11,... | collective-permute-start | bytes 393224 | tf_op jit(solution)/shard_map/ppermute | solution.py:65
  53.6 6.8 %collective-permute-start.11 = (bf16[64,1024]{1,0:T(8,128)(2,1)S(1)}, bf16[64,1024]{1,0:T(8,128)(2,1)S(1)}, u32[]{:S(2)}, u32[]{:S(2)}) collective-permute-start(bf16[64,1024]{1,0:T(8,128)(2,1)S(1)} %collective-permute-done.3.refs_5_), channel_id=1, source_target_pairs={{0,4},{1,5},{4,8},{5,9},{8,12},{9,13},{12,14},{13,15},{14,10},{15,... | collective-permute-start | bytes 393224 | tf_op jit(solution)/shard_map/ppermute | solution.py:65
  63.7 6.3 %collective-permute-start.23 = (bf16[64,1024]{1,0:T(8,128)(2,1)S(1)}, bf16[64,1024]{1,0:T(8,128)(2,1)S(1)}, u32[]{:S(2)}, u32[]{:S(2)}) collective-permute-start(bf16[64,1024]{1,0:T(8,128)(2,1)S(1)} %collective-permute-done.15.refs_17_), channel_id=1, source_target_pairs={{4,0},{5,1},{8,4},{9,5},{12,8},{13,9},{14,12},{15,13},{10,14},{11,... | collective-permute-start | bytes 393224 | tf_op jit(solution)/shard_map/ppermute | solution.py:65
  63.9 6.7 %collective-permute-start.19 = (bf16[64,1024]{1,0:T(8,128)(2,1)S(1)}, bf16[64,1024]{1,0:T(8,128)(2,1)S(1)}, u32[]{:S(2)}, u32[]{:S(2)}) collective-permute-start(bf16[64,1024]{1,0:T(8,128)(2,1)S(1)} %collective-permute-done.11.refs_13_), channel_id=1, source_target_pairs={{0,4},{1,5},{4,8},{5,9},{8,12},{9,13},{12,14},{13,15},{14,10},{15,... | collective-permute-start | bytes 393224 | tf_op jit(solution)/shard_map/ppermute | solution.py:65
  65.8 6.4 %collective-permute-start.22 = (bf16[64,1024]{1,0:T(8,128)(2,1)S(1)}, bf16[64,1024]{1,0:T(8,128)(2,1)S(1)}, u32[]{:S(2)}, u32[]{:S(2)}) collective-permute-start(bf16[64,1024]{1,0:T(8,128)(2,1)S(1)} %collective-permute-done.14.refs_16_), channel_id=1, source_target_pairs={{4,0},{5,1},{8,4},{9,5},{12,8},{13,9},{14,12},{15,13},{10,14},{11,... | collective-permute-start | bytes 393224 | tf_op jit(solution)/shard_map/ppermute | solution.py:65
  74.3 27.6 %collective-permute-start.32 = (bf16[16,2,64,128]{3,2,1,0:T(8,128)(2,1)}, bf16[16,2,64,128]{3,2,1,0:T(8,128)(2,1)}, u32[]{:S(2)}, u32[]{:S(2)}) collective-permute-start(bf16[16,2,64,128]{3,2,1,0:T(8,128)(2,1)} %all-to-all-done), channel_id=1, source_target_pairs={{0,1},{1,0},{2,3},{3,2},{4,5},{5,4},{6,7},{7,6},{8,9},{9,8},{10,11... | collective-permute-start | bytes 1572872 | tf_op jit(solution)/shard_map/ppermute | solution.py:65
  99.0 6.6 %collective-permute-start.31 = (bf16[128,128]{1,0:T(8,128)(2,1)S(1)}, bf16[128,128]{1,0:T(8,128)(2,1)S(1)}, u32[]{:S(2)}, u32[]{:S(2)}) collective-permute-start(bf16[128,128]{1,0:T(8,128)(2,1)S(1)} %get-tuple-element.8), channel_id=1, source_target_pairs={{0,1},{1,3},{2,5},{3,7},{4,9},{5,11},{6,13},{7,15},{8,0},{9,2},{10... | collective-permute-start | bytes 98312 | tf_op jit(solution)/shard_map/ppermute | solution.py:65
  117.8 6.3 %collective-permute-start.45 = (bf16[64,1024]{1,0:T(8,128)(2,1)S(1)}, bf16[64,1024]{1,0:T(8,128)(2,1)S(1)}, u32[]{:S(2)}, u32[]{:S(2)}) collective-permute-start(bf16[64,1024]{1,0:T(8,128)(2,1)S(1)} %get-tuple-element.26), channel_id=1, source_target_pairs={{4,0},{5,1},{8,4},{9,5},{12,8},{13,9},{14,12},{15,13},{10,14},{11,... | collective-permute-start | bytes 393224 | tf_op jit(solution)/shard_map/ppermute | solution.py:65
  117.8 8.5 %collective-permute-start.39 = (bf16[64,1024]{1,0:T(8,128)(2,1)S(1)}, bf16[64,1024]{1,0:T(8,128)(2,1)S(1)}, u32[]{:S(2)}, u32[]{:S(2)}) collective-permute-start(bf16[64,1024]{1,0:T(8,128)(2,1)S(1)} %get-tuple-element.27), channel_id=1, source_target_pairs={{4,0},{5,1},{8,4},{9,5},{12,8},{13,9},{14,12},{15,13},{10,14},{11,... | collective-permute-start | bytes 393224 | tf_op jit(solution)/shard_map/ppermute | solution.py:65
  119.7 6.7 %collective-permute-start.42 = (bf16[64,1024]{1,0:T(8,128)(2,1)S(1)}, bf16[64,1024]{1,0:T(8,128)(2,1)S(1)}, u32[]{:S(2)}, u32[]{:S(2)}) collective-permute-start(bf16[64,1024]{1,0:T(8,128)(2,1)S(1)} %get-tuple-element.25), channel_id=1, source_target_pairs={{0,4},{1,5},{4,8},{5,9},{8,12},{9,13},{12,14},{13,15},{14,10},{15,... | collective-permute-start | bytes 393224 | tf_op jit(solution)/shard_map/ppermute | solution.py:65
  134.0 6.4 %collective-permute-start.47 = (bf16[64,1024]{1,0:T(8,128)(2,1)S(1)}, bf16[64,1024]{1,0:T(8,128)(2,1)S(1)}, u32[]{:S(2)}, u32[]{:S(2)}) collective-permute-start(bf16[64,1024]{1,0:T(8,128)(2,1)S(1)} %get-tuple-element.18), channel_id=1, source_target_pairs={{4,0},{5,1},{8,4},{9,5},{12,8},{13,9},{14,12},{15,13},{10,14},{11,... | collective-permute-start | bytes 393224 | tf_op jit(solution)/shard_map/ppermute | solution.py:65
  142.6 6.9 %collective-permute-start.44 = (bf16[64,1024]{1,0:T(8,128)(2,1)S(1)}, bf16[64,1024]{1,0:T(8,128)(2,1)S(1)}, u32[]{:S(2)}, u32[]{:S(2)}) collective-permute-start(bf16[64,1024]{1,0:T(8,128)(2,1)S(1)} %get-tuple-element.13), channel_id=1, source_target_pairs={{0,4},{1,5},{4,8},{5,9},{8,12},{9,13},{12,14},{13,15},{14,10},{15,... | collective-permute-start | bytes 393224 | tf_op jit(solution)/shard_map/ppermute | solution.py:65
  142.6 6.9 %collective-permute-start.48 = (bf16[64,1024]{1,0:T(8,128)(2,1)S(1)}, bf16[64,1024]{1,0:T(8,128)(2,1)S(1)}, u32[]{:S(2)}, u32[]{:S(2)}) collective-permute-start(bf16[64,1024]{1,0:T(8,128)(2,1)S(1)} %get-tuple-element.14), channel_id=1, source_target_pairs={{4,0},{5,1},{8,4},{9,5},{12,8},{13,9},{14,12},{15,13},{10,14},{11,... | collective-permute-start | bytes 393224 | tf_op jit(solution)/shard_map/ppermute | solution.py:65
  152.1 6.8 %collective-permute-start.55 = (bf16[64,1024]{1,0:T(8,128)(2,1)S(1)}, bf16[64,1024]{1,0:T(8,128)(2,1)S(1)}, u32[]{:S(2)}, u32[]{:S(2)}) collective-permute-start(bf16[64,1024]{1,0:T(8,128)(2,1)S(1)} %get-tuple-element.12.refs_0_), channel_id=1, source_target_pairs={{4,0},{5,1},{8,4},{9,5},{12,8},{13,9},{14,12},{15,13},{10,14},{11,... | collective-permute-start | bytes 393224 | tf_op jit(solution)/shard_map/ppermute | solution.py:65
  166.2 6.5 %collective-permute-start.68 = (bf16[64,1024]{1,0:T(8,128)(2,1)S(1)}, bf16[64,1024]{1,0:T(8,128)(2,1)S(1)}, u32[]{:S(2)}, u32[]{:S(2)}) collective-permute-start(bf16[64,1024]{1,0:T(8,128)(2,1)S(1)} %collective-permute-done.60.refs_13_), channel_id=1, source_target_pairs={{0,4},{1,5},{4,8},{5,9},{8,12},{9,13},{12,14},{13,15},{14,10},{15,... | collective-permute-start | bytes 393224 | tf_op jit(solution)/shard_map/ppermute | solution.py:65
  (71 other events, 471.0 us)

commit v2 on v0

--- a/solution.py
+++ b/solution.py
@@ -1,6 +1,8 @@
 import jax
 import jax.numpy as jnp
 from jax import lax
+from jax.experimental import pallas as pl
+from jax.experimental.pallas import tpu as pltpu
 from jax.sharding import PartitionSpec as P
 
 HD = 128
@@ -9,7 +11,8 @@
 SPAN = 64
 SEQS = 2
 CTX_DEV = 64
-
+TOKENS = SEQS * SPAN
+MIB = 1024 * 1024
 
 epsilon = 1e-05
 
@@ -20,17 +23,346 @@
     return values_f * factor * gain.astype(jnp.float32)
 
 
+def rope_tables(positions):
+    half_width = HD // 2
+    frequency = 500000.0 ** (-jnp.arange(half_width, dtype=jnp.float32) / half_width)
+    angles = positions.astype(jnp.float32)[:, None] * frequency[None, :]
+    return jnp.cos(angles), jnp.sin(angles)
+
+
 def rotate(vectors, positions):
     half_width = vectors.shape[-1] // 2
-    frequency = 500000.0 ** (-jnp.arange(half_width, dtype=jnp.float32) / half_width)
-    angles = positions.astype(jnp.float32)[:, None] * frequency[None, :]
-    cosine = jnp.cos(angles)[:, None, :]
-    sine = jnp.sin(angles)[:, None, :]
+    cosine, sine = rope_tables(positions)
+    cosine, sine = cosine[:, None, :], sine[:, None, :]
     first_half = vectors[..., :half_width]
     second_half = vectors[..., half_width:]
     return jnp.concatenate(
         [first_half * cosine - second_half * sine, second_half * cosine + first_half * sine],
         axis=-1,
+    )
+
+
+CHIPS = 8
+RING = (0, 2, 4, 6, 7, 5, 3, 1)
+ONWARD = [(2 * RING[i], 2 * RING[(i + 1) % CHIPS]) for i in range(CHIPS)] + [
+    (2 * RING[i] + 1, 2 * RING[i - 1] + 1) for i in range(CHIPS)
+]
+SWAP = [(t, t ^ 1) for t in range(2 * CHIPS)]
+STRAIGHT = [(k, 2 * k) for k in range(KVH)] + [(KVH + k, 2 * k + 1) for k in range(KVH)]
+CROSSED = [(k, 2 * k + 1) for k in range(KVH)] + [(KVH + k, 2 * k) for k in range(KVH)]
+VMEM = pl.BlockSpec(memory_space=pltpu.VMEM)
+SMEM = pl.BlockSpec(memory_space=pltpu.SMEM)
+HBM = pl.BlockSpec(memory_space=pltpu.HBM)
+
+
+def ring_place(rank):
+    chip = rank // 2
+    return jnp.where(chip % 2 == 0, chip // 2, CHIPS - 1 - chip // 2)
+
+
+def chip_at(place):
+    place = place % CHIPS
+    return jnp.where(place < CHIPS // 2, 2 * place, 2 * CHIPS - 1 - 2 * place)
+
+
+def send(array, pairs):
+    return lax.ppermute(array, "tp", pairs)
+
+
+def ring_gather(own):
+    straight, crossed = own, send(own, SWAP)
+    blocks = [straight, crossed]
+    for step in range(1, 5):
+        straight = send(straight, ONWARD)
+        blocks += [straight, send(straight, SWAP)]
+        if step < 4:
+            crossed = send(crossed, ONWARD)
+            blocks += [crossed, send(crossed, SWAP)]
+    return blocks
+
+
+def gathered_ids(rank):
+    place, core = ring_place(rank), rank % 2
+    ahead = 2 * core - 1
+    ids = [rank, rank ^ 1]
+    for step in range(1, 5):
+        near, far = 2 * chip_at(place + ahead * step), 2 * chip_at(place - ahead * step)
+        ids += [near + core, far + 1 - core]
+        if step < 4:
+            ids += [near + 1 - core, far + core]
+    return jnp.stack(ids).astype(jnp.int32)
+
+
+SHARES = ((4, 0), (3, 1), (3, 0), (2, 1), (2, 0), (1, 1), (1, 0), (0, 0))
+
+
+def share_ids(rank):
+    place, core = ring_place(rank), rank % 2
+    return jnp.stack(
+        [2 * chip_at(place + (1 - 2 * core) * d) + (core + other) % 2 for d, other in SHARES]
+    ).astype(jnp.int32)
+
+
+def ring_sum(shares):
+    running = {0: shares[4, 0], 1: shares[3, 1]}
+    for step in range(4, 0, -1):
+        for other in range(2):
+            if step == 4 and other == 1:
+                continue
+            if (step, other) not in ((4, 0), (3, 1)):
+                running[other] = (
+                    running[other].astype(jnp.float32) + shares[step, other]
+                ).astype(jnp.bfloat16)
+            running[other] = send(running[other], ONWARD)
+    return running[0], send(running[1], SWAP)
+
+
+def row_factors(blocks):
+    width = blocks[0].shape[1]
+    squares = jnp.zeros((TOKENS, 128), jnp.float32)
+    for block in blocks:
+        for j in range(width // 128):
+            v = block[:, j * 128 : (j + 1) * 128].astype(jnp.float32)
+            squares = squares + v * v
+    mean = jnp.sum(squares, axis=1, keepdims=True) * (1.0 / (len(blocks) * width))
+    return lax.rsqrt(mean + epsilon)
+
+
+def project_kernel(ids, *refs):
+    blocks = refs[:16]
+    gain, cosine, sine, kv_cos, kv_sin, wq, wkv = refs[16:23]
+    q_keep, q_send, kv_straight, kv_crossed = refs[23:27]
+    wq_buf, wkv_buf, kv_buf, q_buf, sems = refs[27:]
+    width = blocks[0].shape[1]
+    copies = []
+    for i in range(16):
+        rows = pl.ds(pl.multiple_of(ids[i] * width, width), width)
+        pair = (
+            pltpu.make_async_copy(wq.at[rows, :], wq_buf.at[i], sems.at[0, i]),
+            pltpu.make_async_copy(wkv.at[rows, :], wkv_buf.at[i], sems.at[1, i]),
+        )
+        for copy in pair:
+            copy.start()
+        copies.append(pair)
+    factor = row_factors(blocks)
+    total = jnp.zeros((TOKENS, 2 * HD), jnp.float32)
+    for i in range(16):
+        normed = (blocks[i][...].astype(jnp.float32) * factor * gain[ids[i]]).astype(jnp.bfloat16)
+        for copy in copies[i]:
+            copy.wait()
+        weights = jnp.concatenate([wq_buf[i], wkv_buf[i]], axis=1)
+        total = total + jnp.dot(normed, weights, preferred_element_type=jnp.float32)
+    q, kv = total[:, :HD], total[:, HD:]
+    q_buf[...] = (q * cosine[...] + pltpu.roll(q, HD // 2, 1) * sine[...]).astype(jnp.bfloat16)
+    kv_buf[...] = (kv * kv_cos[...] + pltpu.roll(kv, HD // 2, 1) * kv_sin[...]).astype(jnp.bfloat16)
+    core_one = ids[0] % 2 == 1
+    holds_keys = ids[0] < KVH
+    first, second = slice(0, SPAN), slice(SPAN, TOKENS)
+    q_keep[...] = jnp.where(core_one, q_buf[second, :], q_buf[first, :])
+    q_send[...] = jnp.where(core_one, q_buf[first, :], q_buf[second, :])
+    kv_straight[...] = jnp.where(holds_keys, kv_buf[first, :], kv_buf[second, :])
+    kv_crossed[...] = jnp.where(holds_keys, kv_buf[second, :], kv_buf[first, :])
+
+
+def project(ids, blocks, gain, tables, q_weight, kv_weight):
+    width = blocks[0].shape[1]
+    return pl.pallas_call(
+        project_kernel,
+        out_shape=[jax.ShapeDtypeStruct((SPAN, HD), jnp.bfloat16)] * 4,
+        in_specs=[SMEM] + [VMEM] * 21 + [HBM] * 2,
+        out_specs=[VMEM] * 4,
+        scratch_shapes=[
+            pltpu.VMEM((16, width, HD), jnp.bfloat16),
+            pltpu.VMEM((16, width, HD), jnp.bfloat16),
+            pltpu.VMEM((TOKENS, HD), jnp.bfloat16),
+            pltpu.VMEM((TOKENS, HD), jnp.bfloat16),
+            pltpu.SemaphoreType.DMA((2, 16)),
+        ],
+        compiler_params=pltpu.CompilerParams(vmem_limit_bytes=32 * MIB),
+        cost_estimate=pl.CostEstimate(
+            flops=4 * TOKENS * 16 * width * HD, bytes_accessed=12 * MIB, transcendentals=0
+        ),
+        name="norm_project",
+    )(ids, *blocks, gain, *tables, q_weight, kv_weight)
+
+
+def attend_kernel(info, q, q_other, straight, crossed, cache, out):
+    core = info[SEQS]
+    fresh_keys = jnp.where(core == 0, straight[...], crossed[...])
+    fresh_values = jnp.where(core == 0, crossed[...], straight[...])
+    scale = HD ** (-0.5)
+    context = cache.shape[0] * cache.shape[2]
+    contract = (((1,), (1,)), ((), ()))
+    queries = jnp.concatenate([q[...], q_other[...]], axis=0)
+    old_keys = cache[:, 0].reshape(context, HD)
+    old_values = cache[:, 1].reshape(context, HD)
+    old = lax.dot_general(queries, old_keys, contract, preferred_element_type=jnp.float32) * scale
+    fresh = (
+        lax.dot_general(queries, fresh_keys, contract, preferred_element_type=jnp.float32) * scale
+    )
+    valid = lax.broadcasted_iota(jnp.int32, old.shape, 1) < info[core]
+    place = lax.broadcasted_iota(jnp.int32, fresh.shape, 0) % SPAN
+    causal = place >= lax.broadcasted_iota(jnp.int32, fresh.shape, 1)
+    old = jnp.where(valid, old, -1e30)
+    fresh = jnp.where(causal, fresh, -1e30)
+    most = jnp.maximum(jnp.max(old, axis=1, keepdims=True), jnp.max(fresh, axis=1, keepdims=True))
+    old_weights = jnp.where(valid, jnp.exp(old - most), 0.0)
+    fresh_weights = jnp.where(causal, jnp.exp(fresh - most), 0.0)
+    totals = jnp.sum(old_weights, axis=1, keepdims=True) + jnp.sum(
+        fresh_weights, axis=1, keepdims=True
+    )
+    summed = jnp.dot(
+        old_weights.astype(jnp.bfloat16), old_values, preferred_element_type=jnp.float32
+    ) + jnp.dot(
+        fresh_weights.astype(jnp.bfloat16), fresh_values, preferred_element_type=jnp.float32
+    )
+    attn = (summed / totals).astype(jnp.bfloat16)
+    out[:, :HD] = attn[:SPAN]
+    out[:, HD:] = attn[SPAN:]
+
+
+def attend(info, q, q_other, straight, crossed, cache):
+    return pl.pallas_call(
+        attend_kernel,
+        out_shape=jax.ShapeDtypeStruct((SPAN, 2 * HD), jnp.bfloat16),
+        in_specs=[SMEM] + [VMEM] * 5,
+        out_specs=VMEM,
+        compiler_params=pltpu.CompilerParams(vmem_limit_bytes=24 * MIB),
+        cost_estimate=pl.CostEstimate(
+            flops=80 * MIB, bytes_accessed=MIB, transcendentals=TOKENS * 1088
+        ),
+        name="attend",
+    )(info, q, q_other, straight, crossed, cache)
+
+
+def output_kernel(ids, attn, attn_other, weight, weight_other, *refs):
+    count = len(refs) - 2
+    outs, (weights, sems) = refs[:count], refs[count:]
+    width = weights.shape[2]
+    copies = []
+    for i in range(count):
+        columns = pl.ds(pl.multiple_of(ids[i] * width, width), width)
+        pair = (
+            pltpu.make_async_copy(weight.at[:, columns], weights.at[i, :HD], sems.at[0, i]),
+            pltpu.make_async_copy(weight_other.at[:, columns], weights.at[i, HD:], sems.at[1, i]),
+        )
+        for copy in pair:
+            copy.start()
+        copies.append(pair)
+    mine = attn[...]
+    theirs = jnp.concatenate([attn_other[:, HD:], attn_other[:, :HD]], axis=1)
+    core_one = ids[count] == 1
+    rows = jnp.concatenate(
+        [jnp.where(core_one, theirs, mine), jnp.where(core_one, mine, theirs)], axis=0
+    )
+    for i in range(count):
+        for copy in copies[i]:
+            copy.wait()
+        outs[i][...] = jnp.dot(
+            rows, weights[i], preferred_element_type=jnp.float32
+        ).astype(outs[i].dtype)
+
+
+def output_shares(ids, core, attn, attn_other, weight, weight_other, width, dtype):
+    count = ids.shape[0]
+    return pl.pallas_call(
+        output_kernel,
+        out_shape=[jax.ShapeDtypeStruct((TOKENS, width), dtype)] * count,
+        in_specs=[SMEM, VMEM, VMEM, HBM, HBM],
+        out_specs=[VMEM] * count,
+        scratch_shapes=[
+            pltpu.VMEM((count, 2 * HD, width), jnp.bfloat16),
+            pltpu.SemaphoreType.DMA((2, count)),
+        ],
+        compiler_params=pltpu.CompilerParams(vmem_limit_bytes=24 * MIB),
+        cost_estimate=pl.CostEstimate(
+            flops=4 * TOKENS * HD * width * count,
+            bytes_accessed=count * MIB,
+            transcendentals=0,
+        ),
+        name="output_shares_%d" % count,
+    )(jnp.concatenate([ids, core[None].astype(jnp.int32)]), attn, attn_other, weight, weight_other)
+
+
+def final_kernel(ids, *refs):
+    blocks, gain, out = refs[:16], refs[16], refs[17]
+    staged, sems = refs[18:]
+    width = blocks[0].shape[1]
+    factor = row_factors(blocks)
+    copies = []
+    for i in range(16):
+        staged[i] = (blocks[i][...].astype(jnp.float32) * factor * gain[ids[i]]).astype(jnp.bfloat16)
+        copy = pltpu.make_async_copy(
+            staged.at[i],
+            out.at[:, pl.ds(pl.multiple_of(ids[i] * width, width), width)],
+            sems.at[i],
+        )
+        copy.start()
+        copies.append(copy)
+    for copy in copies:
+        copy.wait()
+
+
+def final_norm(ids, blocks, gain):
+    width = blocks[0].shape[1]
+    return pl.pallas_call(
+        final_kernel,
+        out_shape=jax.ShapeDtypeStruct((TOKENS, 16 * width), jnp.bfloat16),
+        in_specs=[SMEM] + [VMEM] * 17,
+        out_specs=HBM,
+        scratch_shapes=[
+            pltpu.VMEM((16, TOKENS, width), jnp.bfloat16),
+            pltpu.SemaphoreType.DMA((16,)),
+        ],
+        compiler_params=pltpu.CompilerParams(vmem_limit_bytes=32 * MIB),
+        name="final_norm",
+    )(ids, *blocks, gain)
+
+
+def per_device_ring(
+    residual, attn_gain, ffn_gain, q_weight, kv_weight, o_weight, key_cache, value_cache, prefix
+):
+    rank = lax.axis_index("tp")
+    core = rank % 2
+    width = residual.shape[1]
+    ids = gathered_ids(rank)
+
+    blocks = ring_gather(residual)
+
+    by_head = lambda cache: jnp.transpose(cache.reshape(SEQS, CTX_DEV, KVH, HD), (2, 0, 1, 3))
+    pieces = jnp.stack([by_head(key_cache), by_head(value_cache)], axis=2)
+    pieces = pieces.reshape(2 * KVH, 2, CTX_DEV, HD)
+    pieces, _ = lax.optimization_barrier((pieces, blocks[-4]))
+    cache = lax.all_to_all(pieces, "tp", split_axis=0, concat_axis=0, tiled=True)
+
+    held, _ = lax.optimization_barrier((o_weight, blocks[2]))
+    weight_other = send(held, SWAP)
+
+    positions = (prefix[:, None] + jnp.arange(SPAN, dtype=jnp.int32)[None, :]).reshape(-1)
+    cosine, sine = rope_tables(positions)
+    cosine = jnp.concatenate([cosine, cosine], axis=1)
+    sine = jnp.concatenate([-sine, sine], axis=1)
+    holds_keys = rank < KVH
+    tables = (cosine, sine, jnp.where(holds_keys, cosine, 1.0), jnp.where(holds_keys, sine, 0.0))
+
+    q_keep, q_send, straight, crossed = project(
+        ids, blocks, attn_gain.reshape(16, 1, width).astype(jnp.float32), tables, q_weight, kv_weight
+    )
+    info = jnp.concatenate([prefix, core[None].astype(jnp.int32)])
+    attn = attend(
+        info, q_keep, send(q_send, SWAP), send(straight, STRAIGHT), send(crossed, CROSSED), cache
+    )
+
+    to = share_ids(rank)
+    inputs = (core, attn, send(attn, SWAP), o_weight, weight_other, width)
+    shares = output_shares(to[:2], *inputs, jnp.bfloat16)
+    shares += output_shares(to[2:], *inputs, jnp.float32)
+    shares = dict(zip(SHARES, shares))
+    one_way, other_way = ring_sum(shares)
+    projected = shares[0, 0] + one_way.astype(jnp.float32) + other_way.astype(jnp.float32)
+    hidden = (residual.astype(jnp.float32) + projected).astype(jnp.bfloat16)
+    return final_norm(
+        ids, ring_gather(hidden), ffn_gain.reshape(16, 1, width).astype(jnp.float32)
     )
 
 
@@ -141,7 +473,7 @@
 
 def solution(mesh):
     return jax.shard_map(
-        per_device,
+        per_device_ring if mesh.shape["tp"] == 2 * CHIPS else per_device,
         mesh=mesh,
         in_specs=(
             P("replica", "tp"),

time: 325 us -> 145 us (0.45)
  waiting for transfers between devices: 237 us -> 55.3 us
  starting transfers between devices: 10.7 us -> 58.4 us
  blocking collectives: 20.4 us -> 0 us
  matrix products: 17.6 us -> 0 us
  Pallas kernels: 0 us -> 16.9 us
  other arithmetic: 16.4 us -> 3.37 us
  between operations: 13.4 us -> 0.68 us
    reduce_scatter x1 -> x0, waiting for transfers between devices: 107 us -> none  [per_device(): lax.psum_scatter(lax.dot_general(o_weight, attn, (((0,), (1,)), ((), ()))...]
    all_gather x3 -> x0, waiting for transfers between devices: 101 us -> none  [the longest x1 50.8 us: per_device(): whole_rows = lax.all_gather(residual, 'tp', axis=1, tiled=True)]
    ppermute x0 -> x43, waiting for transfers between devices: none -> 55.3 us  [send(): return lax.ppermute(array, 'tp', pairs)]
    ppermute x0 -> x43, starting transfers between devices: none -> 52 us  [send(): return lax.ppermute(array, 'tp', pairs)]
    all_to_all x3 -> x1, waiting for transfers between devices: 27.6 us -> 0.01 us  [per_device_ring(): lax.all_to_all(pieces, 'tp', split_axis=0, concat_axis=0, tiled=True)]
    all_gather x1 -> x0, blocking collectives: 20.4 us -> none  [per_device(): lax.all_gather(queries.reshape(token_count, HQ_DEV * HD), 'tp', axis=1, t...]
    dot_general x7 -> x0, matrix products: 17.6 us -> none  [the longest x1 6.65 us: per_device(): lax.dot_general(o_weight, attn, (((0,), (1,)), ((), ())), preferred_eleme...]
    pallas_call x0 -> x5, Pallas kernels: none -> 16.9 us  [the longest x1 6.88 us: project(): pl.pallas_call(project_kernel, out_shape=[jax.ShapeDtypeStruct((SPAN, HD)...]
  transfers between devices with their start and end apart: 7 -> 44, of which waited for: 6 -> 24; matrix products, arithmetic and copies ran while one was open for 6% -> 3% of each run, Pallas kernels for 0% -> 8%
where the time goes in v2:
time: 145 us
  starting transfers between devices  58.4 us (40%)
  waiting for transfers between devices  55.3 us (38%)
  Pallas kernels  16.9 us (12%)
  local copies, waits for them, and re-layouts  10.1 us (7%)
  other arithmetic  3.37 us (2%)
    ppermute x43, waiting for transfers between devices, send(): return lax.ppermute(array, 'tp', pairs)  55.3 us
    ppermute x43, starting transfers between devices, send(): return lax.ppermute(array, 'tp', pairs)  52 us
    unnamed x16, local copies, waits for them, and re-layouts  8.77 us
    pallas_call x1, Pallas kernels, project(): pl.pallas_call(project_kernel, out_shape=[jax.ShapeDtypeStruct((SPAN, HD)...  6.88 us
    all_to_all x1, starting transfers between devices, per_device_ring(): lax.all_to_all(pieces, 'tp', split_axis=0, concat_axis=0, tiled=True)  6.41 us
    pallas_call x2, Pallas kernels, output_shares(): pl.pallas_call(output_kernel, out_shape=[jax.ShapeDtypeStruct((TOKENS, wi...  5.07 us
    pallas_call x1, Pallas kernels, final_norm(): pl.pallas_call(final_kernel, out_shape=jax.ShapeDtypeStruct((TOKENS, 16 *...  3.82 us
  transfers between devices with their start and end apart: 44, of which 24 were waited for; matrix products, arithmetic and copies ran while one was open for 3% of the time, Pallas kernels for 8%

profile of v2, /device:TPU:0, one launch (start us, length us, event | category | flops | bytes accessed | tf_op | source)
XLA Modules:
  0.0 144.8 jit_solution(2932554395667564843)
XLA Ops:
  0.0 3.0 %collective-permute-start.1 = (bf16[128,1024]{1,0:T(8,128)(2,1)}, bf16[128,1024]{1,0:T(8,128)(2,1)S(1)}, u32[]{:S(2)}, u32[]{:S(2)}) collective-permute-start(bf16[128,1024]{1,0:T(8,128)(2,1)} %refs_0_.1), channel_id=1, source_target_pairs={{0,4},{4,8},{8,12},{12,14},{14,10},{10,6},{6,2},{2,0},{1,3},{5,1},... | collective-permute-start | bytes 786440 | tf_op jit(solution)/shard_map/ppermute | solution.py:69
  3.0 4.5 %collective-permute-done.1.refs_2_ = bf16[128,1024]{1,0:T(8,128)(2,1)S(1)} collective-permute-done((bf16[128,1024]{1,0:T(8,128)(2,1)}, bf16[128,1024]{1,0:T(8,128)(2,1)S(1)}, u32[]{:S(2)}, u32[]{:S(2)}) %collective-permute-start.1) | collective-permute-done | bytes 262176 | tf_op jit(solution)/shard_map/ppermute | solution.py:69
  8.0 6.3 %collective-permute-done.refs_1_ = bf16[128,1024]{1,0:T(8,128)(2,1)S(1)} collective-permute-done((bf16[128,1024]{1,0:T(8,128)(2,1)}, bf16[128,1024]{1,0:T(8,128)(2,1)S(1)}, u32[]{:S(2)}, u32[]{:S(2)}) %collective-permute-start) | collective-permute-done | bytes 262176 | tf_op jit(solution)/shard_map/ppermute | solution.py:69
  18.0 2.7 %collective-permute-done.3.refs_4_ = bf16[128,1024]{1,0:T(8,128)(2,1)S(1)} collective-permute-done((bf16[128,1024]{1,0:T(8,128)(2,1)S(1)}, bf16[128,1024]{1,0:T(8,128)(2,1)S(1)}, u32[]{:S(2)}, u32[]{:S(2)}) %collective-permute-start.3) | collective-permute-done | bytes 262176 | tf_op jit(solution)/shard_map/ppermute | solution.py:69
  31.0 2.4 %collective-permute-done.11.refs_12_ = bf16[128,1024]{1,0:T(8,128)(2,1)S(1)} collective-permute-done((bf16[128,1024]{1,0:T(8,128)(2,1)S(1)}, bf16[128,1024]{1,0:T(8,128)(2,1)S(1)}, u32[]{:S(2)}, u32[]{:S(2)}) %collective-permute-start.11) | collective-permute-done | bytes 262176 | tf_op jit(solution)/shard_map/ppermute | solution.py:69
  33.5 6.4 %all-to-all-start = ((bf16[16,2,64,128]{3,2,1,0:T(8,128)(2,1)}), bf16[16,2,64,128]{3,2,1,0:T(8,128)(2,1)S(1)}, u32[]{:S(2)}, u32[]{:S(2)}) async-start(bf16[16,2,64,128]{3,2,1,0:T(8,128)(2,1)} %pad_maximum_fusion), calls=%async_computation | async-start | bytes 1048576 | tf_op jit(solution)/shard_map/all_to_all | solution.py:336
  44.9 7.4 %collective-permute-done.13.refs_14_ = bf16[128,1024]{1,0:T(8,128)(2,1)} collective-permute-done((bf16[128,1024]{1,0:T(8,128)(2,1)S(1)}, bf16[128,1024]{1,0:T(8,128)(2,1)}, u32[]{:S(2)}, u32[]{:S(2)}) %collective-permute-start.13) | collective-permute-done | bytes 262176 | tf_op jit(solution)/shard_map/ppermute | solution.py:69
  60.1 6.9 %norm_project.1 = (bf16[64,128]{1,0:T(8,128)(2,1)S(1)}, bf16[64,128]{1,0:T(8,128)(2,1)S(1)}, bf16[64,128]{1,0:T(8,128)(2,1)S(1)}, bf16[64,128]{1,0:T(8,128)(2,1)S(1)}) custom-call(s32[16]{0:T(128)S(1)} %stack.101.ids, bf16[128,1024]{1,0:T(8,128)(2,1)S(1)} %copy-done.5, bf16[128,1024]{1,0:T(8,128)(2,1)S(1)} %collective-permute-done.refs_1_, ...), custom_call_target="tpu_custom_call" | custom-call | flops 1073741824 | bytes 12582912 | tf_op jit(solution)/shard_map/norm_project/pallas_call | solution.py:169
  68.1 3.0 %collective-permute-start.17 = (bf16[64,128]{1,0:T(8,128)(2,1)S(1)}, bf16[64,128]{1,0:T(8,128)(2,1)S(1)}, u32[]{:S(2)}, u32[]{:S(2)}) collective-permute-start(bf16[64,128]{1,0:T(8,128)(2,1)S(1)} %get-tuple-element.22), channel_id=1, source_target_pairs={{0,1},{1,3},{2,5},{3,7},{4,9},{5,11},{6,13},{7,15},{8,0},{9,2},{10... | collective-permute-start | bytes 49160 | tf_op jit(solution)/shard_map/ppermute | solution.py:69
  71.2 4.5 %collective-permute-done.17.crossed = bf16[64,128]{1,0:T(8,128)(2,1)S(1)} collective-permute-done((bf16[64,128]{1,0:T(8,128)(2,1)S(1)}, bf16[64,128]{1,0:T(8,128)(2,1)S(1)}, u32[]{:S(2)}, u32[]{:S(2)}) %collective-permute-start.17) | collective-permute-done | bytes 16416 | tf_op jit(solution)/shard_map/ppermute | solution.py:69
  82.4 3.4 %collective-permute-start.20 = (bf16[128,1024]{1,0:T(8,128)(2,1)S(1)}, bf16[128,1024]{1,0:T(8,128)(2,1)S(1)}, u32[]{:S(2)}, u32[]{:S(2)}) collective-permute-start(bf16[128,1024]{1,0:T(8,128)(2,1)S(1)} %get-tuple-element.26), channel_id=1, source_target_pairs={{0,4},{4,8},{8,12},{12,14},{14,10},{10,6},{6,2},{2,0},{1,3},{5,1},... | collective-permute-start | bytes 786440 | tf_op jit(solution)/shard_map/ppermute | solution.py:69
  88.2 3.0 %output_shares_6.1 = (f32[128,1024]{1,0:T(8,128)S(1)}, f32[128,1024]{1,0:T(8,128)S(1)}, f32[128,1024]{1,0:T(8,128)S(1)}, f32[128,1024]{1,0:T(8,128)S(1)}, f32[12...) custom-call(s32[7]{0:T(128)S(1)} %concatenate.20.ids, bf16[64,256]{1,0:T(8,128)(2,1)S(1)} %attend.1.attn, ...), custom_call_target="tpu_custom_call" | custom-call | flops 402653184 | bytes 6291456 | tf_op jit(solution)/shard_map/output_shares_6/pallas_call | solution.py:268
  91.3 2.3 %collective-permute-start.21 = (bf16[128,1024]{1,0:T(8,128)(2,1)S(1)}, bf16[128,1024]{1,0:T(8,128)(2,1)S(1)}, u32[]{:S(2)}, u32[]{:S(2)}) collective-permute-start(bf16[128,1024]{1,0:T(8,128)(2,1)S(1)} %add_convert_fusion.5), channel_id=1, source_target_pairs={{0,4},{4,8},{8,12},{12,14},{14,10},{10,6},{6,2},{2,0},{1,3},{5,1},... | collective-permute-start | bytes 786440 | tf_op jit(solution)/shard_map/ppermute | solution.py:69
  95.1 2.6 %collective-permute-done.21 = bf16[128,1024]{1,0:T(8,128)(2,1)S(1)} collective-permute-done((bf16[128,1024]{1,0:T(8,128)(2,1)S(1)}, bf16[128,1024]{1,0:T(8,128)(2,1)S(1)}, u32[]{:S(2)}, u32[]{:S(2)}) %collective-permute-start.21) | collective-permute-done | bytes 262176 | tf_op jit(solution)/shard_map/ppermute | solution.py:69
  97.8 2.3 %collective-permute-start.22 = (bf16[128,1024]{1,0:T(8,128)(2,1)S(1)}, bf16[128,1024]{1,0:T(8,128)(2,1)S(1)}, u32[]{:S(2)}, u32[]{:S(2)}) collective-permute-start(bf16[128,1024]{1,0:T(8,128)(2,1)S(1)} %add_convert_fusion.4), channel_id=1, source_target_pairs={{0,4},{4,8},{8,12},{12,14},{14,10},{10,6},{6,2},{2,0},{1,3},{5,1},... | collective-permute-start | bytes 786440 | tf_op jit(solution)/shard_map/ppermute | solution.py:69
  100.6 2.3 %collective-permute-start.26 = (bf16[128,1024]{1,0:T(8,128)(2,1)S(1)}, bf16[128,1024]{1,0:T(8,128)(2,1)S(1)}, u32[]{:S(2)}, u32[]{:S(2)}) collective-permute-start(bf16[128,1024]{1,0:T(8,128)(2,1)S(1)} %add_convert_fusion.1), channel_id=1, source_target_pairs={{0,4},{4,8},{8,12},{12,14},{14,10},{10,6},{6,2},{2,0},{1,3},{5,1},... | collective-permute-start | bytes 786440 | tf_op jit(solution)/shard_map/ppermute | solution.py:69
  104.3 2.3 %collective-permute-start.23 = (bf16[128,1024]{1,0:T(8,128)(2,1)S(1)}, bf16[128,1024]{1,0:T(8,128)(2,1)S(1)}, u32[]{:S(2)}, u32[]{:S(2)}) collective-permute-start(bf16[128,1024]{1,0:T(8,128)(2,1)S(1)} %add_convert_fusion.3), channel_id=1, source_target_pairs={{0,4},{4,8},{8,12},{12,14},{14,10},{10,6},{6,2},{2,0},{1,3},{5,1},... | collective-permute-start | bytes 786440 | tf_op jit(solution)/shard_map/ppermute | solution.py:69
  107.0 3.7 %collective-permute-done.23 = bf16[128,1024]{1,0:T(8,128)(2,1)S(1)} collective-permute-done((bf16[128,1024]{1,0:T(8,128)(2,1)S(1)}, bf16[128,1024]{1,0:T(8,128)(2,1)S(1)}, u32[]{:S(2)}, u32[]{:S(2)}) %collective-permute-start.23) | collective-permute-done | bytes 262176 | tf_op jit(solution)/shard_map/ppermute | solution.py:69
  110.9 2.3 %collective-permute-start.29 = (bf16[128,1024]{1,0:T(8,128)(2,1)S(1)}, bf16[128,1024]{1,0:T(8,128)(2,1)S(1)}, u32[]{:S(2)}, u32[]{:S(2)}) collective-permute-start(bf16[128,1024]{1,0:T(8,128)(2,1)S(1)} %add_convert_fusion.refs_0_), channel_id=1, source_target_pairs={{0,4},{4,8},{8,12},{12,14},{14,10},{10,6},{6,2},{2,0},{1,3},{5,1},... | collective-permute-start | bytes 786440 | tf_op jit(solution)/shard_map/ppermute | solution.py:69
  113.2 4.1 %collective-permute-done.29.refs_2_ = bf16[128,1024]{1,0:T(8,128)(2,1)S(1)} collective-permute-done((bf16[128,1024]{1,0:T(8,128)(2,1)S(1)}, bf16[128,1024]{1,0:T(8,128)(2,1)S(1)}, u32[]{:S(2)}, u32[]{:S(2)}) %collective-permute-start.29) | collective-permute-done | bytes 262176 | tf_op jit(solution)/shard_map/ppermute | solution.py:69
  119.7 4.0 %collective-permute-done.33.refs_6_ = bf16[128,1024]{1,0:T(8,128)(2,1)S(1)} collective-permute-done((bf16[128,1024]{1,0:T(8,128)(2,1)S(1)}, bf16[128,1024]{1,0:T(8,128)(2,1)S(1)}, u32[]{:S(2)}, u32[]{:S(2)}) %collective-permute-start.33) | collective-permute-done | bytes 262176 | tf_op jit(solution)/shard_map/ppermute | solution.py:69
  132.9 2.3 %collective-permute-start.39 = (bf16[128,1024]{1,0:T(8,128)(2,1)S(1)}, bf16[128,1024]{1,0:T(8,128)(2,1)S(1)}, u32[]{:S(2)}, u32[]{:S(2)}) collective-permute-start(bf16[128,1024]{1,0:T(8,128)(2,1)S(1)} %collective-permute-done.35.refs_8_), channel_id=1, source_target_pairs={{0,4},{4,8},{8,12},{12,14},{14,10},{10,6},{6,2},{2,0},{1,3},{5,1},... | collective-permute-start | bytes 786440 | tf_op jit(solution)/shard_map/ppermute | solution.py:69
  136.4 2.8 %collective-permute-done.39.refs_12_ = bf16[128,1024]{1,0:T(8,128)(2,1)S(1)} collective-permute-done((bf16[128,1024]{1,0:T(8,128)(2,1)S(1)}, bf16[128,1024]{1,0:T(8,128)(2,1)S(1)}, u32[]{:S(2)}, u32[]{:S(2)}) %collective-permute-start.39) | collective-permute-done | bytes 262176 | tf_op jit(solution)/shard_map/ppermute | solution.py:69
  140.8 3.8 %final_norm.1 = bf16[128,16384]{1,0:T(8,128)(2,1)} custom-call(s32[16]{0:T(128)S(1)} %stack.101.ids, bf16[128,1024]{1,0:T(8,128)(2,1)S(1)} %add_convert_fusion.refs_0_, bf16[128,1024]{1,0:T(8,128)(2,1)S(1)} %collective-permute-done.28.refs_1_, bf16[128,1024]{1,0:T(8,128)(2,1)S(1)} %collective-permute-done.29.refs_2_, ...), custom_call_target="tpu_custom_call" | custom-call | tf_op jit(solution)/shard_map/final_norm/pallas_call | solution.py:308
  (105 shorter events, 55.5 us)
Async XLA Ops:
  0.0 7.5 %collective-permute-start.1 = (bf16[128,1024]{1,0:T(8,128)(2,1)}, bf16[128,1024]{1,0:T(8,128)(2,1)S(1)}, u32[]{:S(2)}, u32[]{:S(2)}) collective-permute-start(bf16[128,1024]{1,0:T(8,128)(2,1)} %refs_0_.1), channel_id=1, source_target_pairs={{0,4},{4,8},{8,12},{12,14},{14,10},{10,6},{6,2},{2,0},{1,3},{5,1},... | collective-permute-start | bytes 786440 | tf_op jit(solution)/shard_map/ppermute | solution.py:69
  7.5 70.6 %collective-permute-start.19 = (bf16[128,16384]{1,0:T(8,128)(2,1)}, bf16[128,16384]{1,0:T(8,128)(2,1)}, u32[]{:S(2)}, u32[]{:S(2)}) collective-permute-start(bf16[128,16384]{1,0:T(8,128)(2,1)} %weight.3), channel_id=1, source_target_pairs={{0,1},{1,0},{2,3},{3,2},{4,5},{5,4},{6,7},{7,6},{8,9},{9,8},{10,11... | collective-permute-start | bytes 12582920 | tf_op jit(solution)/shard_map/ppermute | solution.py:69
  7.5 6.8 %collective-permute-start = (bf16[128,1024]{1,0:T(8,128)(2,1)}, bf16[128,1024]{1,0:T(8,128)(2,1)S(1)}, u32[]{:S(2)}, u32[]{:S(2)}) collective-permute-start(bf16[128,1024]{1,0:T(8,128)(2,1)} %refs_0_.1), channel_id=1, source_target_pairs={{0,1},{1,0},{2,3},{3,2},{4,5},{5,4},{6,7},{7,6},{8,9},{9,8},{10,11... | collective-permute-start | bytes 786440 | tf_op jit(solution)/shard_map/ppermute | solution.py:69
  16.4 7.1 %collective-permute-start.5 = (bf16[128,1024]{1,0:T(8,128)(2,1)S(1)}, bf16[128,1024]{1,0:T(8,128)(2,1)S(1)}, u32[]{:S(2)}, u32[]{:S(2)}) collective-permute-start(bf16[128,1024]{1,0:T(8,128)(2,1)S(1)} %collective-permute-done.1.refs_2_), channel_id=1, source_target_pairs={{0,4},{4,8},{8,12},{12,14},{14,10},{10,6},{6,2},{2,0},{1,3},{5,1},... | collective-permute-start | bytes 786440 | tf_op jit(solution)/shard_map/ppermute | solution.py:69
  23.5 17.3 %collective-permute-start.9 = (bf16[128,1024]{1,0:T(8,128)(2,1)S(1)}, bf16[128,1024]{1,0:T(8,128)(2,1)S(1)}, u32[]{:S(2)}, u32[]{:S(2)}) collective-permute-start(bf16[128,1024]{1,0:T(8,128)(2,1)S(1)} %collective-permute-done.5.refs_6_), channel_id=1, source_target_pairs={{0,4},{4,8},{8,12},{12,14},{14,10},{10,6},{6,2},{2,0},{1,3},{5,1},... | collective-permute-start | bytes 786440 | tf_op jit(solution)/shard_map/ppermute | solution.py:69
  33.5 42.2 %all-to-all-start = ((bf16[16,2,64,128]{3,2,1,0:T(8,128)(2,1)}), bf16[16,2,64,128]{3,2,1,0:T(8,128)(2,1)S(1)}, u32[]{:S(2)}, u32[]{:S(2)}) async-start(bf16[16,2,64,128]{3,2,1,0:T(8,128)(2,1)} %pad_maximum_fusion), calls=%async_computation | async-start | bytes 1048576 | tf_op jit(solution)/shard_map/all_to_all | solution.py:336
  40.8 11.4 %collective-permute-start.13 = (bf16[128,1024]{1,0:T(8,128)(2,1)S(1)}, bf16[128,1024]{1,0:T(8,128)(2,1)}, u32[]{:S(2)}, u32[]{:S(2)}) collective-permute-start(bf16[128,1024]{1,0:T(8,128)(2,1)S(1)} %collective-permute-done.9.refs_10_), channel_id=1, source_target_pairs={{0,4},{4,8},{8,12},{12,14},{14,10},{10,6},{6,2},{2,0},{1,3},{5,1},... | collective-permute-start | bytes 786440 | tf_op jit(solution)/shard_map/ppermute | solution.py:69
  44.2 10.6 %collective-permute-start.8 = (bf16[128,1024]{1,0:T(8,128)(2,1)S(1)}, bf16[128,1024]{1,0:T(8,128)(2,1)S(1)}, u32[]{:S(2)}, u32[]{:S(2)}) collective-permute-start(bf16[128,1024]{1,0:T(8,128)(2,1)S(1)} %collective-permute-done.7.refs_8_), channel_id=1, source_target_pairs={{0,1},{1,0},{2,3},{3,2},{4,5},{5,4},{6,7},{7,6},{8,9},{9,8},{10,11... | collective-permute-start | bytes 786440 | tf_op jit(solution)/shard_map/ppermute | solution.py:69
  44.3 10.5 %collective-permute-start.10 = (bf16[128,1024]{1,0:T(8,128)(2,1)S(1)}, bf16[128,1024]{1,0:T(8,128)(2,1)S(1)}, u32[]{:S(2)}, u32[]{:S(2)}) collective-permute-start(bf16[128,1024]{1,0:T(8,128)(2,1)S(1)} %collective-permute-done.9.refs_10_), channel_id=1, source_target_pairs={{0,1},{1,0},{2,3},{3,2},{4,5},{5,4},{6,7},{7,6},{8,9},{9,8},{10,11... | collective-permute-start | bytes 786440 | tf_op jit(solution)/shard_map/ppermute | solution.py:69
  44.8 10.1 %collective-permute-start.12 = (bf16[128,1024]{1,0:T(8,128)(2,1)S(1)}, bf16[128,1024]{1,0:T(8,128)(2,1)S(1)}, u32[]{:S(2)}, u32[]{:S(2)}) collective-permute-start(bf16[128,1024]{1,0:T(8,128)(2,1)S(1)} %collective-permute-done.11.refs_12_), channel_id=1, source_target_pairs={{0,1},{1,0},{2,3},{3,2},{4,5},{5,4},{6,7},{7,6},{8,9},{9,8},{10,11... | collective-permute-start | bytes 786440 | tf_op jit(solution)/shard_map/ppermute | solution.py:69
  68.1 7.6 %collective-permute-start.17 = (bf16[64,128]{1,0:T(8,128)(2,1)S(1)}, bf16[64,128]{1,0:T(8,128)(2,1)S(1)}, u32[]{:S(2)}, u32[]{:S(2)}) collective-permute-start(bf16[64,128]{1,0:T(8,128)(2,1)S(1)} %get-tuple-element.22), channel_id=1, source_target_pairs={{0,1},{1,3},{2,5},{3,7},{4,9},{5,11},{6,13},{7,15},{8,0},{9,2},{10... | collective-permute-start | bytes 49160 | tf_op jit(solution)/shard_map/ppermute | solution.py:69
  82.4 8.9 %collective-permute-start.20 = (bf16[128,1024]{1,0:T(8,128)(2,1)S(1)}, bf16[128,1024]{1,0:T(8,128)(2,1)S(1)}, u32[]{:S(2)}, u32[]{:S(2)}) collective-permute-start(bf16[128,1024]{1,0:T(8,128)(2,1)S(1)} %get-tuple-element.26), channel_id=1, source_target_pairs={{0,4},{4,8},{8,12},{12,14},{14,10},{10,6},{6,2},{2,0},{1,3},{5,1},... | collective-permute-start | bytes 786440 | tf_op jit(solution)/shard_map/ppermute | solution.py:69
  85.9 7.9 %collective-permute-start.24 = (bf16[128,1024]{1,0:T(8,128)(2,1)S(1)}, bf16[128,1024]{1,0:T(8,128)(2,1)S(1)}, u32[]{:S(2)}, u32[]{:S(2)}) collective-permute-start(bf16[128,1024]{1,0:T(8,128)(2,1)S(1)} %get-tuple-element.30), channel_id=1, source_target_pairs={{0,4},{4,8},{8,12},{12,14},{14,10},{10,6},{6,2},{2,0},{1,3},{5,1},... | collective-permute-start | bytes 786440 | tf_op jit(solution)/shard_map/ppermute | solution.py:69
  91.3 6.4 %collective-permute-start.21 = (bf16[128,1024]{1,0:T(8,128)(2,1)S(1)}, bf16[128,1024]{1,0:T(8,128)(2,1)S(1)}, u32[]{:S(2)}, u32[]{:S(2)}) collective-permute-start(bf16[128,1024]{1,0:T(8,128)(2,1)S(1)} %add_convert_fusion.5), channel_id=1, source_target_pairs={{0,4},{4,8},{8,12},{12,14},{14,10},{10,6},{6,2},{2,0},{1,3},{5,1},... | collective-permute-start | bytes 786440 | tf_op jit(solution)/shard_map/ppermute | solution.py:69
  93.9 6.7 %collective-permute-start.25 = (bf16[128,1024]{1,0:T(8,128)(2,1)S(1)}, bf16[128,1024]{1,0:T(8,128)(2,1)S(1)}, u32[]{:S(2)}, u32[]{:S(2)}) collective-permute-start(bf16[128,1024]{1,0:T(8,128)(2,1)S(1)} %add_convert_fusion.2), channel_id=1, source_target_pairs={{0,4},{4,8},{8,12},{12,14},{14,10},{10,6},{6,2},{2,0},{1,3},{5,1},... | collective-permute-start | bytes 786440 | tf_op jit(solution)/shard_map/ppermute | solution.py:69
  97.8 6.4 %collective-permute-start.22 = (bf16[128,1024]{1,0:T(8,128)(2,1)S(1)}, bf16[128,1024]{1,0:T(8,128)(2,1)S(1)}, u32[]{:S(2)}, u32[]{:S(2)}) collective-permute-start(bf16[128,1024]{1,0:T(8,128)(2,1)S(1)} %add_convert_fusion.4), channel_id=1, source_target_pairs={{0,4},{4,8},{8,12},{12,14},{14,10},{10,6},{6,2},{2,0},{1,3},{5,1},... | collective-permute-start | bytes 786440 | tf_op jit(solution)/shard_map/ppermute | solution.py:69
  100.6 6.4 %collective-permute-start.26 = (bf16[128,1024]{1,0:T(8,128)(2,1)S(1)}, bf16[128,1024]{1,0:T(8,128)(2,1)S(1)}, u32[]{:S(2)}, u32[]{:S(2)}) collective-permute-start(bf16[128,1024]{1,0:T(8,128)(2,1)S(1)} %add_convert_fusion.1), channel_id=1, source_target_pairs={{0,4},{4,8},{8,12},{12,14},{14,10},{10,6},{6,2},{2,0},{1,3},{5,1},... | collective-permute-start | bytes 786440 | tf_op jit(solution)/shard_map/ppermute | solution.py:69
  104.3 6.4 %collective-permute-start.23 = (bf16[128,1024]{1,0:T(8,128)(2,1)S(1)}, bf16[128,1024]{1,0:T(8,128)(2,1)S(1)}, u32[]{:S(2)}, u32[]{:S(2)}) collective-permute-start(bf16[128,1024]{1,0:T(8,128)(2,1)S(1)} %add_convert_fusion.3), channel_id=1, source_target_pairs={{0,4},{4,8},{8,12},{12,14},{14,10},{10,6},{6,2},{2,0},{1,3},{5,1},... | collective-permute-start | bytes 786440 | tf_op jit(solution)/shard_map/ppermute | solution.py:69
  110.9 6.4 %collective-permute-start.29 = (bf16[128,1024]{1,0:T(8,128)(2,1)S(1)}, bf16[128,1024]{1,0:T(8,128)(2,1)S(1)}, u32[]{:S(2)}, u32[]{:S(2)}) collective-permute-start(bf16[128,1024]{1,0:T(8,128)(2,1)S(1)} %add_convert_fusion.refs_0_), channel_id=1, source_target_pairs={{0,4},{4,8},{8,12},{12,14},{14,10},{10,6},{6,2},{2,0},{1,3},{5,1},... | collective-permute-start | bytes 786440 | tf_op jit(solution)/shard_map/ppermute | solution.py:69
  113.2 6.4 %collective-permute-start.28 = (bf16[128,1024]{1,0:T(8,128)(2,1)S(1)}, bf16[128,1024]{1,0:T(8,128)(2,1)S(1)}, u32[]{:S(2)}, u32[]{:S(2)}) collective-permute-start(bf16[128,1024]{1,0:T(8,128)(2,1)S(1)} %add_convert_fusion.refs_0_), channel_id=1, source_target_pairs={{0,1},{1,0},{2,3},{3,2},{4,5},{5,4},{6,7},{7,6},{8,9},{9,8},{10,11... | collective-permute-start | bytes 786440 | tf_op jit(solution)/shard_map/ppermute | solution.py:69
  119.6 6.9 %collective-permute-start.31 = (bf16[128,1024]{1,0:T(8,128)(2,1)S(1)}, bf16[128,1024]{1,0:T(8,128)(2,1)S(1)}, u32[]{:S(2)}, u32[]{:S(2)}) collective-permute-start(bf16[128,1024]{1,0:T(8,128)(2,1)S(1)} %collective-permute-done.28.refs_1_), channel_id=1, source_target_pairs={{0,4},{4,8},{8,12},{12,14},{14,10},{10,6},{6,2},{2,0},{1,3},{5,1},... | collective-permute-start | bytes 786440 | tf_op jit(solution)/shard_map/ppermute | solution.py:69
  128.8 6.4 %collective-permute-start.30 = (bf16[128,1024]{1,0:T(8,128)(2,1)S(1)}, bf16[128,1024]{1,0:T(8,128)(2,1)S(1)}, u32[]{:S(2)}, u32[]{:S(2)}) collective-permute-start(bf16[128,1024]{1,0:T(8,128)(2,1)S(1)} %collective-permute-done.29.refs_2_), channel_id=1, source_target_pairs={{0,1},{1,0},{2,3},{3,2},{4,5},{5,4},{6,7},{7,6},{8,9},{9,8},{10,11... | collective-permute-start | bytes 786440 | tf_op jit(solution)/shard_map/ppermute | solution.py:69
  128.8 6.9 %collective-permute-start.34 = (bf16[128,1024]{1,0:T(8,128)(2,1)S(1)}, bf16[128,1024]{1,0:T(8,128)(2,1)S(1)}, u32[]{:S(2)}, u32[]{:S(2)}) collective-permute-start(bf16[128,1024]{1,0:T(8,128)(2,1)S(1)} %collective-permute-done.33.refs_6_), channel_id=1, source_target_pairs={{0,1},{1,0},{2,3},{3,2},{4,5},{5,4},{6,7},{7,6},{8,9},{9,8},{10,11... | collective-permute-start | bytes 786440 | tf_op jit(solution)/shard_map/ppermute | solution.py:69
  132.9 6.4 %collective-permute-start.39 = (bf16[128,1024]{1,0:T(8,128)(2,1)S(1)}, bf16[128,1024]{1,0:T(8,128)(2,1)S(1)}, u32[]{:S(2)}, u32[]{:S(2)}) collective-permute-start(bf16[128,1024]{1,0:T(8,128)(2,1)S(1)} %collective-permute-done.35.refs_8_), channel_id=1, source_target_pairs={{0,4},{4,8},{8,12},{12,14},{14,10},{10,6},{6,2},{2,0},{1,3},{5,1},... | collective-permute-start | bytes 786440 | tf_op jit(solution)/shard_map/ppermute | solution.py:69
  (28 other events, 235.8 us)

commit v3 on v2

--- a/solution.py
+++ b/solution.py
@@ -1,3 +1,5 @@
+import functools
+
 import jax
 import jax.numpy as jnp
 from jax import lax
@@ -47,6 +49,12 @@
 ONWARD = [(2 * RING[i], 2 * RING[(i + 1) % CHIPS]) for i in range(CHIPS)] + [
     (2 * RING[i] + 1, 2 * RING[i - 1] + 1) for i in range(CHIPS)
 ]
+ENTER = [(2 * RING[i], 2 * RING[i - 1] + 1) for i in range(CHIPS)] + [
+    (2 * RING[i] + 1, 2 * RING[(i + 1) % CHIPS]) for i in range(CHIPS)
+]
+LEAVE = [(2 * RING[i], 2 * RING[(i + 1) % CHIPS] + 1) for i in range(CHIPS)] + [
+    (2 * RING[i] + 1, 2 * RING[i - 1]) for i in range(CHIPS)
+]
 SWAP = [(t, t ^ 1) for t in range(2 * CHIPS)]
 STRAIGHT = [(k, 2 * k) for k in range(KVH)] + [(KVH + k, 2 * k + 1) for k in range(KVH)]
 CROSSED = [(k, 2 * k + 1) for k in range(KVH)] + [(KVH + k, 2 * k) for k in range(KVH)]
@@ -70,15 +78,27 @@
 
 
 def ring_gather(own):
-    straight, crossed = own, send(own, SWAP)
-    blocks = [straight, crossed]
+    straight, crossed = own, own
+    blocks = [own, send(own, SWAP)]
+    values_f = own.astype(jnp.float32)
+    squares = jnp.sum(values_f * values_f, axis=1)
     for step in range(1, 5):
+        if step > 1:
+            straight, squares = lax.optimization_barrier((straight, squares))
         straight = send(straight, ONWARD)
-        blocks += [straight, send(straight, SWAP)]
+        blocks.append(straight)
         if step < 4:
-            crossed = send(crossed, ONWARD)
+            blocks.append(send(straight, SWAP))
+            squares = squares + send(squares, [(t, t ^ 2**step) for t in range(2 * CHIPS)])
+            crossed = send(crossed, ENTER if step == 1 else ONWARD)
             blocks += [crossed, send(crossed, SWAP)]
-    return blocks
+    squares = squares + send(squares, SWAP)
+    return blocks, squares[None, :]
+
+
+def last_block(block, work):
+    block, work = lax.optimization_barrier((block, work))
+    return [block, send(block, SWAP)], work
 
 
 def gathered_ids(rank):
@@ -113,80 +133,153 @@
                 running[other] = (
                     running[other].astype(jnp.float32) + shares[step, other]
                 ).astype(jnp.bfloat16)
-            running[other] = send(running[other], ONWARD)
-    return running[0], send(running[1], SWAP)
-
-
-def row_factors(blocks):
-    width = blocks[0].shape[1]
-    squares = jnp.zeros((TOKENS, 128), jnp.float32)
-    for block in blocks:
-        for j in range(width // 128):
-            v = block[:, j * 128 : (j + 1) * 128].astype(jnp.float32)
-            squares = squares + v * v
-    mean = jnp.sum(squares, axis=1, keepdims=True) * (1.0 / (len(blocks) * width))
-    return lax.rsqrt(mean + epsilon)
-
-
-def project_kernel(ids, *refs):
-    blocks = refs[:16]
-    gain, cosine, sine, kv_cos, kv_sin, wq, wkv = refs[16:23]
-    q_keep, q_send, kv_straight, kv_crossed = refs[23:27]
-    wq_buf, wkv_buf, kv_buf, q_buf, sems = refs[27:]
-    width = blocks[0].shape[1]
+            running[other] = send(running[other], LEAVE if (step, other) == (1, 1) else ONWARD)
+    return running[0], running[1]
+
+
+def row_factors(squares, features):
+    factor = lax.rsqrt(squares[...] * (1.0 / features) + epsilon)
+    return jnp.transpose(jnp.broadcast_to(factor, (TOKENS, TOKENS)))
+
+
+def normed_block(block, factors, gain_row):
+    return jnp.concatenate(
+        [
+            (block[:, j : j + 128].astype(jnp.float32) * factors * gain_row[:, j : j + 128]).astype(
+                jnp.bfloat16
+            )
+            for j in range(0, block.shape[1], 128)
+        ],
+        axis=1,
+    )
+
+
+def in_hbm(array):
+    return pltpu.with_memory_space_constraint(array, pltpu.HBM)
+
+
+def weight_copies(ids, first, wq, wkv, out, sems):
+    count, width, _ = out.shape
     copies = []
-    for i in range(16):
-        rows = pl.ds(pl.multiple_of(ids[i] * width, width), width)
-        pair = (
-            pltpu.make_async_copy(wq.at[rows, :], wq_buf.at[i], sems.at[0, i]),
-            pltpu.make_async_copy(wkv.at[rows, :], wkv_buf.at[i], sems.at[1, i]),
-        )
+    for i in range(count):
+        rows = pl.ds(pl.multiple_of(ids[first + i] * width, width), width)
+        pair = [
+            pltpu.make_async_copy(weight.at[rows, :], out.at[i, :, pl.ds(j * HD, HD)], sems.at[j, i])
+            for j, weight in enumerate((wq, wkv))
+        ]
         for copy in pair:
             copy.start()
         copies.append(pair)
-    factor = row_factors(blocks)
-    total = jnp.zeros((TOKENS, 2 * HD), jnp.float32)
-    for i in range(16):
-        normed = (blocks[i][...].astype(jnp.float32) * factor * gain[ids[i]]).astype(jnp.bfloat16)
+    return copies
+
+
+def project_kernel(start, count, ahead, with_sum, ids, *refs):
+    blocks, refs = refs[:count], refs[count:]
+    squares, gain, wq, wkv = refs[:4]
+    before, refs = (refs[4], refs[5:]) if with_sum else (None, refs[4:])
+    out, refs = refs[0], refs[1:]
+    next_weights, refs = (refs[0], refs[1:]) if ahead else (None, refs)
+    weights, sems = refs[:2]
+    copies = weight_copies(ids, start, wq, wkv, weights, sems)
+    if ahead:
+        next_copies = weight_copies(ids, start + count, wq, wkv, next_weights, refs[2])
+    width = blocks[0].shape[1]
+    factors = row_factors(squares, 16 * width)
+    total = before[...] if with_sum else jnp.zeros((TOKENS, 2 * HD), jnp.float32)
+    for i in range(count):
+        normed = normed_block(blocks[i], factors, gain[ids[start + i]])
         for copy in copies[i]:
             copy.wait()
-        weights = jnp.concatenate([wq_buf[i], wkv_buf[i]], axis=1)
-        total = total + jnp.dot(normed, weights, preferred_element_type=jnp.float32)
+        total = total + jnp.dot(normed, weights[i], preferred_element_type=jnp.float32)
+    out[...] = total
+    if ahead:
+        for pair in next_copies:
+            for copy in pair:
+                copy.wait()
+
+
+def project_some(ids, start, blocks, squares, gain, wq, wkv, before=None, ahead=0):
+    count, width = len(blocks), blocks[0].shape[1]
+    out_shape = [jax.ShapeDtypeStruct((TOKENS, 2 * HD), jnp.float32)]
+    scratch = [
+        pltpu.VMEM((count, width, 2 * HD), jnp.bfloat16),
+        pltpu.SemaphoreType.DMA((2, count)),
+    ]
+    if ahead:
+        out_shape.append(jax.ShapeDtypeStruct((ahead, width, 2 * HD), jnp.bfloat16))
+        scratch.append(pltpu.SemaphoreType.DMA((2, ahead)))
+    sums = [] if before is None else [before]
+    return pl.pallas_call(
+        functools.partial(project_kernel, start, count, ahead, before is not None),
+        out_shape=out_shape,
+        in_specs=[SMEM] + [VMEM] * (count + 2) + [HBM] * 2 + [VMEM] * len(sums),
+        out_specs=[VMEM] * len(out_shape),
+        scratch_shapes=scratch,
+        compiler_params=pltpu.CompilerParams(vmem_limit_bytes=24 * MIB),
+        cost_estimate=pl.CostEstimate(
+            flops=4 * TOKENS * count * width * HD,
+            bytes_accessed=(count + ahead) * width * HD * 4 + count * TOKENS * width * 2,
+            transcendentals=0,
+        ),
+        name="project_%d" % start,
+    )(ids, *blocks, squares, gain, in_hbm(wq), in_hbm(wkv), *sums)
+
+
+def project_last_kernel(start, count, ids, *refs):
+    blocks, refs = refs[:count], refs[count:]
+    squares, gain, before, weights, cosine, sine, kv_cos, kv_sin = refs[:8]
+    q_keep, q_send, kv_straight, kv_crossed = refs[8:12]
+    factors = row_factors(squares, 16 * blocks[0].shape[1])
+    total = before[...]
+    for i in range(count):
+        normed = normed_block(blocks[i], factors, gain[ids[start + i]])
+        total = total + jnp.dot(normed, weights[i], preferred_element_type=jnp.float32)
     q, kv = total[:, :HD], total[:, HD:]
-    q_buf[...] = (q * cosine[...] + pltpu.roll(q, HD // 2, 1) * sine[...]).astype(jnp.bfloat16)
-    kv_buf[...] = (kv * kv_cos[...] + pltpu.roll(kv, HD // 2, 1) * kv_sin[...]).astype(jnp.bfloat16)
+    q = (q * cosine[...] + pltpu.roll(q, HD // 2, 1) * sine[...]).astype(jnp.bfloat16)
+    kv = (kv * kv_cos[...] + pltpu.roll(kv, HD // 2, 1) * kv_sin[...]).astype(jnp.bfloat16)
     core_one = ids[0] % 2 == 1
     holds_keys = ids[0] < KVH
     first, second = slice(0, SPAN), slice(SPAN, TOKENS)
-    q_keep[...] = jnp.where(core_one, q_buf[second, :], q_buf[first, :])
-    q_send[...] = jnp.where(core_one, q_buf[first, :], q_buf[second, :])
-    kv_straight[...] = jnp.where(holds_keys, kv_buf[first, :], kv_buf[second, :])
-    kv_crossed[...] = jnp.where(holds_keys, kv_buf[second, :], kv_buf[first, :])
-
-
-def project(ids, blocks, gain, tables, q_weight, kv_weight):
-    width = blocks[0].shape[1]
+    q_keep[...] = jnp.where(core_one, q[second], q[first])
+    q_send[...] = jnp.where(core_one, q[first], q[second])
+    kv_straight[...] = jnp.where(holds_keys, kv[first], kv[second])
+    kv_crossed[...] = jnp.where(holds_keys, kv[second], kv[first])
+
+
+def project_last(ids, start, blocks, squares, gain, before, weights, tables):
+    count = len(blocks)
     return pl.pallas_call(
-        project_kernel,
+        functools.partial(project_last_kernel, start, count),
         out_shape=[jax.ShapeDtypeStruct((SPAN, HD), jnp.bfloat16)] * 4,
-        in_specs=[SMEM] + [VMEM] * 21 + [HBM] * 2,
+        in_specs=[SMEM] + [VMEM] * (count + 8),
         out_specs=[VMEM] * 4,
-        scratch_shapes=[
-            pltpu.VMEM((16, width, HD), jnp.bfloat16),
-            pltpu.VMEM((16, width, HD), jnp.bfloat16),
-            pltpu.VMEM((TOKENS, HD), jnp.bfloat16),
-            pltpu.VMEM((TOKENS, HD), jnp.bfloat16),
-            pltpu.SemaphoreType.DMA((2, 16)),
-        ],
-        compiler_params=pltpu.CompilerParams(vmem_limit_bytes=32 * MIB),
+        compiler_params=pltpu.CompilerParams(vmem_limit_bytes=16 * MIB),
         cost_estimate=pl.CostEstimate(
-            flops=4 * TOKENS * 16 * width * HD, bytes_accessed=12 * MIB, transcendentals=0
-        ),
-        name="norm_project",
-    )(ids, *blocks, gain, *tables, q_weight, kv_weight)
-
-
-def attend_kernel(info, q, q_other, straight, crossed, cache, out):
+            flops=2 * TOKENS * weights.size, bytes_accessed=2 * MIB, transcendentals=0
+        ),
+        name="project_last",
+    )(ids, *blocks, squares, gain, before, weights, *tables)
+
+
+def share_copies(to, first, weight, weight_other, out, sems):
+    count, _, width = out.shape
+    copies = []
+    for i in range(count):
+        columns = pl.ds(pl.multiple_of(to[first + i] * width, width), width)
+        pair = [
+            pltpu.make_async_copy(part.at[:, columns], out.at[i, pl.ds(j * HD, HD), :], sems.at[j, i])
+            for j, part in enumerate((weight, weight_other))
+        ]
+        for copy in pair:
+            copy.start()
+        copies.append(pair)
+    return copies
+
+
+def attend_kernel(
+    info, to, q, q_other, straight, crossed, cache, weight, weight_other, out, weights, sems
+):
+    copies = share_copies(to, 0, weight, weight_other, weights, sems)
     core = info[SEQS]
     fresh_keys = jnp.where(core == 0, straight[...], crossed[...])
     fresh_values = jnp.where(core == 0, crossed[...], straight[...])
@@ -219,82 +312,102 @@
     attn = (summed / totals).astype(jnp.bfloat16)
     out[:, :HD] = attn[:SPAN]
     out[:, HD:] = attn[SPAN:]
-
-
-def attend(info, q, q_other, straight, crossed, cache):
+    for pair in copies:
+        for copy in pair:
+            copy.wait()
+
+
+def attend(info, to, q, q_other, straight, crossed, cache, weight, weight_other, ahead):
+    width = weight.shape[1] // 16
     return pl.pallas_call(
         attend_kernel,
-        out_shape=jax.ShapeDtypeStruct((SPAN, 2 * HD), jnp.bfloat16),
-        in_specs=[SMEM] + [VMEM] * 5,
-        out_specs=VMEM,
-        compiler_params=pltpu.CompilerParams(vmem_limit_bytes=24 * MIB),
+        out_shape=[
+            jax.ShapeDtypeStruct((SPAN, 2 * HD), jnp.bfloat16),
+            jax.ShapeDtypeStruct((ahead, 2 * HD, width), jnp.bfloat16),
+        ],
+        in_specs=[SMEM] * 2 + [VMEM] * 5 + [HBM] * 2,
+        out_specs=[VMEM] * 2,
+        scratch_shapes=[pltpu.SemaphoreType.DMA((2, ahead))],
+        compiler_params=pltpu.CompilerParams(vmem_limit_bytes=16 * MIB),
         cost_estimate=pl.CostEstimate(
-            flops=80 * MIB, bytes_accessed=MIB, transcendentals=TOKENS * 1088
+            flops=80 * MIB, bytes_accessed=3 * MIB, transcendentals=TOKENS * 1088
         ),
         name="attend",
-    )(info, q, q_other, straight, crossed, cache)
-
-
-def output_kernel(ids, attn, attn_other, weight, weight_other, *refs):
-    count = len(refs) - 2
-    outs, (weights, sems) = refs[:count], refs[count:]
-    width = weights.shape[2]
-    copies = []
-    for i in range(count):
-        columns = pl.ds(pl.multiple_of(ids[i] * width, width), width)
-        pair = (
-            pltpu.make_async_copy(weight.at[:, columns], weights.at[i, :HD], sems.at[0, i]),
-            pltpu.make_async_copy(weight_other.at[:, columns], weights.at[i, HD:], sems.at[1, i]),
-        )
-        for copy in pair:
-            copy.start()
-        copies.append(pair)
+    )(info, to, q, q_other, straight, crossed, cache, in_hbm(weight), weight_other)
+
+
+def both_heads(core, attn, attn_other):
     mine = attn[...]
     theirs = jnp.concatenate([attn_other[:, HD:], attn_other[:, :HD]], axis=1)
-    core_one = ids[count] == 1
-    rows = jnp.concatenate(
+    core_one = core[0] == 1
+    return jnp.concatenate(
         [jnp.where(core_one, theirs, mine), jnp.where(core_one, mine, theirs)], axis=0
     )
-    for i in range(count):
+
+
+def first_shares_kernel(core, attn, attn_other, weights, *outs):
+    rows = both_heads(core, attn, attn_other)
+    for i, out in enumerate(outs):
+        out[...] = jnp.dot(rows, weights[i], preferred_element_type=jnp.float32).astype(out.dtype)
+
+
+def first_shares(core, attn, attn_other, weights):
+    count, _, width = weights.shape
+    return pl.pallas_call(
+        first_shares_kernel,
+        out_shape=[jax.ShapeDtypeStruct((TOKENS, width), jnp.bfloat16)] * count,
+        in_specs=[SMEM] + [VMEM] * 3,
+        out_specs=[VMEM] * count,
+        compiler_params=pltpu.CompilerParams(vmem_limit_bytes=16 * MIB),
+        cost_estimate=pl.CostEstimate(
+            flops=2 * TOKENS * weights.size, bytes_accessed=count * MIB, transcendentals=0
+        ),
+        name="first_shares",
+    )(core, attn, attn_other, weights)
+
+
+def more_shares_kernel(first, core, to, attn, attn_other, weight, weight_other, *refs):
+    outs, (weights, sems) = refs[:-2], refs[-2:]
+    copies = share_copies(to, first, weight, weight_other, weights, sems)
+    rows = both_heads(core, attn, attn_other)
+    for i, out in enumerate(outs):
         for copy in copies[i]:
             copy.wait()
-        outs[i][...] = jnp.dot(
-            rows, weights[i], preferred_element_type=jnp.float32
-        ).astype(outs[i].dtype)
-
-
-def output_shares(ids, core, attn, attn_other, weight, weight_other, width, dtype):
-    count = ids.shape[0]
+        out[...] = jnp.dot(rows, weights[i], preferred_element_type=jnp.float32)
+
+
+def more_shares(core, to, attn, attn_other, weight, weight_other, first):
+    count, width = len(SHARES) - first, weight.shape[1] // 16
     return pl.pallas_call(
-        output_kernel,
-        out_shape=[jax.ShapeDtypeStruct((TOKENS, width), dtype)] * count,
-        in_specs=[SMEM, VMEM, VMEM, HBM, HBM],
+        functools.partial(more_shares_kernel, first),
+        out_shape=[jax.ShapeDtypeStruct((TOKENS, width), jnp.float32)] * count,
+        in_specs=[SMEM] * 2 + [VMEM] * 2 + [HBM] * 2,
         out_specs=[VMEM] * count,
         scratch_shapes=[
             pltpu.VMEM((count, 2 * HD, width), jnp.bfloat16),
             pltpu.SemaphoreType.DMA((2, count)),
         ],
-        compiler_params=pltpu.CompilerParams(vmem_limit_bytes=24 * MIB),
+        compiler_params=pltpu.CompilerParams(vmem_limit_bytes=16 * MIB),
         cost_estimate=pl.CostEstimate(
             flops=4 * TOKENS * HD * width * count,
             bytes_accessed=count * MIB,
             transcendentals=0,
         ),
-        name="output_shares_%d" % count,
-    )(jnp.concatenate([ids, core[None].astype(jnp.int32)]), attn, attn_other, weight, weight_other)
-
-
-def final_kernel(ids, *refs):
-    blocks, gain, out = refs[:16], refs[16], refs[17]
-    staged, sems = refs[18:]
+        name="more_shares",
+    )(core, to, attn, attn_other, in_hbm(weight), weight_other)
+
+
+def final_kernel(start, count, features, ids, *refs):
+    blocks, squares, gain = refs[:count], refs[count], refs[count + 1]
+    out, staged, sems = refs[-3:]
     width = blocks[0].shape[1]
-    factor = row_factors(blocks)
+    factors = row_factors(squares, features)
     copies = []
-    for i in range(16):
-        staged[i] = (blocks[i][...].astype(jnp.float32) * factor * gain[ids[i]]).astype(jnp.bfloat16)
+    for i in range(count):
+        staged[i] = normed_block(blocks[i], factors, gain[ids[start + i]])
         copy = pltpu.make_async_copy(
             staged.at[i],
-            out.at[:, pl.ds(pl.multiple_of(ids[i] * width, width), width)],
+            out.at[:, pl.ds(pl.multiple_of(ids[start + i] * width, width), width)],
             sems.at[i],
         )
         copy.start()
@@ -303,20 +416,28 @@
         copy.wait()
 
 
-def final_norm(ids, blocks, gain):
-    width = blocks[0].shape[1]
+def final_some(ids, start, blocks, squares, gain, before=None):
+    count, width = len(blocks), blocks[0].shape[1]
+    features = 16 * width
+    kept = [] if before is None else [before]
     return pl.pallas_call(
-        final_kernel,
-        out_shape=jax.ShapeDtypeStruct((TOKENS, 16 * width), jnp.bfloat16),
-        in_specs=[SMEM] + [VMEM] * 17,
+        functools.partial(final_kernel, start, count, features),
+        out_shape=jax.ShapeDtypeStruct((TOKENS, features), jnp.bfloat16),
+        in_specs=[SMEM] + [VMEM] * (count + 2) + [HBM] * len(kept),
         out_specs=HBM,
+        input_output_aliases={count + 3: 0} if kept else {},
         scratch_shapes=[
-            pltpu.VMEM((16, TOKENS, width), jnp.bfloat16),
-            pltpu.SemaphoreType.DMA((16,)),
+            pltpu.VMEM((count, TOKENS, width), jnp.bfloat16),
+            pltpu.SemaphoreType.DMA((count,)),
         ],
-        compiler_params=pltpu.CompilerParams(vmem_limit_bytes=32 * MIB),
-        name="final_norm",
-    )(ids, *blocks, gain)
+        compiler_params=pltpu.CompilerParams(vmem_limit_bytes=16 * MIB),
+        cost_estimate=pl.CostEstimate(
+            flops=4 * TOKENS * width * count,
+            bytes_accessed=4 * TOKENS * width * count,
+            transcendentals=0,
+        ),
+        name="final_%d" % start,
+    )(ids, *blocks, squares, gain, *kept)
 
 
 def per_device_ring(
@@ -326,17 +447,17 @@
     core = rank % 2
     width = residual.shape[1]
     ids = gathered_ids(rank)
-
-    blocks = ring_gather(residual)
+    to = share_ids(rank)
+    core_id = core[None].astype(jnp.int32)
+    info = jnp.concatenate([prefix, core_id])
+
+    blocks, squares = ring_gather(residual)
+    weight_other = send(o_weight, SWAP)
 
     by_head = lambda cache: jnp.transpose(cache.reshape(SEQS, CTX_DEV, KVH, HD), (2, 0, 1, 3))
     pieces = jnp.stack([by_head(key_cache), by_head(value_cache)], axis=2)
     pieces = pieces.reshape(2 * KVH, 2, CTX_DEV, HD)
-    pieces, _ = lax.optimization_barrier((pieces, blocks[-4]))
     cache = lax.all_to_all(pieces, "tp", split_axis=0, concat_axis=0, tiled=True)
-
-    held, _ = lax.optimization_barrier((o_weight, blocks[2]))
-    weight_other = send(held, SWAP)
 
     positions = (prefix[:, None] + jnp.arange(SPAN, dtype=jnp.int32)[None, :]).reshape(-1)
     cosine, sine = rope_tables(positions)
@@ -345,25 +466,39 @@
     holds_keys = rank < KVH
     tables = (cosine, sine, jnp.where(holds_keys, cosine, 1.0), jnp.where(holds_keys, sine, 0.0))
 
-    q_keep, q_send, straight, crossed = project(
-        ids, blocks, attn_gain.reshape(16, 1, width).astype(jnp.float32), tables, q_weight, kv_weight
-    )
-    info = jnp.concatenate([prefix, core[None].astype(jnp.int32)])
-    attn = attend(
-        info, q_keep, send(q_send, SWAP), send(straight, STRAIGHT), send(crossed, CROSSED), cache
-    )
-
-    to = share_ids(rank)
-    inputs = (core, attn, send(attn, SWAP), o_weight, weight_other, width)
-    shares = output_shares(to[:2], *inputs, jnp.bfloat16)
-    shares += output_shares(to[2:], *inputs, jnp.float32)
-    shares = dict(zip(SHARES, shares))
-    one_way, other_way = ring_sum(shares)
-    projected = shares[0, 0] + one_way.astype(jnp.float32) + other_way.astype(jnp.float32)
+    gain = attn_gain.reshape(16, 1, width).astype(jnp.float32)
+    shared = (squares, gain, q_weight, kv_weight)
+    (total,) = project_some(ids, 0, blocks[:10], *shared)
+    last, total = last_block(blocks[14], total)
+    total, last_weights = project_some(ids, 10, blocks[10:14], *shared, before=total, ahead=2)
+    q_keep, q_send, straight, crossed = project_last(
+        ids, 14, last, squares, gain, total, last_weights, tables
+    )
+    attn, first_weights = attend(
+        info,
+        to,
+        q_keep,
+        send(q_send, SWAP),
+        send(straight, STRAIGHT),
+        send(crossed, CROSSED),
+        cache,
+        o_weight,
+        weight_other,
+        2,
+    )
+    attn_other = send(attn, SWAP)
+    shares = list(first_shares(core_id, attn, attn_other, first_weights))
+    shares += more_shares(core_id, to, attn, attn_other, o_weight, weight_other, 2)
+    one_way, other_way = ring_sum(dict(zip(SHARES, shares)))
+    projected = shares[-1] + one_way.astype(jnp.float32) + other_way.astype(jnp.float32)
     hidden = (residual.astype(jnp.float32) + projected).astype(jnp.bfloat16)
-    return final_norm(
-        ids, ring_gather(hidden), ffn_gain.reshape(16, 1, width).astype(jnp.float32)
-    )
+
+    blocks, squares = ring_gather(hidden)
+    gain = ffn_gain.reshape(16, 1, width).astype(jnp.float32)
+    out = final_some(ids, 0, blocks[:10], squares, gain)
+    last, out = last_block(blocks[14], out)
+    out = final_some(ids, 10, blocks[10:14], squares, gain, out)
+    return final_some(ids, 14, last, squares, gain, out)
 
 
 def per_device(

time: 145 us -> 128 us (0.88)
  starting transfers between devices: 58.4 us -> 47.3 us
  local copies, waits for them, and re-layouts: 10.1 us -> 2.3 us
  Pallas kernels: 16.9 us -> 19.2 us
  waiting for transfers between devices: 55.3 us -> 53.5 us
    ppermute x43 -> x50, starting transfers between devices: 52 us -> 42.2 us  [send(): return lax.ppermute(array, 'tp', pairs)]
    unnamed x16 -> x10, local copies, waits for them, and re-layouts: 8.77 us -> 0.97 us
    pallas_call x5 -> x9, Pallas kernels: 16.9 us -> 19.2 us  [the longest x2 7.09 us: project_some(): pl.pallas_call(functools.partial(project_kernel, start, count, ahead, bef...]
    ppermute x43 -> x50, waiting for transfers between devices: 55.3 us -> 53.5 us  [send(): return lax.ppermute(array, 'tp', pairs)]
  transfers between devices with their start and end apart: 44 -> 51, of which waited for: 24 -> 21; matrix products, arithmetic and copies ran while one was open for 3% -> 4% of each run, Pallas kernels for 8% -> 12%
where the time goes in v3:
time: 128 us; the launch traced here: 127 us
  waiting for transfers between devices  53.5 us (42%)
  starting transfers between devices  47.3 us (37%)
  Pallas kernels  19.2 us (15%)
  other arithmetic  4.52 us (4%)
  local copies, waits for them, and re-layouts  2.3 us (2%)
    ppermute x50, waiting for transfers between devices, send(): return lax.ppermute(array, 'tp', pairs)  53.5 us
    ppermute x50, starting transfers between devices, send(): return lax.ppermute(array, 'tp', pairs)  42.2 us
    pallas_call x2, Pallas kernels, project_some(): pl.pallas_call(functools.partial(project_kernel, start, count, ahead, bef...  7.09 us
    pallas_call x3, Pallas kernels, final_some(): pl.pallas_call(functools.partial(final_kernel, start, count, features), o...  5.49 us
    all_to_all x1, starting transfers between devices, per_device_ring(): lax.all_to_all(pieces, 'tp', split_axis=0, concat_axis=0, tiled=True)  5.1 us
    pallas_call x1, Pallas kernels, more_shares(): pl.pallas_call(functools.partial(more_shares_kernel, first), out_shape=[j...  3.1 us
  transfers between devices with their start and end apart: 51, of which 21 were waited for; matrix products, arithmetic and copies ran while one was open for 4% of the time, Pallas kernels for 12%

profile of v3, /device:TPU:0, one launch (start us, length us, event | category | flops | bytes accessed | tf_op | source)
XLA Modules:
  0.0 127.2 jit_solution(11002793281436785765)
XLA Ops:
  0.5 2.6 %collective-permute-start = (bf16[128,1024]{1,0:T(8,128)(2,1)}, bf16[128,1024]{1,0:T(8,128)(2,1)S(1)}, u32[]{:S(2)}, u32[]{:S(2)}) collective-permute-start(bf16[128,1024]{1,0:T(8,128)(2,1)} %refs_0_.1), channel_id=1, source_target_pairs={{0,4},{4,8},{8,12},{12,14},{14,10},{10,6},{6,2},{2,0},{1,3},{5,1},... | collective-permute-start | bytes 786440 | tf_op jit(solution)/shard_map/ppermute | solution.py:77
  7.1 2.4 %collective-permute-done.1 = f32[128]{0:T(128)S(1)} collective-permute-done((f32[128]{0:T(128)S(1)}, f32[128]{0:T(128)S(1)}, u32[]{:S(2)}, u32[]{:S(2)}) %collective-permute-start.1) | collective-permute-done | bytes 544 | tf_op jit(solution)/shard_map/ppermute | solution.py:77
  9.5 2.0 %collective-permute-start.2 = (bf16[128,1024]{1,0:T(8,128)(2,1)S(1)}, bf16[128,1024]{1,0:T(8,128)(2,1)S(1)}, u32[]{:S(2)}, u32[]{:S(2)}) collective-permute-start(bf16[128,1024]{1,0:T(8,128)(2,1)S(1)} %collective-permute-done.refs_2_), channel_id=1, source_target_pairs={{0,4},{4,8},{8,12},{12,14},{14,10},{10,6},{6,2},{2,0},{1,3},{5,1},... | collective-permute-start | bytes 786440 | tf_op jit(solution)/shard_map/ppermute | solution.py:77
  15.4 2.5 %collective-permute-start.12 = (bf16[128,1024]{1,0:T(8,128)(2,1)S(1)}, bf16[128,1024]{1,0:T(8,128)(2,1)S(1)}, u32[]{:S(2)}, u32[]{:S(2)}) collective-permute-start(bf16[128,1024]{1,0:T(8,128)(2,1)S(1)} %collective-permute-done.9.refs_4_), channel_id=1, source_target_pairs={{0,4},{4,8},{8,12},{12,14},{14,10},{10,6},{6,2},{2,0},{1,3},{5,1},... | collective-permute-start | bytes 786440 | tf_op jit(solution)/shard_map/ppermute | solution.py:77
  19.9 5.1 %all-to-all-start = ((bf16[16,2,64,128]{3,2,1,0:T(8,128)(2,1)}), bf16[16,2,64,128]{3,2,1,0:T(8,128)(2,1)S(1)}, u32[]{:S(2)}, u32[]{:S(2)}) async-start(bf16[16,2,64,128]{3,2,1,0:T(8,128)(2,1)} %pad_maximum_fusion), calls=%async_computation | async-start | bytes 1048576 | tf_op jit(solution)/shard_map/all_to_all | solution.py:460
  25.5 2.6 %collective-permute-start.5 = (f32[128]{0:T(128)S(1)}, f32[128]{0:T(128)S(1)}, u32[]{:S(2)}, u32[]{:S(2)}) collective-permute-start(f32[128]{0:T(128)S(1)} %add.281), channel_id=1, source_target_pairs={{0,8},{1,9},{2,10},{3,11},{4,12},{5,13},{6,14},{7,15},{8,0},{9,1},... | collective-permute-start | bytes 1544 | tf_op jit(solution)/shard_map/ppermute | solution.py:77
  28.9 11.4 %collective-permute-done.5 = f32[128]{0:T(128)S(1)} collective-permute-done((f32[128]{0:T(128)S(1)}, f32[128]{0:T(128)S(1)}, u32[]{:S(2)}, u32[]{:S(2)}) %collective-permute-start.5) | collective-permute-done | bytes 544 | tf_op jit(solution)/shard_map/ppermute | solution.py:77
  44.6 2.0 %collective-permute-done.17.refs_2_ = bf16[128,1024]{1,0:T(8,128)(2,1)S(1)} collective-permute-done((bf16[128,1024]{1,0:T(8,128)(2,1)S(1)}, bf16[128,1024]{1,0:T(8,128)(2,1)S(1)}, u32[]{:S(2)}, u32[]{:S(2)}) %collective-permute-start.17) | collective-permute-done | bytes 262176 | tf_op jit(solution)/shard_map/ppermute | solution.py:77
  47.6 4.4 %project_0.1.refs_8_ = f32[128,256]{1,0:T(8,128)S(1)} custom-call(s32[16]{0:T(128)S(1)} %stack.103.ids, bf16[128,1024]{1,0:T(8,128)(2,1)S(1)} %copy-done.1, bf16[128,1024]{1,0:T(8,128)(2,1)S(1)} %collective-permute-done.7.refs_1_, bf16[128,1024]{1,0:T(8,128)(2,1)S(1)} %collective-permute-done.refs_2_, bf16[128,1024]{1,0:T(8,128)(2,1)S(1)} %collective-permute-done.8.refs_3_, ...), custom_call_target="tpu_custom_call" | custom-call | flops 671088640 | bytes 7864320 | tf_op jit(solution)/shard_map/project_0/pallas_call | solution.py:212
  53.1 2.7 %project_10.1 = (f32[128,256]{1,0:T(8,128)S(1)}, bf16[2,1024,256]{2,1,0:T(8,128)(2,1)S(1)}) custom-call(s32[16]{0:T(128)S(1)} %stack.103.ids, bf16[128,1024]{1,0:T(8,128)(2,1)S(1)} %collective-permute-done.4.refs_0_, bf16[128,1024]{1,0:T(8,128)(2,1)S(1)} %collective-permute-done.16.refs_1_, bf16[128,1024]{1,0:T(8,128)(2,1)S(1)} %collective-permute-done.17.refs_2_, ...), custom_call_target="tpu_custom_call" | custom-call | flops 268435456 | bytes 4194304 | tf_op jit(solution)/shard_map/project_10/pallas_call | solution.py:212
  57.5 2.9 %collective-permute-start.21 = (bf16[64,128]{1,0:T(8,128)(2,1)S(1)}, bf16[64,128]{1,0:T(8,128)(2,1)S(1)}, u32[]{:S(2)}, u32[]{:S(2)}) collective-permute-start(bf16[64,128]{1,0:T(8,128)(2,1)S(1)} %get-tuple-element.50), channel_id=1, source_target_pairs={{0,1},{1,3},{2,5},{3,7},{4,9},{5,11},{6,13},{7,15},{8,0},{9,2},{10... | collective-permute-start | bytes 49160 | tf_op jit(solution)/shard_map/ppermute | solution.py:77
  60.7 2.9 %collective-permute-done.21.crossed = bf16[64,128]{1,0:T(8,128)(2,1)S(1)} collective-permute-done((bf16[64,128]{1,0:T(8,128)(2,1)S(1)}, bf16[64,128]{1,0:T(8,128)(2,1)S(1)}, u32[]{:S(2)}, u32[]{:S(2)}) %collective-permute-start.21) | collective-permute-done | bytes 16416 | tf_op jit(solution)/shard_map/ppermute | solution.py:77
  63.7 2.2 %attend.1 = (bf16[64,256]{1,0:T(8,128)(2,1)S(1)}, bf16[2,256,1024]{2,1,0:T(8,128)(2,1)S(1)}) custom-call(s32[3]{0:T(128)S(1)} %pad_add_fusion.info, s32[8]{0:T(128)S(1)} %stack.112.to, bf16[64,128]{1,0:T(8,128)(2,1)S(1)} %get-tuple-element.47.q, bf16[64,128]{1,0:T(8,128)(2,1)S(1)} %collective-permute-done.19.q_other, ...), custom_call_target="tpu_custom_call" | custom-call | flops 83886080 | bytes 3145728 | tf_op jit(solution)/shard_map/attend/pallas_call | solution.py:322
  70.1 3.1 %more_shares.1 = (f32[128,1024]{1,0:T(8,128)S(1)}, f32[128,1024]{1,0:T(8,128)S(1)}, f32[128,1024]{1,0:T(8,128)S(1)}, f32[128,1024]{1,0:T(8,128)S(1)}, f32[128,1024]{1,0:T(8,128)S(1)}, /*index=5*/f32[128,1024]{1,0:T(8,128)S(1)}) custom-call(s32[1]{0:T(128)} %bitcast.16.core, s32[8]{0:T(128)S(1)} %stack.112.to, bf16[64,256]{1,0:T(8,128)(2,1)S(1)} %get-tuple-element.51.attn, ...), custom_call_target="tpu_custom_call" | custom-call | flops 402653184 | bytes 6291456 | tf_op jit(solution)/shard_map/more_shares/pallas_call | solution.py:381
  74.8 1.9 %collective-permute-done.28 = bf16[128,1024]{1,0:T(8,128)(2,1)S(1)} collective-permute-done((bf16[128,1024]{1,0:T(8,128)(2,1)S(1)}, bf16[128,1024]{1,0:T(8,128)(2,1)S(1)}, u32[]{:S(2)}, u32[]{:S(2)}) %collective-permute-start.28) | collective-permute-done | bytes 262176 | tf_op jit(solution)/shard_map/ppermute | solution.py:77
  77.6 2.7 %collective-permute-done.25 = bf16[128,1024]{1,0:T(8,128)(2,1)S(1)} collective-permute-done((bf16[128,1024]{1,0:T(8,128)(2,1)S(1)}, bf16[128,1024]{1,0:T(8,128)(2,1)S(1)}, u32[]{:S(2)}, u32[]{:S(2)}) %collective-permute-start.25) | collective-permute-done | bytes 262176 | tf_op jit(solution)/shard_map/ppermute | solution.py:77
  83.3 3.5 %collective-permute-done.26 = bf16[128,1024]{1,0:T(8,128)(2,1)S(1)} collective-permute-done((bf16[128,1024]{1,0:T(8,128)(2,1)S(1)}, bf16[128,1024]{1,0:T(8,128)(2,1)S(1)}, u32[]{:S(2)}, u32[]{:S(2)}) %collective-permute-start.26) | collective-permute-done | bytes 262176 | tf_op jit(solution)/shard_map/ppermute | solution.py:77
  89.1 4.2 %collective-permute-done.27 = bf16[128,1024]{1,0:T(8,128)(2,1)S(1)} collective-permute-done((bf16[128,1024]{1,0:T(8,128)(2,1)S(1)}, bf16[128,1024]{1,0:T(8,128)(2,1)S(1)}, u32[]{:S(2)}, u32[]{:S(2)}) %collective-permute-start.27) | collective-permute-done | bytes 262176 | tf_op jit(solution)/shard_map/ppermute | solution.py:77
  95.6 5.7 %collective-permute-done.32 = f32[128]{0:T(128)S(1)} collective-permute-done((f32[128]{0:T(128)S(1)}, f32[128]{0:T(128)S(1)}, u32[]{:S(2)}, u32[]{:S(2)}) %collective-permute-start.32) | collective-permute-done | bytes 544 | tf_op jit(solution)/shard_map/ppermute | solution.py:77
  102.3 2.5 %collective-permute-start.34 = (f32[128]{0:T(128)S(1)}, f32[128]{0:T(128)S(1)}, u32[]{:S(2)}, u32[]{:S(2)}) collective-permute-start(f32[128]{0:T(128)S(1)} %add.295), channel_id=1, source_target_pairs={{0,4},{1,5},{2,6},{3,7},{4,0},{5,1},{6,2},{7,3},{8,12},{9,13},{10,... | collective-permute-start | bytes 1544 | tf_op jit(solution)/shard_map/ppermute | solution.py:77
  106.3 2.3 %collective-permute-done.33.refs_6_ = bf16[128,1024]{1,0:T(8,128)(2,1)S(1)} collective-permute-done((bf16[128,1024]{1,0:T(8,128)(2,1)S(1)}, bf16[128,1024]{1,0:T(8,128)(2,1)S(1)}, u32[]{:S(2)}, u32[]{:S(2)}) %collective-permute-start.33) | collective-permute-done | bytes 262176 | tf_op jit(solution)/shard_map/ppermute | solution.py:77
  109.2 2.7 %collective-permute-start.36 = (f32[128]{0:T(128)S(1)}, f32[128]{0:T(128)S(1)}, u32[]{:S(2)}, u32[]{:S(2)}) collective-permute-start(f32[128]{0:T(128)S(1)} %add.296), channel_id=1, source_target_pairs={{0,8},{1,9},{2,10},{3,11},{4,12},{5,13},{6,14},{7,15},{8,0},{9,1},... | collective-permute-start | bytes 1544 | tf_op jit(solution)/shard_map/ppermute | solution.py:77
  113.7 2.4 %collective-permute-start.48 = (bf16[128,1024]{1,0:T(8,128)(2,1)S(1)}, bf16[128,1024]{1,0:T(8,128)(2,1)S(1)}, u32[]{:S(2)}, u32[]{:S(2)}) collective-permute-start(bf16[128,1024]{1,0:T(8,128)(2,1)S(1)} %collective-permute-done.43.refs_8_), channel_id=1, source_target_pairs={{0,4},{4,8},{8,12},{12,14},{14,10},{10,6},{6,2},{2,0},{1,3},{5,1},... | collective-permute-start | bytes 786440 | tf_op jit(solution)/shard_map/ppermute | solution.py:77
  120.3 2.3 %final_0.1.refs_6_ = bf16[128,16384]{1,0:T(8,128)(2,1)} custom-call(s32[16]{0:T(128)S(1)} %stack.103.ids, bf16[128,1024]{1,0:T(8,128)(2,1)S(1)} %get-tuple-element.70.refs_0_, bf16[128,1024]{1,0:T(8,128)(2,1)S(1)} %collective-permute-done.38.refs_1_, bf16[128,1024]{1,0:T(8,128)(2,1)S(1)} %collective-permute-done.31.refs_2_, ...), custom_call_target="tpu_custom_call" | custom-call | flops 5242880 | bytes 5242880 | tf_op jit(solution)/shard_map/final_0/pallas_call | solution.py:423
  (125 shorter events, 47.8 us)
Async XLA Ops:
  0.0 63.6 %collective-permute-start.22 = (bf16[128,16384]{1,0:T(8,128)(2,1)}, bf16[128,16384]{1,0:T(8,128)(2,1)}, u32[]{:S(2)}, u32[]{:S(2)}) collective-permute-start(bf16[128,16384]{1,0:T(8,128)(2,1)} %weight.3), channel_id=1, source_target_pairs={{0,1},{1,0},{2,3},{3,2},{4,5},{5,4},{6,7},{7,6},{8,9},{9,8},{10,11... | collective-permute-start | bytes 12582920 | tf_op jit(solution)/shard_map/ppermute | solution.py:77
  0.5 9.1 %collective-permute-start = (bf16[128,1024]{1,0:T(8,128)(2,1)}, bf16[128,1024]{1,0:T(8,128)(2,1)S(1)}, u32[]{:S(2)}, u32[]{:S(2)}) collective-permute-start(bf16[128,1024]{1,0:T(8,128)(2,1)} %refs_0_.1), channel_id=1, source_target_pairs={{0,4},{4,8},{8,12},{12,14},{14,10},{10,6},{6,2},{2,0},{1,3},{5,1},... | collective-permute-start | bytes 786440 | tf_op jit(solution)/shard_map/ppermute | solution.py:77
  3.1 10.1 %collective-permute-start.9 = (bf16[128,1024]{1,0:T(8,128)(2,1)}, bf16[128,1024]{1,0:T(8,128)(2,1)S(1)}, u32[]{:S(2)}, u32[]{:S(2)}) collective-permute-start(bf16[128,1024]{1,0:T(8,128)(2,1)} %refs_0_.1), channel_id=1, source_target_pairs={{0,3},{4,1},{8,5},{12,9},{14,13},{10,15},{6,11},{2,7},{1,4},{5,8},... | collective-permute-start | bytes 786440 | tf_op jit(solution)/shard_map/ppermute | solution.py:77
  7.1 17.9 %collective-permute-start.7 = (bf16[128,1024]{1,0:T(8,128)(2,1)}, bf16[128,1024]{1,0:T(8,128)(2,1)S(1)}, u32[]{:S(2)}, u32[]{:S(2)}) collective-permute-start(bf16[128,1024]{1,0:T(8,128)(2,1)} %refs_0_.1), channel_id=1, source_target_pairs={{0,1},{1,0},{2,3},{3,2},{4,5},{5,4},{6,7},{7,6},{8,9},{9,8},{10,11... | collective-permute-start | bytes 786440 | tf_op jit(solution)/shard_map/ppermute | solution.py:77
  9.5 8.4 %collective-permute-start.2 = (bf16[128,1024]{1,0:T(8,128)(2,1)S(1)}, bf16[128,1024]{1,0:T(8,128)(2,1)S(1)}, u32[]{:S(2)}, u32[]{:S(2)}) collective-permute-start(bf16[128,1024]{1,0:T(8,128)(2,1)S(1)} %collective-permute-done.refs_2_), channel_id=1, source_target_pairs={{0,4},{4,8},{8,12},{12,14},{14,10},{10,6},{6,2},{2,0},{1,3},{5,1},... | collective-permute-start | bytes 786440 | tf_op jit(solution)/shard_map/ppermute | solution.py:77
  13.2 12.3 %collective-permute-start.8 = (bf16[128,1024]{1,0:T(8,128)(2,1)S(1)}, bf16[128,1024]{1,0:T(8,128)(2,1)S(1)}, u32[]{:S(2)}, u32[]{:S(2)}) collective-permute-start(bf16[128,1024]{1,0:T(8,128)(2,1)S(1)} %collective-permute-done.refs_2_), channel_id=1, source_target_pairs={{0,1},{1,0},{2,3},{3,2},{4,5},{5,4},{6,7},{7,6},{8,9},{9,8},{10,11... | collective-permute-start | bytes 786440 | tf_op jit(solution)/shard_map/ppermute | solution.py:77
  15.4 13.4 %collective-permute-start.12 = (bf16[128,1024]{1,0:T(8,128)(2,1)S(1)}, bf16[128,1024]{1,0:T(8,128)(2,1)S(1)}, u32[]{:S(2)}, u32[]{:S(2)}) collective-permute-start(bf16[128,1024]{1,0:T(8,128)(2,1)S(1)} %collective-permute-done.9.refs_4_), channel_id=1, source_target_pairs={{0,4},{4,8},{8,12},{12,14},{14,10},{10,6},{6,2},{2,0},{1,3},{5,1},... | collective-permute-start | bytes 786440 | tf_op jit(solution)/shard_map/ppermute | solution.py:77
  17.9 22.4 %collective-permute-start.4 = (bf16[128,1024]{1,0:T(8,128)(2,1)S(1)}, bf16[128,1024]{1,0:T(8,128)(2,1)S(1)}, u32[]{:S(2)}, u32[]{:S(2)}) collective-permute-start(bf16[128,1024]{1,0:T(8,128)(2,1)S(1)} %collective-permute-done.2.refs_6_), channel_id=1, source_target_pairs={{0,4},{4,8},{8,12},{12,14},{14,10},{10,6},{6,2},{2,0},{1,3},{5,1},... | collective-permute-start | bytes 786440 | tf_op jit(solution)/shard_map/ppermute | solution.py:77
  19.9 40.8 %all-to-all-start = ((bf16[16,2,64,128]{3,2,1,0:T(8,128)(2,1)}), bf16[16,2,64,128]{3,2,1,0:T(8,128)(2,1)S(1)}, u32[]{:S(2)}, u32[]{:S(2)}) async-start(bf16[16,2,64,128]{3,2,1,0:T(8,128)(2,1)} %pad_maximum_fusion), calls=%async_computation | async-start | bytes 1048576 | tf_op jit(solution)/shard_map/all_to_all | solution.py:460
  25.0 16.7 %collective-permute-start.10 = (bf16[128,1024]{1,0:T(8,128)(2,1)S(1)}, bf16[128,1024]{1,0:T(8,128)(2,1)S(1)}, u32[]{:S(2)}, u32[]{:S(2)}) collective-permute-start(bf16[128,1024]{1,0:T(8,128)(2,1)S(1)} %collective-permute-done.9.refs_4_), channel_id=1, source_target_pairs={{0,1},{1,0},{2,3},{3,2},{4,5},{5,4},{6,7},{7,6},{8,9},{9,8},{10,11... | collective-permute-start | bytes 786440 | tf_op jit(solution)/shard_map/ppermute | solution.py:77
  25.5 14.8 %collective-permute-start.5 = (f32[128]{0:T(128)S(1)}, f32[128]{0:T(128)S(1)}, u32[]{:S(2)}, u32[]{:S(2)}) collective-permute-start(f32[128]{0:T(128)S(1)} %add.281), channel_id=1, source_target_pairs={{0,8},{1,9},{2,10},{3,11},{4,12},{5,13},{6,14},{7,15},{8,0},{9,1},... | collective-permute-start | bytes 1544 | tf_op jit(solution)/shard_map/ppermute | solution.py:77
  28.8 14.6 %collective-permute-start.11 = (bf16[128,1024]{1,0:T(8,128)(2,1)S(1)}, bf16[128,1024]{1,0:T(8,128)(2,1)S(1)}, u32[]{:S(2)}, u32[]{:S(2)}) collective-permute-start(bf16[128,1024]{1,0:T(8,128)(2,1)S(1)} %collective-permute-done.2.refs_6_), channel_id=1, source_target_pairs={{0,1},{1,0},{2,3},{3,2},{4,5},{5,4},{6,7},{7,6},{8,9},{9,8},{10,11... | collective-permute-start | bytes 786440 | tf_op jit(solution)/shard_map/ppermute | solution.py:77
  42.9 9.2 %collective-permute-start.6 = (bf16[128,1024]{1,0:T(8,128)(2,1)S(1)}, bf16[128,1024]{1,0:T(8,128)(2,1)S(1)}, u32[]{:S(2)}, u32[]{:S(2)}) collective-permute-start(bf16[128,1024]{1,0:T(8,128)(2,1)S(1)} %collective-permute-done.4.refs_0_), channel_id=1, source_target_pairs={{0,4},{4,8},{8,12},{12,14},{14,10},{10,6},{6,2},{2,0},{1,3},{5,1},... | collective-permute-start | bytes 786440 | tf_op jit(solution)/shard_map/ppermute | solution.py:77
  43.4 9.6 %collective-permute-start.16 = (bf16[128,1024]{1,0:T(8,128)(2,1)S(1)}, bf16[128,1024]{1,0:T(8,128)(2,1)S(1)}, u32[]{:S(2)}, u32[]{:S(2)}) collective-permute-start(bf16[128,1024]{1,0:T(8,128)(2,1)S(1)} %collective-permute-done.4.refs_0_), channel_id=1, source_target_pairs={{0,1},{1,0},{2,3},{3,2},{4,5},{5,4},{6,7},{7,6},{8,9},{9,8},{10,11... | collective-permute-start | bytes 786440 | tf_op jit(solution)/shard_map/ppermute | solution.py:77
  68.3 8.3 %collective-permute-start.28 = (bf16[128,1024]{1,0:T(8,128)(2,1)S(1)}, bf16[128,1024]{1,0:T(8,128)(2,1)S(1)}, u32[]{:S(2)}, u32[]{:S(2)}) collective-permute-start(bf16[128,1024]{1,0:T(8,128)(2,1)S(1)} %get-tuple-element.58), channel_id=1, source_target_pairs={{0,4},{4,8},{8,12},{12,14},{14,10},{10,6},{6,2},{2,0},{1,3},{5,1},... | collective-permute-start | bytes 786440 | tf_op jit(solution)/shard_map/ppermute | solution.py:77
  93.6 7.8 %collective-permute-start.31 = (bf16[128,1024]{1,0:T(8,128)(2,1)S(1)}, bf16[128,1024]{1,0:T(8,128)(2,1)S(1)}, u32[]{:S(2)}, u32[]{:S(2)}) collective-permute-start(bf16[128,1024]{1,0:T(8,128)(2,1)S(1)} %get-tuple-element.70.refs_0_), channel_id=1, source_target_pairs={{0,4},{4,8},{8,12},{12,14},{14,10},{10,6},{6,2},{2,0},{1,3},{5,1},... | collective-permute-start | bytes 786440 | tf_op jit(solution)/shard_map/ppermute | solution.py:77
  94.4 6.9 %collective-permute-start.32 = (f32[128]{0:T(128)S(1)}, f32[128]{0:T(128)S(1)}, u32[]{:S(2)}, u32[]{:S(2)}) collective-permute-start(f32[128]{0:T(128)S(1)} %get-tuple-element.69), channel_id=1, source_target_pairs={{0,2},{1,3},{2,0},{3,1},{4,6},{5,7},{6,4},{7,5},{8,10},{9,11},{10,... | collective-permute-start | bytes 1544 | tf_op jit(solution)/shard_map/ppermute | solution.py:77
  95.6 9.1 %collective-permute-start.40 = (bf16[128,1024]{1,0:T(8,128)(2,1)S(1)}, bf16[128,1024]{1,0:T(8,128)(2,1)S(1)}, u32[]{:S(2)}, u32[]{:S(2)}) collective-permute-start(bf16[128,1024]{1,0:T(8,128)(2,1)S(1)} %get-tuple-element.70.refs_0_), channel_id=1, source_target_pairs={{0,3},{4,1},{8,5},{12,9},{14,13},{10,15},{6,11},{2,7},{1,4},{5,8},... | collective-permute-start | bytes 786440 | tf_op jit(solution)/shard_map/ppermute | solution.py:77
  101.3 7.2 %collective-permute-start.33 = (bf16[128,1024]{1,0:T(8,128)(2,1)S(1)}, bf16[128,1024]{1,0:T(8,128)(2,1)S(1)}, u32[]{:S(2)}, u32[]{:S(2)}) collective-permute-start(bf16[128,1024]{1,0:T(8,128)(2,1)S(1)} %collective-permute-done.31.refs_2_), channel_id=1, source_target_pairs={{0,4},{4,8},{8,12},{12,14},{14,10},{10,6},{6,2},{2,0},{1,3},{5,1},... | collective-permute-start | bytes 786440 | tf_op jit(solution)/shard_map/ppermute | solution.py:77
  104.7 7.1 %collective-permute-start.43 = (bf16[128,1024]{1,0:T(8,128)(2,1)S(1)}, bf16[128,1024]{1,0:T(8,128)(2,1)S(1)}, u32[]{:S(2)}, u32[]{:S(2)}) collective-permute-start(bf16[128,1024]{1,0:T(8,128)(2,1)S(1)} %collective-permute-done.40.refs_4_), channel_id=1, source_target_pairs={{0,4},{4,8},{8,12},{12,14},{14,10},{10,6},{6,2},{2,0},{1,3},{5,1},... | collective-permute-start | bytes 786440 | tf_op jit(solution)/shard_map/ppermute | solution.py:77
  108.5 7.5 %collective-permute-start.35 = (bf16[128,1024]{1,0:T(8,128)(2,1)S(1)}, bf16[128,1024]{1,0:T(8,128)(2,1)S(1)}, u32[]{:S(2)}, u32[]{:S(2)}) collective-permute-start(bf16[128,1024]{1,0:T(8,128)(2,1)S(1)} %collective-permute-done.33.refs_6_), channel_id=1, source_target_pairs={{0,4},{4,8},{8,12},{12,14},{14,10},{10,6},{6,2},{2,0},{1,3},{5,1},... | collective-permute-start | bytes 786440 | tf_op jit(solution)/shard_map/ppermute | solution.py:77
  108.7 7.4 %collective-permute-start.38 = (bf16[128,1024]{1,0:T(8,128)(2,1)S(1)}, bf16[128,1024]{1,0:T(8,128)(2,1)S(1)}, u32[]{:S(2)}, u32[]{:S(2)}) collective-permute-start(bf16[128,1024]{1,0:T(8,128)(2,1)S(1)} %get-tuple-element.70.refs_0_), channel_id=1, source_target_pairs={{0,1},{1,0},{2,3},{3,2},{4,5},{5,4},{6,7},{7,6},{8,9},{9,8},{10,11... | collective-permute-start | bytes 786440 | tf_op jit(solution)/shard_map/ppermute | solution.py:77
  108.7 7.9 %collective-permute-start.41 = (bf16[128,1024]{1,0:T(8,128)(2,1)S(1)}, bf16[128,1024]{1,0:T(8,128)(2,1)S(1)}, u32[]{:S(2)}, u32[]{:S(2)}) collective-permute-start(bf16[128,1024]{1,0:T(8,128)(2,1)S(1)} %collective-permute-done.40.refs_4_), channel_id=1, source_target_pairs={{0,1},{1,0},{2,3},{3,2},{4,5},{5,4},{6,7},{7,6},{8,9},{9,8},{10,11... | collective-permute-start | bytes 786440 | tf_op jit(solution)/shard_map/ppermute | solution.py:77
  113.7 6.6 %collective-permute-start.48 = (bf16[128,1024]{1,0:T(8,128)(2,1)S(1)}, bf16[128,1024]{1,0:T(8,128)(2,1)S(1)}, u32[]{:S(2)}, u32[]{:S(2)}) collective-permute-start(bf16[128,1024]{1,0:T(8,128)(2,1)S(1)} %collective-permute-done.43.refs_8_), channel_id=1, source_target_pairs={{0,4},{4,8},{8,12},{12,14},{14,10},{10,6},{6,2},{2,0},{1,3},{5,1},... | collective-permute-start | bytes 786440 | tf_op jit(solution)/shard_map/ppermute | solution.py:77
  (32 other events, 212.1 us)

commit v4 on v3

v4 whole, which is shorter than its diff:
```python
import functools

import jax
import jax.numpy as jnp
from jax import lax
from jax.experimental import pallas as pl
from jax.experimental.pallas import tpu as pltpu
from jax.sharding import PartitionSpec as P

HD = 128
KVH = 8
HQ_DEV = 1
SPAN = 64
SEQS = 2
CTX_DEV = 64
TOKENS = SEQS * SPAN
MIB = 1024 * 1024

epsilon = 1e-05


def rms_rows(rows, gain):
    values_f = rows.astype(jnp.float32)
    factor = lax.rsqrt(jnp.mean(values_f * values_f, axis=-1, keepdims=True) + epsilon)
    return values_f * factor * gain.astype(jnp.float32)


def rope_tables(positions):
    half_width = HD // 2
    frequency = 500000.0 ** (-jnp.arange(half_width, dtype=jnp.float32) / half_width)
    angles = positions.astype(jnp.float32)[:, None] * frequency[None, :]
    return jnp.cos(angles), jnp.sin(angles)


def rotate(vectors, positions):
    half_width = vectors.shape[-1] // 2
    cosine, sine = rope_tables(positions)
    cosine, sine = cosine[:, None, :], sine[:, None, :]
    first_half = vectors[..., :half_width]
    second_half = vectors[..., half_width:]
    return jnp.concatenate(
        [first_half * cosine - second_half * sine, second_half * cosine + first_half * sine],
        axis=-1,
    )


CHIPS = 8
RING = (0, 2, 4, 6, 7, 5, 3, 1)
ONWARD = [(2 * RING[i], 2 * RING[(i + 1) % CHIPS]) for i in range(CHIPS)] + [
    (2 * RING[i] + 1, 2 * RING[i - 1] + 1) for i in range(CHIPS)
]
ENTER = [(2 * RING[i], 2 * RING[i - 1] + 1) for i in range(CHIPS)] + [
    (2 * RING[i] + 1, 2 * RING[(i + 1) % CHIPS]) for i in range(CHIPS)
]
LEAVE = [(2 * RING[i], 2 * RING[(i + 1) % CHIPS] + 1) for i in range(CHIPS)] + [
    (2 * RING[i] + 1, 2 * RING[i - 1]) for i in range(CHIPS)
]
SWAP = [(t, t ^ 1) for t in range(2 * CHIPS)]
STRAIGHT = [(k, 2 * k) for k in range(KVH)] + [(KVH + k, 2 * k + 1) for k in range(KVH)]
CROSSED = [(k, 2 * k + 1) for k in range(KVH)] + [(KVH + k, 2 * k) for k in range(KVH)]
VMEM = pl.BlockSpec(memory_space=pltpu.VMEM)
SMEM = pl.BlockSpec(memory_space=pltpu.SMEM)
HBM = pl.BlockSpec(memory_space=pltpu.HBM)


def ring_place(rank):
    chip = rank // 2
    return jnp.where(chip % 2 == 0, chip // 2, CHIPS - 1 - chip // 2)


def chip_at(place):
    place = place % CHIPS
    return jnp.where(place < CHIPS // 2, 2 * place, 2 * CHIPS - 1 - 2 * place)


def send(array, pairs):
    return lax.ppermute(array, "tp", pairs)


def xor(bits):
    return [(t, t ^ bits) for t in range(2 * CHIPS)]


def ring_gather(halves, own, work=None):
    straight, crossed = list(halves), own
    came = [(own,)]
    for step in range(1, 5):
        straight = [send(half, ONWARD) for half in straight]
        came.append(tuple(straight))
        if step < 4:
            if step == 3 and work is not None:
                crossed, work = lax.optimization_barrier((crossed, work))
            crossed = send(crossed, ENTER if step == 1 else ONWARD)
            came.append((crossed,))
    early, _ = lax.optimization_barrier((came[:5], came[5]))
    blocks = []
    for block in early + came[5:]:
        blocks += [block, tuple(send(piece, SWAP) for piece in block)]
    return blocks, work


def gathered_ids(rank):
    place, core = ring_place(rank), rank % 2
    ahead = 2 * core - 1
    ids = [rank, rank ^ 1]
    for step in range(1, 5):
        near, far = 2 * chip_at(place + ahead * step), 2 * chip_at(place - ahead * step)
        ids += [near + core, far + 1 - core]
        if step < 4:
            ids += [near + 1 - core, far + core]
    return jnp.stack(ids).astype(jnp.int32)


SHARES = ((4, 0), (3, 1), (3, 0), (2, 1), (2, 0), (1, 1), (1, 0), (0, 0))


def share_ids(rank):
    place, core = ring_place(rank), rank % 2
    return jnp.stack(
        [2 * chip_at(place + (1 - 2 * core) * d) + (core + other) % 2 for d, other in SHARES]
    ).astype(jnp.int32)


def ring_sum(shares):
    running = {0: shares[4, 0], 1: shares[3, 1]}
    for step in range(4, 0, -1):
        for other in range(2):
            if step == 4 and other == 1:
                continue
            if (step, other) not in ((4, 0), (3, 1)):
                running[other] = [
                    (part.astype(jnp.float32) + share).astype(jnp.bfloat16)
                    for part, share in zip(running[other], shares[step, other])
                ]
            pairs = LEAVE if (step, other) == (1, 1) else ONWARD
            running[other] = [send(part, pairs) for part in running[other]]
    return running[0], running[1][0]


def move_cache(key_cache, value_cache, rank, rank_id, after):
    core = rank % 2
    give = jnp.stack(
        [lax.dynamic_index_in_dim(c, 1 - core, 0, keepdims=False) for c in (key_cache, value_cache)]
    )
    keep, give = pack(rank_id, key_cache, value_cache, send(give, SWAP))
    came = send(give, xor(2))
    pieces = [jnp.stack([keep[m], came[m]]) for m in range(1, 4)]
    pieces, _ = lax.optimization_barrier((pieces, after))
    return [keep, came] + [send(piece, xor(4 * m)) for m, piece in zip(range(1, 4), pieces)]


def pack_kernel(rank, keys, values, theirs, keep, give):
    me = rank[0]
    for m in range(4):
        for j, out in enumerate((keep, give)):
            chip = (me ^ (4 * m + 2 * j)) // 2
            head = pl.ds(pl.multiple_of(chip * HD, HD), HD)
            out[m, 0, 0] = keys[me % 2, :, head]
            out[m, 0, 1] = values[me % 2, :, head]
            out[m, 1, 0] = theirs[0, :, head]
            out[m, 1, 1] = theirs[1, :, head]


def pack(rank_id, key_cache, value_cache, theirs):
    return pl.pallas_call(
        pack_kernel,
        out_shape=[jax.ShapeDtypeStruct((4, 2, 2, CTX_DEV, HD), jnp.bfloat16)] * 2,
        in_specs=[SMEM] + [VMEM] * 3,
        out_specs=[VMEM] * 2,
        compiler_params=pltpu.CompilerParams(vmem_limit_bytes=8 * MIB),
        cost_estimate=pl.CostEstimate(flops=0, bytes_accessed=MIB, transcendentals=0),
        name="pack_cache",
    )(rank_id, key_cache, value_cache, theirs)


def flat(blocks):
    return [piece for block in blocks for piece in block]


def grouped(refs, counts):
    blocks, at = [], 0
    for count in counts:
        blocks.append(refs[at : at + count])
        at += count
    return blocks


def lanes(block, j):
    parts = [piece[:, 128 * j : 128 * j + 128] for piece in block]
    return (parts[0] if len(parts) == 1 else jnp.concatenate(parts, axis=0)).astype(jnp.float32)


def square_sums(blocks, total):
    for block in blocks:
        for j in range(block[0].shape[1] // 128):
            v = lanes(block, j)
            total = total + v * v
    return total


def row_factors(squares, features):
    mean = jnp.sum(squares, axis=1, keepdims=True) * (1.0 / features)
    return lax.rsqrt(mean + epsilon)


def normed_block(block, factors, gain_row):
    return jnp.concatenate(
        [
            (lanes(block, j) * factors * gain_row[:, 128 * j : 128 * j + 128]).astype(jnp.bfloat16)
            for j in range(block[0].shape[1] // 128)
        ],
        axis=1,
    )


def squares_kernel(counts, *refs):
    out = refs[-1]
    out[...] = square_sums(grouped(refs[:-1], counts), jnp.zeros((TOKENS, 128), jnp.float32))


def squares_of(blocks):
    pieces = flat(blocks)
    return pl.pallas_call(
        functools.partial(squares_kernel, [len(block) for block in blocks]),
        out_shape=jax.ShapeDtypeStruct((TOKENS, 128), jnp.float32),
        in_specs=[VMEM] * len(pieces),
        out_specs=VMEM,
        compiler_params=pltpu.CompilerParams(vmem_limit_bytes=16 * MIB),
        cost_estimate=pl.CostEstimate(
            flops=4 * MIB, bytes_accessed=len(blocks) * MIB // 4, transcendentals=0
        ),
        name="squares",
    )(*pieces)


def in_hbm(array):
    return pltpu.with_memory_space_constraint(array, pltpu.HBM)


def load_kernel(ids, wq, wkv, out, sems):
    count, width, _ = out.shape
    copies = []
    for i in range(count):
        rows = pl.ds(pl.multiple_of(ids[i] * width, width), width)
        for j, weight in enumerate((wq, wkv)):
            copies.append(
                pltpu.make_async_copy(
                    weight.at[rows, :], out.at[i, :, pl.ds(j * HD, HD)], sems.at[j, i]
                )
            )
            copies[-1].start()
    for copy in copies:
        copy.wait()


def load_weights(ids, wq, wkv, width):
    return pl.pallas_call(
        load_kernel,
        out_shape=jax.ShapeDtypeStruct((16, width, 2 * HD), jnp.bfloat16),
        in_specs=[SMEM] + [HBM] * 2,
        out_specs=VMEM,
        scratch_shapes=[pltpu.SemaphoreType.DMA((2, 16))],
        compiler_params=pltpu.CompilerParams(vmem_limit_bytes=16 * MIB),
        cost_estimate=pl.CostEstimate(flops=0, bytes_accessed=16 * MIB, transcendentals=0),
        name="load_weights",
    )(ids, in_hbm(wq), in_hbm(wkv))


def project_kernel(counts, ids, *refs):
    blocks, refs = grouped(refs, counts), refs[sum(counts) :]
    squares, gain, weights, cosine, sine, kv_cos, kv_sin = refs[:7]
    q_keep, q_send, kv_straight, kv_crossed = refs[7:11]
    features = 16 * blocks[0][0].shape[1]
    factors = row_factors(square_sums(blocks[14:15] + blocks[1::2], squares[...]), features)
    total = jnp.zeros((TOKENS, 2 * HD), jnp.float32)
    for i in range(16):
        normed = normed_block(blocks[i], factors, gain[ids[i]])
        total = total + jnp.dot(normed, weights[i], preferred_element_type=jnp.float32)
    q, kv = total[:, :HD], total[:, HD:]
    q = (q * cosine[...] + pltpu.roll(q, HD // 2, 1) * sine[...]).astype(jnp.bfloat16)
    kv = (kv * kv_cos[...] + pltpu.roll(kv, HD // 2, 1) * kv_sin[...]).astype(jnp.bfloat16)
    core_one = ids[0] % 2 == 1
    holds_keys = ids[0] < KVH
    first, second = slice(0, SPAN), slice(SPAN, TOKENS)
    q_keep[...] = jnp.where(core_one, q[second], q[first])
    q_send[...] = jnp.where(core_one, q[first], q[second])
    kv_straight[...] = jnp.where(holds_keys, kv[first], kv[second])
    kv_crossed[...] = jnp.where(holds_keys, kv[second], kv[first])


def project(ids, blocks, squares, gain, weights, tables):
    pieces = flat(blocks)
    return pl.pallas_call(
        functools.partial(project_kernel, [len(block) for block in blocks]),
        out_shape=[jax.ShapeDtypeStruct((SPAN, HD), jnp.bfloat16)] * 4,
        in_specs=[SMEM] + [VMEM] * (len(pieces) + 7),
        out_specs=[VMEM] * 4,
        compiler_params=pltpu.CompilerParams(vmem_limit_bytes=24 * MIB),
        cost_estimate=pl.CostEstimate(
            flops=2 * TOKENS * weights.size, bytes_accessed=12 * MIB, transcendentals=0
        ),
        name="norm_project",
    )(ids, *pieces, squares, gain, weights, *tables)


def share_copies(to, first, weight, weight_other, out, sems):
    count, _, width = out.shape
    copies = []
    for i in range(count):
        columns = pl.ds(pl.multiple_of(to[first + i] * width, width), width)
        pair = [
            pltpu.make_async_copy(part.at[:, columns], out.at[i, pl.ds(j * HD, HD), :], sems.at[j, i])
            for j, part in enumerate((weight, weight_other))
        ]
        for copy in pair:
            copy.start()
        copies.append(pair)
    return copies


def cache_rows(cache, which):
    keep, came, rest = cache[0], cache[1], cache[2:]
    groups = [part[0, c, which] for part in (keep, came) for c in range(2)]
    groups += [part[x, c, which] for part in rest for x in range(2) for c in range(2)]
    return jnp.concatenate(groups, axis=0)


CONTRACT = (((1,), (1,)), ((), ()))


def scores_kernel(info, to, q, q_other, *refs):
    cache, weight, weight_other, scores, weights, sems = refs[:5], *refs[5:]
    copies = share_copies(to, 0, weight, weight_other, weights, sems)
    core, rank = info[SEQS], info[SEQS + 1]
    queries = jnp.concatenate([q[...], q_other[...]], axis=0)
    old = lax.dot_general(
        queries, cache_rows(cache, 0), CONTRACT, preferred_element_type=jnp.float32
    )
    lane = lax.broadcasted_iota(jnp.int32, old.shape, 1)
    position = (rank ^ (lane // CTX_DEV)) * CTX_DEV + lane % CTX_DEV
    scores[...] = jnp.where(position < info[core], old * HD ** (-0.5), -1e30)
    for pair in copies:
        for copy in pair:
            copy.wait()


def cache_scores(info, to, q, q_other, cache, weight, weight_other, ahead):
    width = weight.shape[1] // 16
    return pl.pallas_call(
        scores_kernel,
        out_shape=[
            jax.ShapeDtypeStruct((TOKENS, 16 * CTX_DEV), jnp.float32),
            jax.ShapeDtypeStruct((ahead, 2 * HD, width), jnp.bfloat16),
        ],
        in_specs=[SMEM] * 2 + [VMEM] * 7 + [HBM] * 2,
        out_specs=[VMEM] * 2,
        scratch_shapes=[pltpu.SemaphoreType.DMA((2, ahead))],
        compiler_params=pltpu.CompilerParams(vmem_limit_bytes=16 * MIB),
        cost_estimate=pl.CostEstimate(
            flops=32 * MIB, bytes_accessed=3 * MIB, transcendentals=0
        ),
        name="cache_scores",
    )(info, to, q, q_other, *cache, in_hbm(weight), weight_other)


def attend_kernel(info, q, q_other, straight, crossed, scores, *refs):
    cache, out = refs[:5], refs[5]
    core = info[SEQS]
    fresh_keys = jnp.where(core == 0, straight[...], crossed[...])
    fresh_values = jnp.where(core == 0, crossed[...], straight[...])
    queries = jnp.concatenate([q[...], q_other[...]], axis=0)
    old = scores[...]
    valid = old > -1e29
    fresh = lax.dot_general(
        queries, fresh_keys, CONTRACT, preferred_element_type=jnp.float32
    ) * HD ** (-0.5)
    place = lax.broadcasted_iota(jnp.int32, fresh.shape, 0) % SPAN
    causal = place >= lax.broadcasted_iota(jnp.int32, fresh.shape, 1)
    fresh = jnp.where(causal, fresh, -1e30)
    most = jnp.maximum(jnp.max(old, axis=1, keepdims=True), jnp.max(fresh, axis=1, keepdims=True))
    old_weights = jnp.where(valid, jnp.exp(old - most), 0.0)
    fresh_weights = jnp.where(causal, jnp.exp(fresh - most), 0.0)
    totals = jnp.sum(old_weights, axis=1, keepdims=True) + jnp.sum(
        fresh_weights, axis=1, keepdims=True
    )
    summed = jnp.dot(
        old_weights.astype(jnp.bfloat16), cache_rows(cache, 1), preferred_element_type=jnp.float32
    ) + jnp.dot(
        fresh_weights.astype(jnp.bfloat16), fresh_values, preferred_element_type=jnp.float32
    )
    attn = (summed / totals).astype(jnp.bfloat16)
    out[:, :HD] = attn[:SPAN]
    out[:, HD:] = attn[SPAN:]


def attend(info, q, q_other, straight, crossed, scores, cache):
    return pl.pallas_call(
        attend_kernel,
        out_shape=jax.ShapeDtypeStruct((SPAN, 2 * HD), jnp.bfloat16),
        in_specs=[SMEM] + [VMEM] * 10,
        out_specs=VMEM,
        compiler_params=pltpu.CompilerParams(vmem_limit_bytes=16 * MIB),
        cost_estimate=pl.CostEstimate(
            flops=48 * MIB, bytes_accessed=2 * MIB, transcendentals=TOKENS * 1088
        ),
        name="attend",
    )(info, q, q_other, straight, crossed, scores, *cache)


def both_heads(core, attn, attn_other):
    mine = attn[...]
    theirs = jnp.concatenate([attn_other[:, HD:], attn_other[:, :HD]], axis=1)
    core_one = core[0] == 1
    return jnp.concatenate(
        [jnp.where(core_one, theirs, mine), jnp.where(core_one, mine, theirs)], axis=0
    )


def share_shapes(shares, width, dtype):
    half, whole = [((SPAN, width), dtype)] * 2, [((TOKENS, width), dtype)]
    return [jax.ShapeDtypeStruct(*s) for _, other in shares for s in (whole if other else half)]


def share_lists(shares, arrays):
    arrays = list(arrays)
    return {key: [arrays.pop(0) for _ in range(2 - key[1])] for key in shares}


def write_share(value, outs):
    rows = TOKENS // len(outs)
    for i, out in enumerate(outs):
        out[...] = value[i * rows : (i + 1) * rows].astype(out.dtype)


def first_shares_kernel(shares, core, attn, attn_other, weights, *outs):
    rows = both_heads(core, attn, attn_other)
    for i, refs in enumerate(share_lists(shares, outs).values()):
        write_share(jnp.dot(rows, weights[i], preferred_element_type=jnp.float32), refs)


def first_shares(shares, core, attn, attn_other, weights):
    count, _, width = weights.shape
    out_shape = share_shapes(shares, width, jnp.bfloat16)
    arrays = pl.pallas_call(
        functools.partial(first_shares_kernel, shares),
        out_shape=out_shape,
        in_specs=[SMEM] + [VMEM] * 3,
        out_specs=[VMEM] * len(out_shape),
        compiler_params=pltpu.CompilerParams(vmem_limit_bytes=16 * MIB),
        cost_estimate=pl.CostEstimate(
            flops=2 * TOKENS * weights.size, bytes_accessed=count * MIB, transcendentals=0
        ),
        name="first_shares",
    )(core, attn, attn_other, weights)
    return share_lists(shares, arrays)


def more_shares_kernel(first, core, to, attn, attn_other, weight, weight_other, *refs):
    outs, (weights, sems) = refs[:-2], refs[-2:]
    copies = share_copies(to, first, weight, weight_other, weights, sems)
    rows = both_heads(core, attn, attn_other)
    for i, out in enumerate(share_lists(SHARES[first:], outs).values()):
        for copy in copies[i]:
            copy.wait()
        write_share(jnp.dot(rows, weights[i], preferred_element_type=jnp.float32), out)


def more_shares(core, to, attn, attn_other, weight, weight_other, first):
    count, width = len(SHARES) - first, weight.shape[1] // 16
    out_shape = share_shapes(SHARES[first:], width, jnp.float32)
    arrays = pl.pallas_call(
        functools.partial(more_shares_kernel, first),
        out_shape=out_shape,
        in_specs=[SMEM] * 2 + [VMEM] * 2 + [HBM] * 2,
        out_specs=[VMEM] * len(out_shape),
        scratch_shapes=[
            pltpu.VMEM((count, 2 * HD, width), jnp.bfloat16),
            pltpu.SemaphoreType.DMA((2, count)),
        ],
        compiler_params=pltpu.CompilerParams(vmem_limit_bytes=16 * MIB),
        cost_estimate=pl.CostEstimate(
            flops=4 * TOKENS * HD * width * count,
            bytes_accessed=count * MIB,
            transcendentals=0,
        ),
        name="more_shares",
    )(core, to, attn, attn_other, in_hbm(weight), weight_other)
    return share_lists(SHARES[first:], arrays)


def final_kernel(counts, ids, *refs):
    blocks, refs = grouped(refs, counts), refs[sum(counts) :]
    squares, gain, out, staged, sems = refs
    width = blocks[0][0].shape[1]
    factors = row_factors(square_sums(blocks[14:15] + blocks[1::2], squares[...]), 16 * width)
    copies = []
    for i in range(16):
        staged[i] = normed_block(blocks[i], factors, gain[ids[i]])
        copy = pltpu.make_async_copy(
            staged.at[i],
            out.at[:, pl.ds(pl.multiple_of(ids[i] * width, width), width)],
            sems.at[i],
        )
        copy.start()
        copies.append(copy)
    for copy in copies:
        copy.wait()


def final_norm(ids, blocks, squares, gain):
    pieces = flat(blocks)
    width = pieces[0].shape[1]
    return pl.pallas_call(
        functools.partial(final_kernel, [len(block) for block in blocks]),
        out_shape=jax.ShapeDtypeStruct((TOKENS, 16 * width), jnp.bfloat16),
        in_specs=[SMEM] + [VMEM] * (len(pieces) + 2),
        out_specs=HBM,
        scratch_shapes=[
            pltpu.VMEM((16, TOKENS, width), jnp.bfloat16),
            pltpu.SemaphoreType.DMA((16,)),
        ],
        compiler_params=pltpu.CompilerParams(vmem_limit_bytes=24 * MIB),
        cost_estimate=pl.CostEstimate(
            flops=16 * MIB, bytes_accessed=12 * MIB, transcendentals=0
        ),
        name="final_norm",
    )(ids, *pieces, squares, gain)


def per_device_ring(
    residual, attn_gain, ffn_gain, q_weight, kv_weight, o_weight, key_cache, value_cache, prefix
):
    rank = lax.axis_index("tp")
    core = rank % 2
    width = residual.shape[1]
    ids = gathered_ids(rank)
    to = share_ids(rank)
    core_id, rank_id = core[None].astype(jnp.int32), rank[None].astype(jnp.int32)
    info = jnp.concatenate([prefix, core_id, rank_id])

    weights = load_weights(ids, q_weight, kv_weight, width)
    residual_halves = [residual[:SPAN], residual[SPAN:]]
    blocks, weights = ring_gather(residual_halves, residual, weights)
    weight_other = send(o_weight, SWAP)
    cache = move_cache(key_cache, value_cache, rank, rank_id, blocks[12])

    positions = (prefix[:, None] + jnp.arange(SPAN, dtype=jnp.int32)[None, :]).reshape(-1)
    cosine, sine = rope_tables(positions)
    cosine = jnp.concatenate([cosine, cosine], axis=1)
    sine = jnp.concatenate([-sine, sine], axis=1)
    holds_keys = rank < KVH
    tables = (cosine, sine, jnp.where(holds_keys, cosine, 1.0), jnp.where(holds_keys, sine, 0.0))

    gain = attn_gain.reshape(16, 1, width).astype(jnp.float32)
    squares = squares_of(blocks[:14:2])
    q_keep, q_send, straight, crossed = project(
        ids, blocks, squares, gain, weights, tables
    )
    q_other = send(q_send, SWAP)
    scores, first_weights = cache_scores(
        info, to, q_keep, q_other, cache, o_weight, weight_other, 2
    )
    attn = attend(
        info, q_keep, q_other, send(straight, STRAIGHT), send(crossed, CROSSED), scores, cache
    )
    attn_other = send(attn, SWAP)

    shares = first_shares(SHARES[:2], core_id, attn, attn_other, first_weights)
    shares.update(more_shares(core_id, to, attn, attn_other, o_weight, weight_other, 2))
    one_way, other_way = ring_sum(shares)
    hidden = []
    for h, rows in enumerate((slice(0, SPAN), slice(SPAN, TOKENS))):
        projected = shares[0, 0][h] + one_way[h].astype(jnp.float32)
        projected = projected + other_way[rows].astype(jnp.float32)
        hidden.append((residual_halves[h].astype(jnp.float32) + projected).astype(jnp.bfloat16))

    blocks, _ = ring_gather(hidden, jnp.concatenate(hidden, axis=0))
    gain = ffn_gain.reshape(16, 1, width).astype(jnp.float32)
    squares = squares_of(blocks[:14:2])
    return final_norm(ids, blocks, squares, gain)


def per_device(
    residual, attn_gain, ffn_gain, q_weight, kv_weight, o_weight, key_cache, value_cache, prefix
):
    tp_count = lax.axis_size("tp")
    tp_rank = lax.axis_index("tp")
    heads_all = HQ_DEV * tp_count
    group_size = heads_all // KVH
    token_count = SEQS * SPAN
    score_scale = HD ** (-0.5)
    whole_rows = lax.all_gather(residual, "tp", axis=1, tiled=True)
    normed = rms_rows(whole_rows, attn_gain).astype(jnp.bfloat16)
    positions = (prefix[:, None] + jnp.arange(SPAN, dtype=jnp.int32)[None, :]).reshape(-1)
    queries = jnp.dot(normed, q_weight, preferred_element_type=jnp.float32).reshape(
        token_count, HQ_DEV, HD
    )
    queries = rotate(queries, positions).astype(jnp.bfloat16)
    kv_part = jnp.dot(normed, kv_weight, preferred_element_type=jnp.float32)
    kv_whole = lax.all_gather(kv_part, "tp", axis=1, tiled=True)
    new_keys = rotate(kv_whole[:, : KVH * HD].reshape(token_count, KVH, HD), positions).astype(
        jnp.bfloat16
    )
    new_values = kv_whole[:, KVH * HD :].reshape(token_count, KVH, HD).astype(jnp.bfloat16)
    head_ids = tp_rank * HQ_DEV + jnp.arange(HQ_DEV, dtype=jnp.int32)
    own_kv = head_ids // group_size
    own_keys = jnp.take(new_keys, own_kv, axis=1).reshape(SEQS, SPAN, HQ_DEV, HD)
    own_values = jnp.take(new_values, own_kv, axis=1).reshape(SEQS, SPAN, HQ_DEV, HD)
    own_queries = queries.reshape(SEQS, SPAN, HQ_DEV, HD)
    causal = (jnp.arange(SPAN)[:, None] >= jnp.arange(SPAN)[None, :])[None, None]
    fresh_scores = (
        jnp.einsum("schd,skhd->shck", own_queries, own_keys, preferred_element_type=jnp.float32)
        * score_scale
    )
    fresh_scores = jnp.where(causal, fresh_scores, -1e30)
    fresh_max = fresh_scores.max(-1)
    gathered = lax.all_gather(queries.reshape(token_count, HQ_DEV * HD), "tp", axis=1, tiled=True)
    queries_all = gathered.reshape(SEQS, SPAN, KVH, group_size, HD)
    keys_local = key_cache.reshape(SEQS, CTX_DEV, KVH, HD)
    values_local = value_cache.reshape(SEQS, CTX_DEV, KVH, HD)
    local_scores = (
        jnp.einsum("sckgd,sjkd->skgcj", queries_all, keys_local, preferred_element_type=jnp.float32)
        * score_scale
    )
    first_slot = tp_rank * CTX_DEV
    is_valid = ((first_slot + jnp.arange(CTX_DEV, dtype=jnp.int32))[None, :] < prefix[:, None])[
        :, None, None, None, :
    ]
    local_scores = jnp.where(is_valid, local_scores, -1e30)
    local_max = local_scores.max(-1)
    local_weights = jnp.where(is_valid, jnp.exp(local_scores - local_max[..., None]), 0.0)
    local_total = local_weights.sum(-1)
    local_sum = jnp.einsum(
        "skgcj,sjkd->skgcd",
        local_weights.astype(jnp.bfloat16),
        values_local,
        preferred_element_type=jnp.float32,
    )
    sums_in, maxes_in, totals_in = (
        lax.all_to_all(
            local_sum.reshape(1, SEQS, heads_all, SPAN, HD),
            "tp",
            split_axis=2,
            concat_axis=0,
            tiled=True,
        ),
        lax.all_to_all(
            local_max.reshape(1, SEQS, heads_all, SPAN),
            "tp",
            split_axis=2,
            concat_axis=0,
            tiled=True,
        ),
        lax.all_to_all(
            local_total.reshape(1, SEQS, heads_all, SPAN),
            "tp",
            split_axis=2,
            concat_axis=0,
            tiled=True,
        ),
    )
    running_max = jnp.maximum(maxes_in.max(0), fresh_max)
    factors = jnp.exp(maxes_in - running_max[None])
    fresh_weights = jnp.where(causal, jnp.exp(fresh_scores - running_max[..., None]), 0.0)
    totals = (factors * totals_in).sum(0) + fresh_weights.sum(-1)
    summed = (factors[..., None] * sums_in).sum(0)
    summed = summed + jnp.einsum(
        "shck,skhd->shcd",
        fresh_weights.astype(jnp.bfloat16),
        own_values,
        preferred_element_type=jnp.float32,
    )
    attn = (summed / totals[..., None]).astype(jnp.bfloat16)
    attn = jnp.transpose(attn, (0, 2, 1, 3)).reshape(token_count, HQ_DEV * HD)
    share_part = lax.psum_scatter(
        lax.dot_general(
            o_weight, attn, (((0,), (1,)), ((), ())), preferred_element_type=jnp.float32
        ),
        "tp",
        scatter_dimension=0,
        tiled=True,
    )
    hidden = (residual.astype(jnp.float32) + share_part.T).astype(jnp.bfloat16)
    stream = lax.all_gather(hidden, "tp", axis=1, tiled=True)
    return rms_rows(stream, ffn_gain).astype(jnp.bfloat16)


def solution(mesh):
    return jax.shard_map(
        per_device_ring if mesh.shape["tp"] == 2 * CHIPS else per_device,
        mesh=mesh,
        in_specs=(
            P("replica", "tp"),
            P(),
            P(),
            P(None, "tp"),
            P(None, "tp"),
            P("tp", None),
            P("replica", "tp", None),
            P("replica", "tp", None),
            P("replica"),
        ),
        out_specs=P("replica", None),
        check_vma=False,
    )
```

time: 128 us -> 122 us (0.953)
  waiting for transfers between devices: 53.5 us -> 50.5 us
  other arithmetic: 4.52 us -> 1.8 us
  local copies, waits for them, and re-layouts: 2.3 us -> 4.18 us
  Pallas kernels: 19.2 us -> 17.4 us
    all_to_all x1 -> x0, starting transfers between devices: 5.1 us -> none  [per_device_ring(): lax.all_to_all(pieces, 'tp', split_axis=0, concat_axis=0, tiled=True)]
    ppermute x50 -> x67, starting transfers between devices: 42.2 us -> 47.1 us  [send(): return lax.ppermute(array, 'tp', pairs)]
    ppermute x50 -> x67, waiting for transfers between devices: 53.5 us -> 50.5 us  [send(): return lax.ppermute(array, 'tp', pairs)]
    pallas_call x9 -> x10, Pallas kernels: 19.2 us -> 17.4 us  [the longest x1 4.19 us: load_weights(): pl.pallas_call(load_kernel, out_shape=jax.ShapeDtypeStruct((16, width, 2...]
    reduce_sum x2 -> x0, other arithmetic: 1.35 us -> none  [ring_gather(): squares = jnp.sum(values_f * values_f, axis=1)]
  transfers between devices with their start and end apart: 51 -> 67, of which waited for: 21 -> 33; matrix products, arithmetic and copies ran while one was open for 4% -> 3% of each run, Pallas kernels for 12% -> 10%
where the time goes in v4:
time: 122 us
  waiting for transfers between devices  50.5 us (41%)
  starting transfers between devices  47.1 us (39%)
  Pallas kernels  17.4 us (14%)
  local copies, waits for them, and re-layouts  4.18 us (3%)
  other arithmetic  1.8 us (1%)
    ppermute x67, waiting for transfers between devices, send(): return lax.ppermute(array, 'tp', pairs)  50.5 us
    ppermute x67, starting transfers between devices, send(): return lax.ppermute(array, 'tp', pairs)  47.1 us
    pallas_call x1, Pallas kernels, load_weights(): pl.pallas_call(load_kernel, out_shape=jax.ShapeDtypeStruct((16, width, 2...  4.19 us
    pallas_call x1, Pallas kernels, final_norm(): pl.pallas_call(functools.partial(final_kernel, [len(block) for block in b...  3.34 us
    pallas_call x1, Pallas kernels, more_shares(): pl.pallas_call(functools.partial(more_shares_kernel, first), out_shape=ou...  3.1 us
    pallas_call x1, Pallas kernels, project(): pl.pallas_call(functools.partial(project_kernel, [len(block) for block in...  2.63 us
  transfers between devices with their start and end apart: 67, of which 33 were waited for; matrix products, arithmetic and copies ran while one was open for 3% of the time, Pallas kernels for 10%

profile of v4, /device:TPU:0, one launch (start us, length us, event | category | flops | bytes accessed | tf_op | source)
XLA Modules:
  0.0 121.9 jit_solution(4451268097669654561)
XLA Ops:
  1.4 2.6 %collective-permute-start = (bf16[64,1024]{1,0:T(8,128)(2,1)S(1)}, bf16[64,1024]{1,0:T(8,128)(2,1)S(1)}, u32[]{:S(2)}, u32[]{:S(2)}) collective-permute-start(bf16[64,1024]{1,0:T(8,128)(2,1)S(1)} %get-tuple-element.96), channel_id=1, source_target_pairs={{0,4},{4,8},{8,12},{12,14},{14,10},{10,6},{6,2},{2,0},{1,3},{5,1},... | collective-permute-start | bytes 393224 | tf_op jit(solution)/shard_map/ppermute | solution.py:77
  4.1 1.6 %collective-permute-start.1 = (bf16[64,1024]{1,0:T(8,128)(2,1)S(1)}, bf16[64,1024]{1,0:T(8,128)(2,1)S(1)}, u32[]{:S(2)}, u32[]{:S(2)}) collective-permute-start(bf16[64,1024]{1,0:T(8,128)(2,1)S(1)} %get-tuple-element.95), channel_id=1, source_target_pairs={{0,4},{4,8},{8,12},{12,14},{14,10},{10,6},{6,2},{2,0},{1,3},{5,1},... | collective-permute-start | bytes 393224 | tf_op jit(solution)/shard_map/ppermute | solution.py:77
  6.9 2.1 %collective-permute-start.3 = (bf16[64,1024]{1,0:T(8,128)(2,1)S(1)}, bf16[64,1024]{1,0:T(8,128)(2,1)S(1)}, u32[]{:S(2)}, u32[]{:S(2)}) collective-permute-start(bf16[64,1024]{1,0:T(8,128)(2,1)S(1)} %collective-permute-done.refs_1_.refs_2_), channel_id=1, source_target_pairs={{0,4},{4,8},{8,12},{12,14},{14,10},{10,6},{6,2},{2,0},{1,3},{5,1},... | collective-permute-start | bytes 393224 | tf_op jit(solution)/shard_map/ppermute | solution.py:77
  11.9 2.3 %collective-permute-start.6 = (bf16[64,1024]{1,0:T(8,128)(2,1)S(1)}, bf16[64,1024]{1,0:T(8,128)(2,1)S(1)}, u32[]{:S(2)}, u32[]{:S(2)}) collective-permute-start(bf16[64,1024]{1,0:T(8,128)(2,1)S(1)} %collective-permute-done.3.refs_4_.refs_8_), channel_id=1, source_target_pairs={{0,4},{4,8},{8,12},{12,14},{14,10},{10,6},{6,2},{2,0},{1,3},{5,1},... | collective-permute-start | bytes 393224 | tf_op jit(solution)/shard_map/ppermute | solution.py:77
  16.4 2.2 %collective-permute-start.5 = (bf16[128,1024]{1,0:T(8,128)(2,1)S(1)}, bf16[128,1024]{1,0:T(8,128)(2,1)S(1)}, u32[]{:S(2)}, u32[]{:S(2)}) collective-permute-start(bf16[128,1024]{1,0:T(8,128)(2,1)S(1)} %collective-permute-done.2.refs_3_.refs_6_), channel_id=1, source_target_pairs={{0,4},{4,8},{8,12},{12,14},{14,10},{10,6},{6,2},{2,0},{1,3},{5,1},... | collective-permute-start | bytes 786440 | tf_op jit(solution)/shard_map/ppermute | solution.py:77
  18.6 1.6 %collective-permute-start.7 = (bf16[64,1024]{1,0:T(8,128)(2,1)S(1)}, bf16[64,1024]{1,0:T(8,128)(2,1)S(1)}, u32[]{:S(2)}, u32[]{:S(2)}) collective-permute-start(bf16[64,1024]{1,0:T(8,128)(2,1)S(1)} %collective-permute-done.4.refs_5_.refs_9_), channel_id=1, source_target_pairs={{0,4},{4,8},{8,12},{12,14},{14,10},{10,6},{6,2},{2,0},{1,3},{5,1},... | collective-permute-start | bytes 393224 | tf_op jit(solution)/shard_map/ppermute | solution.py:77
  24.2 2.2 %collective-permute-start.19 = (bf16[64,1024]{1,0:T(8,128)(2,1)S(1)}, bf16[64,1024]{1,0:T(8,128)(2,1)S(1)}, u32[]{:S(2)}, u32[]{:S(2)}) collective-permute-start(bf16[64,1024]{1,0:T(8,128)(2,1)S(1)} %collective-permute-done.6.refs_7_.refs_14_), channel_id=1, source_target_pairs={{0,4},{4,8},{8,12},{12,14},{14,10},{10,6},{6,2},{2,0},{1,3},{5,1},... | collective-permute-start | bytes 393224 | tf_op jit(solution)/shard_map/ppermute | solution.py:77
  26.4 1.6 %collective-permute-start.20 = (bf16[64,1024]{1,0:T(8,128)(2,1)S(1)}, bf16[64,1024]{1,0:T(8,128)(2,1)S(1)}, u32[]{:S(2)}, u32[]{:S(2)}) collective-permute-start(bf16[64,1024]{1,0:T(8,128)(2,1)S(1)} %collective-permute-done.7.refs_8_.refs_15_), channel_id=1, source_target_pairs={{0,4},{4,8},{8,12},{12,14},{14,10},{10,6},{6,2},{2,0},{1,3},{5,1},... | collective-permute-start | bytes 393224 | tf_op jit(solution)/shard_map/ppermute | solution.py:77
  28.7 4.2 %load_weights.1.refs_26_ = bf16[16,1024,256]{2,1,0:T(8,128)(2,1)S(1)} custom-call(s32[16]{0:T(128)S(1)} %stack.108.ids, bf16[16384,128]{1,0:T(8,128)(2,1)} %wq.1, bf16[16384,128]{1,0:T(8,128)(2,1)} %wkv.1), custom_call_target="tpu_custom_call" | custom-call | bytes 16777216 | tf_op jit(solution)/shard_map/load_weights/pallas_call | solution.py:257
  37.7 4.0 %collective-permute-done.17.refs_9_.refs_18_ = bf16[128,1024]{1,0:T(8,128)(2,1)S(1)} collective-permute-done((bf16[128,1024]{1,0:T(8,128)(2,1)S(1)}, bf16[128,1024]{1,0:T(8,128)(2,1)S(1)}, u32[]{:S(2)}, u32[]{:S(2)}) %collective-permute-start.17) | collective-permute-done | bytes 262176 | tf_op jit(solution)/shard_map/ppermute | solution.py:77
  42.3 1.5 %collective-permute-start.29 = (bf16[2,2,2,64,128]{4,3,2,1,0:T(8,128)(2,1)S(1)}, bf16[2,2,2,64,128]{4,3,2,1,0:T(8,128)(2,1)S(1)}, u32[]{:S(2)}, u32[]{:S(2)}) collective-permute-start(bf16[2,2,2,64,128]{4,3,2,1,0:T(8,128)(2,1)S(1)} %pad_maximum_fusion.3), channel_id=1, source_target_pairs={{0,8},{1,9},{2,10},{3,11},{4,12},{5,13},{6,14},{7,15},{8,0},{9,1},... | collective-permute-start | bytes 393224 | tf_op jit(solution)/shard_map/ppermute | solution.py:77
  44.3 2.5 %collective-permute-start.30 = (bf16[2,2,2,64,128]{4,3,2,1,0:T(8,128)(2,1)S(1)}, bf16[2,2,2,64,128]{4,3,2,1,0:T(8,128)(2,1)S(1)}, u32[]{:S(2)}, u32[]{:S(2)}) collective-permute-start(bf16[2,2,2,64,128]{4,3,2,1,0:T(8,128)(2,1)S(1)} %pad_maximum_fusion.4), channel_id=1, source_target_pairs={{0,12},{1,13},{2,14},{3,15},{4,8},{5,9},{6,10},{7,11},{8,4},{9,5},... | collective-permute-start | bytes 393224 | tf_op jit(solution)/shard_map/ppermute | solution.py:77
  46.8 2.6 %norm_project.1 = (bf16[64,128]{1,0:T(8,128)(2,1)S(1)}, bf16[64,128]{1,0:T(8,128)(2,1)S(1)}, bf16[64,128]{1,0:T(8,128)(2,1)S(1)}, bf16[64,128]{1,0:T(8,128)(2,1)S(1)}) custom-call(s32[16]{0:T(128)S(1)} %stack.108.ids, bf16[128,1024]{1,0:T(8,128)(2,1)S(1)} %copy-done, bf16[128,1024]{1,0:T(8,128)(2,1)S(1)} %collective-permute-done.8.refs_1_, ...), custom_call_target="tpu_custom_call" | custom-call | flops 1073741824 | bytes 12582912 | tf_op jit(solution)/shard_map/norm_project/pallas_call | solution.py:293
  50.6 4.6 %collective-permute-done.29.refs_3_ = bf16[2,2,2,64,128]{4,3,2,1,0:T(8,128)(2,1)S(1)} collective-permute-done((bf16[2,2,2,64,128]{4,3,2,1,0:T(8,128)(2,1)S(1)}, bf16[2,2,2,64,128]{4,3,2,1,0:T(8,128)(2,1)S(1)}, u32[]{:S(2)}, u32[]{:S(2)}) %collective-permute-start.29) | collective-permute-done | bytes 131104 | tf_op jit(solution)/shard_map/ppermute | solution.py:77
  55.4 1.8 %cache_scores.1 = (f32[128,1024]{1,0:T(8,128)S(1)}, bf16[2,256,1024]{2,1,0:T(8,128)(2,1)S(1)}) custom-call(s32[4]{0:T(128)S(1)} %pad_add_fusion.info, s32[8]{0:T(128)S(1)} %stack.117.to, bf16[64,128]{1,0:T(8,128)(2,1)S(1)} %get-tuple-element.54.q, bf16[64,128]{1,0:T(8,128)(2,1)S(1)} %collective-permute-done.23.q_other, ...), custom_call_target="tpu_custom_call" | custom-call | flops 33554432 | bytes 3145728 | tf_op jit(solution)/shard_map/cache_scores/pallas_call | solution.py:349
  57.2 2.6 %collective-permute-done.25.crossed = bf16[64,128]{1,0:T(8,128)(2,1)S(1)} collective-permute-done((bf16[64,128]{1,0:T(8,128)(2,1)S(1)}, bf16[64,128]{1,0:T(8,128)(2,1)S(1)}, u32[]{:S(2)}, u32[]{:S(2)}) %collective-permute-start.25) | collective-permute-done | bytes 16416 | tf_op jit(solution)/shard_map/ppermute | solution.py:77
  64.9 3.1 %more_shares.1 = (f32[64,1024]{1,0:T(8,128)S(1)}, f32[64,1024]{1,0:T(8,128)S(1)}, f32[128,1024]{1,0:T(8,128)S(1)}, f32[64,1024]{1,0:T(8,128)S(1)}, f32[64,1024]{...) custom-call(s32[1]{0:T(128)} %bitcast.16.core, ...), custom_call_target="tpu_custom_call" | custom-call | flops 402653184 | bytes 6291456 | tf_op jit(solution)/shard_map/more_shares/pallas_call | solution.py:471
  68.5 3.2 %collective-permute-done.40 = bf16[64,1024]{1,0:T(8,128)(2,1)S(1)} collective-permute-done((bf16[64,1024]{1,0:T(8,128)(2,1)S(1)}, bf16[64,1024]{1,0:T(8,128)(2,1)S(1)}, u32[]{:S(2)}, u32[]{:S(2)}) %collective-permute-start.40) | collective-permute-done | bytes 131104 | tf_op jit(solution)/shard_map/ppermute | solution.py:77
  73.6 2.0 %collective-permute-start.38 = (bf16[128,1024]{1,0:T(8,128)(2,1)S(1)}, bf16[128,1024]{1,0:T(8,128)(2,1)S(1)}, u32[]{:S(2)}, u32[]{:S(2)}) collective-permute-start(bf16[128,1024]{1,0:T(8,128)(2,1)S(1)} %add_convert_fusion.1), channel_id=1, source_target_pairs={{0,4},{4,8},{8,12},{12,14},{14,10},{10,6},{6,2},{2,0},{1,3},{5,1},... | collective-permute-start | bytes 786440 | tf_op jit(solution)/shard_map/ppermute | solution.py:77
  78.6 2.4 %collective-permute-done.38 = bf16[128,1024]{1,0:T(8,128)(2,1)S(1)} collective-permute-done((bf16[128,1024]{1,0:T(8,128)(2,1)S(1)}, bf16[128,1024]{1,0:T(8,128)(2,1)S(1)}, u32[]{:S(2)}, u32[]{:S(2)}) %collective-permute-start.38) | collective-permute-done | bytes 262176 | tf_op jit(solution)/shard_map/ppermute | solution.py:77
  83.8 4.2 %collective-permute-done.43 = bf16[64,1024]{1,0:T(8,128)(2,1)S(1)} collective-permute-done((bf16[64,1024]{1,0:T(8,128)(2,1)S(1)}, bf16[64,1024]{1,0:T(8,128)(2,1)S(1)}, u32[]{:S(2)}, u32[]{:S(2)}) %collective-permute-start.43) | collective-permute-done | bytes 131104 | tf_op jit(solution)/shard_map/ppermute | solution.py:77
  91.0 4.5 %collective-permute-done.44.refs_1_.refs_2_ = bf16[64,1024]{1,0:T(8,128)(2,1)S(1)} collective-permute-done((bf16[64,1024]{1,0:T(8,128)(2,1)S(1)}, bf16[64,1024]{1,0:T(8,128)(2,1)S(1)}, u32[]{:S(2)}, u32[]{:S(2)}) %collective-permute-start.44) | collective-permute-done | bytes 131104 | tf_op jit(solution)/shard_map/ppermute | solution.py:77
  102.8 3.2 %collective-permute-done.50.refs_7_.refs_14_ = bf16[64,1024]{1,0:T(8,128)(2,1)S(1)} collective-permute-done((bf16[64,1024]{1,0:T(8,128)(2,1)S(1)}, bf16[64,1024]{1,0:T(8,128)(2,1)S(1)}, u32[]{:S(2)}, u32[]{:S(2)}) %collective-permute-start.50) | collective-permute-done | bytes 131104 | tf_op jit(solution)/shard_map/ppermute | solution.py:77
  118.4 3.3 %final_norm.1 = bf16[128,16384]{1,0:T(8,128)(2,1)} custom-call(s32[16]{0:T(128)S(1)} %stack.108.ids, bf16[128,1024]{1,0:T(8,128)(2,1)S(1)} %pad_maximum_fusion.1.refs_0_, bf16[128,1024]{1,0:T(8,128)(2,1)S(1)} %collective-permute-done.52.refs_1_, bf16[64,1024]{1,0:T(8,128)(2,1)S(1)} %collective-permute-done.44.refs_1_.refs_2_, ...), custom_call_target="tpu_custom_call" | custom-call | flops 16777216 | bytes 12582912 | tf_op jit(solution)/shard_map/final_norm/pallas_call | solution.py:513
  (160 shorter events, 55.2 us)
Async XLA Ops:
  0.0 55.4 %collective-permute-start.31 = (bf16[128,16384]{1,0:T(8,128)(2,1)}, bf16[128,16384]{1,0:T(8,128)(2,1)}, u32[]{:S(2)}, u32[]{:S(2)}) collective-permute-start(bf16[128,16384]{1,0:T(8,128)(2,1)} %weight.1), channel_id=1, source_target_pairs={{0,1},{1,0},{2,3},{3,2},{4,5},{5,4},{6,7},{7,6},{8,9},{9,8},{10,11... | collective-permute-start | bytes 12582920 | tf_op jit(solution)/shard_map/ppermute | solution.py:77
  9.0 7.4 %collective-permute-start.2 = (bf16[128,1024]{1,0:T(8,128)(2,1)}, bf16[128,1024]{1,0:T(8,128)(2,1)S(1)}, u32[]{:S(2)}, u32[]{:S(2)}) collective-permute-start(bf16[128,1024]{1,0:T(8,128)(2,1)} %refs_0_.1), channel_id=1, source_target_pairs={{0,3},{4,1},{8,5},{12,9},{14,13},{10,15},{6,11},{2,7},{1,4},{5,8},... | collective-permute-start | bytes 786440 | tf_op jit(solution)/shard_map/ppermute | solution.py:77
  9.5 9.1 %collective-permute-start.4 = (bf16[64,1024]{1,0:T(8,128)(2,1)S(1)}, bf16[64,1024]{1,0:T(8,128)(2,1)S(1)}, u32[]{:S(2)}, u32[]{:S(2)}) collective-permute-start(bf16[64,1024]{1,0:T(8,128)(2,1)S(1)} %collective-permute-done.1.refs_2_.refs_3_), channel_id=1, source_target_pairs={{0,4},{4,8},{8,12},{12,14},{14,10},{10,6},{6,2},{2,0},{1,3},{5,1},... | collective-permute-start | bytes 393224 | tf_op jit(solution)/shard_map/ppermute | solution.py:77
  11.9 8.3 %collective-permute-start.6 = (bf16[64,1024]{1,0:T(8,128)(2,1)S(1)}, bf16[64,1024]{1,0:T(8,128)(2,1)S(1)}, u32[]{:S(2)}, u32[]{:S(2)}) collective-permute-start(bf16[64,1024]{1,0:T(8,128)(2,1)S(1)} %collective-permute-done.3.refs_4_.refs_8_), channel_id=1, source_target_pairs={{0,4},{4,8},{8,12},{12,14},{14,10},{10,6},{6,2},{2,0},{1,3},{5,1},... | collective-permute-start | bytes 393224 | tf_op jit(solution)/shard_map/ppermute | solution.py:77
  16.4 10.0 %collective-permute-start.5 = (bf16[128,1024]{1,0:T(8,128)(2,1)S(1)}, bf16[128,1024]{1,0:T(8,128)(2,1)S(1)}, u32[]{:S(2)}, u32[]{:S(2)}) collective-permute-start(bf16[128,1024]{1,0:T(8,128)(2,1)S(1)} %collective-permute-done.2.refs_3_.refs_6_), channel_id=1, source_target_pairs={{0,4},{4,8},{8,12},{12,14},{14,10},{10,6},{6,2},{2,0},{1,3},{5,1},... | collective-permute-start | bytes 786440 | tf_op jit(solution)/shard_map/ppermute | solution.py:77
  23.1 11.6 %collective-permute-start.27 = (bf16[4,2,2,64,128]{4,3,2,1,0:T(8,128)(2,1)S(1)}, bf16[4,2,2,64,128]{4,3,2,1,0:T(8,128)(2,1)S(1)}, u32[]{:S(2)}, u32[]{:S(2)}) collective-permute-start(bf16[4,2,2,64,128]{4,3,2,1,0:T(8,128)(2,1)S(1)} %get-tuple-element.59), channel_id=1, source_target_pairs={{0,2},{1,3},{2,0},{3,1},{4,6},{5,7},{6,4},{7,5},{8,10},{9,11},{10,... | collective-permute-start | bytes 786440 | tf_op jit(solution)/shard_map/ppermute | solution.py:77
  24.2 9.1 %collective-permute-start.19 = (bf16[64,1024]{1,0:T(8,128)(2,1)S(1)}, bf16[64,1024]{1,0:T(8,128)(2,1)S(1)}, u32[]{:S(2)}, u32[]{:S(2)}) collective-permute-start(bf16[64,1024]{1,0:T(8,128)(2,1)S(1)} %collective-permute-done.6.refs_7_.refs_14_), channel_id=1, source_target_pairs={{0,4},{4,8},{8,12},{12,14},{14,10},{10,6},{6,2},{2,0},{1,3},{5,1},... | collective-permute-start | bytes 393224 | tf_op jit(solution)/shard_map/ppermute | solution.py:77
  26.4 6.5 %collective-permute-start.16 = (bf16[64,1024]{1,0:T(8,128)(2,1)S(1)}, bf16[64,1024]{1,0:T(8,128)(2,1)S(1)}, u32[]{:S(2)}, u32[]{:S(2)}) collective-permute-start(bf16[64,1024]{1,0:T(8,128)(2,1)S(1)} %collective-permute-done.7.refs_8_.refs_15_), channel_id=1, source_target_pairs={{0,1},{1,0},{2,3},{3,2},{4,5},{5,4},{6,7},{7,6},{8,9},{9,8},{10,11... | collective-permute-start | bytes 393224 | tf_op jit(solution)/shard_map/ppermute | solution.py:77
  26.4 8.3 %collective-permute-start.20 = (bf16[64,1024]{1,0:T(8,128)(2,1)S(1)}, bf16[64,1024]{1,0:T(8,128)(2,1)S(1)}, u32[]{:S(2)}, u32[]{:S(2)}) collective-permute-start(bf16[64,1024]{1,0:T(8,128)(2,1)S(1)} %collective-permute-done.7.refs_8_.refs_15_), channel_id=1, source_target_pairs={{0,4},{4,8},{8,12},{12,14},{14,10},{10,6},{6,2},{2,0},{1,3},{5,1},... | collective-permute-start | bytes 393224 | tf_op jit(solution)/shard_map/ppermute | solution.py:77
  35.3 6.4 %collective-permute-start.17 = (bf16[128,1024]{1,0:T(8,128)(2,1)S(1)}, bf16[128,1024]{1,0:T(8,128)(2,1)S(1)}, u32[]{:S(2)}, u32[]{:S(2)}) collective-permute-start(bf16[128,1024]{1,0:T(8,128)(2,1)S(1)} %collective-permute-done.5.refs_6_.refs_12_), channel_id=1, source_target_pairs={{0,4},{4,8},{8,12},{12,14},{14,10},{10,6},{6,2},{2,0},{1,3},{5,1},... | collective-permute-start | bytes 786440 | tf_op jit(solution)/shard_map/ppermute | solution.py:77
  37.4 6.9 %collective-permute-start.14 = (bf16[128,1024]{1,0:T(8,128)(2,1)S(1)}, bf16[128,1024]{1,0:T(8,128)(2,1)S(1)}, u32[]{:S(2)}, u32[]{:S(2)}) collective-permute-start(bf16[128,1024]{1,0:T(8,128)(2,1)S(1)} %collective-permute-done.5.refs_6_.refs_12_), channel_id=1, source_target_pairs={{0,1},{1,0},{2,3},{3,2},{4,5},{5,4},{6,7},{7,6},{8,9},{9,8},{10,11... | collective-permute-start | bytes 786440 | tf_op jit(solution)/shard_map/ppermute | solution.py:77
  41.7 8.2 %collective-permute-start.28 = (bf16[2,2,2,64,128]{4,3,2,1,0:T(8,128)(2,1)S(1)}, bf16[2,2,2,64,128]{4,3,2,1,0:T(8,128)(2,1)S(1)}, u32[]{:S(2)}, u32[]{:S(2)}) collective-permute-start(bf16[2,2,2,64,128]{4,3,2,1,0:T(8,128)(2,1)S(1)} %pad_maximum_fusion.2), channel_id=1, source_target_pairs={{0,4},{1,5},{2,6},{3,7},{4,0},{5,1},{6,2},{7,3},{8,12},{9,13},{10,... | collective-permute-start | bytes 393224 | tf_op jit(solution)/shard_map/ppermute | solution.py:77
  42.3 12.9 %collective-permute-start.29 = (bf16[2,2,2,64,128]{4,3,2,1,0:T(8,128)(2,1)S(1)}, bf16[2,2,2,64,128]{4,3,2,1,0:T(8,128)(2,1)S(1)}, u32[]{:S(2)}, u32[]{:S(2)}) collective-permute-start(bf16[2,2,2,64,128]{4,3,2,1,0:T(8,128)(2,1)S(1)} %pad_maximum_fusion.3), channel_id=1, source_target_pairs={{0,8},{1,9},{2,10},{3,11},{4,12},{5,13},{6,14},{7,15},{8,0},{9,1},... | collective-permute-start | bytes 393224 | tf_op jit(solution)/shard_map/ppermute | solution.py:77
  44.3 11.1 %collective-permute-start.30 = (bf16[2,2,2,64,128]{4,3,2,1,0:T(8,128)(2,1)S(1)}, bf16[2,2,2,64,128]{4,3,2,1,0:T(8,128)(2,1)S(1)}, u32[]{:S(2)}, u32[]{:S(2)}) collective-permute-start(bf16[2,2,2,64,128]{4,3,2,1,0:T(8,128)(2,1)S(1)} %pad_maximum_fusion.4), channel_id=1, source_target_pairs={{0,12},{1,13},{2,14},{3,15},{4,8},{5,9},{6,10},{7,11},{8,4},{9,5},... | collective-permute-start | bytes 393224 | tf_op jit(solution)/shard_map/ppermute | solution.py:77
  49.9 7.3 %collective-permute-start.24 = (bf16[64,128]{1,0:T(8,128)(2,1)S(1)}, bf16[64,128]{1,0:T(8,128)(2,1)S(1)}, u32[]{:S(2)}, u32[]{:S(2)}) collective-permute-start(bf16[64,128]{1,0:T(8,128)(2,1)S(1)} %get-tuple-element.56), channel_id=1, source_target_pairs={{0,0},{1,2},{2,4},{3,6},{4,8},{5,10},{6,12},{7,14},{8,1},{9,3},{10... | collective-permute-start | bytes 49160 | tf_op jit(solution)/shard_map/ppermute | solution.py:77
  62.5 11.0 %collective-permute-start.37 = (bf16[128,1024]{1,0:T(8,128)(2,1)S(1)}, bf16[128,1024]{1,0:T(8,128)(2,1)S(1)}, u32[]{:S(2)}, u32[]{:S(2)}) collective-permute-start(bf16[128,1024]{1,0:T(8,128)(2,1)S(1)} %get-tuple-element.70), channel_id=1, source_target_pairs={{0,4},{4,8},{8,12},{12,14},{14,10},{10,6},{6,2},{2,0},{1,3},{5,1},... | collective-permute-start | bytes 786440 | tf_op jit(solution)/shard_map/ppermute | solution.py:77
  64.0 7.7 %collective-permute-start.40 = (bf16[64,1024]{1,0:T(8,128)(2,1)S(1)}, bf16[64,1024]{1,0:T(8,128)(2,1)S(1)}, u32[]{:S(2)}, u32[]{:S(2)}) collective-permute-start(bf16[64,1024]{1,0:T(8,128)(2,1)S(1)} %get-tuple-element.74), channel_id=1, source_target_pairs={{0,4},{4,8},{8,12},{12,14},{14,10},{10,6},{6,2},{2,0},{1,3},{5,1},... | collective-permute-start | bytes 393224 | tf_op jit(solution)/shard_map/ppermute | solution.py:77
  73.6 7.4 %collective-permute-start.38 = (bf16[128,1024]{1,0:T(8,128)(2,1)S(1)}, bf16[128,1024]{1,0:T(8,128)(2,1)S(1)}, u32[]{:S(2)}, u32[]{:S(2)}) collective-permute-start(bf16[128,1024]{1,0:T(8,128)(2,1)S(1)} %add_convert_fusion.1), channel_id=1, source_target_pairs={{0,4},{4,8},{8,12},{12,14},{14,10},{10,6},{6,2},{2,0},{1,3},{5,1},... | collective-permute-start | bytes 786440 | tf_op jit(solution)/shard_map/ppermute | solution.py:77
  81.0 6.9 %collective-permute-start.39 = (bf16[128,1024]{1,0:T(8,128)(2,1)S(1)}, bf16[128,1024]{1,0:T(8,128)(2,1)S(1)}, u32[]{:S(2)}, u32[]{:S(2)}) collective-permute-start(bf16[128,1024]{1,0:T(8,128)(2,1)S(1)} %add_convert_fusion), channel_id=1, source_target_pairs={{0,5},{4,9},{8,13},{12,15},{14,11},{10,7},{6,3},{2,1},{1,2},{5,0},... | collective-permute-start | bytes 786440 | tf_op jit(solution)/shard_map/ppermute | solution.py:77
  88.2 9.6 %collective-permute-start.46 = (bf16[128,1024]{1,0:T(8,128)(2,1)S(1)}, bf16[128,1024]{1,0:T(8,128)(2,1)S(1)}, u32[]{:S(2)}, u32[]{:S(2)}) collective-permute-start(bf16[128,1024]{1,0:T(8,128)(2,1)S(1)} %pad_maximum_fusion.1.refs_0_), channel_id=1, source_target_pairs={{0,3},{4,1},{8,5},{12,9},{14,13},{10,15},{6,11},{2,7},{1,4},{5,8},... | collective-permute-start | bytes 786440 | tf_op jit(solution)/shard_map/ppermute | solution.py:77
  89.1 6.4 %collective-permute-start.44 = (bf16[64,1024]{1,0:T(8,128)(2,1)S(1)}, bf16[64,1024]{1,0:T(8,128)(2,1)S(1)}, u32[]{:S(2)}, u32[]{:S(2)}) collective-permute-start(bf16[64,1024]{1,0:T(8,128)(2,1)S(1)} %get-tuple-element.87), channel_id=1, source_target_pairs={{0,4},{4,8},{8,12},{12,14},{14,10},{10,6},{6,2},{2,0},{1,3},{5,1},... | collective-permute-start | bytes 393224 | tf_op jit(solution)/shard_map/ppermute | solution.py:77
  90.0 6.8 %collective-permute-start.45 = (bf16[64,1024]{1,0:T(8,128)(2,1)S(1)}, bf16[64,1024]{1,0:T(8,128)(2,1)S(1)}, u32[]{:S(2)}, u32[]{:S(2)}) collective-permute-start(bf16[64,1024]{1,0:T(8,128)(2,1)S(1)} %get-tuple-element.88), channel_id=1, source_target_pairs={{0,4},{4,8},{8,12},{12,14},{14,10},{10,6},{6,2},{2,0},{1,3},{5,1},... | collective-permute-start | bytes 393224 | tf_op jit(solution)/shard_map/ppermute | solution.py:77
  97.8 11.9 %collective-permute-start.49 = (bf16[128,1024]{1,0:T(8,128)(2,1)S(1)}, bf16[128,1024]{1,0:T(8,128)(2,1)S(1)}, u32[]{:S(2)}, u32[]{:S(2)}) collective-permute-start(bf16[128,1024]{1,0:T(8,128)(2,1)S(1)} %collective-permute-done.46.refs_3_.refs_6_), channel_id=1, source_target_pairs={{0,4},{4,8},{8,12},{12,14},{14,10},{10,6},{6,2},{2,0},{1,3},{5,1},... | collective-permute-start | bytes 786440 | tf_op jit(solution)/shard_map/ppermute | solution.py:77
  109.7 6.9 %collective-permute-start.61 = (bf16[128,1024]{1,0:T(8,128)(2,1)S(1)}, bf16[128,1024]{1,0:T(8,128)(2,1)S(1)}, u32[]{:S(2)}, u32[]{:S(2)}) collective-permute-start(bf16[128,1024]{1,0:T(8,128)(2,1)S(1)} %collective-permute-done.49.refs_6_.refs_12_), channel_id=1, source_target_pairs={{0,4},{4,8},{8,12},{12,14},{14,10},{10,6},{6,2},{2,0},{1,3},{5,1},... | collective-permute-start | bytes 786440 | tf_op jit(solution)/shard_map/ppermute | solution.py:77
  (49 other events, 258.0 us)

commit v5 on v4

--- a/solution.py
+++ b/solution.py
@@ -56,8 +56,7 @@
     (2 * RING[i] + 1, 2 * RING[i - 1]) for i in range(CHIPS)
 ]
 SWAP = [(t, t ^ 1) for t in range(2 * CHIPS)]
-STRAIGHT = [(k, 2 * k) for k in range(KVH)] + [(KVH + k, 2 * k + 1) for k in range(KVH)]
-CROSSED = [(k, 2 * k + 1) for k in range(KVH)] + [(KVH + k, 2 * k) for k in range(KVH)]
+FRESH = [(k, 2 * k) for k in range(KVH)] + [(KVH + k, 2 * k + 1) for k in range(KVH)]
 VMEM = pl.BlockSpec(memory_space=pltpu.VMEM)
 SMEM = pl.BlockSpec(memory_space=pltpu.SMEM)
 HBM = pl.BlockSpec(memory_space=pltpu.HBM)
@@ -81,33 +80,44 @@
     return [(t, t ^ bits) for t in range(2 * CHIPS)]
 
 
-def ring_gather(halves, own, work=None):
-    straight, crossed = list(halves), own
+def after(array, *others):
+    return lax.optimization_barrier((array, others))[0]
+
+
+def ring_gather(parts, own, ready=None):
+    streams, crossed = list(parts), own
     came = [(own,)]
     for step in range(1, 5):
-        straight = [send(half, ONWARD) for half in straight]
-        came.append(tuple(straight))
+        if step == 4 and ready is not None:
+            streams = after(streams, ready)
+        streams = [send(part, ONWARD) for part in streams]
+        came.append(tuple(streams))
         if step < 4:
-            if step == 3 and work is not None:
-                crossed, work = lax.optimization_barrier((crossed, work))
             crossed = send(crossed, ENTER if step == 1 else ONWARD)
             came.append((crossed,))
-    early, _ = lax.optimization_barrier((came[:5], came[5]))
-    blocks = []
-    for block in early + came[5:]:
-        blocks += [block, tuple(send(piece, SWAP) for piece in block)]
-    return blocks, work
+    return came
+
+
+def both_cores(came):
+    mine = flat(came)
+    return mine + [send(piece, SWAP) for piece in mine]
+
+
+def block_refs(refs, parts):
+    counts = (1,) + (parts, 1) * 3 + (parts,)
+    return grouped(refs, counts * 2)
 
 
 def gathered_ids(rank):
-    place, core = ring_place(rank), rank % 2
-    ahead = 2 * core - 1
-    ids = [rank, rank ^ 1]
-    for step in range(1, 5):
-        near, far = 2 * chip_at(place + ahead * step), 2 * chip_at(place - ahead * step)
-        ids += [near + core, far + 1 - core]
-        if step < 4:
-            ids += [near + 1 - core, far + core]
+    place = ring_place(rank)
+    ids = []
+    for side in range(2):
+        device = rank ^ side
+        core = device % 2
+        ids.append(device)
+        for step in range(1, 5):
+            chip = 2 * chip_at(place + (2 * core - 1) * step)
+            ids += [chip + core, chip + 1 - core] if step < 4 else [chip + core]
     return jnp.stack(ids).astype(jnp.int32)
 
 
@@ -121,56 +131,71 @@
     ).astype(jnp.int32)
 
 
-def ring_sum(shares):
-    running = {0: shares[4, 0], 1: shares[3, 1]}
-    for step in range(4, 0, -1):
-        for other in range(2):
-            if step == 4 and other == 1:
-                continue
-            if (step, other) not in ((4, 0), (3, 1)):
-                running[other] = [
-                    (part.astype(jnp.float32) + share).astype(jnp.bfloat16)
-                    for part, share in zip(running[other], shares[step, other])
-                ]
-            pairs = LEAVE if (step, other) == (1, 1) else ONWARD
-            running[other] = [send(part, pairs) for part in running[other]]
-    return running[0], running[1][0]
-
-
-def move_cache(key_cache, value_cache, rank, rank_id, after):
+def ring_sum(shares, more_shares):
+    streams, crossed = shares[4, 0], shares[3, 1][0]
+    for step in range(1, 5):
+        streams = [send(part, ONWARD) for part in streams]
+        if step < 4:
+            crossed = send(crossed, LEAVE if step == 3 else ONWARD)
+        if step == 1:
+            shares.update(more_shares(streams[0]))
+        if step < 4:
+            streams = [add_share(part, share) for part, share in zip(streams, shares[4 - step, 0])]
+        if step < 3:
+            crossed = add_share(crossed, shares[3 - step, 1][0])
+    return streams, crossed
+
+
+def add_share(part, share):
+    return (part.astype(jnp.float32) + share).astype(jnp.bfloat16)
+
+
+def split_cache(key_cache, value_cache, rank, rank_id):
     core = rank % 2
     give = jnp.stack(
         [lax.dynamic_index_in_dim(c, 1 - core, 0, keepdims=False) for c in (key_cache, value_cache)]
     )
-    keep, give = pack(rank_id, key_cache, value_cache, send(give, SWAP))
+    return pack(rank_id, key_cache, value_cache, send(give, SWAP))
+
+
+def move_cache(parts, *when):
+    keep, give = parts
     came = send(give, xor(2))
     pieces = [jnp.stack([keep[m], came[m]]) for m in range(1, 4)]
-    pieces, _ = lax.optimization_barrier((pieces, after))
     return [keep, came] + [send(piece, xor(4 * m)) for m, piece in zip(range(1, 4), pieces)]
 
 
-def pack_kernel(rank, keys, values, theirs, keep, give):
+def pack_kernel(rank, keys, values, theirs, keep, give, sems):
     me = rank[0]
+    copies = []
     for m in range(4):
         for j, out in enumerate((keep, give)):
             chip = (me ^ (4 * m + 2 * j)) // 2
             head = pl.ds(pl.multiple_of(chip * HD, HD), HD)
-            out[m, 0, 0] = keys[me % 2, :, head]
-            out[m, 0, 1] = values[me % 2, :, head]
+            for k, cache in enumerate((keys, values)):
+                copies.append(
+                    pltpu.make_async_copy(
+                        cache.at[me % 2, :, head], out.at[m, 0, k], sems.at[m, j, k]
+                    )
+                )
+                copies[-1].start()
             out[m, 1, 0] = theirs[0, :, head]
             out[m, 1, 1] = theirs[1, :, head]
+    for copy in copies:
+        copy.wait()
 
 
 def pack(rank_id, key_cache, value_cache, theirs):
     return pl.pallas_call(
         pack_kernel,
         out_shape=[jax.ShapeDtypeStruct((4, 2, 2, CTX_DEV, HD), jnp.bfloat16)] * 2,
-        in_specs=[SMEM] + [VMEM] * 3,
+        in_specs=[SMEM] + [HBM] * 2 + [VMEM],
         out_specs=[VMEM] * 2,
+        scratch_shapes=[pltpu.SemaphoreType.DMA((4, 2, 2))],
         compiler_params=pltpu.CompilerParams(vmem_limit_bytes=8 * MIB),
         cost_estimate=pl.CostEstimate(flops=0, bytes_accessed=MIB, transcendentals=0),
         name="pack_cache",
-    )(rank_id, key_cache, value_cache, theirs)
+    )(rank_id, in_hbm(key_cache), in_hbm(value_cache), theirs)
 
 
 def flat(blocks):
@@ -211,26 +236,6 @@
         ],
         axis=1,
     )
-
-
-def squares_kernel(counts, *refs):
-    out = refs[-1]
-    out[...] = square_sums(grouped(refs[:-1], counts), jnp.zeros((TOKENS, 128), jnp.float32))
-
-
-def squares_of(blocks):
-    pieces = flat(blocks)
-    return pl.pallas_call(
-        functools.partial(squares_kernel, [len(block) for block in blocks]),
-        out_shape=jax.ShapeDtypeStruct((TOKENS, 128), jnp.float32),
-        in_specs=[VMEM] * len(pieces),
-        out_specs=VMEM,
-        compiler_params=pltpu.CompilerParams(vmem_limit_bytes=16 * MIB),
-        cost_estimate=pl.CostEstimate(
-            flops=4 * MIB, bytes_accessed=len(blocks) * MIB // 4, transcendentals=0
-        ),
-        name="squares",
-    )(*pieces)
 
 
 def in_hbm(array):
@@ -266,12 +271,17 @@
     )(ids, in_hbm(wq), in_hbm(wkv))
 
 
-def project_kernel(counts, ids, *refs):
-    blocks, refs = grouped(refs, counts), refs[sum(counts) :]
-    squares, gain, weights, cosine, sine, kv_cos, kv_sin = refs[:7]
-    q_keep, q_send, kv_straight, kv_crossed = refs[7:11]
-    features = 16 * blocks[0][0].shape[1]
-    factors = row_factors(square_sums(blocks[14:15] + blocks[1::2], squares[...]), features)
+def all_factors(blocks):
+    total = square_sums(blocks, jnp.zeros((TOKENS, 128), jnp.float32))
+    return row_factors(total, 16 * blocks[0][0].shape[1])
+
+
+def project_kernel(parts, ids, *refs):
+    count = 8 * (parts + 1)
+    blocks, refs = block_refs(refs[:count], parts), refs[count:]
+    gain, weights, cosine, sine, kv_cos, kv_sin = refs[:6]
+    q_keep, q_send, fresh = refs[6:]
+    factors = all_factors(blocks)
     total = jnp.zeros((TOKENS, 2 * HD), jnp.float32)
     for i in range(16):
         normed = normed_block(blocks[i], factors, gain[ids[i]])
@@ -280,27 +290,24 @@
     q = (q * cosine[...] + pltpu.roll(q, HD // 2, 1) * sine[...]).astype(jnp.bfloat16)
     kv = (kv * kv_cos[...] + pltpu.roll(kv, HD // 2, 1) * kv_sin[...]).astype(jnp.bfloat16)
     core_one = ids[0] % 2 == 1
-    holds_keys = ids[0] < KVH
-    first, second = slice(0, SPAN), slice(SPAN, TOKENS)
-    q_keep[...] = jnp.where(core_one, q[second], q[first])
-    q_send[...] = jnp.where(core_one, q[first], q[second])
-    kv_straight[...] = jnp.where(holds_keys, kv[first], kv[second])
-    kv_crossed[...] = jnp.where(holds_keys, kv[second], kv[first])
-
-
-def project(ids, blocks, squares, gain, weights, tables):
-    pieces = flat(blocks)
+    q_keep[...] = jnp.where(core_one, q[SPAN:], q[:SPAN])
+    q_send[...] = jnp.where(core_one, q[:SPAN], q[SPAN:])
+    fresh[...] = kv
+
+
+def project(ids, arrays, gain, weights, tables):
     return pl.pallas_call(
-        functools.partial(project_kernel, [len(block) for block in blocks]),
-        out_shape=[jax.ShapeDtypeStruct((SPAN, HD), jnp.bfloat16)] * 4,
-        in_specs=[SMEM] + [VMEM] * (len(pieces) + 7),
-        out_specs=[VMEM] * 4,
+        functools.partial(project_kernel, len(arrays) // 8 - 1),
+        out_shape=[jax.ShapeDtypeStruct((SPAN, HD), jnp.bfloat16)] * 2
+        + [jax.ShapeDtypeStruct((TOKENS, HD), jnp.bfloat16)],
+        in_specs=[SMEM] + [VMEM] * (len(arrays) + 6),
+        out_specs=[VMEM] * 3,
         compiler_params=pltpu.CompilerParams(vmem_limit_bytes=24 * MIB),
         cost_estimate=pl.CostEstimate(
             flops=2 * TOKENS * weights.size, bytes_accessed=12 * MIB, transcendentals=0
         ),
         name="norm_project",
-    )(ids, *pieces, squares, gain, weights, *tables)
+    )(ids, *arrays, gain, weights, *tables)
 
 
 def share_copies(to, first, weight, weight_other, out, sems):
@@ -363,11 +370,12 @@
     )(info, to, q, q_other, *cache, in_hbm(weight), weight_other)
 
 
-def attend_kernel(info, q, q_other, straight, crossed, scores, *refs):
+def attend_kernel(info, q, q_other, fresh_own, fresh_other, scores, *refs):
     cache, out = refs[:5], refs[5]
     core = info[SEQS]
-    fresh_keys = jnp.where(core == 0, straight[...], crossed[...])
-    fresh_values = jnp.where(core == 0, crossed[...], straight[...])
+    came = fresh_other[...]
+    fresh_keys = jnp.where(core == 0, fresh_own[:SPAN, :], came)
+    fresh_values = jnp.where(core == 0, came, fresh_own[SPAN:, :])
     queries = jnp.concatenate([q[...], q_other[...]], axis=0)
     old = scores[...]
     valid = old > -1e29
@@ -393,7 +401,7 @@
     out[:, HD:] = attn[SPAN:]
 
 
-def attend(info, q, q_other, straight, crossed, scores, cache):
+def attend(info, q, q_other, fresh_own, fresh_other, scores, cache):
     return pl.pallas_call(
         attend_kernel,
         out_shape=jax.ShapeDtypeStruct((SPAN, 2 * HD), jnp.bfloat16),
@@ -404,7 +412,7 @@
             flops=48 * MIB, bytes_accessed=2 * MIB, transcendentals=TOKENS * 1088
         ),
         name="attend",
-    )(info, q, q_other, straight, crossed, scores, *cache)
+    )(info, q, q_other, fresh_own, fresh_other, scores, *cache)
 
 
 def both_heads(core, attn, attn_other):
@@ -455,21 +463,21 @@
     return share_lists(shares, arrays)
 
 
-def more_shares_kernel(first, core, to, attn, attn_other, weight, weight_other, *refs):
+def more_shares_kernel(first, last, core, to, attn, attn_other, weight, weight_other, *refs):
     outs, (weights, sems) = refs[:-2], refs[-2:]
     copies = share_copies(to, first, weight, weight_other, weights, sems)
     rows = both_heads(core, attn, attn_other)
-    for i, out in enumerate(share_lists(SHARES[first:], outs).values()):
+    for i, out in enumerate(share_lists(SHARES[first:last], outs).values()):
         for copy in copies[i]:
             copy.wait()
         write_share(jnp.dot(rows, weights[i], preferred_element_type=jnp.float32), out)
 
 
-def more_shares(core, to, attn, attn_other, weight, weight_other, first):
-    count, width = len(SHARES) - first, weight.shape[1] // 16
-    out_shape = share_shapes(SHARES[first:], width, jnp.float32)
+def more_shares(core, to, attn, attn_other, weight, weight_other, first, last):
+    count, width = last - first, weight.shape[1] // 16
+    out_shape = share_shapes(SHARES[first:last], width, jnp.float32)
     arrays = pl.pallas_call(
-        functools.partial(more_shares_kernel, first),
+        functools.partial(more_shares_kernel, first, last),
         out_shape=out_shape,
         in_specs=[SMEM] * 2 + [VMEM] * 2 + [HBM] * 2,
         out_specs=[VMEM] * len(out_shape),
@@ -483,16 +491,17 @@
             bytes_accessed=count * MIB,
             transcendentals=0,
         ),
-        name="more_shares",
+        name="shares_%d" % first,
     )(core, to, attn, attn_other, in_hbm(weight), weight_other)
-    return share_lists(SHARES[first:], arrays)
-
-
-def final_kernel(counts, ids, *refs):
-    blocks, refs = grouped(refs, counts), refs[sum(counts) :]
-    squares, gain, out, staged, sems = refs
-    width = blocks[0][0].shape[1]
-    factors = row_factors(square_sums(blocks[14:15] + blocks[1::2], squares[...]), 16 * width)
+    return share_lists(SHARES[first:last], arrays)
+
+
+def final_kernel(parts, ids, *refs):
+    count = 8 * (parts + 1)
+    blocks, refs = block_refs(refs[:count], parts), refs[count:]
+    gain, out, staged, sems = refs
+    width = staged.shape[2]
+    factors = all_factors(blocks)
     copies = []
     for i in range(16):
         staged[i] = normed_block(blocks[i], factors, gain[ids[i]])
@@ -507,13 +516,12 @@
         copy.wait()
 
 
-def final_norm(ids, blocks, squares, gain):
-    pieces = flat(blocks)
-    width = pieces[0].shape[1]
+def final_norm(ids, arrays, gain):
+    width = arrays[0].shape[1]
     return pl.pallas_call(
-        functools.partial(final_kernel, [len(block) for block in blocks]),
+        functools.partial(final_kernel, len(arrays) // 8 - 1),
         out_shape=jax.ShapeDtypeStruct((TOKENS, 16 * width), jnp.bfloat16),
-        in_specs=[SMEM] + [VMEM] * (len(pieces) + 2),
+        in_specs=[SMEM] + [VMEM] * (len(arrays) + 1),
         out_specs=HBM,
         scratch_shapes=[
             pltpu.VMEM((16, TOKENS, width), jnp.bfloat16),
@@ -524,7 +532,7 @@
             flops=16 * MIB, bytes_accessed=12 * MIB, transcendentals=0
         ),
         name="final_norm",
-    )(ids, *pieces, squares, gain)
+    )(ids, *arrays, gain)
 
 
 def per_device_ring(
@@ -538,11 +546,11 @@
     core_id, rank_id = core[None].astype(jnp.int32), rank[None].astype(jnp.int32)
     info = jnp.concatenate([prefix, core_id, rank_id])
 
+    weight_other = send(o_weight, SWAP)
+    parts = split_cache(key_cache, value_cache, rank, rank_id)
+    came = ring_gather([residual], residual, weight_other)
     weights = load_weights(ids, q_weight, kv_weight, width)
-    residual_halves = [residual[:SPAN], residual[SPAN:]]
-    blocks, weights = ring_gather(residual_halves, residual, weights)
-    weight_other = send(o_weight, SWAP)
-    cache = move_cache(key_cache, value_cache, rank, rank_id, blocks[12])
+    cache = move_cache(parts)
 
     positions = (prefix[:, None] + jnp.arange(SPAN, dtype=jnp.int32)[None, :]).reshape(-1)
     cosine, sine = rope_tables(positions)
@@ -552,32 +560,35 @@
     tables = (cosine, sine, jnp.where(holds_keys, cosine, 1.0), jnp.where(holds_keys, sine, 0.0))
 
     gain = attn_gain.reshape(16, 1, width).astype(jnp.float32)
-    squares = squares_of(blocks[:14:2])
-    q_keep, q_send, straight, crossed = project(
-        ids, blocks, squares, gain, weights, tables
-    )
+    arrays = both_cores(came)
+    arrays[0] = after(arrays[0], cache[1])
+    q_keep, q_send, fresh = project(ids, arrays, gain, weights, tables)
     q_other = send(q_send, SWAP)
+    fresh_own = send(fresh, FRESH)
+    fresh_other = send(jnp.where(core == 0, fresh_own[SPAN:], fresh_own[:SPAN]), SWAP)
     scores, first_weights = cache_scores(
         info, to, q_keep, q_other, cache, o_weight, weight_other, 2
     )
-    attn = attend(
-        info, q_keep, q_other, send(straight, STRAIGHT), send(crossed, CROSSED), scores, cache
-    )
+    attn = attend(info, q_keep, q_other, fresh_own, fresh_other, scores, cache)
     attn_other = send(attn, SWAP)
 
     shares = first_shares(SHARES[:2], core_id, attn, attn_other, first_weights)
-    shares.update(more_shares(core_id, to, attn, attn_other, o_weight, weight_other, 2))
-    one_way, other_way = ring_sum(shares)
+    inputs = (attn, attn_other, o_weight, weight_other)
+    shares.update(more_shares(core_id, to, *inputs, 2, 4))
+    one_way, other_way = ring_sum(
+        shares, lambda came: more_shares(core_id, after(to, came), *inputs, 4, len(SHARES))
+    )
     hidden = []
     for h, rows in enumerate((slice(0, SPAN), slice(SPAN, TOKENS))):
         projected = shares[0, 0][h] + one_way[h].astype(jnp.float32)
         projected = projected + other_way[rows].astype(jnp.float32)
-        hidden.append((residual_halves[h].astype(jnp.float32) + projected).astype(jnp.bfloat16))
-
-    blocks, _ = ring_gather(hidden, jnp.concatenate(hidden, axis=0))
+        hidden.append((residual[rows].astype(jnp.float32) + projected).astype(jnp.bfloat16))
+
+    hidden = jnp.concatenate(hidden, axis=0)
+    came = ring_gather([hidden], hidden)
+    arrays = both_cores(came)
     gain = ffn_gain.reshape(16, 1, width).astype(jnp.float32)
-    squares = squares_of(blocks[:14:2])
-    return final_norm(ids, blocks, squares, gain)
+    return final_norm(ids, arrays, gain)
 
 
 def per_device(

time: 122 us -> 118 us (0.967)
  waiting for transfers between devices: 50.5 us -> 43.3 us
  Pallas kernels: 17.4 us -> 20.3 us
  local copies, waits for them, and re-layouts: 4.18 us -> 1.29 us
  other arithmetic: 1.8 us -> 3.87 us
    ppermute x67 -> x51, waiting for transfers between devices: 50.5 us -> 43.3 us  [send(): return lax.ppermute(array, 'tp', pairs)]
    pallas_call x5 -> x4, Pallas kernels: 9.9 us -> 11.8 us  [the longest x2 4.67 us: more_shares(): pl.pallas_call(functools.partial(more_shares_kernel, first, last), out_sh...]
    unnamed x12 -> x6, local copies, waits for them, and re-layouts: 1.92 us -> 0.02 us
    another operation x3, other arithmetic: 0.04 us -> 1.35 us  [move_cache(): pieces = [jnp.stack([keep[m], came[m]]) for m in range(1, 4)]]
    ppermute x67 -> x51, starting transfers between devices: 47.1 us -> 48.1 us  [send(): return lax.ppermute(array, 'tp', pairs)]
  transfers between devices with their start and end apart: 67 -> 51, of which waited for: 33 -> 17; matrix products, arithmetic and copies ran while one was open for 3% -> 4% of each run, Pallas kernels for 10% -> 13%
where the time goes in v5:
time: 118 us
  starting transfers between devices  48.1 us (41%)
  waiting for transfers between devices  43.3 us (37%)
  Pallas kernels  20.3 us (17%)
  other arithmetic  3.87 us (3%)
  local copies, waits for them, and re-layouts  1.29 us (1%)
    ppermute x51, starting transfers between devices, send(): return lax.ppermute(array, 'tp', pairs)  48.1 us
    ppermute x51, waiting for transfers between devices, send(): return lax.ppermute(array, 'tp', pairs)  43.3 us
    pallas_call x2, Pallas kernels, more_shares(): pl.pallas_call(functools.partial(more_shares_kernel, first, last), out_sh...  4.67 us
    pallas_call x1, Pallas kernels, load_weights(): pl.pallas_call(load_kernel, out_shape=jax.ShapeDtypeStruct((16, width, 2...  4.19 us
    pallas_call x1, Pallas kernels, final_norm(): pl.pallas_call(functools.partial(final_kernel, len(arrays) // 8 - 1), out...  3.65 us
    pallas_call x1, Pallas kernels, project(): pl.pallas_call(functools.partial(project_kernel, len(arrays) // 8 - 1), o...  3.52 us
  transfers between devices with their start and end apart: 51, of which 17 were waited for; matrix products, arithmetic and copies ran while one was open for 4% of the time, Pallas kernels for 13%

profile of v5, /device:TPU:0, one launch (start us, length us, event | category | flops | bytes accessed | tf_op | source)
XLA Modules:
  0.0 117.8 jit_solution(7941531702533129128)
XLA Ops:
  0.5 2.6 %collective-permute-start.2 = (bf16[128,1024]{1,0:T(8,128)(2,1)}, bf16[128,1024]{1,0:T(8,128)(2,1)S(1)}, u32[]{:S(2)}, u32[]{:S(2)}) collective-permute-start(bf16[128,1024]{1,0:T(8,128)(2,1)} %refs_0_), channel_id=1, source_target_pairs={{0,4},{4,8},{8,12},{12,14},{14,10},{10,6},{6,2},{2,0},{1,3},{5,1},... | collective-permute-start | bytes 786440 | tf_op jit(solution)/shard_map/ppermute | solution.py:76
  5.7 3.3 %collective-permute-done.2.refs_1_ = bf16[128,1024]{1,0:T(8,128)(2,1)S(1)} collective-permute-done((bf16[128,1024]{1,0:T(8,128)(2,1)}, bf16[128,1024]{1,0:T(8,128)(2,1)S(1)}, u32[]{:S(2)}, u32[]{:S(2)}) %collective-permute-start.2) | collective-permute-done | bytes 262176 | tf_op jit(solution)/shard_map/ppermute | solution.py:76
  9.0 2.4 %collective-permute-start.4 = (bf16[128,1024]{1,0:T(8,128)(2,1)S(1)}, bf16[128,1024]{1,0:T(8,128)(2,1)S(1)}, u32[]{:S(2)}, u32[]{:S(2)}) collective-permute-start(bf16[128,1024]{1,0:T(8,128)(2,1)S(1)} %collective-permute-done.2.refs_1_), channel_id=1, source_target_pairs={{0,4},{4,8},{8,12},{12,14},{14,10},{10,6},{6,2},{2,0},{1,3},{5,1},... | collective-permute-start | bytes 786440 | tf_op jit(solution)/shard_map/ppermute | solution.py:76
  13.8 2.2 %collective-permute-done.4.refs_3_ = bf16[128,1024]{1,0:T(8,128)(2,1)S(1)} collective-permute-done((bf16[128,1024]{1,0:T(8,128)(2,1)S(1)}, bf16[128,1024]{1,0:T(8,128)(2,1)S(1)}, u32[]{:S(2)}, u32[]{:S(2)}) %collective-permute-start.4) | collective-permute-done | bytes 262176 | tf_op jit(solution)/shard_map/ppermute | solution.py:76
  16.0 1.8 %collective-permute-start.6 = (bf16[128,1024]{1,0:T(8,128)(2,1)S(1)}, bf16[128,1024]{1,0:T(8,128)(2,1)S(1)}, u32[]{:S(2)}, u32[]{:S(2)}) collective-permute-start(bf16[128,1024]{1,0:T(8,128)(2,1)S(1)} %collective-permute-done.4.refs_3_), channel_id=1, source_target_pairs={{0,4},{4,8},{8,12},{12,14},{14,10},{10,6},{6,2},{2,0},{1,3},{5,1},... | collective-permute-start | bytes 786440 | tf_op jit(solution)/shard_map/ppermute | solution.py:76
  19.7 5.4 %collective-permute-done.6.refs_5_ = bf16[128,1024]{1,0:T(8,128)(2,1)S(1)} collective-permute-done((bf16[128,1024]{1,0:T(8,128)(2,1)S(1)}, bf16[128,1024]{1,0:T(8,128)(2,1)S(1)}, u32[]{:S(2)}, u32[]{:S(2)}) %collective-permute-start.6) | collective-permute-done | bytes 262176 | tf_op jit(solution)/shard_map/ppermute | solution.py:76
  27.0 4.2 %load_weights.1.refs_17_ = bf16[16,1024,256]{2,1,0:T(8,128)(2,1)S(1)} custom-call(s32[16]{0:T(128)S(1)} %stack.108.ids, bf16[16384,128]{1,0:T(8,128)(2,1)} %wq.1, bf16[16384,128]{1,0:T(8,128)(2,1)} %wkv.1), custom_call_target="tpu_custom_call" | custom-call | bytes 16777216 | tf_op jit(solution)/shard_map/load_weights/pallas_call | solution.py:262
  32.3 2.1 %collective-permute-done.9.refs_7_ = bf16[128,1024]{1,0:T(8,128)(2,1)} collective-permute-done((bf16[128,1024]{1,0:T(8,128)(2,1)S(1)}, bf16[128,1024]{1,0:T(8,128)(2,1)}, u32[]{:S(2)}, u32[]{:S(2)}) %collective-permute-start.9) | collective-permute-done | bytes 262176 | tf_op jit(solution)/shard_map/ppermute | solution.py:76
  37.3 2.2 %collective-permute-start.22 = (bf16[2,2,2,64,128]{4,3,2,1,0:T(8,128)(2,1)}, bf16[2,2,2,64,128]{4,3,2,1,0:T(8,128)(2,1)S(1)}, u32[]{:S(2)}, u32[]{:S(2)}) collective-permute-start(bf16[2,2,2,64,128]{4,3,2,1,0:T(8,128)(2,1)} %pad_maximum_fusion.3), channel_id=1, source_target_pairs={{0,8},{1,9},{2,10},{3,11},{4,12},{5,13},{6,14},{7,15},{8,0},{9,1},... | collective-permute-start | bytes 393224 | tf_op jit(solution)/shard_map/ppermute | solution.py:76
  39.5 3.5 %norm_project.1 = (bf16[64,128]{1,0:T(8,128)(2,1)S(1)}, bf16[64,128]{1,0:T(8,128)(2,1)S(1)}, bf16[128,128]{1,0:T(8,128)(2,1)S(1)}) custom-call(s32[16]{0:T(128)S(1)} %stack.108.ids, bf16[128,1024]{1,0:T(8,128)(2,1)S(1)} %copy-done, bf16[128,1024]{1,0:T(8,128)(2,1)S(1)} %collective-permute-done.2.refs_1_, ...), custom_call_target="tpu_custom_call" | custom-call | flops 1073741824 | bytes 12582912 | tf_op jit(solution)/shard_map/norm_project/pallas_call | solution.py:299
  43.8 3.0 %collective-permute-start.23 = (bf16[2,2,2,64,128]{4,3,2,1,0:T(8,128)(2,1)S(1)}, bf16[2,2,2,64,128]{4,3,2,1,0:T(8,128)(2,1)S(1)}, u32[]{:S(2)}, u32[]{:S(2)}) collective-permute-start(bf16[2,2,2,64,128]{4,3,2,1,0:T(8,128)(2,1)S(1)} %pad_maximum_fusion.4), channel_id=1, source_target_pairs={{0,12},{1,13},{2,14},{3,15},{4,8},{5,9},{6,10},{7,11},{8,4},{9,5},... | collective-permute-start | bytes 393224 | tf_op jit(solution)/shard_map/ppermute | solution.py:76
  50.9 1.8 %cache_scores.1 = (f32[128,1024]{1,0:T(8,128)S(1)}, bf16[2,256,1024]{2,1,0:T(8,128)(2,1)S(1)}) custom-call(s32[4]{0:T(128)S(1)} %pad_add_fusion.info, s32[8]{0:T(128)S(1)} %stack.117.to, bf16[64,128]{1,0:T(8,128)(2,1)S(1)} %get-tuple-element.31.q, bf16[64,128]{1,0:T(8,128)(2,1)S(1)} %collective-permute-done.18.q_other, ...), custom_call_target="tpu_custom_call" | custom-call | flops 33554432 | bytes 3145728 | tf_op jit(solution)/shard_map/cache_scores/pallas_call | solution.py:356
  53.8 2.4 %collective-permute-start.24 = (bf16[64,256]{1,0:T(8,128)(2,1)S(1)}, bf16[64,256]{1,0:T(8,128)(2,1)S(1)}, u32[]{:S(2)}, u32[]{:S(2)}) collective-permute-start(bf16[64,256]{1,0:T(8,128)(2,1)S(1)} %attend.1.attn), channel_id=1, source_target_pairs={{0,1},{1,0},{2,3},{3,2},{4,5},{5,4},{6,7},{7,6},{8,9},{9,8},{10,11... | collective-permute-start | bytes 98312 | tf_op jit(solution)/shard_map/ppermute | solution.py:76
  57.4 2.7 %collective-permute-start.32 = (bf16[64,1024]{1,0:T(8,128)(2,1)S(1)}, bf16[64,1024]{1,0:T(8,128)(2,1)S(1)}, u32[]{:S(2)}, u32[]{:S(2)}) collective-permute-start(bf16[64,1024]{1,0:T(8,128)(2,1)S(1)} %get-tuple-element.47), channel_id=1, source_target_pairs={{0,4},{4,8},{8,12},{12,14},{14,10},{10,6},{6,2},{2,0},{1,3},{5,1},... | collective-permute-start | bytes 393224 | tf_op jit(solution)/shard_map/ppermute | solution.py:76
  61.7 2.1 %shares_2.1 = (f32[64,1024]{1,0:T(8,128)S(1)}, f32[64,1024]{1,0:T(8,128)S(1)}, f32[128,1024]{1,0:T(8,128)S(1)}) custom-call(s32[1]{0:T(128)} %bitcast.16.core, s32[8]{0:T(128)S(1)} %stack.117.to, bf16[64,256]{1,0:T(8,128)(2,1)S(1)} %attend.1.attn, bf16[64,256]{1,0:T(8,128)(2,1)S(1)} %collective-permute-done.24.attn_other, bf16[128,16384]{1,0:T(8,128)(2,1)} %weight.3, ...), custom_call_target="tpu_custom_call" | custom-call | flops 134217728 | bytes 2097152 | tf_op jit(solution)/shard_map/shares_2/pallas_call | solution.py:479
  65.2 1.6 %collective-permute-start.26 = (bf16[64,1024]{1,0:T(8,128)(2,1)S(1)}, bf16[64,1024]{1,0:T(8,128)(2,1)S(1)}, u32[]{:S(2)}, u32[]{:S(2)}) collective-permute-start(bf16[64,1024]{1,0:T(8,128)(2,1)S(1)} %add_convert_fusion.9), channel_id=1, source_target_pairs={{0,4},{4,8},{8,12},{12,14},{14,10},{10,6},{6,2},{2,0},{1,3},{5,1},... | collective-permute-start | bytes 393224 | tf_op jit(solution)/shard_map/ppermute | solution.py:76
  66.7 2.6 %shares_4.1 = (f32[64,1024]{1,0:T(8,128)S(1)}, f32[64,1024]{1,0:T(8,128)S(1)}, f32[128,1024]{1,0:T(8,128)S(1)}, f32[64,1024]{1,0:T(8,128)S(1)}, f32[64,1024]{1,0...) custom-call(s32[1]{0:T(128)} %bitcast.16.core, s32[8]{0:T(128)S(1)} %stack.117.to, ...), custom_call_target="tpu_custom_call" | custom-call | flops 268435456 | bytes 4194304 | tf_op jit(solution)/shard_map/shares_4/pallas_call | solution.py:479
  80.2 4.3 %collective-permute-done.28 = bf16[64,1024]{1,0:T(8,128)(2,1)S(1)} collective-permute-done((bf16[64,1024]{1,0:T(8,128)(2,1)S(1)}, bf16[64,1024]{1,0:T(8,128)(2,1)S(1)}, u32[]{:S(2)}, u32[]{:S(2)}) %collective-permute-start.28) | collective-permute-done | bytes 131104 | tf_op jit(solution)/shard_map/ppermute | solution.py:76
  86.6 6.7 %collective-permute-done.36.refs_1_ = bf16[128,1024]{1,0:T(8,128)(2,1)S(1)} collective-permute-done((bf16[128,1024]{1,0:T(8,128)(2,1)S(1)}, bf16[128,1024]{1,0:T(8,128)(2,1)S(1)}, u32[]{:S(2)}, u32[]{:S(2)}) %collective-permute-start.36) | collective-permute-done | bytes 262176 | tf_op jit(solution)/shard_map/ppermute | solution.py:76
  94.5 1.6 %collective-permute-start.39 = (bf16[128,1024]{1,0:T(8,128)(2,1)S(1)}, bf16[128,1024]{1,0:T(8,128)(2,1)S(1)}, u32[]{:S(2)}, u32[]{:S(2)}) collective-permute-start(bf16[128,1024]{1,0:T(8,128)(2,1)S(1)} %collective-permute-done.37.refs_2_), channel_id=1, source_target_pairs={{0,4},{4,8},{8,12},{12,14},{14,10},{10,6},{6,2},{2,0},{1,3},{5,1},... | collective-permute-start | bytes 786440 | tf_op jit(solution)/shard_map/ppermute | solution.py:76
  96.2 3.5 %collective-permute-done.38.refs_3_ = bf16[128,1024]{1,0:T(8,128)(2,1)S(1)} collective-permute-done((bf16[128,1024]{1,0:T(8,128)(2,1)S(1)}, bf16[128,1024]{1,0:T(8,128)(2,1)S(1)}, u32[]{:S(2)}, u32[]{:S(2)}) %collective-permute-start.38) | collective-permute-done | bytes 262176 | tf_op jit(solution)/shard_map/ppermute | solution.py:76
  103.7 2.4 %collective-permute-done.40.refs_5_ = bf16[128,1024]{1,0:T(8,128)(2,1)S(1)} collective-permute-done((bf16[128,1024]{1,0:T(8,128)(2,1)S(1)}, bf16[128,1024]{1,0:T(8,128)(2,1)S(1)}, u32[]{:S(2)}, u32[]{:S(2)}) %collective-permute-start.40) | collective-permute-done | bytes 262176 | tf_op jit(solution)/shard_map/ppermute | solution.py:76
  108.9 3.6 %collective-permute-done.42.refs_7_ = bf16[128,1024]{1,0:T(8,128)(2,1)S(1)} collective-permute-done((bf16[128,1024]{1,0:T(8,128)(2,1)S(1)}, bf16[128,1024]{1,0:T(8,128)(2,1)S(1)}, u32[]{:S(2)}, u32[]{:S(2)}) %collective-permute-start.42) | collective-permute-done | bytes 262176 | tf_op jit(solution)/shard_map/ppermute | solution.py:76
  114.0 3.6 %final_norm.1 = bf16[128,16384]{1,0:T(8,128)(2,1)} custom-call(s32[16]{0:T(128)S(1)} %stack.108.ids, bf16[128,1024]{1,0:T(8,128)(2,1)S(1)} %pad_maximum_fusion.1.refs_0_, bf16[128,1024]{1,0:T(8,128)(2,1)S(1)} %collective-permute-done.36.refs_1_, bf16[128,1024]{1,0:T(8,128)(2,1)S(1)} %collective-permute-done.37.refs_2_, ...), custom_call_target="tpu_custom_call" | custom-call | flops 16777216 | bytes 12582912 | tf_op jit(solution)/shard_map/final_norm/pallas_call | solution.py:521
  (121 shorter events, 45.4 us)
Async XLA Ops:
  0.0 25.1 %collective-permute-start.8 = (bf16[128,16384]{1,0:T(8,128)(2,1)}, bf16[128,16384]{1,0:T(8,128)(2,1)}, u32[]{:S(2)}, u32[]{:S(2)}) collective-permute-start(bf16[128,16384]{1,0:T(8,128)(2,1)} %weight.3), channel_id=1, source_target_pairs={{0,1},{1,0},{2,3},{3,2},{4,5},{5,4},{6,7},{7,6},{8,9},{9,8},{10,11... | collective-permute-start | bytes 12582920 | tf_op jit(solution)/shard_map/ppermute | solution.py:76
  0.5 8.6 %collective-permute-start.2 = (bf16[128,1024]{1,0:T(8,128)(2,1)}, bf16[128,1024]{1,0:T(8,128)(2,1)S(1)}, u32[]{:S(2)}, u32[]{:S(2)}) collective-permute-start(bf16[128,1024]{1,0:T(8,128)(2,1)} %refs_0_), channel_id=1, source_target_pairs={{0,4},{4,8},{8,12},{12,14},{14,10},{10,6},{6,2},{2,0},{1,3},{5,1},... | collective-permute-start | bytes 786440 | tf_op jit(solution)/shard_map/ppermute | solution.py:76
  3.0 9.2 %collective-permute-start.3 = (bf16[128,1024]{1,0:T(8,128)(2,1)}, bf16[128,1024]{1,0:T(8,128)(2,1)S(1)}, u32[]{:S(2)}, u32[]{:S(2)}) collective-permute-start(bf16[128,1024]{1,0:T(8,128)(2,1)} %refs_0_), channel_id=1, source_target_pairs={{0,3},{4,1},{8,5},{12,9},{14,13},{10,15},{6,11},{2,7},{1,4},{5,8},... | collective-permute-start | bytes 786440 | tf_op jit(solution)/shard_map/ppermute | solution.py:76
  4.4 20.8 %collective-permute-start.10 = (bf16[128,1024]{1,0:T(8,128)(2,1)}, bf16[128,1024]{1,0:T(8,128)(2,1)S(1)}, u32[]{:S(2)}, u32[]{:S(2)}) collective-permute-start(bf16[128,1024]{1,0:T(8,128)(2,1)} %refs_0_), channel_id=1, source_target_pairs={{0,1},{1,0},{2,3},{3,2},{4,5},{5,4},{6,7},{7,6},{8,9},{9,8},{10,11... | collective-permute-start | bytes 786440 | tf_op jit(solution)/shard_map/ppermute | solution.py:76
  9.0 7.0 %collective-permute-start.4 = (bf16[128,1024]{1,0:T(8,128)(2,1)S(1)}, bf16[128,1024]{1,0:T(8,128)(2,1)S(1)}, u32[]{:S(2)}, u32[]{:S(2)}) collective-permute-start(bf16[128,1024]{1,0:T(8,128)(2,1)S(1)} %collective-permute-done.2.refs_1_), channel_id=1, source_target_pairs={{0,4},{4,8},{8,12},{12,14},{14,10},{10,6},{6,2},{2,0},{1,3},{5,1},... | collective-permute-start | bytes 786440 | tf_op jit(solution)/shard_map/ppermute | solution.py:76
  11.4 6.8 %collective-permute-start = (bf16[2,64,1024]{2,1,0:T(8,128)(2,1)S(1)}, bf16[2,64,1024]{2,1,0:T(8,128)(2,1)S(1)}, u32[]{:S(2)}, u32[]{:S(2)}) collective-permute-start(bf16[2,64,1024]{2,1,0:T(8,128)(2,1)S(1)} %pad_maximum_fusion), channel_id=1, source_target_pairs={{0,1},{1,0},{2,3},{3,2},{4,5},{5,4},{6,7},{7,6},{8,9},{9,8},{10,11... | collective-permute-start | bytes 786440 | tf_op jit(solution)/shard_map/ppermute | solution.py:76
  12.3 7.4 %collective-permute-start.5 = (bf16[128,1024]{1,0:T(8,128)(2,1)S(1)}, bf16[128,1024]{1,0:T(8,128)(2,1)S(1)}, u32[]{:S(2)}, u32[]{:S(2)}) collective-permute-start(bf16[128,1024]{1,0:T(8,128)(2,1)S(1)} %collective-permute-done.3.refs_2_), channel_id=1, source_target_pairs={{0,4},{4,8},{8,12},{12,14},{14,10},{10,6},{6,2},{2,0},{1,3},{5,1},... | collective-permute-start | bytes 786440 | tf_op jit(solution)/shard_map/ppermute | solution.py:76
  16.0 9.1 %collective-permute-start.6 = (bf16[128,1024]{1,0:T(8,128)(2,1)S(1)}, bf16[128,1024]{1,0:T(8,128)(2,1)S(1)}, u32[]{:S(2)}, u32[]{:S(2)}) collective-permute-start(bf16[128,1024]{1,0:T(8,128)(2,1)S(1)} %collective-permute-done.4.refs_3_), channel_id=1, source_target_pairs={{0,4},{4,8},{8,12},{12,14},{14,10},{10,6},{6,2},{2,0},{1,3},{5,1},... | collective-permute-start | bytes 786440 | tf_op jit(solution)/shard_map/ppermute | solution.py:76
  19.3 11.9 %collective-permute-start.1 = (bf16[4,2,2,64,128]{4,3,2,1,0:T(8,128)(2,1)S(1)}, bf16[4,2,2,64,128]{4,3,2,1,0:T(8,128)(2,1)S(1)}, u32[]{:S(2)}, u32[]{:S(2)}) collective-permute-start(bf16[4,2,2,64,128]{4,3,2,1,0:T(8,128)(2,1)S(1)} %get-tuple-element.28), channel_id=1, source_target_pairs={{0,2},{1,3},{2,0},{3,1},{4,6},{5,7},{6,4},{7,5},{8,10},{9,11},{10,... | collective-permute-start | bytes 786440 | tf_op jit(solution)/shard_map/ppermute | solution.py:76
  19.7 11.9 %collective-permute-start.11 = (bf16[128,1024]{1,0:T(8,128)(2,1)S(1)}, bf16[128,1024]{1,0:T(8,128)(2,1)S(1)}, u32[]{:S(2)}, u32[]{:S(2)}) collective-permute-start(bf16[128,1024]{1,0:T(8,128)(2,1)S(1)} %collective-permute-done.2.refs_1_), channel_id=1, source_target_pairs={{0,1},{1,0},{2,3},{3,2},{4,5},{5,4},{6,7},{7,6},{8,9},{9,8},{10,11... | collective-permute-start | bytes 786440 | tf_op jit(solution)/shard_map/ppermute | solution.py:76
  25.1 6.7 %collective-permute-start.12 = (bf16[128,1024]{1,0:T(8,128)(2,1)S(1)}, bf16[128,1024]{1,0:T(8,128)(2,1)S(1)}, u32[]{:S(2)}, u32[]{:S(2)}) collective-permute-start(bf16[128,1024]{1,0:T(8,128)(2,1)S(1)} %collective-permute-done.3.refs_2_), channel_id=1, source_target_pairs={{0,1},{1,0},{2,3},{3,2},{4,5},{5,4},{6,7},{7,6},{8,9},{9,8},{10,11... | collective-permute-start | bytes 786440 | tf_op jit(solution)/shard_map/ppermute | solution.py:76
  25.1 7.0 %collective-permute-start.7 = (bf16[128,1024]{1,0:T(8,128)(2,1)S(1)}, bf16[128,1024]{1,0:T(8,128)(2,1)}, u32[]{:S(2)}, u32[]{:S(2)}) collective-permute-start(bf16[128,1024]{1,0:T(8,128)(2,1)S(1)} %collective-permute-done.5.refs_4_), channel_id=1, source_target_pairs={{0,4},{4,8},{8,12},{12,14},{14,10},{10,6},{6,2},{2,0},{1,3},{5,1},... | collective-permute-start | bytes 786440 | tf_op jit(solution)/shard_map/ppermute | solution.py:76
  25.1 9.3 %collective-permute-start.9 = (bf16[128,1024]{1,0:T(8,128)(2,1)S(1)}, bf16[128,1024]{1,0:T(8,128)(2,1)}, u32[]{:S(2)}, u32[]{:S(2)}) collective-permute-start(bf16[128,1024]{1,0:T(8,128)(2,1)S(1)} %collective-permute-done.6.refs_5_), channel_id=1, source_target_pairs={{0,4},{4,8},{8,12},{12,14},{14,10},{10,6},{6,2},{2,0},{1,3},{5,1},... | collective-permute-start | bytes 786440 | tf_op jit(solution)/shard_map/ppermute | solution.py:76
  31.8 7.7 %collective-permute-start.15 = (bf16[128,1024]{1,0:T(8,128)(2,1)S(1)}, bf16[128,1024]{1,0:T(8,128)(2,1)S(1)}, u32[]{:S(2)}, u32[]{:S(2)}) collective-permute-start(bf16[128,1024]{1,0:T(8,128)(2,1)S(1)} %collective-permute-done.6.refs_5_), channel_id=1, source_target_pairs={{0,1},{1,0},{2,3},{3,2},{4,5},{5,4},{6,7},{7,6},{8,9},{9,8},{10,11... | collective-permute-start | bytes 786440 | tf_op jit(solution)/shard_map/ppermute | solution.py:76
  32.1 7.4 %collective-permute-start.16 = (bf16[128,1024]{1,0:T(8,128)(2,1)}, bf16[128,1024]{1,0:T(8,128)(2,1)S(1)}, u32[]{:S(2)}, u32[]{:S(2)}) collective-permute-start(bf16[128,1024]{1,0:T(8,128)(2,1)} %collective-permute-done.7.refs_6_), channel_id=1, source_target_pairs={{0,1},{1,0},{2,3},{3,2},{4,5},{5,4},{6,7},{7,6},{8,9},{9,8},{10,11... | collective-permute-start | bytes 786440 | tf_op jit(solution)/shard_map/ppermute | solution.py:76
  35.8 14.0 %collective-permute-start.21 = (bf16[2,2,2,64,128]{4,3,2,1,0:T(8,128)(2,1)}, bf16[2,2,2,64,128]{4,3,2,1,0:T(8,128)(2,1)S(1)}, u32[]{:S(2)}, u32[]{:S(2)}) collective-permute-start(bf16[2,2,2,64,128]{4,3,2,1,0:T(8,128)(2,1)} %pad_maximum_fusion.2), channel_id=1, source_target_pairs={{0,4},{1,5},{2,6},{3,7},{4,0},{5,1},{6,2},{7,3},{8,12},{9,13},{10,... | collective-permute-start | bytes 393224 | tf_op jit(solution)/shard_map/ppermute | solution.py:76
  37.3 12.5 %collective-permute-start.22 = (bf16[2,2,2,64,128]{4,3,2,1,0:T(8,128)(2,1)}, bf16[2,2,2,64,128]{4,3,2,1,0:T(8,128)(2,1)S(1)}, u32[]{:S(2)}, u32[]{:S(2)}) collective-permute-start(bf16[2,2,2,64,128]{4,3,2,1,0:T(8,128)(2,1)} %pad_maximum_fusion.3), channel_id=1, source_target_pairs={{0,8},{1,9},{2,10},{3,11},{4,12},{5,13},{6,14},{7,15},{8,0},{9,1},... | collective-permute-start | bytes 393224 | tf_op jit(solution)/shard_map/ppermute | solution.py:76
  43.8 7.1 %collective-permute-start.23 = (bf16[2,2,2,64,128]{4,3,2,1,0:T(8,128)(2,1)S(1)}, bf16[2,2,2,64,128]{4,3,2,1,0:T(8,128)(2,1)S(1)}, u32[]{:S(2)}, u32[]{:S(2)}) collective-permute-start(bf16[2,2,2,64,128]{4,3,2,1,0:T(8,128)(2,1)S(1)} %pad_maximum_fusion.4), channel_id=1, source_target_pairs={{0,12},{1,13},{2,14},{3,15},{4,8},{5,9},{6,10},{7,11},{8,4},{9,5},... | collective-permute-start | bytes 393224 | tf_op jit(solution)/shard_map/ppermute | solution.py:76
  61.6 9.3 %collective-permute-start.29 = (bf16[128,1024]{1,0:T(8,128)(2,1)S(1)}, bf16[128,1024]{1,0:T(8,128)(2,1)S(1)}, u32[]{:S(2)}, u32[]{:S(2)}) collective-permute-start(bf16[128,1024]{1,0:T(8,128)(2,1)S(1)} %get-tuple-element.43), channel_id=1, source_target_pairs={{0,4},{4,8},{8,12},{12,14},{14,10},{10,6},{6,2},{2,0},{1,3},{5,1},... | collective-permute-start | bytes 786440 | tf_op jit(solution)/shard_map/ppermute | solution.py:76
  65.2 7.2 %collective-permute-start.26 = (bf16[64,1024]{1,0:T(8,128)(2,1)S(1)}, bf16[64,1024]{1,0:T(8,128)(2,1)S(1)}, u32[]{:S(2)}, u32[]{:S(2)}) collective-permute-start(bf16[64,1024]{1,0:T(8,128)(2,1)S(1)} %add_convert_fusion.9), channel_id=1, source_target_pairs={{0,4},{4,8},{8,12},{12,14},{14,10},{10,6},{6,2},{2,0},{1,3},{5,1},... | collective-permute-start | bytes 393224 | tf_op jit(solution)/shard_map/ppermute | solution.py:76
  77.4 7.1 %collective-permute-start.31 = (bf16[128,1024]{1,0:T(8,128)(2,1)S(1)}, bf16[128,1024]{1,0:T(8,128)(2,1)S(1)}, u32[]{:S(2)}, u32[]{:S(2)}) collective-permute-start(bf16[128,1024]{1,0:T(8,128)(2,1)S(1)} %add_convert_fusion), channel_id=1, source_target_pairs={{0,5},{4,9},{8,13},{12,15},{14,11},{10,7},{6,3},{2,1},{1,2},{5,0},... | collective-permute-start | bytes 786440 | tf_op jit(solution)/shard_map/ppermute | solution.py:76
  84.7 8.6 %collective-permute-start.36 = (bf16[128,1024]{1,0:T(8,128)(2,1)S(1)}, bf16[128,1024]{1,0:T(8,128)(2,1)S(1)}, u32[]{:S(2)}, u32[]{:S(2)}) collective-permute-start(bf16[128,1024]{1,0:T(8,128)(2,1)S(1)} %pad_maximum_fusion.1.refs_0_), channel_id=1, source_target_pairs={{0,4},{4,8},{8,12},{12,14},{14,10},{10,6},{6,2},{2,0},{1,3},{5,1},... | collective-permute-start | bytes 786440 | tf_op jit(solution)/shard_map/ppermute | solution.py:76
  86.0 8.5 %collective-permute-start.37 = (bf16[128,1024]{1,0:T(8,128)(2,1)S(1)}, bf16[128,1024]{1,0:T(8,128)(2,1)S(1)}, u32[]{:S(2)}, u32[]{:S(2)}) collective-permute-start(bf16[128,1024]{1,0:T(8,128)(2,1)S(1)} %pad_maximum_fusion.1.refs_0_), channel_id=1, source_target_pairs={{0,3},{4,1},{8,5},{12,9},{14,13},{10,15},{6,11},{2,7},{1,4},{5,8},... | collective-permute-start | bytes 786440 | tf_op jit(solution)/shard_map/ppermute | solution.py:76
  94.5 8.0 %collective-permute-start.39 = (bf16[128,1024]{1,0:T(8,128)(2,1)S(1)}, bf16[128,1024]{1,0:T(8,128)(2,1)S(1)}, u32[]{:S(2)}, u32[]{:S(2)}) collective-permute-start(bf16[128,1024]{1,0:T(8,128)(2,1)S(1)} %collective-permute-done.37.refs_2_), channel_id=1, source_target_pairs={{0,4},{4,8},{8,12},{12,14},{14,10},{10,6},{6,2},{2,0},{1,3},{5,1},... | collective-permute-start | bytes 786440 | tf_op jit(solution)/shard_map/ppermute | solution.py:76
  (30 other events, 209.3 us)

commit v6 on v5

--- a/solution.py
+++ b/solution.py
@@ -84,28 +84,21 @@
     return lax.optimization_barrier((array, others))[0]
 
 
-def ring_gather(parts, own, ready=None):
-    streams, crossed = list(parts), own
-    came = [(own,)]
+def ring_gather(own, ready=None, direct=False):
+    straight, swapped = own, send(own, SWAP)
+    crossed = own if direct else swapped
+    mine, theirs = [own], [swapped]
     for step in range(1, 5):
         if step == 4 and ready is not None:
-            streams = after(streams, ready)
-        streams = [send(part, ONWARD) for part in streams]
-        came.append(tuple(streams))
+            straight = after(straight, ready)
+        straight = send(straight, ONWARD)
+        mine.append(straight)
+        theirs.append(send(straight, SWAP))
         if step < 4:
-            crossed = send(crossed, ENTER if step == 1 else ONWARD)
-            came.append((crossed,))
-    return came
-
-
-def both_cores(came):
-    mine = flat(came)
-    return mine + [send(piece, SWAP) for piece in mine]
-
-
-def block_refs(refs, parts):
-    counts = (1,) + (parts, 1) * 3 + (parts,)
-    return grouped(refs, counts * 2)
+            crossed = send(crossed, ENTER if direct and step == 1 else ONWARD)
+            mine.append(crossed)
+            theirs.append(send(crossed, SWAP))
+    return mine, theirs
 
 
 def gathered_ids(rank):
@@ -131,14 +124,12 @@
     ).astype(jnp.int32)
 
 
-def ring_sum(shares, more_shares):
+def ring_sum(shares):
     streams, crossed = shares[4, 0], shares[3, 1][0]
     for step in range(1, 5):
         streams = [send(part, ONWARD) for part in streams]
         if step < 4:
             crossed = send(crossed, LEAVE if step == 3 else ONWARD)
-        if step == 1:
-            shares.update(more_shares(streams[0]))
         if step < 4:
             streams = [add_share(part, share) for part, share in zip(streams, shares[4 - step, 0])]
         if step < 3:
@@ -155,14 +146,33 @@
     give = jnp.stack(
         [lax.dynamic_index_in_dim(c, 1 - core, 0, keepdims=False) for c in (key_cache, value_cache)]
     )
-    return pack(rank_id, key_cache, value_cache, send(give, SWAP))
-
-
-def move_cache(parts, *when):
+    theirs = send(give, SWAP)
+    return pack(rank_id, key_cache, value_cache, theirs)
+
+
+def move_cache(parts):
     keep, give = parts
     came = send(give, xor(2))
-    pieces = [jnp.stack([keep[m], came[m]]) for m in range(1, 4)]
-    return [keep, came] + [send(piece, xor(4 * m)) for m, piece in zip(range(1, 4), pieces)]
+    pieces = stack_pieces(keep, came)
+    return [keep, came] + [send(piece, xor(4 * m)) for m, piece in zip(range(1, 4), pieces)], pieces
+
+
+def stack_kernel(keep, came, *outs):
+    for m, out in enumerate(outs, 1):
+        out[0] = keep[m]
+        out[1] = came[m]
+
+
+def stack_pieces(keep, came):
+    return pl.pallas_call(
+        stack_kernel,
+        out_shape=[jax.ShapeDtypeStruct((2,) + keep.shape[1:], keep.dtype)] * 3,
+        in_specs=[VMEM] * 2,
+        out_specs=[VMEM] * 3,
+        compiler_params=pltpu.CompilerParams(vmem_limit_bytes=8 * MIB),
+        cost_estimate=pl.CostEstimate(flops=0, bytes_accessed=MIB, transcendentals=0),
+        name="stack_cache",
+    )(keep, came)
 
 
 def pack_kernel(rank, keys, values, theirs, keep, give, sems):
@@ -198,26 +208,13 @@
     )(rank_id, in_hbm(key_cache), in_hbm(value_cache), theirs)
 
 
-def flat(blocks):
-    return [piece for block in blocks for piece in block]
-
-
-def grouped(refs, counts):
-    blocks, at = [], 0
-    for count in counts:
-        blocks.append(refs[at : at + count])
-        at += count
-    return blocks
-
-
 def lanes(block, j):
-    parts = [piece[:, 128 * j : 128 * j + 128] for piece in block]
-    return (parts[0] if len(parts) == 1 else jnp.concatenate(parts, axis=0)).astype(jnp.float32)
+    return block[:, 128 * j : 128 * j + 128].astype(jnp.float32)
 
 
 def square_sums(blocks, total):
     for block in blocks:
-        for j in range(block[0].shape[1] // 128):
+        for j in range(block.shape[1] // 128):
             v = lanes(block, j)
             total = total + v * v
     return total
@@ -232,7 +229,7 @@
     return jnp.concatenate(
         [
             (lanes(block, j) * factors * gain_row[:, 128 * j : 128 * j + 128]).astype(jnp.bfloat16)
-            for j in range(block[0].shape[1] // 128)
+            for j in range(block.shape[1] // 128)
         ],
         axis=1,
     )
@@ -242,15 +239,18 @@
     return pltpu.with_memory_space_constraint(array, pltpu.HBM)
 
 
-def load_kernel(ids, wq, wkv, out, sems):
-    count, width, _ = out.shape
+def load_kernel(axis, blocks, first, second, out, sems):
+    count, width = out.shape[0], out.shape[1 + axis]
     copies = []
     for i in range(count):
-        rows = pl.ds(pl.multiple_of(ids[i] * width, width), width)
-        for j, weight in enumerate((wq, wkv)):
+        block = pl.ds(pl.multiple_of(blocks[i] * width, width), width)
+        for j, weight in enumerate((first, second)):
+            half = pl.ds(j * HD, HD)
             copies.append(
                 pltpu.make_async_copy(
-                    weight.at[rows, :], out.at[i, :, pl.ds(j * HD, HD)], sems.at[j, i]
+                    weight.at[:, block] if axis else weight.at[block, :],
+                    out.at[i, half, :] if axis else out.at[i, :, half],
+                    sems.at[j, i],
                 )
             )
             copies[-1].start()
@@ -258,27 +258,30 @@
         copy.wait()
 
 
-def load_weights(ids, wq, wkv, width):
+def load_weights(blocks, first, second, width, axis):
+    count = blocks.shape[0]
+    shape = (count, 2 * HD, width) if axis else (count, width, 2 * HD)
     return pl.pallas_call(
-        load_kernel,
-        out_shape=jax.ShapeDtypeStruct((16, width, 2 * HD), jnp.bfloat16),
+        functools.partial(load_kernel, axis),
+        out_shape=jax.ShapeDtypeStruct(shape, jnp.bfloat16),
         in_specs=[SMEM] + [HBM] * 2,
         out_specs=VMEM,
-        scratch_shapes=[pltpu.SemaphoreType.DMA((2, 16))],
+        scratch_shapes=[pltpu.SemaphoreType.DMA((2, count))],
         compiler_params=pltpu.CompilerParams(vmem_limit_bytes=16 * MIB),
-        cost_estimate=pl.CostEstimate(flops=0, bytes_accessed=16 * MIB, transcendentals=0),
-        name="load_weights",
-    )(ids, in_hbm(wq), in_hbm(wkv))
+        cost_estimate=pl.CostEstimate(
+            flops=0, bytes_accessed=8 * count * HD * width, transcendentals=0
+        ),
+        name="load_weights_%d" % axis,
+    )(blocks, first, second)
 
 
 def all_factors(blocks):
     total = square_sums(blocks, jnp.zeros((TOKENS, 128), jnp.float32))
-    return row_factors(total, 16 * blocks[0][0].shape[1])
-
-
-def project_kernel(parts, ids, *refs):
-    count = 8 * (parts + 1)
-    blocks, refs = block_refs(refs[:count], parts), refs[count:]
+    return row_factors(total, 16 * blocks[0].shape[1])
+
+
+def project_kernel(ids, *refs):
+    blocks, refs = refs[:16], refs[16:]
     gain, weights, cosine, sine, kv_cos, kv_sin = refs[:6]
     q_keep, q_send, fresh = refs[6:]
     factors = all_factors(blocks)
@@ -297,7 +300,7 @@
 
 def project(ids, arrays, gain, weights, tables):
     return pl.pallas_call(
-        functools.partial(project_kernel, len(arrays) // 8 - 1),
+        project_kernel,
         out_shape=[jax.ShapeDtypeStruct((SPAN, HD), jnp.bfloat16)] * 2
         + [jax.ShapeDtypeStruct((TOKENS, HD), jnp.bfloat16)],
         in_specs=[SMEM] + [VMEM] * (len(arrays) + 6),
@@ -310,21 +313,6 @@
     )(ids, *arrays, gain, weights, *tables)
 
 
-def share_copies(to, first, weight, weight_other, out, sems):
-    count, _, width = out.shape
-    copies = []
-    for i in range(count):
-        columns = pl.ds(pl.multiple_of(to[first + i] * width, width), width)
-        pair = [
-            pltpu.make_async_copy(part.at[:, columns], out.at[i, pl.ds(j * HD, HD), :], sems.at[j, i])
-            for j, part in enumerate((weight, weight_other))
-        ]
-        for copy in pair:
-            copy.start()
-        copies.append(pair)
-    return copies
-
-
 def cache_rows(cache, which):
     keep, came, rest = cache[0], cache[1], cache[2:]
     groups = [part[0, c, which] for part in (keep, came) for c in range(2)]
@@ -335,9 +323,8 @@
 CONTRACT = (((1,), (1,)), ((), ()))
 
 
-def scores_kernel(info, to, q, q_other, *refs):
-    cache, weight, weight_other, scores, weights, sems = refs[:5], *refs[5:]
-    copies = share_copies(to, 0, weight, weight_other, weights, sems)
+def scores_kernel(info, q, q_other, *refs):
+    cache, scores = refs[:5], refs[5]
     core, rank = info[SEQS], info[SEQS + 1]
     queries = jnp.concatenate([q[...], q_other[...]], axis=0)
     old = lax.dot_general(
@@ -346,28 +333,18 @@
     lane = lax.broadcasted_iota(jnp.int32, old.shape, 1)
     position = (rank ^ (lane // CTX_DEV)) * CTX_DEV + lane % CTX_DEV
     scores[...] = jnp.where(position < info[core], old * HD ** (-0.5), -1e30)
-    for pair in copies:
-        for copy in pair:
-            copy.wait()
-
-
-def cache_scores(info, to, q, q_other, cache, weight, weight_other, ahead):
-    width = weight.shape[1] // 16
+
+
+def cache_scores(info, q, q_other, cache):
     return pl.pallas_call(
         scores_kernel,
-        out_shape=[
-            jax.ShapeDtypeStruct((TOKENS, 16 * CTX_DEV), jnp.float32),
-            jax.ShapeDtypeStruct((ahead, 2 * HD, width), jnp.bfloat16),
-        ],
-        in_specs=[SMEM] * 2 + [VMEM] * 7 + [HBM] * 2,
-        out_specs=[VMEM] * 2,
-        scratch_shapes=[pltpu.SemaphoreType.DMA((2, ahead))],
+        out_shape=jax.ShapeDtypeStruct((TOKENS, 16 * CTX_DEV), jnp.float32),
+        in_specs=[SMEM] + [VMEM] * 7,
+        out_specs=VMEM,
         compiler_params=pltpu.CompilerParams(vmem_limit_bytes=16 * MIB),
-        cost_estimate=pl.CostEstimate(
-            flops=32 * MIB, bytes_accessed=3 * MIB, transcendentals=0
-        ),
+        cost_estimate=pl.CostEstimate(flops=32 * MIB, bytes_accessed=MIB, transcendentals=0),
         name="cache_scores",
-    )(info, to, q, q_other, *cache, in_hbm(weight), weight_other)
+    )(info, q, q_other, *cache)
 
 
 def attend_kernel(info, q, q_other, fresh_own, fresh_other, scores, *refs):
@@ -440,65 +417,33 @@
         out[...] = value[i * rows : (i + 1) * rows].astype(out.dtype)
 
 
-def first_shares_kernel(shares, core, attn, attn_other, weights, *outs):
+def shares_kernel(first, last, core, attn, attn_other, weights, *outs):
     rows = both_heads(core, attn, attn_other)
-    for i, refs in enumerate(share_lists(shares, outs).values()):
-        write_share(jnp.dot(rows, weights[i], preferred_element_type=jnp.float32), refs)
-
-
-def first_shares(shares, core, attn, attn_other, weights):
-    count, _, width = weights.shape
-    out_shape = share_shapes(shares, width, jnp.bfloat16)
+    for i, refs in enumerate(share_lists(SHARES[first:last], outs).values()):
+        write_share(jnp.dot(rows, weights[first + i], preferred_element_type=jnp.float32), refs)
+
+
+def shares_of(core, attn, attn_other, weights, first, last, dtype=jnp.float32):
+    width = weights.shape[2]
+    out_shape = share_shapes(SHARES[first:last], width, dtype)
     arrays = pl.pallas_call(
-        functools.partial(first_shares_kernel, shares),
+        functools.partial(shares_kernel, first, last),
         out_shape=out_shape,
         in_specs=[SMEM] + [VMEM] * 3,
         out_specs=[VMEM] * len(out_shape),
         compiler_params=pltpu.CompilerParams(vmem_limit_bytes=16 * MIB),
         cost_estimate=pl.CostEstimate(
-            flops=2 * TOKENS * weights.size, bytes_accessed=count * MIB, transcendentals=0
-        ),
-        name="first_shares",
+            flops=4 * TOKENS * HD * width * (last - first),
+            bytes_accessed=(last - first) * MIB,
+            transcendentals=0,
+        ),
+        name="shares_%d" % first,
     )(core, attn, attn_other, weights)
-    return share_lists(shares, arrays)
-
-
-def more_shares_kernel(first, last, core, to, attn, attn_other, weight, weight_other, *refs):
-    outs, (weights, sems) = refs[:-2], refs[-2:]
-    copies = share_copies(to, first, weight, weight_other, weights, sems)
-    rows = both_heads(core, attn, attn_other)
-    for i, out in enumerate(share_lists(SHARES[first:last], outs).values()):
-        for copy in copies[i]:
-            copy.wait()
-        write_share(jnp.dot(rows, weights[i], preferred_element_type=jnp.float32), out)
-
-
-def more_shares(core, to, attn, attn_other, weight, weight_other, first, last):
-    count, width = last - first, weight.shape[1] // 16
-    out_shape = share_shapes(SHARES[first:last], width, jnp.float32)
-    arrays = pl.pallas_call(
-        functools.partial(more_shares_kernel, first, last),
-        out_shape=out_shape,
-        in_specs=[SMEM] * 2 + [VMEM] * 2 + [HBM] * 2,
-        out_specs=[VMEM] * len(out_shape),
-        scratch_shapes=[
-            pltpu.VMEM((count, 2 * HD, width), jnp.bfloat16),
-            pltpu.SemaphoreType.DMA((2, count)),
-        ],
-        compiler_params=pltpu.CompilerParams(vmem_limit_bytes=16 * MIB),
-        cost_estimate=pl.CostEstimate(
-            flops=4 * TOKENS * HD * width * count,
-            bytes_accessed=count * MIB,
-            transcendentals=0,
-        ),
-        name="shares_%d" % first,
-    )(core, to, attn, attn_other, in_hbm(weight), weight_other)
     return share_lists(SHARES[first:last], arrays)
 
 
-def final_kernel(parts, ids, *refs):
-    count = 8 * (parts + 1)
-    blocks, refs = block_refs(refs[:count], parts), refs[count:]
+def final_kernel(ids, *refs):
+    blocks, refs = refs[:16], refs[16:]
     gain, out, staged, sems = refs
     width = staged.shape[2]
     factors = all_factors(blocks)
@@ -519,7 +464,7 @@
 def final_norm(ids, arrays, gain):
     width = arrays[0].shape[1]
     return pl.pallas_call(
-        functools.partial(final_kernel, len(arrays) // 8 - 1),
+        final_kernel,
         out_shape=jax.ShapeDtypeStruct((TOKENS, 16 * width), jnp.bfloat16),
         in_specs=[SMEM] + [VMEM] * (len(arrays) + 1),
         out_specs=HBM,
@@ -548,9 +493,9 @@
 
     weight_other = send(o_weight, SWAP)
     parts = split_cache(key_cache, value_cache, rank, rank_id)
-    came = ring_gather([residual], residual, weight_other)
-    weights = load_weights(ids, q_weight, kv_weight, width)
-    cache = move_cache(parts)
+    cache, pieces = move_cache(parts)
+    mine, theirs = ring_gather(residual, weight_other, direct=True)
+    weights = load_weights(ids, in_hbm(q_weight), in_hbm(kv_weight), width, 0)
 
     positions = (prefix[:, None] + jnp.arange(SPAN, dtype=jnp.int32)[None, :]).reshape(-1)
     cosine, sine = rope_tables(positions)
@@ -560,24 +505,20 @@
     tables = (cosine, sine, jnp.where(holds_keys, cosine, 1.0), jnp.where(holds_keys, sine, 0.0))
 
     gain = attn_gain.reshape(16, 1, width).astype(jnp.float32)
-    arrays = both_cores(came)
-    arrays[0] = after(arrays[0], cache[1])
-    q_keep, q_send, fresh = project(ids, arrays, gain, weights, tables)
+    mine[0] = after(mine[0], pieces)
+    q_keep, q_send, fresh = project(ids, mine + theirs, gain, weights, tables)
+    o_weights = load_weights(after(to, fresh), in_hbm(o_weight), weight_other, width, 1)
     q_other = send(q_send, SWAP)
     fresh_own = send(fresh, FRESH)
     fresh_other = send(jnp.where(core == 0, fresh_own[SPAN:], fresh_own[:SPAN]), SWAP)
-    scores, first_weights = cache_scores(
-        info, to, q_keep, q_other, cache, o_weight, weight_other, 2
-    )
+    scores = cache_scores(info, after(q_keep, o_weights), q_other, cache)
     attn = attend(info, q_keep, q_other, fresh_own, fresh_other, scores, cache)
     attn_other = send(attn, SWAP)
 
-    shares = first_shares(SHARES[:2], core_id, attn, attn_other, first_weights)
-    inputs = (attn, attn_other, o_weight, weight_other)
-    shares.update(more_shares(core_id, to, *inputs, 2, 4))
-    one_way, other_way = ring_sum(
-        shares, lambda came: more_shares(core_id, after(to, came), *inputs, 4, len(SHARES))
-    )
+    inputs = (core_id, attn, attn_other, o_weights)
+    shares = shares_of(*inputs, 0, 2, jnp.bfloat16)
+    shares.update(shares_of(*inputs, 2, len(SHARES)))
+    one_way, other_way = ring_sum(shares)
     hidden = []
     for h, rows in enumerate((slice(0, SPAN), slice(SPAN, TOKENS))):
         projected = shares[0, 0][h] + one_way[h].astype(jnp.float32)
@@ -585,10 +526,9 @@
         hidden.append((residual[rows].astype(jnp.float32) + projected).astype(jnp.bfloat16))
 
     hidden = jnp.concatenate(hidden, axis=0)
-    came = ring_gather([hidden], hidden)
-    arrays = both_cores(came)
+    mine, theirs = ring_gather(hidden)
     gain = ffn_gain.reshape(16, 1, width).astype(jnp.float32)
-    return final_norm(ids, arrays, gain)
+    return final_norm(ids, mine + theirs, gain)
 
 
 def per_device(

time: 118 us -> 120 us (1.017)
  waiting for transfers between devices: 43.3 us -> 57.6 us
  starting transfers between devices: 48.1 us -> 37.8 us
  Pallas kernels: 20.3 us -> 18.1 us
  local copies, waits for them, and re-layouts: 1.29 us -> 3.2 us
  other arithmetic: 3.87 us -> 2.49 us
    ppermute x51, waiting for transfers between devices: 43.3 us -> 57.6 us  [send(): return lax.ppermute(array, 'tp', pairs)]
    ppermute x51, starting transfers between devices: 48.1 us -> 37.8 us  [send(): return lax.ppermute(array, 'tp', pairs)]
    pallas_call x7 -> x8, Pallas kernels: 18.1 us -> 15.2 us  [the longest x2 7.03 us: load_weights(): pl.pallas_call(functools.partial(load_kernel, axis), out_shape=jax.ShapeD...]
    unnamed x6 -> x12, local copies, waits for them, and re-layouts: 0.02 us -> 1.96 us
    another operation x3 -> x0, other arithmetic: 1.35 us -> none  [move_cache(): pieces = [jnp.stack([keep[m], came[m]]) for m in range(1, 4)]]
  transfers between devices with their start and end apart: 51 -> 51, of which waited for: 17 -> 23; matrix products, arithmetic and copies ran while one was open for 4% -> 3% of each run, Pallas kernels for 13% -> 9%
where the time goes in v6:
time: 120 us
  waiting for transfers between devices  57.6 us (48%)
  starting transfers between devices  37.8 us (31%)
  Pallas kernels  18.1 us (15%)
  local copies, waits for them, and re-layouts  3.2 us (3%)
  other arithmetic  2.49 us (2%)
    ppermute x51, waiting for transfers between devices, send(): return lax.ppermute(array, 'tp', pairs)  57.6 us
    ppermute x51, starting transfers between devices, send(): return lax.ppermute(array, 'tp', pairs)  37.8 us
    pallas_call x2, Pallas kernels, load_weights(): pl.pallas_call(functools.partial(load_kernel, axis), out_shape=jax.ShapeD...  7.03 us
    pallas_call x1, Pallas kernels, final_norm(): pl.pallas_call(final_kernel, out_shape=jax.ShapeDtypeStruct((TOKENS, 16 *...  3.64 us
    pallas_call x1, Pallas kernels, project(): pl.pallas_call(project_kernel, out_shape=[jax.ShapeDtypeStruct((SPAN, HD)...  2.82 us
  transfers between devices with their start and end apart: 51, of which 23 were waited for; matrix products, arithmetic and copies ran while one was open for 3% of the time, Pallas kernels for 9%

profile of v6, /device:TPU:0, one launch (start us, length us, event | category | flops | bytes accessed | tf_op | source)
XLA Modules:
  0.0 119.8 jit_solution(12069661704324417065)
XLA Ops:
  0.5 2.6 %collective-permute-start.2 = (bf16[128,1024]{1,0:T(8,128)(2,1)}, bf16[128,1024]{1,0:T(8,128)(2,1)S(1)}, u32[]{:S(2)}, u32[]{:S(2)}) collective-permute-start(bf16[128,1024]{1,0:T(8,128)(2,1)} %refs_0_), channel_id=1, source_target_pairs={{0,4},{4,8},{8,12},{12,14},{14,10},{10,6},{6,2},{2,0},{1,3},{5,1},... | collective-permute-start | bytes 786440 | tf_op jit(solution)/shard_map/ppermute | solution.py:76
  4.4 4.7 %collective-permute-done.2.refs_1_ = bf16[128,1024]{1,0:T(8,128)(2,1)S(1)} collective-permute-done((bf16[128,1024]{1,0:T(8,128)(2,1)}, bf16[128,1024]{1,0:T(8,128)(2,1)S(1)}, u32[]{:S(2)}, u32[]{:S(2)}) %collective-permute-start.2) | collective-permute-done | bytes 262176 | tf_op jit(solution)/shard_map/ppermute | solution.py:76
  9.0 2.4 %collective-permute-start.4 = (bf16[128,1024]{1,0:T(8,128)(2,1)S(1)}, bf16[128,1024]{1,0:T(8,128)(2,1)S(1)}, u32[]{:S(2)}, u32[]{:S(2)}) collective-permute-start(bf16[128,1024]{1,0:T(8,128)(2,1)S(1)} %collective-permute-done.2.refs_1_), channel_id=1, source_target_pairs={{0,4},{4,8},{8,12},{12,14},{14,10},{10,6},{6,2},{2,0},{1,3},{5,1},... | collective-permute-start | bytes 786440 | tf_op jit(solution)/shard_map/ppermute | solution.py:76
  14.2 1.9 %collective-permute-done.4.refs_3_ = bf16[128,1024]{1,0:T(8,128)(2,1)S(1)} collective-permute-done((bf16[128,1024]{1,0:T(8,128)(2,1)S(1)}, bf16[128,1024]{1,0:T(8,128)(2,1)S(1)}, u32[]{:S(2)}, u32[]{:S(2)}) %collective-permute-start.4) | collective-permute-done | bytes 262176 | tf_op jit(solution)/shard_map/ppermute | solution.py:76
  17.8 1.8 %pack_cache.1 = (bf16[4,2,2,64,128]{4,3,2,1,0:T(8,128)(2,1)S(1)}, bf16[4,2,2,64,128]{4,3,2,1,0:T(8,128)(2,1)}) custom-call(s32[1]{0:T(128)} %bitcast.rank, bf16[2,64,1024]{2,1,0:T(8,128)(2,1)} %keys.1, bf16[2,64,1024]{2,1,0:T(8,128)(2,1)} %values.1, bf16[2,64,1024]{2,1,0:T(8,128)(2,1)S(1)} %collective-permute-done.theirs), custom_call_target="tpu_custom_call" | custom-call | bytes 1048576 | tf_op jit(solution)/shard_map/pack_cache/pallas_call | solution.py:199
  20.3 2.1 %collective-permute-done.6.refs_5_ = bf16[128,1024]{1,0:T(8,128)(2,1)S(1)} collective-permute-done((bf16[128,1024]{1,0:T(8,128)(2,1)S(1)}, bf16[128,1024]{1,0:T(8,128)(2,1)S(1)}, u32[]{:S(2)}, u32[]{:S(2)}) %collective-permute-start.6) | collective-permute-done | bytes 262176 | tf_op jit(solution)/shard_map/ppermute | solution.py:76
  22.4 1.8 %collective-permute-start.7 = (bf16[128,1024]{1,0:T(8,128)(2,1)S(1)}, bf16[128,1024]{1,0:T(8,128)(2,1)S(1)}, u32[]{:S(2)}, u32[]{:S(2)}) collective-permute-start(bf16[128,1024]{1,0:T(8,128)(2,1)S(1)} %collective-permute-done.5.refs_4_), channel_id=1, source_target_pairs={{0,4},{4,8},{8,12},{12,14},{14,10},{10,6},{6,2},{2,0},{1,3},{5,1},... | collective-permute-start | bytes 786440 | tf_op jit(solution)/shard_map/ppermute | solution.py:76
  27.4 4.2 %load_weights_0.1.refs_17_ = bf16[16,1024,256]{2,1,0:T(8,128)(2,1)S(1)} custom-call(s32[16]{0:T(128)S(1)} %stack.99.blocks.ids, bf16[16384,128]{1,0:T(8,128)(2,1)} %first.2, bf16[16384,128]{1,0:T(8,128)(2,1)} %second.1), custom_call_target="tpu_custom_call" | custom-call | bytes 16777216 | tf_op jit(solution)/shard_map/load_weights_0/pallas_call | solution.py:264
  36.7 2.8 %norm_project.1 = (bf16[64,128]{1,0:T(8,128)(2,1)S(1)}, bf16[64,128]{1,0:T(8,128)(2,1)S(1)}, bf16[128,128]{1,0:T(8,128)(2,1)S(1)}) custom-call(s32[16]{0:T(128)S(1)} %stack.99.blocks.ids, bf16[128,1024]{1,0:T(8,128)(2,1)S(1)} %copy-done, bf16[128,1024]{1,0:T(8,128)(2,1)S(1)} %collective-permute-done.2.refs_1_, ...), custom_call_target="tpu_custom_call" | custom-call | flops 1073741824 | bytes 12582912 | tf_op jit(solution)/shard_map/norm_project/pallas_call | solution.py:302
  40.2 4.6 %collective-permute-start.21 = (bf16[2,2,2,64,128]{4,3,2,1,0:T(8,128)(2,1)}, bf16[2,2,2,64,128]{4,3,2,1,0:T(8,128)(2,1)S(1)}, u32[]{:S(2)}, u32[]{:S(2)}) collective-permute-start(bf16[2,2,2,64,128]{4,3,2,1,0:T(8,128)(2,1)} %copy-done.3), channel_id=1, source_target_pairs={{0,4},{1,5},{2,6},{3,7},{4,0},{5,1},{6,2},{7,3},{8,12},{9,13},{10,... | collective-permute-start | bytes 393224 | tf_op jit(solution)/shard_map/ppermute | solution.py:76
  48.0 2.8 %load_weights_1.1.weights = bf16[8,256,1024]{2,1,0:T(8,128)(2,1)S(1)} custom-call(s32[8]{0:T(128)S(1)} %stack.109.blocks, bf16[128,16384]{1,0:T(8,128)(2,1)} %first.3, bf16[128,16384]{1,0:T(8,128)(2,1)} %collective-permute-done.8.second), custom_call_target="tpu_custom_call" | custom-call | bytes 8388608 | tf_op jit(solution)/shard_map/load_weights_1/pallas_call | solution.py:264
  50.9 6.9 %collective-permute-done.22.refs_3_ = bf16[2,2,2,64,128]{4,3,2,1,0:T(8,128)(2,1)S(1)} collective-permute-done((bf16[2,2,2,64,128]{4,3,2,1,0:T(8,128)(2,1)}, bf16[2,2,2,64,128]{4,3,2,1,0:T(8,128)(2,1)S(1)}, u32[]{:S(2)}, u32[]{:S(2)}) %collective-permute-start.22) | collective-permute-done | bytes 131104 | tf_op jit(solution)/shard_map/ppermute | solution.py:76
  61.3 2.0 %collective-permute-start.32 = (bf16[64,1024]{1,0:T(8,128)(2,1)S(1)}, bf16[64,1024]{1,0:T(8,128)(2,1)S(1)}, u32[]{:S(2)}, u32[]{:S(2)}) collective-permute-start(bf16[64,1024]{1,0:T(8,128)(2,1)S(1)} %get-tuple-element.51), channel_id=1, source_target_pairs={{0,4},{4,8},{8,12},{12,14},{14,10},{10,6},{6,2},{2,0},{1,3},{5,1},... | collective-permute-start | bytes 393224 | tf_op jit(solution)/shard_map/ppermute | solution.py:76
  66.3 2.0 %collective-permute-start.33 = (bf16[64,1024]{1,0:T(8,128)(2,1)S(1)}, bf16[64,1024]{1,0:T(8,128)(2,1)S(1)}, u32[]{:S(2)}, u32[]{:S(2)}) collective-permute-start(bf16[64,1024]{1,0:T(8,128)(2,1)S(1)} %add_convert_fusion.5), channel_id=1, source_target_pairs={{0,4},{4,8},{8,12},{12,14},{14,10},{10,6},{6,2},{2,0},{1,3},{5,1},... | collective-permute-start | bytes 393224 | tf_op jit(solution)/shard_map/ppermute | solution.py:76
  68.3 2.7 %collective-permute-done.25 = bf16[64,1024]{1,0:T(8,128)(2,1)S(1)} collective-permute-done((bf16[64,1024]{1,0:T(8,128)(2,1)S(1)}, bf16[64,1024]{1,0:T(8,128)(2,1)S(1)}, u32[]{:S(2)}, u32[]{:S(2)}) %collective-permute-start.25) | collective-permute-done | bytes 131104 | tf_op jit(solution)/shard_map/ppermute | solution.py:76
  83.5 5.1 %collective-permute-done.28 = bf16[64,1024]{1,0:T(8,128)(2,1)S(1)} collective-permute-done((bf16[64,1024]{1,0:T(8,128)(2,1)S(1)}, bf16[64,1024]{1,0:T(8,128)(2,1)S(1)}, u32[]{:S(2)}, u32[]{:S(2)}) %collective-permute-start.28) | collective-permute-done | bytes 131104 | tf_op jit(solution)/shard_map/ppermute | solution.py:76
  90.5 4.8 %collective-permute-done.36.refs_1_ = bf16[128,1024]{1,0:T(8,128)(2,1)S(1)} collective-permute-done((bf16[128,1024]{1,0:T(8,128)(2,1)S(1)}, bf16[128,1024]{1,0:T(8,128)(2,1)S(1)}, u32[]{:S(2)}, u32[]{:S(2)}) %collective-permute-start.36) | collective-permute-done | bytes 262176 | tf_op jit(solution)/shard_map/ppermute | solution.py:76
  95.5 2.6 %collective-permute-done.38.refs_2_ = bf16[128,1024]{1,0:T(8,128)(2,1)S(1)} collective-permute-done((bf16[128,1024]{1,0:T(8,128)(2,1)S(1)}, bf16[128,1024]{1,0:T(8,128)(2,1)S(1)}, u32[]{:S(2)}, u32[]{:S(2)}) %collective-permute-start.38) | collective-permute-done | bytes 262176 | tf_op jit(solution)/shard_map/ppermute | solution.py:76
  98.3 3.4 %collective-permute-done.39.refs_3_ = bf16[128,1024]{1,0:T(8,128)(2,1)S(1)} collective-permute-done((bf16[128,1024]{1,0:T(8,128)(2,1)S(1)}, bf16[128,1024]{1,0:T(8,128)(2,1)S(1)}, u32[]{:S(2)}, u32[]{:S(2)}) %collective-permute-start.39) | collective-permute-done | bytes 262176 | tf_op jit(solution)/shard_map/ppermute | solution.py:76
  102.4 2.1 %collective-permute-done.40.refs_4_ = bf16[128,1024]{1,0:T(8,128)(2,1)S(1)} collective-permute-done((bf16[128,1024]{1,0:T(8,128)(2,1)S(1)}, bf16[128,1024]{1,0:T(8,128)(2,1)S(1)}, u32[]{:S(2)}, u32[]{:S(2)}) %collective-permute-start.40) | collective-permute-done | bytes 262176 | tf_op jit(solution)/shard_map/ppermute | solution.py:76
  104.7 3.4 %collective-permute-done.41.refs_5_ = bf16[128,1024]{1,0:T(8,128)(2,1)S(1)} collective-permute-done((bf16[128,1024]{1,0:T(8,128)(2,1)S(1)}, bf16[128,1024]{1,0:T(8,128)(2,1)S(1)}, u32[]{:S(2)}, u32[]{:S(2)}) %collective-permute-start.41) | collective-permute-done | bytes 262176 | tf_op jit(solution)/shard_map/ppermute | solution.py:76
  108.8 2.0 %collective-permute-done.42.refs_6_ = bf16[128,1024]{1,0:T(8,128)(2,1)S(1)} collective-permute-done((bf16[128,1024]{1,0:T(8,128)(2,1)S(1)}, bf16[128,1024]{1,0:T(8,128)(2,1)S(1)}, u32[]{:S(2)}, u32[]{:S(2)}) %collective-permute-start.42) | collective-permute-done | bytes 262176 | tf_op jit(solution)/shard_map/ppermute | solution.py:76
  110.9 3.6 %collective-permute-done.43.refs_7_ = bf16[128,1024]{1,0:T(8,128)(2,1)S(1)} collective-permute-done((bf16[128,1024]{1,0:T(8,128)(2,1)S(1)}, bf16[128,1024]{1,0:T(8,128)(2,1)S(1)}, u32[]{:S(2)}, u32[]{:S(2)}) %collective-permute-start.43) | collective-permute-done | bytes 262176 | tf_op jit(solution)/shard_map/ppermute | solution.py:76
  116.0 3.6 %final_norm.1 = bf16[128,16384]{1,0:T(8,128)(2,1)} custom-call(s32[16]{0:T(128)S(1)} %stack.99.blocks.ids, bf16[128,1024]{1,0:T(8,128)(2,1)S(1)} %pad_maximum_fusion.1.refs_0_, bf16[128,1024]{1,0:T(8,128)(2,1)S(1)} %collective-permute-done.36.refs_1_, bf16[128,1024]{1,0:T(8,128)(2,1)S(1)} %collective-permute-done.38.refs_2_, ...), custom_call_target="tpu_custom_call" | custom-call | flops 16777216 | bytes 12582912 | tf_op jit(solution)/shard_map/final_norm/pallas_call | solution.py:466
  (123 shorter events, 43.3 us)
Async XLA Ops:
  0.0 22.4 %collective-permute-start.8 = (bf16[128,16384]{1,0:T(8,128)(2,1)}, bf16[128,16384]{1,0:T(8,128)(2,1)}, u32[]{:S(2)}, u32[]{:S(2)}) collective-permute-start(bf16[128,16384]{1,0:T(8,128)(2,1)} %first.3), channel_id=1, source_target_pairs={{0,1},{1,0},{2,3},{3,2},{4,5},{5,4},{6,7},{7,6},{8,9},{9,8},{10,11... | collective-permute-start | bytes 12582920 | tf_op jit(solution)/shard_map/ppermute | solution.py:76
  0.5 8.6 %collective-permute-start.2 = (bf16[128,1024]{1,0:T(8,128)(2,1)}, bf16[128,1024]{1,0:T(8,128)(2,1)S(1)}, u32[]{:S(2)}, u32[]{:S(2)}) collective-permute-start(bf16[128,1024]{1,0:T(8,128)(2,1)} %refs_0_), channel_id=1, source_target_pairs={{0,4},{4,8},{8,12},{12,14},{14,10},{10,6},{6,2},{2,0},{1,3},{5,1},... | collective-permute-start | bytes 786440 | tf_op jit(solution)/shard_map/ppermute | solution.py:76
  3.0 9.5 %collective-permute-start.3 = (bf16[128,1024]{1,0:T(8,128)(2,1)}, bf16[128,1024]{1,0:T(8,128)(2,1)S(1)}, u32[]{:S(2)}, u32[]{:S(2)}) collective-permute-start(bf16[128,1024]{1,0:T(8,128)(2,1)} %refs_0_), channel_id=1, source_target_pairs={{0,3},{4,1},{8,5},{12,9},{14,13},{10,15},{6,11},{2,7},{1,4},{5,8},... | collective-permute-start | bytes 786440 | tf_op jit(solution)/shard_map/ppermute | solution.py:76
  9.0 7.0 %collective-permute-start.4 = (bf16[128,1024]{1,0:T(8,128)(2,1)S(1)}, bf16[128,1024]{1,0:T(8,128)(2,1)S(1)}, u32[]{:S(2)}, u32[]{:S(2)}) collective-permute-start(bf16[128,1024]{1,0:T(8,128)(2,1)S(1)} %collective-permute-done.2.refs_1_), channel_id=1, source_target_pairs={{0,4},{4,8},{8,12},{12,14},{14,10},{10,6},{6,2},{2,0},{1,3},{5,1},... | collective-permute-start | bytes 786440 | tf_op jit(solution)/shard_map/ppermute | solution.py:76
  12.5 7.4 %collective-permute-start.5 = (bf16[128,1024]{1,0:T(8,128)(2,1)S(1)}, bf16[128,1024]{1,0:T(8,128)(2,1)S(1)}, u32[]{:S(2)}, u32[]{:S(2)}) collective-permute-start(bf16[128,1024]{1,0:T(8,128)(2,1)S(1)} %collective-permute-done.3.refs_2_), channel_id=1, source_target_pairs={{0,4},{4,8},{8,12},{12,14},{14,10},{10,6},{6,2},{2,0},{1,3},{5,1},... | collective-permute-start | bytes 786440 | tf_op jit(solution)/shard_map/ppermute | solution.py:76
  19.6 12.0 %collective-permute-start.1 = (bf16[4,2,2,64,128]{4,3,2,1,0:T(8,128)(2,1)}, bf16[4,2,2,64,128]{4,3,2,1,0:T(8,128)(2,1)S(1)}, u32[]{:S(2)}, u32[]{:S(2)}) collective-permute-start(bf16[4,2,2,64,128]{4,3,2,1,0:T(8,128)(2,1)} %get-tuple-element.31), channel_id=1, source_target_pairs={{0,2},{1,3},{2,0},{3,1},{4,6},{5,7},{6,4},{7,5},{8,10},{9,11},{10,... | collective-permute-start | bytes 786440 | tf_op jit(solution)/shard_map/ppermute | solution.py:76
  20.0 12.1 %collective-permute-start.11 = (bf16[128,1024]{1,0:T(8,128)(2,1)S(1)}, bf16[128,1024]{1,0:T(8,128)(2,1)S(1)}, u32[]{:S(2)}, u32[]{:S(2)}) collective-permute-start(bf16[128,1024]{1,0:T(8,128)(2,1)S(1)} %collective-permute-done.2.refs_1_), channel_id=1, source_target_pairs={{0,1},{1,0},{2,3},{3,2},{4,5},{5,4},{6,7},{7,6},{8,9},{9,8},{10,11... | collective-permute-start | bytes 786440 | tf_op jit(solution)/shard_map/ppermute | solution.py:76
  22.4 9.8 %collective-permute-start.12 = (bf16[128,1024]{1,0:T(8,128)(2,1)S(1)}, bf16[128,1024]{1,0:T(8,128)(2,1)S(1)}, u32[]{:S(2)}, u32[]{:S(2)}) collective-permute-start(bf16[128,1024]{1,0:T(8,128)(2,1)S(1)} %collective-permute-done.3.refs_2_), channel_id=1, source_target_pairs={{0,1},{1,0},{2,3},{3,2},{4,5},{5,4},{6,7},{7,6},{8,9},{9,8},{10,11... | collective-permute-start | bytes 786440 | tf_op jit(solution)/shard_map/ppermute | solution.py:76
  22.4 10.1 %collective-permute-start.7 = (bf16[128,1024]{1,0:T(8,128)(2,1)S(1)}, bf16[128,1024]{1,0:T(8,128)(2,1)S(1)}, u32[]{:S(2)}, u32[]{:S(2)}) collective-permute-start(bf16[128,1024]{1,0:T(8,128)(2,1)S(1)} %collective-permute-done.5.refs_4_), channel_id=1, source_target_pairs={{0,4},{4,8},{8,12},{12,14},{14,10},{10,6},{6,2},{2,0},{1,3},{5,1},... | collective-permute-start | bytes 786440 | tf_op jit(solution)/shard_map/ppermute | solution.py:76
  24.2 10.0 %collective-permute-start.9 = (bf16[128,1024]{1,0:T(8,128)(2,1)S(1)}, bf16[128,1024]{1,0:T(8,128)(2,1)S(1)}, u32[]{:S(2)}, u32[]{:S(2)}) collective-permute-start(bf16[128,1024]{1,0:T(8,128)(2,1)S(1)} %collective-permute-done.6.refs_5_), channel_id=1, source_target_pairs={{0,4},{4,8},{8,12},{12,14},{14,10},{10,6},{6,2},{2,0},{1,3},{5,1},... | collective-permute-start | bytes 786440 | tf_op jit(solution)/shard_map/ppermute | solution.py:76
  39.5 7.7 %collective-permute-start.19 = (bf16[128,128]{1,0:T(8,128)(2,1)S(1)}, bf16[128,128]{1,0:T(8,128)(2,1)S(1)}, u32[]{:S(2)}, u32[]{:S(2)}) collective-permute-start(bf16[128,128]{1,0:T(8,128)(2,1)S(1)} %get-tuple-element.39), channel_id=1, source_target_pairs={{0,0},{1,2},{2,4},{3,6},{4,8},{5,10},{6,12},{7,14},{8,1},{9,3},{10... | collective-permute-start | bytes 98312 | tf_op jit(solution)/shard_map/ppermute | solution.py:76
  40.2 10.7 %collective-permute-start.21 = (bf16[2,2,2,64,128]{4,3,2,1,0:T(8,128)(2,1)}, bf16[2,2,2,64,128]{4,3,2,1,0:T(8,128)(2,1)S(1)}, u32[]{:S(2)}, u32[]{:S(2)}) collective-permute-start(bf16[2,2,2,64,128]{4,3,2,1,0:T(8,128)(2,1)} %copy-done.3), channel_id=1, source_target_pairs={{0,4},{1,5},{2,6},{3,7},{4,0},{5,1},{6,2},{7,3},{8,12},{9,13},{10,... | collective-permute-start | bytes 393224 | tf_op jit(solution)/shard_map/ppermute | solution.py:76
  44.7 13.0 %collective-permute-start.22 = (bf16[2,2,2,64,128]{4,3,2,1,0:T(8,128)(2,1)}, bf16[2,2,2,64,128]{4,3,2,1,0:T(8,128)(2,1)S(1)}, u32[]{:S(2)}, u32[]{:S(2)}) collective-permute-start(bf16[2,2,2,64,128]{4,3,2,1,0:T(8,128)(2,1)} %copy-done.2), channel_id=1, source_target_pairs={{0,8},{1,9},{2,10},{3,11},{4,12},{5,13},{6,14},{7,15},{8,0},{9,1},... | collective-permute-start | bytes 393224 | tf_op jit(solution)/shard_map/ppermute | solution.py:76
  46.3 11.5 %collective-permute-start.23 = (bf16[2,2,2,64,128]{4,3,2,1,0:T(8,128)(2,1)}, bf16[2,2,2,64,128]{4,3,2,1,0:T(8,128)(2,1)S(1)}, u32[]{:S(2)}, u32[]{:S(2)}) collective-permute-start(bf16[2,2,2,64,128]{4,3,2,1,0:T(8,128)(2,1)} %copy-done.1), channel_id=1, source_target_pairs={{0,12},{1,13},{2,14},{3,15},{4,8},{5,9},{6,10},{7,11},{8,4},{9,5},... | collective-permute-start | bytes 393224 | tf_op jit(solution)/shard_map/ppermute | solution.py:76
  47.2 10.6 %collective-permute-start.18 = (bf16[64,128]{1,0:T(8,128)(2,1)S(1)}, bf16[64,128]{1,0:T(8,128)(2,1)S(1)}, u32[]{:S(2)}, u32[]{:S(2)}) collective-permute-start(bf16[64,128]{1,0:T(8,128)(2,1)S(1)} %get-tuple-element.38), channel_id=1, source_target_pairs={{0,1},{1,0},{2,3},{3,2},{4,5},{5,4},{6,7},{7,6},{8,9},{9,8},{10,11... | collective-permute-start | bytes 49160 | tf_op jit(solution)/shard_map/ppermute | solution.py:76
  47.2 11.4 %collective-permute-start.20 = (bf16[64,128]{1,0:T(8,128)(2,1)S(1)}, bf16[64,128]{1,0:T(8,128)(2,1)S(1)}, u32[]{:S(2)}, u32[]{:S(2)}) collective-permute-start(bf16[64,128]{1,0:T(8,128)(2,1)S(1)} %slice_select_fusion), channel_id=1, source_target_pairs={{0,1},{1,0},{2,3},{3,2},{4,5},{5,4},{6,7},{7,6},{8,9},{9,8},{10,11... | collective-permute-start | bytes 49160 | tf_op jit(solution)/shard_map/ppermute | solution.py:76
  63.3 10.7 %collective-permute-start.29 = (bf16[128,1024]{1,0:T(8,128)(2,1)S(1)}, bf16[128,1024]{1,0:T(8,128)(2,1)S(1)}, u32[]{:S(2)}, u32[]{:S(2)}) collective-permute-start(bf16[128,1024]{1,0:T(8,128)(2,1)S(1)} %get-tuple-element.47), channel_id=1, source_target_pairs={{0,4},{4,8},{8,12},{12,14},{14,10},{10,6},{6,2},{2,0},{1,3},{5,1},... | collective-permute-start | bytes 786440 | tf_op jit(solution)/shard_map/ppermute | solution.py:76
  64.0 7.1 %collective-permute-start.25 = (bf16[64,1024]{1,0:T(8,128)(2,1)S(1)}, bf16[64,1024]{1,0:T(8,128)(2,1)S(1)}, u32[]{:S(2)}, u32[]{:S(2)}) collective-permute-start(bf16[64,1024]{1,0:T(8,128)(2,1)S(1)} %get-tuple-element.43), channel_id=1, source_target_pairs={{0,4},{4,8},{8,12},{12,14},{14,10},{10,6},{6,2},{2,0},{1,3},{5,1},... | collective-permute-start | bytes 393224 | tf_op jit(solution)/shard_map/ppermute | solution.py:76
  74.0 6.7 %collective-permute-start.30 = (bf16[128,1024]{1,0:T(8,128)(2,1)S(1)}, bf16[128,1024]{1,0:T(8,128)(2,1)S(1)}, u32[]{:S(2)}, u32[]{:S(2)}) collective-permute-start(bf16[128,1024]{1,0:T(8,128)(2,1)S(1)} %add_convert_fusion.1), channel_id=1, source_target_pairs={{0,4},{4,8},{8,12},{12,14},{14,10},{10,6},{6,2},{2,0},{1,3},{5,1},... | collective-permute-start | bytes 786440 | tf_op jit(solution)/shard_map/ppermute | solution.py:76
  80.8 7.8 %collective-permute-start.31 = (bf16[128,1024]{1,0:T(8,128)(2,1)S(1)}, bf16[128,1024]{1,0:T(8,128)(2,1)S(1)}, u32[]{:S(2)}, u32[]{:S(2)}) collective-permute-start(bf16[128,1024]{1,0:T(8,128)(2,1)S(1)} %add_convert_fusion), channel_id=1, source_target_pairs={{0,5},{4,9},{8,13},{12,15},{14,11},{10,7},{6,3},{2,1},{1,2},{5,0},... | collective-permute-start | bytes 786440 | tf_op jit(solution)/shard_map/ppermute | solution.py:76
  82.2 6.5 %collective-permute-start.28 = (bf16[64,1024]{1,0:T(8,128)(2,1)S(1)}, bf16[64,1024]{1,0:T(8,128)(2,1)S(1)}, u32[]{:S(2)}, u32[]{:S(2)}) collective-permute-start(bf16[64,1024]{1,0:T(8,128)(2,1)S(1)} %add_convert_fusion.7), channel_id=1, source_target_pairs={{0,4},{4,8},{8,12},{12,14},{14,10},{10,6},{6,2},{2,0},{1,3},{5,1},... | collective-permute-start | bytes 393224 | tf_op jit(solution)/shard_map/ppermute | solution.py:76
  88.9 6.4 %collective-permute-start.36 = (bf16[128,1024]{1,0:T(8,128)(2,1)S(1)}, bf16[128,1024]{1,0:T(8,128)(2,1)S(1)}, u32[]{:S(2)}, u32[]{:S(2)}) collective-permute-start(bf16[128,1024]{1,0:T(8,128)(2,1)S(1)} %pad_maximum_fusion.1.refs_0_), channel_id=1, source_target_pairs={{0,4},{4,8},{8,12},{12,14},{14,10},{10,6},{6,2},{2,0},{1,3},{5,1},... | collective-permute-start | bytes 786440 | tf_op jit(solution)/shard_map/ppermute | solution.py:76
  90.4 7.7 %collective-permute-start.38 = (bf16[128,1024]{1,0:T(8,128)(2,1)S(1)}, bf16[128,1024]{1,0:T(8,128)(2,1)S(1)}, u32[]{:S(2)}, u32[]{:S(2)}) collective-permute-start(bf16[128,1024]{1,0:T(8,128)(2,1)S(1)} %collective-permute-done.37.refs_8_), channel_id=1, source_target_pairs={{0,4},{4,8},{8,12},{12,14},{14,10},{10,6},{6,2},{2,0},{1,3},{5,1},... | collective-permute-start | bytes 786440 | tf_op jit(solution)/shard_map/ppermute | solution.py:76
  102.3 6.5 %collective-permute-start.45 = (bf16[128,1024]{1,0:T(8,128)(2,1)S(1)}, bf16[128,1024]{1,0:T(8,128)(2,1)S(1)}, u32[]{:S(2)}, u32[]{:S(2)}) collective-permute-start(bf16[128,1024]{1,0:T(8,128)(2,1)S(1)} %collective-permute-done.38.refs_2_), channel_id=1, source_target_pairs={{0,1},{1,0},{2,3},{3,2},{4,5},{5,4},{6,7},{7,6},{8,9},{9,8},{10,11... | collective-permute-start | bytes 786440 | tf_op jit(solution)/shard_map/ppermute | solution.py:76
  (33 other events, 208.2 us)

commit v7 on v6

--- a/solution.py
+++ b/solution.py
@@ -125,16 +125,15 @@
 
 
 def ring_sum(shares):
-    streams, crossed = shares[4, 0], shares[3, 1][0]
+    straight, crossed = shares[4, 0], shares[3, 1]
     for step in range(1, 5):
-        streams = [send(part, ONWARD) for part in streams]
+        straight = send(straight, ONWARD)
         if step < 4:
             crossed = send(crossed, LEAVE if step == 3 else ONWARD)
-        if step < 4:
-            streams = [add_share(part, share) for part, share in zip(streams, shares[4 - step, 0])]
+            straight = add_share(straight, shares[4 - step, 0])
         if step < 3:
-            crossed = add_share(crossed, shares[3 - step, 1][0])
-    return streams, crossed
+            crossed = add_share(crossed, shares[3 - step, 1])
+    return straight, crossed
 
 
 def add_share(part, share):
@@ -401,45 +400,30 @@
     )
 
 
-def share_shapes(shares, width, dtype):
-    half, whole = [((SPAN, width), dtype)] * 2, [((TOKENS, width), dtype)]
-    return [jax.ShapeDtypeStruct(*s) for _, other in shares for s in (whole if other else half)]
-
-
-def share_lists(shares, arrays):
-    arrays = list(arrays)
-    return {key: [arrays.pop(0) for _ in range(2 - key[1])] for key in shares}
-
-
-def write_share(value, outs):
-    rows = TOKENS // len(outs)
+def shares_kernel(first, core, attn, attn_other, weights, *outs):
+    rows = both_heads(core, attn, attn_other)
     for i, out in enumerate(outs):
-        out[...] = value[i * rows : (i + 1) * rows].astype(out.dtype)
-
-
-def shares_kernel(first, last, core, attn, attn_other, weights, *outs):
-    rows = both_heads(core, attn, attn_other)
-    for i, refs in enumerate(share_lists(SHARES[first:last], outs).values()):
-        write_share(jnp.dot(rows, weights[first + i], preferred_element_type=jnp.float32), refs)
+        out[...] = jnp.dot(
+            rows, weights[first + i], preferred_element_type=jnp.float32
+        ).astype(out.dtype)
 
 
 def shares_of(core, attn, attn_other, weights, first, last, dtype=jnp.float32):
-    width = weights.shape[2]
-    out_shape = share_shapes(SHARES[first:last], width, dtype)
+    count, width = last - first, weights.shape[2]
     arrays = pl.pallas_call(
-        functools.partial(shares_kernel, first, last),
-        out_shape=out_shape,
+        functools.partial(shares_kernel, first),
+        out_shape=[jax.ShapeDtypeStruct((TOKENS, width), dtype)] * count,
         in_specs=[SMEM] + [VMEM] * 3,
-        out_specs=[VMEM] * len(out_shape),
+        out_specs=[VMEM] * count,
         compiler_params=pltpu.CompilerParams(vmem_limit_bytes=16 * MIB),
         cost_estimate=pl.CostEstimate(
-            flops=4 * TOKENS * HD * width * (last - first),
-            bytes_accessed=(last - first) * MIB,
+            flops=4 * TOKENS * HD * width * count,
+            bytes_accessed=count * MIB,
             transcendentals=0,
         ),
         name="shares_%d" % first,
     )(core, attn, attn_other, weights)
-    return share_lists(SHARES[first:last], arrays)
+    return dict(zip(SHARES[first:last], arrays))
 
 
 def final_kernel(ids, *refs):
@@ -509,7 +493,7 @@
     q_keep, q_send, fresh = project(ids, mine + theirs, gain, weights, tables)
     o_weights = load_weights(after(to, fresh), in_hbm(o_weight), weight_other, width, 1)
     q_other = send(q_send, SWAP)
-    fresh_own = send(fresh, FRESH)
+    fresh_own = send(after(fresh, cache[3:]), FRESH)
     fresh_other = send(jnp.where(core == 0, fresh_own[SPAN:], fresh_own[:SPAN]), SWAP)
     scores = cache_scores(info, after(q_keep, o_weights), q_other, cache)
     attn = attend(info, q_keep, q_other, fresh_own, fresh_other, scores, cache)
@@ -519,13 +503,9 @@
     shares = shares_of(*inputs, 0, 2, jnp.bfloat16)
     shares.update(shares_of(*inputs, 2, len(SHARES)))
     one_way, other_way = ring_sum(shares)
-    hidden = []
-    for h, rows in enumerate((slice(0, SPAN), slice(SPAN, TOKENS))):
-        projected = shares[0, 0][h] + one_way[h].astype(jnp.float32)
-        projected = projected + other_way[rows].astype(jnp.float32)
-        hidden.append((residual[rows].astype(jnp.float32) + projected).astype(jnp.bfloat16))
-
-    hidden = jnp.concatenate(hidden, axis=0)
+    projected = shares[0, 0] + one_way.astype(jnp.float32) + other_way.astype(jnp.float32)
+    hidden = (residual.astype(jnp.float32) + projected).astype(jnp.bfloat16)
+
     mine, theirs = ring_gather(hidden)
     gain = ffn_gain.reshape(16, 1, width).astype(jnp.float32)
     return final_norm(ids, mine + theirs, gain)

time: 120 us -> 121 us (level)
  starting transfers between devices: 37.8 us -> 47.1 us
  waiting for transfers between devices: 57.6 us -> 48.9 us
    ppermute x51 -> x47, starting transfers between devices: 37.8 us -> 47.1 us  [send(): return lax.ppermute(array, 'tp', pairs)]
    ppermute x51 -> x47, waiting for transfers between devices: 57.6 us -> 48.9 us  [send(): return lax.ppermute(array, 'tp', pairs)]
  transfers between devices with their start and end apart: 51 -> 47, of which waited for: 23 -> 22; matrix products, arithmetic and copies ran while one was open for 3% -> 3% of each run, Pallas kernels for 9% -> 11%
where the time goes in v7:
time: 121 us
  waiting for transfers between devices  48.9 us (40%)
  starting transfers between devices  47.1 us (39%)
  Pallas kernels  18.8 us (16%)
  local copies, waits for them, and re-layouts  2.63 us (2%)
  other arithmetic  2.44 us (2%)
    ppermute x47, waiting for transfers between devices, send(): return lax.ppermute(array, 'tp', pairs)  48.9 us
    ppermute x47, starting transfers between devices, send(): return lax.ppermute(array, 'tp', pairs)  47.1 us
    pallas_call x2, Pallas kernels, load_weights(): pl.pallas_call(functools.partial(load_kernel, axis), out_shape=jax.ShapeD...  7.03 us
    pallas_call x1, Pallas kernels, final_norm(): pl.pallas_call(final_kernel, out_shape=jax.ShapeDtypeStruct((TOKENS, 16 *...  3.64 us
    pallas_call x1, Pallas kernels, project(): pl.pallas_call(project_kernel, out_shape=[jax.ShapeDtypeStruct((SPAN, HD)...  3.55 us
  transfers between devices with their start and end apart: 47, of which 22 were waited for; matrix products, arithmetic and copies ran while one was open for 3% of the time, Pallas kernels for 11%

profile of v7, /device:TPU:0, one launch (start us, length us, event | category | flops | bytes accessed | tf_op | source)
XLA Modules:
  0.0 120.6 jit_solution(5520375267259883516)
XLA Ops:
  0.5 2.6 %collective-permute-start.2 = (bf16[128,1024]{1,0:T(8,128)(2,1)}, bf16[128,1024]{1,0:T(8,128)(2,1)S(1)}, u32[]{:S(2)}, u32[]{:S(2)}) collective-permute-start(bf16[128,1024]{1,0:T(8,128)(2,1)} %refs_0_), channel_id=1, source_target_pairs={{0,4},{4,8},{8,12},{12,14},{14,10},{10,6},{6,2},{2,0},{1,3},{5,1},... | collective-permute-start | bytes 786440 | tf_op jit(solution)/shard_map/ppermute | solution.py:76
  4.4 4.7 %collective-permute-done.2.refs_1_ = bf16[128,1024]{1,0:T(8,128)(2,1)S(1)} collective-permute-done((bf16[128,1024]{1,0:T(8,128)(2,1)}, bf16[128,1024]{1,0:T(8,128)(2,1)S(1)}, u32[]{:S(2)}, u32[]{:S(2)}) %collective-permute-start.2) | collective-permute-done | bytes 262176 | tf_op jit(solution)/shard_map/ppermute | solution.py:76
  9.0 2.4 %collective-permute-start.4 = (bf16[128,1024]{1,0:T(8,128)(2,1)S(1)}, bf16[128,1024]{1,0:T(8,128)(2,1)S(1)}, u32[]{:S(2)}, u32[]{:S(2)}) collective-permute-start(bf16[128,1024]{1,0:T(8,128)(2,1)S(1)} %collective-permute-done.2.refs_1_), channel_id=1, source_target_pairs={{0,4},{4,8},{8,12},{12,14},{14,10},{10,6},{6,2},{2,0},{1,3},{5,1},... | collective-permute-start | bytes 786440 | tf_op jit(solution)/shard_map/ppermute | solution.py:76
  12.5 1.6 %collective-permute-start.5 = (bf16[128,1024]{1,0:T(8,128)(2,1)S(1)}, bf16[128,1024]{1,0:T(8,128)(2,1)S(1)}, u32[]{:S(2)}, u32[]{:S(2)}) collective-permute-start(bf16[128,1024]{1,0:T(8,128)(2,1)S(1)} %collective-permute-done.3.refs_2_), channel_id=1, source_target_pairs={{0,4},{4,8},{8,12},{12,14},{14,10},{10,6},{6,2},{2,0},{1,3},{5,1},... | collective-permute-start | bytes 786440 | tf_op jit(solution)/shard_map/ppermute | solution.py:76
  14.2 1.9 %collective-permute-done.4.refs_3_ = bf16[128,1024]{1,0:T(8,128)(2,1)S(1)} collective-permute-done((bf16[128,1024]{1,0:T(8,128)(2,1)S(1)}, bf16[128,1024]{1,0:T(8,128)(2,1)S(1)}, u32[]{:S(2)}, u32[]{:S(2)}) %collective-permute-start.4) | collective-permute-done | bytes 262176 | tf_op jit(solution)/shard_map/ppermute | solution.py:76
  16.0 1.8 %collective-permute-start.6 = (bf16[128,1024]{1,0:T(8,128)(2,1)S(1)}, bf16[128,1024]{1,0:T(8,128)(2,1)S(1)}, u32[]{:S(2)}, u32[]{:S(2)}) collective-permute-start(bf16[128,1024]{1,0:T(8,128)(2,1)S(1)} %collective-permute-done.4.refs_3_), channel_id=1, source_target_pairs={{0,4},{4,8},{8,12},{12,14},{14,10},{10,6},{6,2},{2,0},{1,3},{5,1},... | collective-permute-start | bytes 786440 | tf_op jit(solution)/shard_map/ppermute | solution.py:76
  19.6 3.1 %collective-permute-done.6.refs_5_ = bf16[128,1024]{1,0:T(8,128)(2,1)S(1)} collective-permute-done((bf16[128,1024]{1,0:T(8,128)(2,1)S(1)}, bf16[128,1024]{1,0:T(8,128)(2,1)S(1)}, u32[]{:S(2)}, u32[]{:S(2)}) %collective-permute-start.6) | collective-permute-done | bytes 262176 | tf_op jit(solution)/shard_map/ppermute | solution.py:76
  28.6 2.3 %collective-permute-done.7.refs_6_ = bf16[128,1024]{1,0:T(8,128)(2,1)} collective-permute-done((bf16[128,1024]{1,0:T(8,128)(2,1)S(1)}, bf16[128,1024]{1,0:T(8,128)(2,1)}, u32[]{:S(2)}, u32[]{:S(2)}) %collective-permute-start.7) | collective-permute-done | bytes 262176 | tf_op jit(solution)/shard_map/ppermute | solution.py:76
  30.9 2.8 %collective-permute-done.9.refs_7_ = bf16[128,1024]{1,0:T(8,128)(2,1)} collective-permute-done((bf16[128,1024]{1,0:T(8,128)(2,1)S(1)}, bf16[128,1024]{1,0:T(8,128)(2,1)}, u32[]{:S(2)}, u32[]{:S(2)}) %collective-permute-start.9) | collective-permute-done | bytes 262176 | tf_op jit(solution)/shard_map/ppermute | solution.py:76
  37.6 2.5 %collective-permute-start.20 = (bf16[2,2,2,64,128]{4,3,2,1,0:T(8,128)(2,1)}, bf16[2,2,2,64,128]{4,3,2,1,0:T(8,128)(2,1)S(1)}, u32[]{:S(2)}, u32[]{:S(2)}) collective-permute-start(bf16[2,2,2,64,128]{4,3,2,1,0:T(8,128)(2,1)} %get-tuple-element.30), channel_id=1, source_target_pairs={{0,12},{1,13},{2,14},{3,15},{4,8},{5,9},{6,10},{7,11},{8,4},{9,5},... | collective-permute-start | bytes 393224 | tf_op jit(solution)/shard_map/ppermute | solution.py:76
  41.4 4.2 %load_weights_0.1.refs_17_ = bf16[16,1024,256]{2,1,0:T(8,128)(2,1)S(1)} custom-call(s32[16]{0:T(128)S(1)} %stack.99.blocks.ids, bf16[16384,128]{1,0:T(8,128)(2,1)} %first.2, bf16[16384,128]{1,0:T(8,128)(2,1)} %second.1), custom_call_target="tpu_custom_call" | custom-call | bytes 16777216 | tf_op jit(solution)/shard_map/load_weights_0/pallas_call | solution.py:263
  45.6 3.6 %norm_project.1 = (bf16[64,128]{1,0:T(8,128)(2,1)S(1)}, bf16[64,128]{1,0:T(8,128)(2,1)S(1)}, bf16[128,128]{1,0:T(8,128)(2,1)S(1)}) custom-call(s32[16]{0:T(128)S(1)} %stack.99.blocks.ids, bf16[128,1024]{1,0:T(8,128)(2,1)S(1)} %copy-done, bf16[128,1024]{1,0:T(8,128)(2,1)S(1)} %collective-permute-done.2.refs_1_, ...), custom_call_target="tpu_custom_call" | custom-call | flops 1073741824 | bytes 12582912 | tf_op jit(solution)/shard_map/norm_project/pallas_call | solution.py:301
  49.9 4.8 %collective-permute-start.23 = (bf16[2,2,2,64,128]{4,3,2,1,0:T(8,128)(2,1)}, bf16[2,2,2,64,128]{4,3,2,1,0:T(8,128)(2,1)S(1)}, u32[]{:S(2)}, u32[]{:S(2)}) collective-permute-start(bf16[2,2,2,64,128]{4,3,2,1,0:T(8,128)(2,1)} %copy-done.5), channel_id=1, source_target_pairs={{0,4},{1,5},{2,6},{3,7},{4,0},{5,1},{6,2},{7,3},{8,12},{9,13},{10,... | collective-permute-start | bytes 393224 | tf_op jit(solution)/shard_map/ppermute | solution.py:76
  54.7 2.3 %collective-permute-start.18 = (bf16[64,128]{1,0:T(8,128)(2,1)S(1)}, bf16[64,128]{1,0:T(8,128)(2,1)S(1)}, u32[]{:S(2)}, u32[]{:S(2)}) collective-permute-start(bf16[64,128]{1,0:T(8,128)(2,1)S(1)} %get-tuple-element.34), channel_id=1, source_target_pairs={{0,1},{1,0},{2,3},{3,2},{4,5},{5,4},{6,7},{7,6},{8,9},{9,8},{10,11... | collective-permute-start | bytes 49160 | tf_op jit(solution)/shard_map/ppermute | solution.py:76
  57.3 2.8 %load_weights_1.1.weights = bf16[8,256,1024]{2,1,0:T(8,128)(2,1)S(1)} custom-call(s32[8]{0:T(128)S(1)} %stack.109.blocks, bf16[128,16384]{1,0:T(8,128)(2,1)} %first.3, bf16[128,16384]{1,0:T(8,128)(2,1)} %collective-permute-done.8.second), custom_call_target="tpu_custom_call" | custom-call | bytes 8388608 | tf_op jit(solution)/shard_map/load_weights_1/pallas_call | solution.py:263
  66.1 4.1 %collective-permute-done.25 = bf16[128,1024]{1,0:T(8,128)(2,1)S(1)} collective-permute-done((bf16[128,1024]{1,0:T(8,128)(2,1)S(1)}, bf16[128,1024]{1,0:T(8,128)(2,1)S(1)}, u32[]{:S(2)}, u32[]{:S(2)}) %collective-permute-start.25) | collective-permute-done | bytes 262176 | tf_op jit(solution)/shard_map/ppermute | solution.py:76
  74.7 2.0 %collective-permute-done.26 = bf16[128,1024]{1,0:T(8,128)(2,1)S(1)} collective-permute-done((bf16[128,1024]{1,0:T(8,128)(2,1)S(1)}, bf16[128,1024]{1,0:T(8,128)(2,1)S(1)}, u32[]{:S(2)}, u32[]{:S(2)}) %collective-permute-start.26) | collective-permute-done | bytes 262176 | tf_op jit(solution)/shard_map/ppermute | solution.py:76
  79.7 3.5 %collective-permute-done.27 = bf16[128,1024]{1,0:T(8,128)(2,1)S(1)} collective-permute-done((bf16[128,1024]{1,0:T(8,128)(2,1)S(1)}, bf16[128,1024]{1,0:T(8,128)(2,1)S(1)}, u32[]{:S(2)}, u32[]{:S(2)}) %collective-permute-start.27) | collective-permute-done | bytes 262176 | tf_op jit(solution)/shard_map/ppermute | solution.py:76
  85.5 4.2 %collective-permute-done.28 = bf16[128,1024]{1,0:T(8,128)(2,1)S(1)} collective-permute-done((bf16[128,1024]{1,0:T(8,128)(2,1)S(1)}, bf16[128,1024]{1,0:T(8,128)(2,1)S(1)}, u32[]{:S(2)}, u32[]{:S(2)}) %collective-permute-start.28) | collective-permute-done | bytes 262176 | tf_op jit(solution)/shard_map/ppermute | solution.py:76
  93.0 3.3 %collective-permute-done.32.refs_1_ = bf16[128,1024]{1,0:T(8,128)(2,1)S(1)} collective-permute-done((bf16[128,1024]{1,0:T(8,128)(2,1)S(1)}, bf16[128,1024]{1,0:T(8,128)(2,1)S(1)}, u32[]{:S(2)}, u32[]{:S(2)}) %collective-permute-start.32) | collective-permute-done | bytes 262176 | tf_op jit(solution)/shard_map/ppermute | solution.py:76
  100.7 2.0 %collective-permute-done.35.refs_3_ = bf16[128,1024]{1,0:T(8,128)(2,1)S(1)} collective-permute-done((bf16[128,1024]{1,0:T(8,128)(2,1)S(1)}, bf16[128,1024]{1,0:T(8,128)(2,1)S(1)}, u32[]{:S(2)}, u32[]{:S(2)}) %collective-permute-start.35) | collective-permute-done | bytes 262176 | tf_op jit(solution)/shard_map/ppermute | solution.py:76
  107.1 2.0 %collective-permute-done.37.refs_5_ = bf16[128,1024]{1,0:T(8,128)(2,1)S(1)} collective-permute-done((bf16[128,1024]{1,0:T(8,128)(2,1)S(1)}, bf16[128,1024]{1,0:T(8,128)(2,1)S(1)}, u32[]{:S(2)}, u32[]{:S(2)}) %collective-permute-start.37) | collective-permute-done | bytes 262176 | tf_op jit(solution)/shard_map/ppermute | solution.py:76
  111.9 3.6 %collective-permute-done.39.refs_7_ = bf16[128,1024]{1,0:T(8,128)(2,1)S(1)} collective-permute-done((bf16[128,1024]{1,0:T(8,128)(2,1)S(1)}, bf16[128,1024]{1,0:T(8,128)(2,1)S(1)}, u32[]{:S(2)}, u32[]{:S(2)}) %collective-permute-start.39) | collective-permute-done | bytes 262176 | tf_op jit(solution)/shard_map/ppermute | solution.py:76
  117.0 3.6 %final_norm.1 = bf16[128,16384]{1,0:T(8,128)(2,1)} custom-call(s32[16]{0:T(128)S(1)} %stack.99.blocks.ids, bf16[128,1024]{1,0:T(8,128)(2,1)S(1)} %add_convert_fusion.refs_0_, bf16[128,1024]{1,0:T(8,128)(2,1)S(1)} %collective-permute-done.32.refs_1_, bf16[128,1024]{1,0:T(8,128)(2,1)S(1)} %collective-permute-done.34.refs_2_, ...), custom_call_target="tpu_custom_call" | custom-call | flops 16777216 | bytes 12582912 | tf_op jit(solution)/shard_map/final_norm/pallas_call | solution.py:450
  (115 shorter events, 48.2 us)
Async XLA Ops:
  0.0 22.7 %collective-permute-start.8 = (bf16[128,16384]{1,0:T(8,128)(2,1)}, bf16[128,16384]{1,0:T(8,128)(2,1)}, u32[]{:S(2)}, u32[]{:S(2)}) collective-permute-start(bf16[128,16384]{1,0:T(8,128)(2,1)} %first.3), channel_id=1, source_target_pairs={{0,1},{1,0},{2,3},{3,2},{4,5},{5,4},{6,7},{7,6},{8,9},{9,8},{10,11... | collective-permute-start | bytes 12582920 | tf_op jit(solution)/shard_map/ppermute | solution.py:76
  0.5 8.6 %collective-permute-start.2 = (bf16[128,1024]{1,0:T(8,128)(2,1)}, bf16[128,1024]{1,0:T(8,128)(2,1)S(1)}, u32[]{:S(2)}, u32[]{:S(2)}) collective-permute-start(bf16[128,1024]{1,0:T(8,128)(2,1)} %refs_0_), channel_id=1, source_target_pairs={{0,4},{4,8},{8,12},{12,14},{14,10},{10,6},{6,2},{2,0},{1,3},{5,1},... | collective-permute-start | bytes 786440 | tf_op jit(solution)/shard_map/ppermute | solution.py:76
  3.0 9.5 %collective-permute-start.3 = (bf16[128,1024]{1,0:T(8,128)(2,1)}, bf16[128,1024]{1,0:T(8,128)(2,1)S(1)}, u32[]{:S(2)}, u32[]{:S(2)}) collective-permute-start(bf16[128,1024]{1,0:T(8,128)(2,1)} %refs_0_), channel_id=1, source_target_pairs={{0,3},{4,1},{8,5},{12,9},{14,13},{10,15},{6,11},{2,7},{1,4},{5,8},... | collective-permute-start | bytes 786440 | tf_op jit(solution)/shard_map/ppermute | solution.py:76
  9.0 7.0 %collective-permute-start.4 = (bf16[128,1024]{1,0:T(8,128)(2,1)S(1)}, bf16[128,1024]{1,0:T(8,128)(2,1)S(1)}, u32[]{:S(2)}, u32[]{:S(2)}) collective-permute-start(bf16[128,1024]{1,0:T(8,128)(2,1)S(1)} %collective-permute-done.2.refs_1_), channel_id=1, source_target_pairs={{0,4},{4,8},{8,12},{12,14},{14,10},{10,6},{6,2},{2,0},{1,3},{5,1},... | collective-permute-start | bytes 786440 | tf_op jit(solution)/shard_map/ppermute | solution.py:76
  12.5 6.7 %collective-permute-start.5 = (bf16[128,1024]{1,0:T(8,128)(2,1)S(1)}, bf16[128,1024]{1,0:T(8,128)(2,1)S(1)}, u32[]{:S(2)}, u32[]{:S(2)}) collective-permute-start(bf16[128,1024]{1,0:T(8,128)(2,1)S(1)} %collective-permute-done.3.refs_2_), channel_id=1, source_target_pairs={{0,4},{4,8},{8,12},{12,14},{14,10},{10,6},{6,2},{2,0},{1,3},{5,1},... | collective-permute-start | bytes 786440 | tf_op jit(solution)/shard_map/ppermute | solution.py:76
  16.0 6.6 %collective-permute-start.6 = (bf16[128,1024]{1,0:T(8,128)(2,1)S(1)}, bf16[128,1024]{1,0:T(8,128)(2,1)S(1)}, u32[]{:S(2)}, u32[]{:S(2)}) collective-permute-start(bf16[128,1024]{1,0:T(8,128)(2,1)S(1)} %collective-permute-done.4.refs_3_), channel_id=1, source_target_pairs={{0,4},{4,8},{8,12},{12,14},{14,10},{10,6},{6,2},{2,0},{1,3},{5,1},... | collective-permute-start | bytes 786440 | tf_op jit(solution)/shard_map/ppermute | solution.py:76
  18.9 9.1 %collective-permute-start.1 = (bf16[4,2,2,64,128]{4,3,2,1,0:T(8,128)(2,1)S(1)}, bf16[4,2,2,64,128]{4,3,2,1,0:T(8,128)(2,1)S(1)}, u32[]{:S(2)}, u32[]{:S(2)}) collective-permute-start(bf16[4,2,2,64,128]{4,3,2,1,0:T(8,128)(2,1)S(1)} %get-tuple-element.27), channel_id=1, source_target_pairs={{0,2},{1,3},{2,0},{3,1},{4,6},{5,7},{6,4},{7,5},{8,10},{9,11},{10,... | collective-permute-start | bytes 786440 | tf_op jit(solution)/shard_map/ppermute | solution.py:76
  19.3 8.8 %collective-permute-start.11 = (bf16[128,1024]{1,0:T(8,128)(2,1)S(1)}, bf16[128,1024]{1,0:T(8,128)(2,1)S(1)}, u32[]{:S(2)}, u32[]{:S(2)}) collective-permute-start(bf16[128,1024]{1,0:T(8,128)(2,1)S(1)} %collective-permute-done.2.refs_1_), channel_id=1, source_target_pairs={{0,1},{1,0},{2,3},{3,2},{4,5},{5,4},{6,7},{7,6},{8,9},{9,8},{10,11... | collective-permute-start | bytes 786440 | tf_op jit(solution)/shard_map/ppermute | solution.py:76
  22.7 8.3 %collective-permute-start.7 = (bf16[128,1024]{1,0:T(8,128)(2,1)S(1)}, bf16[128,1024]{1,0:T(8,128)(2,1)}, u32[]{:S(2)}, u32[]{:S(2)}) collective-permute-start(bf16[128,1024]{1,0:T(8,128)(2,1)S(1)} %collective-permute-done.5.refs_4_), channel_id=1, source_target_pairs={{0,4},{4,8},{8,12},{12,14},{14,10},{10,6},{6,2},{2,0},{1,3},{5,1},... | collective-permute-start | bytes 786440 | tf_op jit(solution)/shard_map/ppermute | solution.py:76
  24.2 9.6 %collective-permute-start.9 = (bf16[128,1024]{1,0:T(8,128)(2,1)S(1)}, bf16[128,1024]{1,0:T(8,128)(2,1)}, u32[]{:S(2)}, u32[]{:S(2)}) collective-permute-start(bf16[128,1024]{1,0:T(8,128)(2,1)S(1)} %collective-permute-done.6.refs_5_), channel_id=1, source_target_pairs={{0,4},{4,8},{8,12},{12,14},{14,10},{10,6},{6,2},{2,0},{1,3},{5,1},... | collective-permute-start | bytes 786440 | tf_op jit(solution)/shard_map/ppermute | solution.py:76
  28.0 7.4 %collective-permute-start.13 = (bf16[128,1024]{1,0:T(8,128)(2,1)S(1)}, bf16[128,1024]{1,0:T(8,128)(2,1)S(1)}, u32[]{:S(2)}, u32[]{:S(2)}) collective-permute-start(bf16[128,1024]{1,0:T(8,128)(2,1)S(1)} %collective-permute-done.4.refs_3_), channel_id=1, source_target_pairs={{0,1},{1,0},{2,3},{3,2},{4,5},{5,4},{6,7},{7,6},{8,9},{9,8},{10,11... | collective-permute-start | bytes 786440 | tf_op jit(solution)/shard_map/ppermute | solution.py:76
  28.0 8.9 %collective-permute-start.14 = (bf16[128,1024]{1,0:T(8,128)(2,1)S(1)}, bf16[128,1024]{1,0:T(8,128)(2,1)S(1)}, u32[]{:S(2)}, u32[]{:S(2)}) collective-permute-start(bf16[128,1024]{1,0:T(8,128)(2,1)S(1)} %collective-permute-done.5.refs_4_), channel_id=1, source_target_pairs={{0,1},{1,0},{2,3},{3,2},{4,5},{5,4},{6,7},{7,6},{8,9},{9,8},{10,11... | collective-permute-start | bytes 786440 | tf_op jit(solution)/shard_map/ppermute | solution.py:76
  28.6 16.9 %collective-permute-start.15 = (bf16[128,1024]{1,0:T(8,128)(2,1)S(1)}, bf16[128,1024]{1,0:T(8,128)(2,1)}, u32[]{:S(2)}, u32[]{:S(2)}) collective-permute-start(bf16[128,1024]{1,0:T(8,128)(2,1)S(1)} %collective-permute-done.6.refs_5_), channel_id=1, source_target_pairs={{0,1},{1,0},{2,3},{3,2},{4,5},{5,4},{6,7},{7,6},{8,9},{9,8},{10,11... | collective-permute-start | bytes 786440 | tf_op jit(solution)/shard_map/ppermute | solution.py:76
  30.9 14.7 %collective-permute-start.16 = (bf16[128,1024]{1,0:T(8,128)(2,1)}, bf16[128,1024]{1,0:T(8,128)(2,1)}, u32[]{:S(2)}, u32[]{:S(2)}) collective-permute-start(bf16[128,1024]{1,0:T(8,128)(2,1)} %collective-permute-done.7.refs_6_), channel_id=1, source_target_pairs={{0,1},{1,0},{2,3},{3,2},{4,5},{5,4},{6,7},{7,6},{8,9},{9,8},{10,11... | collective-permute-start | bytes 786440 | tf_op jit(solution)/shard_map/ppermute | solution.py:76
  33.7 11.9 %collective-permute-start.17 = (bf16[128,1024]{1,0:T(8,128)(2,1)}, bf16[128,1024]{1,0:T(8,128)(2,1)}, u32[]{:S(2)}, u32[]{:S(2)}) collective-permute-start(bf16[128,1024]{1,0:T(8,128)(2,1)} %collective-permute-done.9.refs_7_), channel_id=1, source_target_pairs={{0,1},{1,0},{2,3},{3,2},{4,5},{5,4},{6,7},{7,6},{8,9},{9,8},{10,11... | collective-permute-start | bytes 786440 | tf_op jit(solution)/shard_map/ppermute | solution.py:76
  35.4 13.8 %collective-permute-start.19 = (bf16[2,2,2,64,128]{4,3,2,1,0:T(8,128)(2,1)}, bf16[2,2,2,64,128]{4,3,2,1,0:T(8,128)(2,1)S(1)}, u32[]{:S(2)}, u32[]{:S(2)}) collective-permute-start(bf16[2,2,2,64,128]{4,3,2,1,0:T(8,128)(2,1)} %get-tuple-element.29), channel_id=1, source_target_pairs={{0,8},{1,9},{2,10},{3,11},{4,12},{5,13},{6,14},{7,15},{8,0},{9,1},... | collective-permute-start | bytes 393224 | tf_op jit(solution)/shard_map/ppermute | solution.py:76
  37.6 11.6 %collective-permute-start.20 = (bf16[2,2,2,64,128]{4,3,2,1,0:T(8,128)(2,1)}, bf16[2,2,2,64,128]{4,3,2,1,0:T(8,128)(2,1)S(1)}, u32[]{:S(2)}, u32[]{:S(2)}) collective-permute-start(bf16[2,2,2,64,128]{4,3,2,1,0:T(8,128)(2,1)} %get-tuple-element.30), channel_id=1, source_target_pairs={{0,12},{1,13},{2,14},{3,15},{4,8},{5,9},{6,10},{7,11},{8,4},{9,5},... | collective-permute-start | bytes 393224 | tf_op jit(solution)/shard_map/ppermute | solution.py:76
  49.2 7.8 %collective-permute-start.21 = (bf16[128,128]{1,0:T(8,128)(2,1)S(1)}, bf16[128,128]{1,0:T(8,128)(2,1)S(1)}, u32[]{:S(2)}, u32[]{:S(2)}) collective-permute-start(bf16[128,128]{1,0:T(8,128)(2,1)S(1)} %get-tuple-element.36), channel_id=1, source_target_pairs={{0,0},{1,2},{2,4},{3,6},{4,8},{5,10},{6,12},{7,14},{8,1},{9,3},{10... | collective-permute-start | bytes 98312 | tf_op jit(solution)/shard_map/ppermute | solution.py:76
  49.9 10.3 %collective-permute-start.23 = (bf16[2,2,2,64,128]{4,3,2,1,0:T(8,128)(2,1)}, bf16[2,2,2,64,128]{4,3,2,1,0:T(8,128)(2,1)S(1)}, u32[]{:S(2)}, u32[]{:S(2)}) collective-permute-start(bf16[2,2,2,64,128]{4,3,2,1,0:T(8,128)(2,1)} %copy-done.5), channel_id=1, source_target_pairs={{0,4},{1,5},{2,6},{3,7},{4,0},{5,1},{6,2},{7,3},{8,12},{9,13},{10,... | collective-permute-start | bytes 393224 | tf_op jit(solution)/shard_map/ppermute | solution.py:76
  63.8 6.4 %collective-permute-start.25 = (bf16[128,1024]{1,0:T(8,128)(2,1)S(1)}, bf16[128,1024]{1,0:T(8,128)(2,1)S(1)}, u32[]{:S(2)}, u32[]{:S(2)}) collective-permute-start(bf16[128,1024]{1,0:T(8,128)(2,1)S(1)} %get-tuple-element.40), channel_id=1, source_target_pairs={{0,4},{4,8},{8,12},{12,14},{14,10},{10,6},{6,2},{2,0},{1,3},{5,1},... | collective-permute-start | bytes 786440 | tf_op jit(solution)/shard_map/ppermute | solution.py:76
  65.4 7.6 %collective-permute-start.29 = (bf16[128,1024]{1,0:T(8,128)(2,1)S(1)}, bf16[128,1024]{1,0:T(8,128)(2,1)S(1)}, u32[]{:S(2)}, u32[]{:S(2)}) collective-permute-start(bf16[128,1024]{1,0:T(8,128)(2,1)S(1)} %get-tuple-element.44), channel_id=1, source_target_pairs={{0,4},{4,8},{8,12},{12,14},{14,10},{10,6},{6,2},{2,0},{1,3},{5,1},... | collective-permute-start | bytes 786440 | tf_op jit(solution)/shard_map/ppermute | solution.py:76
  70.3 6.4 %collective-permute-start.26 = (bf16[128,1024]{1,0:T(8,128)(2,1)S(1)}, bf16[128,1024]{1,0:T(8,128)(2,1)S(1)}, u32[]{:S(2)}, u32[]{:S(2)}) collective-permute-start(bf16[128,1024]{1,0:T(8,128)(2,1)S(1)} %add_convert_fusion.5), channel_id=1, source_target_pairs={{0,4},{4,8},{8,12},{12,14},{14,10},{10,6},{6,2},{2,0},{1,3},{5,1},... | collective-permute-start | bytes 786440 | tf_op jit(solution)/shard_map/ppermute | solution.py:76
  91.5 7.6 %collective-permute-start.34 = (bf16[128,1024]{1,0:T(8,128)(2,1)S(1)}, bf16[128,1024]{1,0:T(8,128)(2,1)S(1)}, u32[]{:S(2)}, u32[]{:S(2)}) collective-permute-start(bf16[128,1024]{1,0:T(8,128)(2,1)S(1)} %collective-permute-done.33.refs_8_), channel_id=1, source_target_pairs={{0,4},{4,8},{8,12},{12,14},{14,10},{10,6},{6,2},{2,0},{1,3},{5,1},... | collective-permute-start | bytes 786440 | tf_op jit(solution)/shard_map/ppermute | solution.py:76
  104.3 6.9 %collective-permute-start.41 = (bf16[128,1024]{1,0:T(8,128)(2,1)S(1)}, bf16[128,1024]{1,0:T(8,128)(2,1)S(1)}, u32[]{:S(2)}, u32[]{:S(2)}) collective-permute-start(bf16[128,1024]{1,0:T(8,128)(2,1)S(1)} %collective-permute-done.34.refs_2_), channel_id=1, source_target_pairs={{0,1},{1,0},{2,3},{3,2},{4,5},{5,4},{6,7},{7,6},{8,9},{9,8},{10,11... | collective-permute-start | bytes 786440 | tf_op jit(solution)/shard_map/ppermute | solution.py:76
  (31 other events, 200.0 us)

commit v8 on v5

--- a/solution.py
+++ b/solution.py
@@ -84,28 +84,20 @@
     return lax.optimization_barrier((array, others))[0]
 
 
-def ring_gather(parts, own, ready=None):
-    streams, crossed = list(parts), own
-    came = [(own,)]
+def ring_gather(own, ready=None, direct=False):
+    straight, swapped = own, None if direct else send(own, SWAP)
+    crossed = own if direct else swapped
+    mine = [own]
     for step in range(1, 5):
         if step == 4 and ready is not None:
-            streams = after(streams, ready)
-        streams = [send(part, ONWARD) for part in streams]
-        came.append(tuple(streams))
+            straight = after(straight, ready)
+        straight = send(straight, ONWARD)
+        mine.append(straight)
         if step < 4:
-            crossed = send(crossed, ENTER if step == 1 else ONWARD)
-            came.append((crossed,))
-    return came
-
-
-def both_cores(came):
-    mine = flat(came)
-    return mine + [send(piece, SWAP) for piece in mine]
-
-
-def block_refs(refs, parts):
-    counts = (1,) + (parts, 1) * 3 + (parts,)
-    return grouped(refs, counts * 2)
+            crossed = send(crossed, ENTER if direct and step == 1 else ONWARD)
+            mine.append(crossed)
+    theirs = [send(own, SWAP) if direct else swapped]
+    return mine, theirs + [send(block, SWAP) for block in mine[1:]]
 
 
 def gathered_ids(rank):
@@ -131,19 +123,16 @@
     ).astype(jnp.int32)
 
 
-def ring_sum(shares, more_shares):
-    streams, crossed = shares[4, 0], shares[3, 1][0]
+def ring_sum(shares):
+    straight, crossed = shares[4, 0], shares[3, 1]
     for step in range(1, 5):
-        streams = [send(part, ONWARD) for part in streams]
+        straight = send(straight, ONWARD)
         if step < 4:
             crossed = send(crossed, LEAVE if step == 3 else ONWARD)
-        if step == 1:
-            shares.update(more_shares(streams[0]))
-        if step < 4:
-            streams = [add_share(part, share) for part, share in zip(streams, shares[4 - step, 0])]
+            straight = add_share(straight, shares[4 - step, 0])
         if step < 3:
-            crossed = add_share(crossed, shares[3 - step, 1][0])
-    return streams, crossed
+            crossed = add_share(crossed, shares[3 - step, 1])
+    return straight, crossed
 
 
 def add_share(part, share):
@@ -198,26 +187,13 @@
     )(rank_id, in_hbm(key_cache), in_hbm(value_cache), theirs)
 
 
-def flat(blocks):
-    return [piece for block in blocks for piece in block]
-
-
-def grouped(refs, counts):
-    blocks, at = [], 0
-    for count in counts:
-        blocks.append(refs[at : at + count])
-        at += count
-    return blocks
-
-
 def lanes(block, j):
-    parts = [piece[:, 128 * j : 128 * j + 128] for piece in block]
-    return (parts[0] if len(parts) == 1 else jnp.concatenate(parts, axis=0)).astype(jnp.float32)
+    return block[:, 128 * j : 128 * j + 128].astype(jnp.float32)
 
 
 def square_sums(blocks, total):
     for block in blocks:
-        for j in range(block[0].shape[1] // 128):
+        for j in range(block.shape[1] // 128):
             v = lanes(block, j)
             total = total + v * v
     return total
@@ -232,7 +208,7 @@
     return jnp.concatenate(
         [
             (lanes(block, j) * factors * gain_row[:, 128 * j : 128 * j + 128]).astype(jnp.bfloat16)
-            for j in range(block[0].shape[1] // 128)
+            for j in range(block.shape[1] // 128)
         ],
         axis=1,
     )
@@ -273,12 +249,11 @@
 
 def all_factors(blocks):
     total = square_sums(blocks, jnp.zeros((TOKENS, 128), jnp.float32))
-    return row_factors(total, 16 * blocks[0][0].shape[1])
-
-
-def project_kernel(parts, ids, *refs):
-    count = 8 * (parts + 1)
-    blocks, refs = block_refs(refs[:count], parts), refs[count:]
+    return row_factors(total, 16 * blocks[0].shape[1])
+
+
+def project_kernel(ids, *refs):
+    blocks, refs = refs[:16], refs[16:]
     gain, weights, cosine, sine, kv_cos, kv_sin = refs[:6]
     q_keep, q_send, fresh = refs[6:]
     factors = all_factors(blocks)
@@ -297,7 +272,7 @@
 
 def project(ids, arrays, gain, weights, tables):
     return pl.pallas_call(
-        functools.partial(project_kernel, len(arrays) // 8 - 1),
+        project_kernel,
         out_shape=[jax.ShapeDtypeStruct((SPAN, HD), jnp.bfloat16)] * 2
         + [jax.ShapeDtypeStruct((TOKENS, HD), jnp.bfloat16)],
         in_specs=[SMEM] + [VMEM] * (len(arrays) + 6),
@@ -424,33 +399,17 @@
     )
 
 
-def share_shapes(shares, width, dtype):
-    half, whole = [((SPAN, width), dtype)] * 2, [((TOKENS, width), dtype)]
-    return [jax.ShapeDtypeStruct(*s) for _, other in shares for s in (whole if other else half)]
-
-
-def share_lists(shares, arrays):
-    arrays = list(arrays)
-    return {key: [arrays.pop(0) for _ in range(2 - key[1])] for key in shares}
-
-
-def write_share(value, outs):
-    rows = TOKENS // len(outs)
+def first_shares_kernel(core, attn, attn_other, weights, *outs):
+    rows = both_heads(core, attn, attn_other)
     for i, out in enumerate(outs):
-        out[...] = value[i * rows : (i + 1) * rows].astype(out.dtype)
-
-
-def first_shares_kernel(shares, core, attn, attn_other, weights, *outs):
-    rows = both_heads(core, attn, attn_other)
-    for i, refs in enumerate(share_lists(shares, outs).values()):
-        write_share(jnp.dot(rows, weights[i], preferred_element_type=jnp.float32), refs)
+        out[...] = jnp.dot(rows, weights[i], preferred_element_type=jnp.float32).astype(out.dtype)
 
 
 def first_shares(shares, core, attn, attn_other, weights):
     count, _, width = weights.shape
-    out_shape = share_shapes(shares, width, jnp.bfloat16)
+    out_shape = [jax.ShapeDtypeStruct((TOKENS, width), jnp.bfloat16)] * count
     arrays = pl.pallas_call(
-        functools.partial(first_shares_kernel, shares),
+        first_shares_kernel,
         out_shape=out_shape,
         in_specs=[SMEM] + [VMEM] * 3,
         out_specs=[VMEM] * len(out_shape),
@@ -460,24 +419,24 @@
         ),
         name="first_shares",
     )(core, attn, attn_other, weights)
-    return share_lists(shares, arrays)
-
-
-def more_shares_kernel(first, last, core, to, attn, attn_other, weight, weight_other, *refs):
+    return dict(zip(shares, arrays))
+
+
+def more_shares_kernel(first, core, to, attn, attn_other, weight, weight_other, *refs):
     outs, (weights, sems) = refs[:-2], refs[-2:]
     copies = share_copies(to, first, weight, weight_other, weights, sems)
     rows = both_heads(core, attn, attn_other)
-    for i, out in enumerate(share_lists(SHARES[first:last], outs).values()):
+    for i, out in enumerate(outs):
         for copy in copies[i]:
             copy.wait()
-        write_share(jnp.dot(rows, weights[i], preferred_element_type=jnp.float32), out)
+        out[...] = jnp.dot(rows, weights[i], preferred_element_type=jnp.float32)
 
 
 def more_shares(core, to, attn, attn_other, weight, weight_other, first, last):
     count, width = last - first, weight.shape[1] // 16
-    out_shape = share_shapes(SHARES[first:last], width, jnp.float32)
+    out_shape = [jax.ShapeDtypeStruct((TOKENS, width), jnp.float32)] * count
     arrays = pl.pallas_call(
-        functools.partial(more_shares_kernel, first, last),
+        functools.partial(more_shares_kernel, first),
         out_shape=out_shape,
         in_specs=[SMEM] * 2 + [VMEM] * 2 + [HBM] * 2,
         out_specs=[VMEM] * len(out_shape),
@@ -493,12 +452,11 @@
         ),
         name="shares_%d" % first,
     )(core, to, attn, attn_other, in_hbm(weight), weight_other)
-    return share_lists(SHARES[first:last], arrays)
-
-
-def final_kernel(parts, ids, *refs):
-    count = 8 * (parts + 1)
-    blocks, refs = block_refs(refs[:count], parts), refs[count:]
+    return dict(zip(SHARES[first:last], arrays))
+
+
+def final_kernel(ids, *refs):
+    blocks, refs = refs[:16], refs[16:]
     gain, out, staged, sems = refs
     width = staged.shape[2]
     factors = all_factors(blocks)
@@ -519,7 +477,7 @@
 def final_norm(ids, arrays, gain):
     width = arrays[0].shape[1]
     return pl.pallas_call(
-        functools.partial(final_kernel, len(arrays) // 8 - 1),
+        final_kernel,
         out_shape=jax.ShapeDtypeStruct((TOKENS, 16 * width), jnp.bfloat16),
         in_specs=[SMEM] + [VMEM] * (len(arrays) + 1),
         out_specs=HBM,
@@ -548,7 +506,7 @@
 
     weight_other = send(o_weight, SWAP)
     parts = split_cache(key_cache, value_cache, rank, rank_id)
-    came = ring_gather([residual], residual, weight_other)
+    mine, theirs = ring_gather(residual, weight_other, direct=True)
     weights = load_weights(ids, q_weight, kv_weight, width)
     cache = move_cache(parts)
 
@@ -560,9 +518,8 @@
     tables = (cosine, sine, jnp.where(holds_keys, cosine, 1.0), jnp.where(holds_keys, sine, 0.0))
 
     gain = attn_gain.reshape(16, 1, width).astype(jnp.float32)
-    arrays = both_cores(came)
-    arrays[0] = after(arrays[0], cache[1])
-    q_keep, q_send, fresh = project(ids, arrays, gain, weights, tables)
+    mine[0] = after(mine[0], cache[1])
+    q_keep, q_send, fresh = project(ids, mine + theirs, gain, weights, tables)
     q_other = send(q_send, SWAP)
     fresh_own = send(fresh, FRESH)
     fresh_other = send(jnp.where(core == 0, fresh_own[SPAN:], fresh_own[:SPAN]), SWAP)
@@ -574,21 +531,15 @@
 
     shares = first_shares(SHARES[:2], core_id, attn, attn_other, first_weights)
     inputs = (attn, attn_other, o_weight, weight_other)
-    shares.update(more_shares(core_id, to, *inputs, 2, 4))
-    one_way, other_way = ring_sum(
-        shares, lambda came: more_shares(core_id, after(to, came), *inputs, 4, len(SHARES))
-    )
-    hidden = []
-    for h, rows in enumerate((slice(0, SPAN), slice(SPAN, TOKENS))):
-        projected = shares[0, 0][h] + one_way[h].astype(jnp.float32)
-        projected = projected + other_way[rows].astype(jnp.float32)
-        hidden.append((residual[rows].astype(jnp.float32) + projected).astype(jnp.bfloat16))
-
-    hidden = jnp.concatenate(hidden, axis=0)
-    came = ring_gather([hidden], hidden)
-    arrays = both_cores(came)
+    for first, last in ((2, 4), (4, len(SHARES))):
+        shares.update(more_shares(core_id, to, *inputs, first, last))
+    one_way, other_way = ring_sum(shares)
+    projected = shares[0, 0] + one_way.astype(jnp.float32) + other_way.astype(jnp.float32)
+    hidden = (residual.astype(jnp.float32) + projected).astype(jnp.bfloat16)
+
+    mine, theirs = ring_gather(hidden)
     gain = ffn_gain.reshape(16, 1, width).astype(jnp.float32)
-    return final_norm(ids, arrays, gain)
+    return final_norm(ids, mine + theirs, gain)
 
 
 def per_device(

time: 118 us -> 116 us (0.983)
  waiting for transfers between devices: 43.3 us -> 40.5 us
  starting transfers between devices: 48.1 us -> 49.3 us
    ppermute x51 -> x47, waiting for transfers between devices: 43.3 us -> 40.5 us  [send(): return lax.ppermute(array, 'tp', pairs)]
    ppermute x51 -> x47, starting transfers between devices: 48.1 us -> 49.3 us  [send(): return lax.ppermute(array, 'tp', pairs)]
  transfers between devices with their start and end apart: 51 -> 47, of which waited for: 17 -> 19; matrix products, arithmetic and copies ran while one was open for 4% -> 4% of each run, Pallas kernels for 13% -> 13%
where the time goes in v8:
time: 116 us
  starting transfers between devices  49.3 us (42%)
  waiting for transfers between devices  40.5 us (35%)
  Pallas kernels  20.3 us (18%)
  other arithmetic  3.84 us (3%)
  local copies, waits for them, and re-layouts  1.29 us (1%)
    ppermute x47, starting transfers between devices, send(): return lax.ppermute(array, 'tp', pairs)  49.3 us
    ppermute x47, waiting for transfers between devices, send(): return lax.ppermute(array, 'tp', pairs)  40.5 us
    pallas_call x2, Pallas kernels, more_shares(): pl.pallas_call(functools.partial(more_shares_kernel, first), out_shape=ou...  4.67 us
    pallas_call x1, Pallas kernels, load_weights(): pl.pallas_call(load_kernel, out_shape=jax.ShapeDtypeStruct((16, width, 2...  4.19 us
    pallas_call x1, Pallas kernels, final_norm(): pl.pallas_call(final_kernel, out_shape=jax.ShapeDtypeStruct((TOKENS, 16 *...  3.65 us
    pallas_call x1, Pallas kernels, project(): pl.pallas_call(project_kernel, out_shape=[jax.ShapeDtypeStruct((SPAN, HD)...  3.52 us
  transfers between devices with their start and end apart: 47, of which 19 were waited for; matrix products, arithmetic and copies ran while one was open for 4% of the time, Pallas kernels for 13%

profile of v8, /device:TPU:0, one launch (start us, length us, event | category | flops | bytes accessed | tf_op | source)
XLA Modules:
  0.0 115.9 jit_solution(12790896190220232841)
XLA Ops:
  0.5 2.6 %collective-permute-start.2 = (bf16[128,1024]{1,0:T(8,128)(2,1)}, bf16[128,1024]{1,0:T(8,128)(2,1)S(1)}, u32[]{:S(2)}, u32[]{:S(2)}) collective-permute-start(bf16[128,1024]{1,0:T(8,128)(2,1)} %refs_0_), channel_id=1, source_target_pairs={{0,4},{4,8},{8,12},{12,14},{14,10},{10,6},{6,2},{2,0},{1,3},{5,1},... | collective-permute-start | bytes 786440 | tf_op jit(solution)/shard_map/ppermute | solution.py:76
  5.7 3.3 %collective-permute-done.2.refs_1_ = bf16[128,1024]{1,0:T(8,128)(2,1)S(1)} collective-permute-done((bf16[128,1024]{1,0:T(8,128)(2,1)}, bf16[128,1024]{1,0:T(8,128)(2,1)S(1)}, u32[]{:S(2)}, u32[]{:S(2)}) %collective-permute-start.2) | collective-permute-done | bytes 262176 | tf_op jit(solution)/shard_map/ppermute | solution.py:76
  9.0 2.4 %collective-permute-start.4 = (bf16[128,1024]{1,0:T(8,128)(2,1)S(1)}, bf16[128,1024]{1,0:T(8,128)(2,1)S(1)}, u32[]{:S(2)}, u32[]{:S(2)}) collective-permute-start(bf16[128,1024]{1,0:T(8,128)(2,1)S(1)} %collective-permute-done.2.refs_1_), channel_id=1, source_target_pairs={{0,4},{4,8},{8,12},{12,14},{14,10},{10,6},{6,2},{2,0},{1,3},{5,1},... | collective-permute-start | bytes 786440 | tf_op jit(solution)/shard_map/ppermute | solution.py:76
  13.8 2.2 %collective-permute-done.4.refs_3_ = bf16[128,1024]{1,0:T(8,128)(2,1)S(1)} collective-permute-done((bf16[128,1024]{1,0:T(8,128)(2,1)S(1)}, bf16[128,1024]{1,0:T(8,128)(2,1)S(1)}, u32[]{:S(2)}, u32[]{:S(2)}) %collective-permute-start.4) | collective-permute-done | bytes 262176 | tf_op jit(solution)/shard_map/ppermute | solution.py:76
  19.7 5.4 %collective-permute-done.6.refs_5_ = bf16[128,1024]{1,0:T(8,128)(2,1)S(1)} collective-permute-done((bf16[128,1024]{1,0:T(8,128)(2,1)S(1)}, bf16[128,1024]{1,0:T(8,128)(2,1)S(1)}, u32[]{:S(2)}, u32[]{:S(2)}) %collective-permute-start.6) | collective-permute-done | bytes 262176 | tf_op jit(solution)/shard_map/ppermute | solution.py:76
  27.0 4.2 %load_weights.1.refs_17_ = bf16[16,1024,256]{2,1,0:T(8,128)(2,1)S(1)} custom-call(s32[16]{0:T(128)S(1)} %stack.108.ids, bf16[16384,128]{1,0:T(8,128)(2,1)} %wq.1, bf16[16384,128]{1,0:T(8,128)(2,1)} %wkv.1), custom_call_target="tpu_custom_call" | custom-call | bytes 16777216 | tf_op jit(solution)/shard_map/load_weights/pallas_call | solution.py:238
  32.3 2.1 %collective-permute-done.9.refs_7_ = bf16[128,1024]{1,0:T(8,128)(2,1)} collective-permute-done((bf16[128,1024]{1,0:T(8,128)(2,1)S(1)}, bf16[128,1024]{1,0:T(8,128)(2,1)}, u32[]{:S(2)}, u32[]{:S(2)}) %collective-permute-start.9) | collective-permute-done | bytes 262176 | tf_op jit(solution)/shard_map/ppermute | solution.py:76
  37.3 2.2 %collective-permute-start.22 = (bf16[2,2,2,64,128]{4,3,2,1,0:T(8,128)(2,1)}, bf16[2,2,2,64,128]{4,3,2,1,0:T(8,128)(2,1)S(1)}, u32[]{:S(2)}, u32[]{:S(2)}) collective-permute-start(bf16[2,2,2,64,128]{4,3,2,1,0:T(8,128)(2,1)} %pad_maximum_fusion.2), channel_id=1, source_target_pairs={{0,8},{1,9},{2,10},{3,11},{4,12},{5,13},{6,14},{7,15},{8,0},{9,1},... | collective-permute-start | bytes 393224 | tf_op jit(solution)/shard_map/ppermute | solution.py:76
  39.5 3.5 %norm_project.1 = (bf16[64,128]{1,0:T(8,128)(2,1)S(1)}, bf16[64,128]{1,0:T(8,128)(2,1)S(1)}, bf16[128,128]{1,0:T(8,128)(2,1)S(1)}) custom-call(s32[16]{0:T(128)S(1)} %stack.108.ids, bf16[128,1024]{1,0:T(8,128)(2,1)S(1)} %copy-done, bf16[128,1024]{1,0:T(8,128)(2,1)S(1)} %collective-permute-done.2.refs_1_, ...), custom_call_target="tpu_custom_call" | custom-call | flops 1073741824 | bytes 12582912 | tf_op jit(solution)/shard_map/norm_project/pallas_call | solution.py:274
  43.8 3.0 %collective-permute-start.23 = (bf16[2,2,2,64,128]{4,3,2,1,0:T(8,128)(2,1)S(1)}, bf16[2,2,2,64,128]{4,3,2,1,0:T(8,128)(2,1)S(1)}, u32[]{:S(2)}, u32[]{:S(2)}) collective-permute-start(bf16[2,2,2,64,128]{4,3,2,1,0:T(8,128)(2,1)S(1)} %pad_maximum_fusion.3), channel_id=1, source_target_pairs={{0,12},{1,13},{2,14},{3,15},{4,8},{5,9},{6,10},{7,11},{8,4},{9,5},... | collective-permute-start | bytes 393224 | tf_op jit(solution)/shard_map/ppermute | solution.py:76
  53.8 2.4 %collective-permute-start.24 = (bf16[64,256]{1,0:T(8,128)(2,1)S(1)}, bf16[64,256]{1,0:T(8,128)(2,1)S(1)}, u32[]{:S(2)}, u32[]{:S(2)}) collective-permute-start(bf16[64,256]{1,0:T(8,128)(2,1)S(1)} %attend.1.attn), channel_id=1, source_target_pairs={{0,1},{1,0},{2,3},{3,2},{4,5},{5,4},{6,7},{7,6},{8,9},{9,8},{10,11... | collective-permute-start | bytes 98312 | tf_op jit(solution)/shard_map/ppermute | solution.py:76
  57.4 2.7 %collective-permute-start.25 = (bf16[128,1024]{1,0:T(8,128)(2,1)S(1)}, bf16[128,1024]{1,0:T(8,128)(2,1)S(1)}, u32[]{:S(2)}, u32[]{:S(2)}) collective-permute-start(bf16[128,1024]{1,0:T(8,128)(2,1)S(1)} %get-tuple-element.32), channel_id=1, source_target_pairs={{0,4},{4,8},{8,12},{12,14},{14,10},{10,6},{6,2},{2,0},{1,3},{5,1},... | collective-permute-start | bytes 786440 | tf_op jit(solution)/shard_map/ppermute | solution.py:76
  61.6 2.1 %shares_2.1 = (f32[128,1024]{1,0:T(8,128)S(1)}, f32[128,1024]{1,0:T(8,128)S(1)}) custom-call(s32[1]{0:T(128)} %bitcast.16.core, s32[8]{0:T(128)S(1)} %stack.117.to, bf16[64,256]{1,0:T(8,128)(2,1)S(1)} %attend.1.attn, bf16[64,256]{1,0:T(8,128)(2,1)S(1)} %collective-permute-done.24.attn_other, bf16[128,16384]{1,0:T(8,128)(2,1)} %weight.3, ...), custom_call_target="tpu_custom_call" | custom-call | flops 134217728 | bytes 2097152 | tf_op jit(solution)/shard_map/shares_2/pallas_call | solution.py:438
  64.1 2.5 %collective-permute-start.26 = (bf16[128,1024]{1,0:T(8,128)(2,1)S(1)}, bf16[128,1024]{1,0:T(8,128)(2,1)S(1)}, u32[]{:S(2)}, u32[]{:S(2)}) collective-permute-start(bf16[128,1024]{1,0:T(8,128)(2,1)S(1)} %add_convert_fusion.5), channel_id=1, source_target_pairs={{0,4},{4,8},{8,12},{12,14},{14,10},{10,6},{6,2},{2,0},{1,3},{5,1},... | collective-permute-start | bytes 786440 | tf_op jit(solution)/shard_map/ppermute | solution.py:76
  66.5 2.6 %shares_4.1 = (f32[128,1024]{1,0:T(8,128)S(1)}, f32[128,1024]{1,0:T(8,128)S(1)}, f32[128,1024]{1,0:T(8,128)S(1)}, f32[128,1024]{1,0:T(8,128)S(1)}) custom-call(s32[1]{0:T(128)} %bitcast.16.core, s32[8]{0:T(128)S(1)} %stack.117.to, bf16[64,256]{1,0:T(8,128)(2,1)S(1)} %attend.1.attn, bf16[64,256]{1,0:T(8,128)(2,1)S(1)} %collective-permute-done.24.attn_other, ...), custom_call_target="tpu_custom_call" | custom-call | flops 268435456 | bytes 4194304 | tf_op jit(solution)/shard_map/shares_4/pallas_call | solution.py:438
  70.9 2.1 %collective-permute-start.27 = (bf16[128,1024]{1,0:T(8,128)(2,1)S(1)}, bf16[128,1024]{1,0:T(8,128)(2,1)S(1)}, u32[]{:S(2)}, u32[]{:S(2)}) collective-permute-start(bf16[128,1024]{1,0:T(8,128)(2,1)S(1)} %add_convert_fusion.4), channel_id=1, source_target_pairs={{0,4},{4,8},{8,12},{12,14},{14,10},{10,6},{6,2},{2,0},{1,3},{5,1},... | collective-permute-start | bytes 786440 | tf_op jit(solution)/shard_map/ppermute | solution.py:76
  73.0 2.6 %collective-permute-done.30 = bf16[128,1024]{1,0:T(8,128)(2,1)S(1)} collective-permute-done((bf16[128,1024]{1,0:T(8,128)(2,1)S(1)}, bf16[128,1024]{1,0:T(8,128)(2,1)S(1)}, u32[]{:S(2)}, u32[]{:S(2)}) %collective-permute-start.30) | collective-permute-done | bytes 262176 | tf_op jit(solution)/shard_map/ppermute | solution.py:76
  75.8 2.7 %collective-permute-done.27 = bf16[128,1024]{1,0:T(8,128)(2,1)S(1)} collective-permute-done((bf16[128,1024]{1,0:T(8,128)(2,1)S(1)}, bf16[128,1024]{1,0:T(8,128)(2,1)S(1)}, u32[]{:S(2)}, u32[]{:S(2)}) %collective-permute-start.27) | collective-permute-done | bytes 262176 | tf_op jit(solution)/shard_map/ppermute | solution.py:76
  81.6 3.4 %collective-permute-done.28 = bf16[128,1024]{1,0:T(8,128)(2,1)S(1)} collective-permute-done((bf16[128,1024]{1,0:T(8,128)(2,1)S(1)}, bf16[128,1024]{1,0:T(8,128)(2,1)S(1)}, u32[]{:S(2)}, u32[]{:S(2)}) %collective-permute-start.28) | collective-permute-done | bytes 262176 | tf_op jit(solution)/shard_map/ppermute | solution.py:76
  88.3 3.3 %collective-permute-done.32.refs_1_ = bf16[128,1024]{1,0:T(8,128)(2,1)S(1)} collective-permute-done((bf16[128,1024]{1,0:T(8,128)(2,1)S(1)}, bf16[128,1024]{1,0:T(8,128)(2,1)S(1)}, u32[]{:S(2)}, u32[]{:S(2)}) %collective-permute-start.32) | collective-permute-done | bytes 262176 | tf_op jit(solution)/shard_map/ppermute | solution.py:76
  96.0 2.0 %collective-permute-done.35.refs_3_ = bf16[128,1024]{1,0:T(8,128)(2,1)S(1)} collective-permute-done((bf16[128,1024]{1,0:T(8,128)(2,1)S(1)}, bf16[128,1024]{1,0:T(8,128)(2,1)S(1)}, u32[]{:S(2)}, u32[]{:S(2)}) %collective-permute-start.35) | collective-permute-done | bytes 262176 | tf_op jit(solution)/shard_map/ppermute | solution.py:76
  102.4 2.0 %collective-permute-done.37.refs_5_ = bf16[128,1024]{1,0:T(8,128)(2,1)S(1)} collective-permute-done((bf16[128,1024]{1,0:T(8,128)(2,1)S(1)}, bf16[128,1024]{1,0:T(8,128)(2,1)S(1)}, u32[]{:S(2)}, u32[]{:S(2)}) %collective-permute-start.37) | collective-permute-done | bytes 262176 | tf_op jit(solution)/shard_map/ppermute | solution.py:76
  107.2 3.6 %collective-permute-done.39.refs_7_ = bf16[128,1024]{1,0:T(8,128)(2,1)S(1)} collective-permute-done((bf16[128,1024]{1,0:T(8,128)(2,1)S(1)}, bf16[128,1024]{1,0:T(8,128)(2,1)S(1)}, u32[]{:S(2)}, u32[]{:S(2)}) %collective-permute-start.39) | collective-permute-done | bytes 262176 | tf_op jit(solution)/shard_map/ppermute | solution.py:76
  112.3 3.6 %final_norm.1 = bf16[128,16384]{1,0:T(8,128)(2,1)} custom-call(s32[16]{0:T(128)S(1)} %stack.108.ids, bf16[128,1024]{1,0:T(8,128)(2,1)S(1)} %add_convert_fusion.refs_0_, bf16[128,1024]{1,0:T(8,128)(2,1)S(1)} %collective-permute-done.32.refs_1_, bf16[128,1024]{1,0:T(8,128)(2,1)S(1)} %collective-permute-done.34.refs_2_, ...), custom_call_target="tpu_custom_call" | custom-call | flops 16777216 | bytes 12582912 | tf_op jit(solution)/shard_map/final_norm/pallas_call | solution.py:479
  (109 shorter events, 46.8 us)
Async XLA Ops:
  0.0 25.1 %collective-permute-start.8 = (bf16[128,16384]{1,0:T(8,128)(2,1)}, bf16[128,16384]{1,0:T(8,128)(2,1)}, u32[]{:S(2)}, u32[]{:S(2)}) collective-permute-start(bf16[128,16384]{1,0:T(8,128)(2,1)} %weight.3), channel_id=1, source_target_pairs={{0,1},{1,0},{2,3},{3,2},{4,5},{5,4},{6,7},{7,6},{8,9},{9,8},{10,11... | collective-permute-start | bytes 12582920 | tf_op jit(solution)/shard_map/ppermute | solution.py:76
  0.5 8.6 %collective-permute-start.2 = (bf16[128,1024]{1,0:T(8,128)(2,1)}, bf16[128,1024]{1,0:T(8,128)(2,1)S(1)}, u32[]{:S(2)}, u32[]{:S(2)}) collective-permute-start(bf16[128,1024]{1,0:T(8,128)(2,1)} %refs_0_), channel_id=1, source_target_pairs={{0,4},{4,8},{8,12},{12,14},{14,10},{10,6},{6,2},{2,0},{1,3},{5,1},... | collective-permute-start | bytes 786440 | tf_op jit(solution)/shard_map/ppermute | solution.py:76
  3.0 9.2 %collective-permute-start.3 = (bf16[128,1024]{1,0:T(8,128)(2,1)}, bf16[128,1024]{1,0:T(8,128)(2,1)S(1)}, u32[]{:S(2)}, u32[]{:S(2)}) collective-permute-start(bf16[128,1024]{1,0:T(8,128)(2,1)} %refs_0_), channel_id=1, source_target_pairs={{0,3},{4,1},{8,5},{12,9},{14,13},{10,15},{6,11},{2,7},{1,4},{5,8},... | collective-permute-start | bytes 786440 | tf_op jit(solution)/shard_map/ppermute | solution.py:76
  4.4 20.8 %collective-permute-start.10 = (bf16[128,1024]{1,0:T(8,128)(2,1)}, bf16[128,1024]{1,0:T(8,128)(2,1)S(1)}, u32[]{:S(2)}, u32[]{:S(2)}) collective-permute-start(bf16[128,1024]{1,0:T(8,128)(2,1)} %refs_0_), channel_id=1, source_target_pairs={{0,1},{1,0},{2,3},{3,2},{4,5},{5,4},{6,7},{7,6},{8,9},{9,8},{10,11... | collective-permute-start | bytes 786440 | tf_op jit(solution)/shard_map/ppermute | solution.py:76
  9.0 7.0 %collective-permute-start.4 = (bf16[128,1024]{1,0:T(8,128)(2,1)S(1)}, bf16[128,1024]{1,0:T(8,128)(2,1)S(1)}, u32[]{:S(2)}, u32[]{:S(2)}) collective-permute-start(bf16[128,1024]{1,0:T(8,128)(2,1)S(1)} %collective-permute-done.2.refs_1_), channel_id=1, source_target_pairs={{0,4},{4,8},{8,12},{12,14},{14,10},{10,6},{6,2},{2,0},{1,3},{5,1},... | collective-permute-start | bytes 786440 | tf_op jit(solution)/shard_map/ppermute | solution.py:76
  11.4 6.8 %collective-permute-start = (bf16[2,64,1024]{2,1,0:T(8,128)(2,1)S(1)}, bf16[2,64,1024]{2,1,0:T(8,128)(2,1)S(1)}, u32[]{:S(2)}, u32[]{:S(2)}) collective-permute-start(bf16[2,64,1024]{2,1,0:T(8,128)(2,1)S(1)} %pad_maximum_fusion), channel_id=1, source_target_pairs={{0,1},{1,0},{2,3},{3,2},{4,5},{5,4},{6,7},{7,6},{8,9},{9,8},{10,11... | collective-permute-start | bytes 786440 | tf_op jit(solution)/shard_map/ppermute | solution.py:76
  12.3 7.4 %collective-permute-start.5 = (bf16[128,1024]{1,0:T(8,128)(2,1)S(1)}, bf16[128,1024]{1,0:T(8,128)(2,1)S(1)}, u32[]{:S(2)}, u32[]{:S(2)}) collective-permute-start(bf16[128,1024]{1,0:T(8,128)(2,1)S(1)} %collective-permute-done.3.refs_2_), channel_id=1, source_target_pairs={{0,4},{4,8},{8,12},{12,14},{14,10},{10,6},{6,2},{2,0},{1,3},{5,1},... | collective-permute-start | bytes 786440 | tf_op jit(solution)/shard_map/ppermute | solution.py:76
  16.0 9.1 %collective-permute-start.6 = (bf16[128,1024]{1,0:T(8,128)(2,1)S(1)}, bf16[128,1024]{1,0:T(8,128)(2,1)S(1)}, u32[]{:S(2)}, u32[]{:S(2)}) collective-permute-start(bf16[128,1024]{1,0:T(8,128)(2,1)S(1)} %collective-permute-done.4.refs_3_), channel_id=1, source_target_pairs={{0,4},{4,8},{8,12},{12,14},{14,10},{10,6},{6,2},{2,0},{1,3},{5,1},... | collective-permute-start | bytes 786440 | tf_op jit(solution)/shard_map/ppermute | solution.py:76
  19.3 11.9 %collective-permute-start.1 = (bf16[4,2,2,64,128]{4,3,2,1,0:T(8,128)(2,1)S(1)}, bf16[4,2,2,64,128]{4,3,2,1,0:T(8,128)(2,1)S(1)}, u32[]{:S(2)}, u32[]{:S(2)}) collective-permute-start(bf16[4,2,2,64,128]{4,3,2,1,0:T(8,128)(2,1)S(1)} %get-tuple-element.22), channel_id=1, source_target_pairs={{0,2},{1,3},{2,0},{3,1},{4,6},{5,7},{6,4},{7,5},{8,10},{9,11},{10,... | collective-permute-start | bytes 786440 | tf_op jit(solution)/shard_map/ppermute | solution.py:76
  19.7 11.9 %collective-permute-start.11 = (bf16[128,1024]{1,0:T(8,128)(2,1)S(1)}, bf16[128,1024]{1,0:T(8,128)(2,1)S(1)}, u32[]{:S(2)}, u32[]{:S(2)}) collective-permute-start(bf16[128,1024]{1,0:T(8,128)(2,1)S(1)} %collective-permute-done.2.refs_1_), channel_id=1, source_target_pairs={{0,1},{1,0},{2,3},{3,2},{4,5},{5,4},{6,7},{7,6},{8,9},{9,8},{10,11... | collective-permute-start | bytes 786440 | tf_op jit(solution)/shard_map/ppermute | solution.py:76
  25.1 6.7 %collective-permute-start.12 = (bf16[128,1024]{1,0:T(8,128)(2,1)S(1)}, bf16[128,1024]{1,0:T(8,128)(2,1)S(1)}, u32[]{:S(2)}, u32[]{:S(2)}) collective-permute-start(bf16[128,1024]{1,0:T(8,128)(2,1)S(1)} %collective-permute-done.3.refs_2_), channel_id=1, source_target_pairs={{0,1},{1,0},{2,3},{3,2},{4,5},{5,4},{6,7},{7,6},{8,9},{9,8},{10,11... | collective-permute-start | bytes 786440 | tf_op jit(solution)/shard_map/ppermute | solution.py:76
  25.1 7.0 %collective-permute-start.7 = (bf16[128,1024]{1,0:T(8,128)(2,1)S(1)}, bf16[128,1024]{1,0:T(8,128)(2,1)}, u32[]{:S(2)}, u32[]{:S(2)}) collective-permute-start(bf16[128,1024]{1,0:T(8,128)(2,1)S(1)} %collective-permute-done.5.refs_4_), channel_id=1, source_target_pairs={{0,4},{4,8},{8,12},{12,14},{14,10},{10,6},{6,2},{2,0},{1,3},{5,1},... | collective-permute-start | bytes 786440 | tf_op jit(solution)/shard_map/ppermute | solution.py:76
  25.1 9.3 %collective-permute-start.9 = (bf16[128,1024]{1,0:T(8,128)(2,1)S(1)}, bf16[128,1024]{1,0:T(8,128)(2,1)}, u32[]{:S(2)}, u32[]{:S(2)}) collective-permute-start(bf16[128,1024]{1,0:T(8,128)(2,1)S(1)} %collective-permute-done.6.refs_5_), channel_id=1, source_target_pairs={{0,4},{4,8},{8,12},{12,14},{14,10},{10,6},{6,2},{2,0},{1,3},{5,1},... | collective-permute-start | bytes 786440 | tf_op jit(solution)/shard_map/ppermute | solution.py:76
  31.8 7.7 %collective-permute-start.15 = (bf16[128,1024]{1,0:T(8,128)(2,1)S(1)}, bf16[128,1024]{1,0:T(8,128)(2,1)S(1)}, u32[]{:S(2)}, u32[]{:S(2)}) collective-permute-start(bf16[128,1024]{1,0:T(8,128)(2,1)S(1)} %collective-permute-done.6.refs_5_), channel_id=1, source_target_pairs={{0,1},{1,0},{2,3},{3,2},{4,5},{5,4},{6,7},{7,6},{8,9},{9,8},{10,11... | collective-permute-start | bytes 786440 | tf_op jit(solution)/shard_map/ppermute | solution.py:76
  32.1 7.4 %collective-permute-start.16 = (bf16[128,1024]{1,0:T(8,128)(2,1)}, bf16[128,1024]{1,0:T(8,128)(2,1)S(1)}, u32[]{:S(2)}, u32[]{:S(2)}) collective-permute-start(bf16[128,1024]{1,0:T(8,128)(2,1)} %collective-permute-done.7.refs_6_), channel_id=1, source_target_pairs={{0,1},{1,0},{2,3},{3,2},{4,5},{5,4},{6,7},{7,6},{8,9},{9,8},{10,11... | collective-permute-start | bytes 786440 | tf_op jit(solution)/shard_map/ppermute | solution.py:76
  35.8 14.0 %collective-permute-start.21 = (bf16[2,2,2,64,128]{4,3,2,1,0:T(8,128)(2,1)}, bf16[2,2,2,64,128]{4,3,2,1,0:T(8,128)(2,1)S(1)}, u32[]{:S(2)}, u32[]{:S(2)}) collective-permute-start(bf16[2,2,2,64,128]{4,3,2,1,0:T(8,128)(2,1)} %pad_maximum_fusion.1), channel_id=1, source_target_pairs={{0,4},{1,5},{2,6},{3,7},{4,0},{5,1},{6,2},{7,3},{8,12},{9,13},{10,... | collective-permute-start | bytes 393224 | tf_op jit(solution)/shard_map/ppermute | solution.py:76
  37.3 12.5 %collective-permute-start.22 = (bf16[2,2,2,64,128]{4,3,2,1,0:T(8,128)(2,1)}, bf16[2,2,2,64,128]{4,3,2,1,0:T(8,128)(2,1)S(1)}, u32[]{:S(2)}, u32[]{:S(2)}) collective-permute-start(bf16[2,2,2,64,128]{4,3,2,1,0:T(8,128)(2,1)} %pad_maximum_fusion.2), channel_id=1, source_target_pairs={{0,8},{1,9},{2,10},{3,11},{4,12},{5,13},{6,14},{7,15},{8,0},{9,1},... | collective-permute-start | bytes 393224 | tf_op jit(solution)/shard_map/ppermute | solution.py:76
  43.8 7.1 %collective-permute-start.23 = (bf16[2,2,2,64,128]{4,3,2,1,0:T(8,128)(2,1)S(1)}, bf16[2,2,2,64,128]{4,3,2,1,0:T(8,128)(2,1)S(1)}, u32[]{:S(2)}, u32[]{:S(2)}) collective-permute-start(bf16[2,2,2,64,128]{4,3,2,1,0:T(8,128)(2,1)S(1)} %pad_maximum_fusion.3), channel_id=1, source_target_pairs={{0,12},{1,13},{2,14},{3,15},{4,8},{5,9},{6,10},{7,11},{8,4},{9,5},... | collective-permute-start | bytes 393224 | tf_op jit(solution)/shard_map/ppermute | solution.py:76
  57.4 6.6 %collective-permute-start.25 = (bf16[128,1024]{1,0:T(8,128)(2,1)S(1)}, bf16[128,1024]{1,0:T(8,128)(2,1)S(1)}, u32[]{:S(2)}, u32[]{:S(2)}) collective-permute-start(bf16[128,1024]{1,0:T(8,128)(2,1)S(1)} %get-tuple-element.32), channel_id=1, source_target_pairs={{0,4},{4,8},{8,12},{12,14},{14,10},{10,6},{6,2},{2,0},{1,3},{5,1},... | collective-permute-start | bytes 786440 | tf_op jit(solution)/shard_map/ppermute | solution.py:76
  60.1 9.1 %collective-permute-start.29 = (bf16[128,1024]{1,0:T(8,128)(2,1)S(1)}, bf16[128,1024]{1,0:T(8,128)(2,1)S(1)}, u32[]{:S(2)}, u32[]{:S(2)}) collective-permute-start(bf16[128,1024]{1,0:T(8,128)(2,1)S(1)} %get-tuple-element.36), channel_id=1, source_target_pairs={{0,4},{4,8},{8,12},{12,14},{14,10},{10,6},{6,2},{2,0},{1,3},{5,1},... | collective-permute-start | bytes 786440 | tf_op jit(solution)/shard_map/ppermute | solution.py:76
  64.1 6.8 %collective-permute-start.26 = (bf16[128,1024]{1,0:T(8,128)(2,1)S(1)}, bf16[128,1024]{1,0:T(8,128)(2,1)S(1)}, u32[]{:S(2)}, u32[]{:S(2)}) collective-permute-start(bf16[128,1024]{1,0:T(8,128)(2,1)S(1)} %add_convert_fusion.5), channel_id=1, source_target_pairs={{0,4},{4,8},{8,12},{12,14},{14,10},{10,6},{6,2},{2,0},{1,3},{5,1},... | collective-permute-start | bytes 786440 | tf_op jit(solution)/shard_map/ppermute | solution.py:76
  70.9 7.6 %collective-permute-start.27 = (bf16[128,1024]{1,0:T(8,128)(2,1)S(1)}, bf16[128,1024]{1,0:T(8,128)(2,1)S(1)}, u32[]{:S(2)}, u32[]{:S(2)}) collective-permute-start(bf16[128,1024]{1,0:T(8,128)(2,1)S(1)} %add_convert_fusion.4), channel_id=1, source_target_pairs={{0,4},{4,8},{8,12},{12,14},{14,10},{10,6},{6,2},{2,0},{1,3},{5,1},... | collective-permute-start | bytes 786440 | tf_op jit(solution)/shard_map/ppermute | solution.py:76
  86.8 7.6 %collective-permute-start.34 = (bf16[128,1024]{1,0:T(8,128)(2,1)S(1)}, bf16[128,1024]{1,0:T(8,128)(2,1)S(1)}, u32[]{:S(2)}, u32[]{:S(2)}) collective-permute-start(bf16[128,1024]{1,0:T(8,128)(2,1)S(1)} %collective-permute-done.33.refs_8_), channel_id=1, source_target_pairs={{0,4},{4,8},{8,12},{12,14},{14,10},{10,6},{6,2},{2,0},{1,3},{5,1},... | collective-permute-start | bytes 786440 | tf_op jit(solution)/shard_map/ppermute | solution.py:76
  99.6 6.9 %collective-permute-start.41 = (bf16[128,1024]{1,0:T(8,128)(2,1)S(1)}, bf16[128,1024]{1,0:T(8,128)(2,1)S(1)}, u32[]{:S(2)}, u32[]{:S(2)}) collective-permute-start(bf16[128,1024]{1,0:T(8,128)(2,1)S(1)} %collective-permute-done.34.refs_2_), channel_id=1, source_target_pairs={{0,1},{1,0},{2,3},{3,2},{4,5},{5,4},{6,7},{7,6},{8,9},{9,8},{10,11... | collective-permute-start | bytes 786440 | tf_op jit(solution)/shard_map/ppermute | solution.py:76
  (26 other events, 180.8 us)

commit v9 on v8

--- a/solution.py
+++ b/solution.py
@@ -84,11 +84,13 @@
     return lax.optimization_barrier((array, others))[0]
 
 
-def ring_gather(own, ready=None, direct=False):
+def ring_gather(own, ready=None, direct=False, early=None):
     straight, swapped = own, None if direct else send(own, SWAP)
     crossed = own if direct else swapped
     mine = [own]
     for step in range(1, 5):
+        if step == 2 and early is not None:
+            straight = after(straight, early)
         if step == 4 and ready is not None:
             straight = after(straight, ready)
         straight = send(straight, ONWARD)
@@ -506,8 +508,8 @@
 
     weight_other = send(o_weight, SWAP)
     parts = split_cache(key_cache, value_cache, rank, rank_id)
-    mine, theirs = ring_gather(residual, weight_other, direct=True)
     weights = load_weights(ids, q_weight, kv_weight, width)
+    mine, theirs = ring_gather(residual, weight_other, direct=True, early=weights)
     cache = move_cache(parts)
 
     positions = (prefix[:, None] + jnp.arange(SPAN, dtype=jnp.int32)[None, :]).reshape(-1)

time: 116 us -> 120 us (1.034)
  starting transfers between devices: 49.3 us -> 40.4 us
  waiting for transfers between devices: 40.5 us -> 49.2 us
  local copies, waits for them, and re-layouts: 1.29 us -> 7.01 us
  other arithmetic: 3.84 us -> 2.43 us
    ppermute x47, starting transfers between devices: 49.3 us -> 40.4 us  [send(): return lax.ppermute(array, 'tp', pairs)]
    ppermute x47, waiting for transfers between devices: 40.5 us -> 49.2 us  [send(): return lax.ppermute(array, 'tp', pairs)]
    unnamed x6 -> x16, local copies, waits for them, and re-layouts: 0.02 us -> 6.71 us
  transfers between devices with their start and end apart: 47 -> 47, of which waited for: 19 -> 22; matrix products, arithmetic and copies ran while one was open for 4% -> 2% of each run, Pallas kernels for 13% -> 13%
where the time goes in v9:
time: 120 us
  waiting for transfers between devices  49.2 us (41%)
  starting transfers between devices  40.4 us (34%)
  Pallas kernels  20.3 us (17%)
  local copies, waits for them, and re-layouts  7.01 us (6%)
  other arithmetic  2.43 us (2%)
    ppermute x47, waiting for transfers between devices, send(): return lax.ppermute(array, 'tp', pairs)  49.2 us
    ppermute x47, starting transfers between devices, send(): return lax.ppermute(array, 'tp', pairs)  40.4 us
    unnamed x16, local copies, waits for them, and re-layouts  6.71 us
    pallas_call x2, Pallas kernels, more_shares(): pl.pallas_call(functools.partial(more_shares_kernel, first), out_shape=ou...  4.67 us
    pallas_call x1, Pallas kernels, load_weights(): pl.pallas_call(load_kernel, out_shape=jax.ShapeDtypeStruct((16, width, 2...  4.19 us
    pallas_call x1, Pallas kernels, final_norm(): pl.pallas_call(final_kernel, out_shape=jax.ShapeDtypeStruct((TOKENS, 16 *...  3.65 us
    pallas_call x1, Pallas kernels, project(): pl.pallas_call(project_kernel, out_shape=[jax.ShapeDtypeStruct((SPAN, HD)...  3.5 us
  transfers between devices with their start and end apart: 47, of which 22 were waited for; matrix products, arithmetic and copies ran while one was open for 2% of the time, Pallas kernels for 13%

profile of v9, /device:TPU:0, one launch (start us, length us, event | category | flops | bytes accessed | tf_op | source)
XLA Modules:
  0.0 119.9 jit_solution(17483593768034748227)
XLA Ops:
  0.5 2.6 %collective-permute-start.2 = (bf16[128,1024]{1,0:T(8,128)(2,1)}, bf16[128,1024]{1,0:T(8,128)(2,1)S(1)}, u32[]{:S(2)}, u32[]{:S(2)}) collective-permute-start(bf16[128,1024]{1,0:T(8,128)(2,1)} %refs_0_), channel_id=1, source_target_pairs={{0,4},{4,8},{8,12},{12,14},{14,10},{10,6},{6,2},{2,0},{1,3},{5,1},... | collective-permute-start | bytes 786440 | tf_op jit(solution)/shard_map/ppermute | solution.py:76
  4.9 4.2 %load_weights.1.refs_17_ = bf16[16,1024,256]{2,1,0:T(8,128)(2,1)S(1)} custom-call(s32[16]{0:T(128)S(1)} %stack.108.ids, bf16[16384,128]{1,0:T(8,128)(2,1)} %wq.1, bf16[16384,128]{1,0:T(8,128)(2,1)} %wkv.1), custom_call_target="tpu_custom_call" | custom-call | bytes 16777216 | tf_op jit(solution)/shard_map/load_weights/pallas_call | solution.py:240
  9.1 3.3 %copy-done = bf16[16,1024,256]{2,1,0:T(8,128)(2,1)} copy-done((bf16[16,1024,256]{2,1,0:T(8,128)(2,1)}, bf16[16,1024,256]{2,1,0:T(8,128)(2,1)S(1)}, u32[]{:S(2)}) %copy-start) | copy-done | bytes 8388632
  15.7 3.1 %collective-permute-done.4.refs_3_ = bf16[128,1024]{1,0:T(8,128)(2,1)S(1)} collective-permute-done((bf16[128,1024]{1,0:T(8,128)(2,1)S(1)}, bf16[128,1024]{1,0:T(8,128)(2,1)S(1)}, u32[]{:S(2)}, u32[]{:S(2)}) %collective-permute-start.4) | collective-permute-done | bytes 262176 | tf_op jit(solution)/shard_map/ppermute | solution.py:76
  22.5 4.3 %collective-permute-done.6.refs_5_ = bf16[128,1024]{1,0:T(8,128)(2,1)S(1)} collective-permute-done((bf16[128,1024]{1,0:T(8,128)(2,1)S(1)}, bf16[128,1024]{1,0:T(8,128)(2,1)S(1)}, u32[]{:S(2)}, u32[]{:S(2)}) %collective-permute-start.6) | collective-permute-done | bytes 262176 | tf_op jit(solution)/shard_map/ppermute | solution.py:76
  28.4 2.4 %collective-permute-done.1.refs_1_ = bf16[4,2,2,64,128]{4,3,2,1,0:T(8,128)(2,1)S(1)} collective-permute-done((bf16[4,2,2,64,128]{4,3,2,1,0:T(8,128)(2,1)S(1)}, bf16[4,2,2,64,128]{4,3,2,1,0:T(8,128)(2,1)S(1)}, u32[]{:S(2)}, u32[]{:S(2)}) %collective-permute-start.1) | collective-permute-done | bytes 262176 | tf_op jit(solution)/shard_map/ppermute | solution.py:76
  31.4 2.3 %collective-permute-done.7.refs_6_ = bf16[128,1024]{1,0:T(8,128)(2,1)} collective-permute-done((bf16[128,1024]{1,0:T(8,128)(2,1)S(1)}, bf16[128,1024]{1,0:T(8,128)(2,1)}, u32[]{:S(2)}, u32[]{:S(2)}) %collective-permute-start.7) | collective-permute-done | bytes 262176 | tf_op jit(solution)/shard_map/ppermute | solution.py:76
  33.7 2.8 %collective-permute-done.9.refs_7_ = bf16[128,1024]{1,0:T(8,128)(2,1)} collective-permute-done((bf16[128,1024]{1,0:T(8,128)(2,1)S(1)}, bf16[128,1024]{1,0:T(8,128)(2,1)}, u32[]{:S(2)}, u32[]{:S(2)}) %collective-permute-start.9) | collective-permute-done | bytes 262176 | tf_op jit(solution)/shard_map/ppermute | solution.py:76
  39.8 3.4 %copy-done.1 = bf16[16,1024,256]{2,1,0:T(8,128)(2,1)S(1)} copy-done((bf16[16,1024,256]{2,1,0:T(8,128)(2,1)S(1)}, bf16[16,1024,256]{2,1,0:T(8,128)(2,1)}, u32[]{:S(2)}) %copy-start.1) | copy-done | bytes 8388632
  43.1 3.5 %norm_project.1 = (bf16[64,128]{1,0:T(8,128)(2,1)S(1)}, bf16[64,128]{1,0:T(8,128)(2,1)S(1)}, bf16[128,128]{1,0:T(8,128)(2,1)S(1)}) custom-call(s32[16]{0:T(128)S(1)} %stack.108.ids, bf16[128,1024]{1,0:T(8,128)(2,1)S(1)} %copy-done.2, bf16[128,1024]{1,0:T(8,128)(2,1)S(1)} %collective-permute-done.2.refs_1_, ...), custom_call_target="tpu_custom_call" | custom-call | flops 1073741824 | bytes 12582912 | tf_op jit(solution)/shard_map/norm_project/pallas_call | solution.py:276
  47.3 3.9 %collective-permute-start.23 = (bf16[2,2,2,64,128]{4,3,2,1,0:T(8,128)(2,1)S(1)}, bf16[2,2,2,64,128]{4,3,2,1,0:T(8,128)(2,1)S(1)}, u32[]{:S(2)}, u32[]{:S(2)}) collective-permute-start(bf16[2,2,2,64,128]{4,3,2,1,0:T(8,128)(2,1)S(1)} %pad_maximum_fusion.3), channel_id=1, source_target_pairs={{0,12},{1,13},{2,14},{3,15},{4,8},{5,9},{6,10},{7,11},{8,4},{9,5},... | collective-permute-start | bytes 393224 | tf_op jit(solution)/shard_map/ppermute | solution.py:76
  61.0 3.0 %collective-permute-start.25 = (bf16[128,1024]{1,0:T(8,128)(2,1)S(1)}, bf16[128,1024]{1,0:T(8,128)(2,1)S(1)}, u32[]{:S(2)}, u32[]{:S(2)}) collective-permute-start(bf16[128,1024]{1,0:T(8,128)(2,1)S(1)} %get-tuple-element.34), channel_id=1, source_target_pairs={{0,4},{4,8},{8,12},{12,14},{14,10},{10,6},{6,2},{2,0},{1,3},{5,1},... | collective-permute-start | bytes 786440 | tf_op jit(solution)/shard_map/ppermute | solution.py:76
  64.7 2.1 %shares_2.1 = (f32[128,1024]{1,0:T(8,128)S(1)}, f32[128,1024]{1,0:T(8,128)S(1)}) custom-call(s32[1]{0:T(128)} %bitcast.16.core, s32[8]{0:T(128)S(1)} %stack.117.to, bf16[64,256]{1,0:T(8,128)(2,1)S(1)} %attend.1.attn, bf16[64,256]{1,0:T(8,128)(2,1)S(1)} %collective-permute-done.24.attn_other, bf16[128,16384]{1,0:T(8,128)(2,1)} %weight.3, ...), custom_call_target="tpu_custom_call" | custom-call | flops 134217728 | bytes 2097152 | tf_op jit(solution)/shard_map/shares_2/pallas_call | solution.py:440
  67.9 2.5 %collective-permute-start.26 = (bf16[128,1024]{1,0:T(8,128)(2,1)S(1)}, bf16[128,1024]{1,0:T(8,128)(2,1)S(1)}, u32[]{:S(2)}, u32[]{:S(2)}) collective-permute-start(bf16[128,1024]{1,0:T(8,128)(2,1)S(1)} %add_convert_fusion.5), channel_id=1, source_target_pairs={{0,4},{4,8},{8,12},{12,14},{14,10},{10,6},{6,2},{2,0},{1,3},{5,1},... | collective-permute-start | bytes 786440 | tf_op jit(solution)/shard_map/ppermute | solution.py:76
  70.5 2.6 %shares_4.1 = (f32[128,1024]{1,0:T(8,128)S(1)}, f32[128,1024]{1,0:T(8,128)S(1)}, f32[128,1024]{1,0:T(8,128)S(1)}, f32[128,1024]{1,0:T(8,128)S(1)}) custom-call(s32[1]{0:T(128)} %bitcast.16.core, s32[8]{0:T(128)S(1)} %stack.117.to, bf16[64,256]{1,0:T(8,128)(2,1)S(1)} %attend.1.attn, bf16[64,256]{1,0:T(8,128)(2,1)S(1)} %collective-permute-done.24.attn_other, ...), custom_call_target="tpu_custom_call" | custom-call | flops 268435456 | bytes 4194304 | tf_op jit(solution)/shard_map/shares_4/pallas_call | solution.py:440
  74.4 2.5 %collective-permute-start.27 = (bf16[128,1024]{1,0:T(8,128)(2,1)S(1)}, bf16[128,1024]{1,0:T(8,128)(2,1)S(1)}, u32[]{:S(2)}, u32[]{:S(2)}) collective-permute-start(bf16[128,1024]{1,0:T(8,128)(2,1)S(1)} %add_convert_fusion.4), channel_id=1, source_target_pairs={{0,4},{4,8},{8,12},{12,14},{14,10},{10,6},{6,2},{2,0},{1,3},{5,1},... | collective-permute-start | bytes 786440 | tf_op jit(solution)/shard_map/ppermute | solution.py:76
  77.0 2.6 %collective-permute-done.30 = bf16[128,1024]{1,0:T(8,128)(2,1)S(1)} collective-permute-done((bf16[128,1024]{1,0:T(8,128)(2,1)S(1)}, bf16[128,1024]{1,0:T(8,128)(2,1)S(1)}, u32[]{:S(2)}, u32[]{:S(2)}) %collective-permute-start.30) | collective-permute-done | bytes 262176 | tf_op jit(solution)/shard_map/ppermute | solution.py:76
  79.7 2.7 %collective-permute-done.27 = bf16[128,1024]{1,0:T(8,128)(2,1)S(1)} collective-permute-done((bf16[128,1024]{1,0:T(8,128)(2,1)S(1)}, bf16[128,1024]{1,0:T(8,128)(2,1)S(1)}, u32[]{:S(2)}, u32[]{:S(2)}) %collective-permute-start.27) | collective-permute-done | bytes 262176 | tf_op jit(solution)/shard_map/ppermute | solution.py:76
  85.5 3.4 %collective-permute-done.28 = bf16[128,1024]{1,0:T(8,128)(2,1)S(1)} collective-permute-done((bf16[128,1024]{1,0:T(8,128)(2,1)S(1)}, bf16[128,1024]{1,0:T(8,128)(2,1)S(1)}, u32[]{:S(2)}, u32[]{:S(2)}) %collective-permute-start.28) | collective-permute-done | bytes 262176 | tf_op jit(solution)/shard_map/ppermute | solution.py:76
  91.6 4.0 %collective-permute-done.32.refs_1_ = bf16[128,1024]{1,0:T(8,128)(2,1)S(1)} collective-permute-done((bf16[128,1024]{1,0:T(8,128)(2,1)S(1)}, bf16[128,1024]{1,0:T(8,128)(2,1)S(1)}, u32[]{:S(2)}, u32[]{:S(2)}) %collective-permute-start.32) | collective-permute-done | bytes 262176 | tf_op jit(solution)/shard_map/ppermute | solution.py:76
  99.3 2.6 %collective-permute-done.35.refs_3_ = bf16[128,1024]{1,0:T(8,128)(2,1)S(1)} collective-permute-done((bf16[128,1024]{1,0:T(8,128)(2,1)S(1)}, bf16[128,1024]{1,0:T(8,128)(2,1)S(1)}, u32[]{:S(2)}, u32[]{:S(2)}) %collective-permute-start.35) | collective-permute-done | bytes 262176 | tf_op jit(solution)/shard_map/ppermute | solution.py:76
  105.7 2.6 %collective-permute-done.37.refs_5_ = bf16[128,1024]{1,0:T(8,128)(2,1)S(1)} collective-permute-done((bf16[128,1024]{1,0:T(8,128)(2,1)S(1)}, bf16[128,1024]{1,0:T(8,128)(2,1)S(1)}, u32[]{:S(2)}, u32[]{:S(2)}) %collective-permute-start.37) | collective-permute-done | bytes 262176 | tf_op jit(solution)/shard_map/ppermute | solution.py:76
  111.1 3.6 %collective-permute-done.39.refs_7_ = bf16[128,1024]{1,0:T(8,128)(2,1)S(1)} collective-permute-done((bf16[128,1024]{1,0:T(8,128)(2,1)S(1)}, bf16[128,1024]{1,0:T(8,128)(2,1)S(1)}, u32[]{:S(2)}, u32[]{:S(2)}) %collective-permute-start.39) | collective-permute-done | bytes 262176 | tf_op jit(solution)/shard_map/ppermute | solution.py:76
  116.2 3.6 %final_norm.1 = bf16[128,16384]{1,0:T(8,128)(2,1)} custom-call(s32[16]{0:T(128)S(1)} %stack.108.ids, bf16[128,1024]{1,0:T(8,128)(2,1)S(1)} %add_convert_fusion.refs_0_, bf16[128,1024]{1,0:T(8,128)(2,1)S(1)} %collective-permute-done.32.refs_1_, bf16[128,1024]{1,0:T(8,128)(2,1)S(1)} %collective-permute-done.34.refs_2_, ...), custom_call_target="tpu_custom_call" | custom-call | flops 16777216 | bytes 12582912 | tf_op jit(solution)/shard_map/final_norm/pallas_call | solution.py:481
  (119 shorter events, 45.8 us)
Async XLA Ops:
  0.0 26.8 %collective-permute-start.8 = (bf16[128,16384]{1,0:T(8,128)(2,1)}, bf16[128,16384]{1,0:T(8,128)(2,1)}, u32[]{:S(2)}, u32[]{:S(2)}) collective-permute-start(bf16[128,16384]{1,0:T(8,128)(2,1)} %weight.3), channel_id=1, source_target_pairs={{0,1},{1,0},{2,3},{3,2},{4,5},{5,4},{6,7},{7,6},{8,9},{9,8},{10,11... | collective-permute-start | bytes 12582920 | tf_op jit(solution)/shard_map/ppermute | solution.py:76
  0.5 11.9 %collective-permute-start.2 = (bf16[128,1024]{1,0:T(8,128)(2,1)}, bf16[128,1024]{1,0:T(8,128)(2,1)S(1)}, u32[]{:S(2)}, u32[]{:S(2)}) collective-permute-start(bf16[128,1024]{1,0:T(8,128)(2,1)} %refs_0_), channel_id=1, source_target_pairs={{0,4},{4,8},{8,12},{12,14},{14,10},{10,6},{6,2},{2,0},{1,3},{5,1},... | collective-permute-start | bytes 786440 | tf_op jit(solution)/shard_map/ppermute | solution.py:76
  3.0 11.2 %collective-permute-start.3 = (bf16[128,1024]{1,0:T(8,128)(2,1)}, bf16[128,1024]{1,0:T(8,128)(2,1)S(1)}, u32[]{:S(2)}, u32[]{:S(2)}) collective-permute-start(bf16[128,1024]{1,0:T(8,128)(2,1)} %refs_0_), channel_id=1, source_target_pairs={{0,3},{4,1},{8,5},{12,9},{14,13},{10,15},{6,11},{2,7},{1,4},{5,8},... | collective-permute-start | bytes 786440 | tf_op jit(solution)/shard_map/ppermute | solution.py:76
  4.4 22.4 %collective-permute-start.10 = (bf16[128,1024]{1,0:T(8,128)(2,1)}, bf16[128,1024]{1,0:T(8,128)(2,1)S(1)}, u32[]{:S(2)}, u32[]{:S(2)}) collective-permute-start(bf16[128,1024]{1,0:T(8,128)(2,1)} %refs_0_), channel_id=1, source_target_pairs={{0,1},{1,0},{2,3},{3,2},{4,5},{5,4},{6,7},{7,6},{8,9},{9,8},{10,11... | collective-permute-start | bytes 786440 | tf_op jit(solution)/shard_map/ppermute | solution.py:76
  12.4 6.4 %collective-permute-start.4 = (bf16[128,1024]{1,0:T(8,128)(2,1)S(1)}, bf16[128,1024]{1,0:T(8,128)(2,1)S(1)}, u32[]{:S(2)}, u32[]{:S(2)}) collective-permute-start(bf16[128,1024]{1,0:T(8,128)(2,1)S(1)} %collective-permute-done.2.refs_1_), channel_id=1, source_target_pairs={{0,4},{4,8},{8,12},{12,14},{14,10},{10,6},{6,2},{2,0},{1,3},{5,1},... | collective-permute-start | bytes 786440 | tf_op jit(solution)/shard_map/ppermute | solution.py:76
  14.1 6.8 %collective-permute-start = (bf16[2,64,1024]{2,1,0:T(8,128)(2,1)S(1)}, bf16[2,64,1024]{2,1,0:T(8,128)(2,1)S(1)}, u32[]{:S(2)}, u32[]{:S(2)}) collective-permute-start(bf16[2,64,1024]{2,1,0:T(8,128)(2,1)S(1)} %pad_maximum_fusion), channel_id=1, source_target_pairs={{0,1},{1,0},{2,3},{3,2},{4,5},{5,4},{6,7},{7,6},{8,9},{9,8},{10,11... | collective-permute-start | bytes 786440 | tf_op jit(solution)/shard_map/ppermute | solution.py:76
  14.2 8.2 %collective-permute-start.5 = (bf16[128,1024]{1,0:T(8,128)(2,1)S(1)}, bf16[128,1024]{1,0:T(8,128)(2,1)S(1)}, u32[]{:S(2)}, u32[]{:S(2)}) collective-permute-start(bf16[128,1024]{1,0:T(8,128)(2,1)S(1)} %collective-permute-done.3.refs_2_), channel_id=1, source_target_pairs={{0,4},{4,8},{8,12},{12,14},{14,10},{10,6},{6,2},{2,0},{1,3},{5,1},... | collective-permute-start | bytes 786440 | tf_op jit(solution)/shard_map/ppermute | solution.py:76
  18.8 7.9 %collective-permute-start.6 = (bf16[128,1024]{1,0:T(8,128)(2,1)S(1)}, bf16[128,1024]{1,0:T(8,128)(2,1)S(1)}, u32[]{:S(2)}, u32[]{:S(2)}) collective-permute-start(bf16[128,1024]{1,0:T(8,128)(2,1)S(1)} %collective-permute-done.4.refs_3_), channel_id=1, source_target_pairs={{0,4},{4,8},{8,12},{12,14},{14,10},{10,6},{6,2},{2,0},{1,3},{5,1},... | collective-permute-start | bytes 786440 | tf_op jit(solution)/shard_map/ppermute | solution.py:76
  22.0 8.9 %collective-permute-start.1 = (bf16[4,2,2,64,128]{4,3,2,1,0:T(8,128)(2,1)S(1)}, bf16[4,2,2,64,128]{4,3,2,1,0:T(8,128)(2,1)S(1)}, u32[]{:S(2)}, u32[]{:S(2)}) collective-permute-start(bf16[4,2,2,64,128]{4,3,2,1,0:T(8,128)(2,1)S(1)} %get-tuple-element.23), channel_id=1, source_target_pairs={{0,2},{1,3},{2,0},{3,1},{4,6},{5,7},{6,4},{7,5},{8,10},{9,11},{10,... | collective-permute-start | bytes 786440 | tf_op jit(solution)/shard_map/ppermute | solution.py:76
  22.5 8.4 %collective-permute-start.11 = (bf16[128,1024]{1,0:T(8,128)(2,1)S(1)}, bf16[128,1024]{1,0:T(8,128)(2,1)S(1)}, u32[]{:S(2)}, u32[]{:S(2)}) collective-permute-start(bf16[128,1024]{1,0:T(8,128)(2,1)S(1)} %collective-permute-done.2.refs_1_), channel_id=1, source_target_pairs={{0,1},{1,0},{2,3},{3,2},{4,5},{5,4},{6,7},{7,6},{8,9},{9,8},{10,11... | collective-permute-start | bytes 786440 | tf_op jit(solution)/shard_map/ppermute | solution.py:76
  26.8 7.0 %collective-permute-start.7 = (bf16[128,1024]{1,0:T(8,128)(2,1)S(1)}, bf16[128,1024]{1,0:T(8,128)(2,1)}, u32[]{:S(2)}, u32[]{:S(2)}) collective-permute-start(bf16[128,1024]{1,0:T(8,128)(2,1)S(1)} %collective-permute-done.5.refs_4_), channel_id=1, source_target_pairs={{0,4},{4,8},{8,12},{12,14},{14,10},{10,6},{6,2},{2,0},{1,3},{5,1},... | collective-permute-start | bytes 786440 | tf_op jit(solution)/shard_map/ppermute | solution.py:76
  26.8 9.8 %collective-permute-start.9 = (bf16[128,1024]{1,0:T(8,128)(2,1)S(1)}, bf16[128,1024]{1,0:T(8,128)(2,1)}, u32[]{:S(2)}, u32[]{:S(2)}) collective-permute-start(bf16[128,1024]{1,0:T(8,128)(2,1)S(1)} %collective-permute-done.6.refs_5_), channel_id=1, source_target_pairs={{0,4},{4,8},{8,12},{12,14},{14,10},{10,6},{6,2},{2,0},{1,3},{5,1},... | collective-permute-start | bytes 786440 | tf_op jit(solution)/shard_map/ppermute | solution.py:76
  30.8 7.1 %collective-permute-start.13 = (bf16[128,1024]{1,0:T(8,128)(2,1)S(1)}, bf16[128,1024]{1,0:T(8,128)(2,1)S(1)}, u32[]{:S(2)}, u32[]{:S(2)}) collective-permute-start(bf16[128,1024]{1,0:T(8,128)(2,1)S(1)} %collective-permute-done.4.refs_3_), channel_id=1, source_target_pairs={{0,1},{1,0},{2,3},{3,2},{4,5},{5,4},{6,7},{7,6},{8,9},{9,8},{10,11... | collective-permute-start | bytes 786440 | tf_op jit(solution)/shard_map/ppermute | solution.py:76
  30.8 7.1 %collective-permute-start.14 = (bf16[128,1024]{1,0:T(8,128)(2,1)S(1)}, bf16[128,1024]{1,0:T(8,128)(2,1)S(1)}, u32[]{:S(2)}, u32[]{:S(2)}) collective-permute-start(bf16[128,1024]{1,0:T(8,128)(2,1)S(1)} %collective-permute-done.5.refs_4_), channel_id=1, source_target_pairs={{0,1},{1,0},{2,3},{3,2},{4,5},{5,4},{6,7},{7,6},{8,9},{9,8},{10,11... | collective-permute-start | bytes 786440 | tf_op jit(solution)/shard_map/ppermute | solution.py:76
  31.3 8.4 %collective-permute-start.15 = (bf16[128,1024]{1,0:T(8,128)(2,1)S(1)}, bf16[128,1024]{1,0:T(8,128)(2,1)S(1)}, u32[]{:S(2)}, u32[]{:S(2)}) collective-permute-start(bf16[128,1024]{1,0:T(8,128)(2,1)S(1)} %collective-permute-done.6.refs_5_), channel_id=1, source_target_pairs={{0,1},{1,0},{2,3},{3,2},{4,5},{5,4},{6,7},{7,6},{8,9},{9,8},{10,11... | collective-permute-start | bytes 786440 | tf_op jit(solution)/shard_map/ppermute | solution.py:76
  37.9 14.9 %collective-permute-start.21 = (bf16[2,2,2,64,128]{4,3,2,1,0:T(8,128)(2,1)}, bf16[2,2,2,64,128]{4,3,2,1,0:T(8,128)(2,1)S(1)}, u32[]{:S(2)}, u32[]{:S(2)}) collective-permute-start(bf16[2,2,2,64,128]{4,3,2,1,0:T(8,128)(2,1)} %pad_maximum_fusion.1), channel_id=1, source_target_pairs={{0,4},{1,5},{2,6},{3,7},{4,0},{5,1},{6,2},{7,3},{8,12},{9,13},{10,... | collective-permute-start | bytes 393224 | tf_op jit(solution)/shard_map/ppermute | solution.py:76
  37.9 14.9 %collective-permute-start.22 = (bf16[2,2,2,64,128]{4,3,2,1,0:T(8,128)(2,1)}, bf16[2,2,2,64,128]{4,3,2,1,0:T(8,128)(2,1)S(1)}, u32[]{:S(2)}, u32[]{:S(2)}) collective-permute-start(bf16[2,2,2,64,128]{4,3,2,1,0:T(8,128)(2,1)} %pad_maximum_fusion.2), channel_id=1, source_target_pairs={{0,8},{1,9},{2,10},{3,11},{4,12},{5,13},{6,14},{7,15},{8,0},{9,1},... | collective-permute-start | bytes 393224 | tf_op jit(solution)/shard_map/ppermute | solution.py:76
  47.3 7.5 %collective-permute-start.23 = (bf16[2,2,2,64,128]{4,3,2,1,0:T(8,128)(2,1)S(1)}, bf16[2,2,2,64,128]{4,3,2,1,0:T(8,128)(2,1)S(1)}, u32[]{:S(2)}, u32[]{:S(2)}) collective-permute-start(bf16[2,2,2,64,128]{4,3,2,1,0:T(8,128)(2,1)S(1)} %pad_maximum_fusion.3), channel_id=1, source_target_pairs={{0,12},{1,13},{2,14},{3,15},{4,8},{5,9},{6,10},{7,11},{8,4},{9,5},... | collective-permute-start | bytes 393224 | tf_op jit(solution)/shard_map/ppermute | solution.py:76
  61.0 6.9 %collective-permute-start.25 = (bf16[128,1024]{1,0:T(8,128)(2,1)S(1)}, bf16[128,1024]{1,0:T(8,128)(2,1)S(1)}, u32[]{:S(2)}, u32[]{:S(2)}) collective-permute-start(bf16[128,1024]{1,0:T(8,128)(2,1)S(1)} %get-tuple-element.34), channel_id=1, source_target_pairs={{0,4},{4,8},{8,12},{12,14},{14,10},{10,6},{6,2},{2,0},{1,3},{5,1},... | collective-permute-start | bytes 786440 | tf_op jit(solution)/shard_map/ppermute | solution.py:76
  64.0 9.1 %collective-permute-start.29 = (bf16[128,1024]{1,0:T(8,128)(2,1)S(1)}, bf16[128,1024]{1,0:T(8,128)(2,1)S(1)}, u32[]{:S(2)}, u32[]{:S(2)}) collective-permute-start(bf16[128,1024]{1,0:T(8,128)(2,1)S(1)} %get-tuple-element.38), channel_id=1, source_target_pairs={{0,4},{4,8},{8,12},{12,14},{14,10},{10,6},{6,2},{2,0},{1,3},{5,1},... | collective-permute-start | bytes 786440 | tf_op jit(solution)/shard_map/ppermute | solution.py:76
  67.9 6.4 %collective-permute-start.26 = (bf16[128,1024]{1,0:T(8,128)(2,1)S(1)}, bf16[128,1024]{1,0:T(8,128)(2,1)S(1)}, u32[]{:S(2)}, u32[]{:S(2)}) collective-permute-start(bf16[128,1024]{1,0:T(8,128)(2,1)S(1)} %add_convert_fusion.5), channel_id=1, source_target_pairs={{0,4},{4,8},{8,12},{12,14},{14,10},{10,6},{6,2},{2,0},{1,3},{5,1},... | collective-permute-start | bytes 786440 | tf_op jit(solution)/shard_map/ppermute | solution.py:76
  74.4 8.0 %collective-permute-start.27 = (bf16[128,1024]{1,0:T(8,128)(2,1)S(1)}, bf16[128,1024]{1,0:T(8,128)(2,1)S(1)}, u32[]{:S(2)}, u32[]{:S(2)}) collective-permute-start(bf16[128,1024]{1,0:T(8,128)(2,1)S(1)} %add_convert_fusion.4), channel_id=1, source_target_pairs={{0,4},{4,8},{8,12},{12,14},{14,10},{10,6},{6,2},{2,0},{1,3},{5,1},... | collective-permute-start | bytes 786440 | tf_op jit(solution)/shard_map/ppermute | solution.py:76
  90.6 7.7 %collective-permute-start.34 = (bf16[128,1024]{1,0:T(8,128)(2,1)S(1)}, bf16[128,1024]{1,0:T(8,128)(2,1)S(1)}, u32[]{:S(2)}, u32[]{:S(2)}) collective-permute-start(bf16[128,1024]{1,0:T(8,128)(2,1)S(1)} %collective-permute-done.33.refs_8_), channel_id=1, source_target_pairs={{0,4},{4,8},{8,12},{12,14},{14,10},{10,6},{6,2},{2,0},{1,3},{5,1},... | collective-permute-start | bytes 786440 | tf_op jit(solution)/shard_map/ppermute | solution.py:76
  102.9 6.9 %collective-permute-start.41 = (bf16[128,1024]{1,0:T(8,128)(2,1)S(1)}, bf16[128,1024]{1,0:T(8,128)(2,1)S(1)}, u32[]{:S(2)}, u32[]{:S(2)}) collective-permute-start(bf16[128,1024]{1,0:T(8,128)(2,1)S(1)} %collective-permute-done.34.refs_2_), channel_id=1, source_target_pairs={{0,1},{1,0},{2,3},{3,2},{4,5},{5,4},{6,7},{7,6},{8,9},{9,8},{10,11... | collective-permute-start | bytes 786440 | tf_op jit(solution)/shard_map/ppermute | solution.py:76
  (31 other events, 247.4 us)

commit v10 on v9

--- a/solution.py
+++ b/solution.py
@@ -239,7 +239,7 @@
 def load_weights(ids, wq, wkv, width):
     return pl.pallas_call(
         load_kernel,
-        out_shape=jax.ShapeDtypeStruct((16, width, 2 * HD), jnp.bfloat16),
+        out_shape=pltpu.VMEM((16, width, 2 * HD), jnp.bfloat16),
         in_specs=[SMEM] + [HBM] * 2,
         out_specs=VMEM,
         scratch_shapes=[pltpu.SemaphoreType.DMA((2, 16))],
@@ -284,7 +284,7 @@
             flops=2 * TOKENS * weights.size, bytes_accessed=12 * MIB, transcendentals=0
         ),
         name="norm_project",
-    )(ids, *arrays, gain, weights, *tables)
+    )(ids, *arrays, gain, pltpu.with_memory_space_constraint(weights, pltpu.VMEM), *tables)
 
 
 def share_copies(to, first, weight, weight_other, out, sems):

time: 120 us -> 120 us (level)
  no operation moved by 1% of the time
where the time goes in v10:
time: 120 us
  waiting for transfers between devices  49.2 us (41%)
  starting transfers between devices  40.4 us (34%)
  Pallas kernels  20.3 us (17%)
  local copies, waits for them, and re-layouts  7.01 us (6%)
  other arithmetic  2.43 us (2%)
    ppermute x47, waiting for transfers between devices, send(): return lax.ppermute(array, 'tp', pairs)  49.2 us
    ppermute x47, starting transfers between devices, send(): return lax.ppermute(array, 'tp', pairs)  40.4 us
    unnamed x16, local copies, waits for them, and re-layouts  6.71 us
    pallas_call x2, Pallas kernels, more_shares(): pl.pallas_call(functools.partial(more_shares_kernel, first), out_shape=ou...  4.67 us
    pallas_call x1, Pallas kernels, load_weights(): pl.pallas_call(load_kernel, out_shape=pltpu.VMEM((16, width, 2 * HD), jnp...  4.19 us
    pallas_call x1, Pallas kernels, final_norm(): pl.pallas_call(final_kernel, out_shape=jax.ShapeDtypeStruct((TOKENS, 16 *...  3.65 us
    pallas_call x1, Pallas kernels, project(): pl.pallas_call(project_kernel, out_shape=[jax.ShapeDtypeStruct((SPAN, HD)...  3.5 us
  transfers between devices with their start and end apart: 47, of which 22 were waited for; matrix products, arithmetic and copies ran while one was open for 2% of the time, Pallas kernels for 13%

profile of v10, /device:TPU:0, one launch (start us, length us, event | category | flops | bytes accessed | tf_op | source)
XLA Modules:
  0.0 119.9 jit_solution(17483593768034748227)
XLA Ops:
  0.5 2.6 %collective-permute-start.2 = (bf16[128,1024]{1,0:T(8,128)(2,1)}, bf16[128,1024]{1,0:T(8,128)(2,1)S(1)}, u32[]{:S(2)}, u32[]{:S(2)}) collective-permute-start(bf16[128,1024]{1,0:T(8,128)(2,1)} %refs_0_), channel_id=1, source_target_pairs={{0,4},{4,8},{8,12},{12,14},{14,10},{10,6},{6,2},{2,0},{1,3},{5,1},... | collective-permute-start | bytes 786440 | tf_op jit(solution)/shard_map/ppermute | solution.py:76
  4.9 4.2 %load_weights.1.refs_17_ = bf16[16,1024,256]{2,1,0:T(8,128)(2,1)S(1)} custom-call(s32[16]{0:T(128)S(1)} %stack.108.ids, bf16[16384,128]{1,0:T(8,128)(2,1)} %wq.1, bf16[16384,128]{1,0:T(8,128)(2,1)} %wkv.1), custom_call_target="tpu_custom_call" | custom-call | bytes 16777216 | tf_op jit(solution)/shard_map/load_weights/pallas_call | solution.py:240
  9.1 3.3 %copy-done = bf16[16,1024,256]{2,1,0:T(8,128)(2,1)} copy-done((bf16[16,1024,256]{2,1,0:T(8,128)(2,1)}, bf16[16,1024,256]{2,1,0:T(8,128)(2,1)S(1)}, u32[]{:S(2)}) %copy-start) | copy-done | bytes 8388632
  15.7 3.1 %collective-permute-done.4.refs_3_ = bf16[128,1024]{1,0:T(8,128)(2,1)S(1)} collective-permute-done((bf16[128,1024]{1,0:T(8,128)(2,1)S(1)}, bf16[128,1024]{1,0:T(8,128)(2,1)S(1)}, u32[]{:S(2)}, u32[]{:S(2)}) %collective-permute-start.4) | collective-permute-done | bytes 262176 | tf_op jit(solution)/shard_map/ppermute | solution.py:76
  22.5 4.3 %collective-permute-done.6.refs_5_ = bf16[128,1024]{1,0:T(8,128)(2,1)S(1)} collective-permute-done((bf16[128,1024]{1,0:T(8,128)(2,1)S(1)}, bf16[128,1024]{1,0:T(8,128)(2,1)S(1)}, u32[]{:S(2)}, u32[]{:S(2)}) %collective-permute-start.6) | collective-permute-done | bytes 262176 | tf_op jit(solution)/shard_map/ppermute | solution.py:76
  28.4 2.4 %collective-permute-done.1.refs_1_ = bf16[4,2,2,64,128]{4,3,2,1,0:T(8,128)(2,1)S(1)} collective-permute-done((bf16[4,2,2,64,128]{4,3,2,1,0:T(8,128)(2,1)S(1)}, bf16[4,2,2,64,128]{4,3,2,1,0:T(8,128)(2,1)S(1)}, u32[]{:S(2)}, u32[]{:S(2)}) %collective-permute-start.1) | collective-permute-done | bytes 262176 | tf_op jit(solution)/shard_map/ppermute | solution.py:76
  31.4 2.3 %collective-permute-done.7.refs_6_ = bf16[128,1024]{1,0:T(8,128)(2,1)} collective-permute-done((bf16[128,1024]{1,0:T(8,128)(2,1)S(1)}, bf16[128,1024]{1,0:T(8,128)(2,1)}, u32[]{:S(2)}, u32[]{:S(2)}) %collective-permute-start.7) | collective-permute-done | bytes 262176 | tf_op jit(solution)/shard_map/ppermute | solution.py:76
  33.7 2.8 %collective-permute-done.9.refs_7_ = bf16[128,1024]{1,0:T(8,128)(2,1)} collective-permute-done((bf16[128,1024]{1,0:T(8,128)(2,1)S(1)}, bf16[128,1024]{1,0:T(8,128)(2,1)}, u32[]{:S(2)}, u32[]{:S(2)}) %collective-permute-start.9) | collective-permute-done | bytes 262176 | tf_op jit(solution)/shard_map/ppermute | solution.py:76
  39.8 3.4 %copy-done.1 = bf16[16,1024,256]{2,1,0:T(8,128)(2,1)S(1)} copy-done((bf16[16,1024,256]{2,1,0:T(8,128)(2,1)S(1)}, bf16[16,1024,256]{2,1,0:T(8,128)(2,1)}, u32[]{:S(2)}) %copy-start.1) | copy-done | bytes 8388632
  43.1 3.5 %norm_project.1 = (bf16[64,128]{1,0:T(8,128)(2,1)S(1)}, bf16[64,128]{1,0:T(8,128)(2,1)S(1)}, bf16[128,128]{1,0:T(8,128)(2,1)S(1)}) custom-call(s32[16]{0:T(128)S(1)} %stack.108.ids, bf16[128,1024]{1,0:T(8,128)(2,1)S(1)} %copy-done.2, bf16[128,1024]{1,0:T(8,128)(2,1)S(1)} %collective-permute-done.2.refs_1_, ...), custom_call_target="tpu_custom_call" | custom-call | flops 1073741824 | bytes 12582912 | tf_op jit(solution)/shard_map/norm_project/pallas_call | solution.py:276
  47.3 3.9 %collective-permute-start.23 = (bf16[2,2,2,64,128]{4,3,2,1,0:T(8,128)(2,1)S(1)}, bf16[2,2,2,64,128]{4,3,2,1,0:T(8,128)(2,1)S(1)}, u32[]{:S(2)}, u32[]{:S(2)}) collective-permute-start(bf16[2,2,2,64,128]{4,3,2,1,0:T(8,128)(2,1)S(1)} %pad_maximum_fusion.3), channel_id=1, source_target_pairs={{0,12},{1,13},{2,14},{3,15},{4,8},{5,9},{6,10},{7,11},{8,4},{9,5},... | collective-permute-start | bytes 393224 | tf_op jit(solution)/shard_map/ppermute | solution.py:76
  61.0 3.0 %collective-permute-start.25 = (bf16[128,1024]{1,0:T(8,128)(2,1)S(1)}, bf16[128,1024]{1,0:T(8,128)(2,1)S(1)}, u32[]{:S(2)}, u32[]{:S(2)}) collective-permute-start(bf16[128,1024]{1,0:T(8,128)(2,1)S(1)} %get-tuple-element.34), channel_id=1, source_target_pairs={{0,4},{4,8},{8,12},{12,14},{14,10},{10,6},{6,2},{2,0},{1,3},{5,1},... | collective-permute-start | bytes 786440 | tf_op jit(solution)/shard_map/ppermute | solution.py:76
  64.7 2.1 %shares_2.1 = (f32[128,1024]{1,0:T(8,128)S(1)}, f32[128,1024]{1,0:T(8,128)S(1)}) custom-call(s32[1]{0:T(128)} %bitcast.16.core, s32[8]{0:T(128)S(1)} %stack.117.to, bf16[64,256]{1,0:T(8,128)(2,1)S(1)} %attend.1.attn, bf16[64,256]{1,0:T(8,128)(2,1)S(1)} %collective-permute-done.24.attn_other, bf16[128,16384]{1,0:T(8,128)(2,1)} %weight.3, ...), custom_call_target="tpu_custom_call" | custom-call | flops 134217728 | bytes 2097152 | tf_op jit(solution)/shard_map/shares_2/pallas_call | solution.py:440
  67.9 2.5 %collective-permute-start.26 = (bf16[128,1024]{1,0:T(8,128)(2,1)S(1)}, bf16[128,1024]{1,0:T(8,128)(2,1)S(1)}, u32[]{:S(2)}, u32[]{:S(2)}) collective-permute-start(bf16[128,1024]{1,0:T(8,128)(2,1)S(1)} %add_convert_fusion.5), channel_id=1, source_target_pairs={{0,4},{4,8},{8,12},{12,14},{14,10},{10,6},{6,2},{2,0},{1,3},{5,1},... | collective-permute-start | bytes 786440 | tf_op jit(solution)/shard_map/ppermute | solution.py:76
  70.5 2.6 %shares_4.1 = (f32[128,1024]{1,0:T(8,128)S(1)}, f32[128,1024]{1,0:T(8,128)S(1)}, f32[128,1024]{1,0:T(8,128)S(1)}, f32[128,1024]{1,0:T(8,128)S(1)}) custom-call(s32[1]{0:T(128)} %bitcast.16.core, s32[8]{0:T(128)S(1)} %stack.117.to, bf16[64,256]{1,0:T(8,128)(2,1)S(1)} %attend.1.attn, bf16[64,256]{1,0:T(8,128)(2,1)S(1)} %collective-permute-done.24.attn_other, ...), custom_call_target="tpu_custom_call" | custom-call | flops 268435456 | bytes 4194304 | tf_op jit(solution)/shard_map/shares_4/pallas_call | solution.py:440
  74.4 2.5 %collective-permute-start.27 = (bf16[128,1024]{1,0:T(8,128)(2,1)S(1)}, bf16[128,1024]{1,0:T(8,128)(2,1)S(1)}, u32[]{:S(2)}, u32[]{:S(2)}) collective-permute-start(bf16[128,1024]{1,0:T(8,128)(2,1)S(1)} %add_convert_fusion.4), channel_id=1, source_target_pairs={{0,4},{4,8},{8,12},{12,14},{14,10},{10,6},{6,2},{2,0},{1,3},{5,1},... | collective-permute-start | bytes 786440 | tf_op jit(solution)/shard_map/ppermute | solution.py:76
  77.0 2.6 %collective-permute-done.30 = bf16[128,1024]{1,0:T(8,128)(2,1)S(1)} collective-permute-done((bf16[128,1024]{1,0:T(8,128)(2,1)S(1)}, bf16[128,1024]{1,0:T(8,128)(2,1)S(1)}, u32[]{:S(2)}, u32[]{:S(2)}) %collective-permute-start.30) | collective-permute-done | bytes 262176 | tf_op jit(solution)/shard_map/ppermute | solution.py:76
  79.7 2.7 %collective-permute-done.27 = bf16[128,1024]{1,0:T(8,128)(2,1)S(1)} collective-permute-done((bf16[128,1024]{1,0:T(8,128)(2,1)S(1)}, bf16[128,1024]{1,0:T(8,128)(2,1)S(1)}, u32[]{:S(2)}, u32[]{:S(2)}) %collective-permute-start.27) | collective-permute-done | bytes 262176 | tf_op jit(solution)/shard_map/ppermute | solution.py:76
  85.5 3.4 %collective-permute-done.28 = bf16[128,1024]{1,0:T(8,128)(2,1)S(1)} collective-permute-done((bf16[128,1024]{1,0:T(8,128)(2,1)S(1)}, bf16[128,1024]{1,0:T(8,128)(2,1)S(1)}, u32[]{:S(2)}, u32[]{:S(2)}) %collective-permute-start.28) | collective-permute-done | bytes 262176 | tf_op jit(solution)/shard_map/ppermute | solution.py:76
  91.6 4.0 %collective-permute-done.32.refs_1_ = bf16[128,1024]{1,0:T(8,128)(2,1)S(1)} collective-permute-done((bf16[128,1024]{1,0:T(8,128)(2,1)S(1)}, bf16[128,1024]{1,0:T(8,128)(2,1)S(1)}, u32[]{:S(2)}, u32[]{:S(2)}) %collective-permute-start.32) | collective-permute-done | bytes 262176 | tf_op jit(solution)/shard_map/ppermute | solution.py:76
  99.3 2.6 %collective-permute-done.35.refs_3_ = bf16[128,1024]{1,0:T(8,128)(2,1)S(1)} collective-permute-done((bf16[128,1024]{1,0:T(8,128)(2,1)S(1)}, bf16[128,1024]{1,0:T(8,128)(2,1)S(1)}, u32[]{:S(2)}, u32[]{:S(2)}) %collective-permute-start.35) | collective-permute-done | bytes 262176 | tf_op jit(solution)/shard_map/ppermute | solution.py:76
  105.7 2.6 %collective-permute-done.37.refs_5_ = bf16[128,1024]{1,0:T(8,128)(2,1)S(1)} collective-permute-done((bf16[128,1024]{1,0:T(8,128)(2,1)S(1)}, bf16[128,1024]{1,0:T(8,128)(2,1)S(1)}, u32[]{:S(2)}, u32[]{:S(2)}) %collective-permute-start.37) | collective-permute-done | bytes 262176 | tf_op jit(solution)/shard_map/ppermute | solution.py:76
  111.1 3.6 %collective-permute-done.39.refs_7_ = bf16[128,1024]{1,0:T(8,128)(2,1)S(1)} collective-permute-done((bf16[128,1024]{1,0:T(8,128)(2,1)S(1)}, bf16[128,1024]{1,0:T(8,128)(2,1)S(1)}, u32[]{:S(2)}, u32[]{:S(2)}) %collective-permute-start.39) | collective-permute-done | bytes 262176 | tf_op jit(solution)/shard_map/ppermute | solution.py:76
  116.2 3.6 %final_norm.1 = bf16[128,16384]{1,0:T(8,128)(2,1)} custom-call(s32[16]{0:T(128)S(1)} %stack.108.ids, bf16[128,1024]{1,0:T(8,128)(2,1)S(1)} %add_convert_fusion.refs_0_, bf16[128,1024]{1,0:T(8,128)(2,1)S(1)} %collective-permute-done.32.refs_1_, bf16[128,1024]{1,0:T(8,128)(2,1)S(1)} %collective-permute-done.34.refs_2_, ...), custom_call_target="tpu_custom_call" | custom-call | flops 16777216 | bytes 12582912 | tf_op jit(solution)/shard_map/final_norm/pallas_call | solution.py:481
  (119 shorter events, 45.8 us)
Async XLA Ops:
  0.0 26.8 %collective-permute-start.8 = (bf16[128,16384]{1,0:T(8,128)(2,1)}, bf16[128,16384]{1,0:T(8,128)(2,1)}, u32[]{:S(2)}, u32[]{:S(2)}) collective-permute-start(bf16[128,16384]{1,0:T(8,128)(2,1)} %weight.3), channel_id=1, source_target_pairs={{0,1},{1,0},{2,3},{3,2},{4,5},{5,4},{6,7},{7,6},{8,9},{9,8},{10,11... | collective-permute-start | bytes 12582920 | tf_op jit(solution)/shard_map/ppermute | solution.py:76
  0.5 11.9 %collective-permute-start.2 = (bf16[128,1024]{1,0:T(8,128)(2,1)}, bf16[128,1024]{1,0:T(8,128)(2,1)S(1)}, u32[]{:S(2)}, u32[]{:S(2)}) collective-permute-start(bf16[128,1024]{1,0:T(8,128)(2,1)} %refs_0_), channel_id=1, source_target_pairs={{0,4},{4,8},{8,12},{12,14},{14,10},{10,6},{6,2},{2,0},{1,3},{5,1},... | collective-permute-start | bytes 786440 | tf_op jit(solution)/shard_map/ppermute | solution.py:76
  3.0 11.2 %collective-permute-start.3 = (bf16[128,1024]{1,0:T(8,128)(2,1)}, bf16[128,1024]{1,0:T(8,128)(2,1)S(1)}, u32[]{:S(2)}, u32[]{:S(2)}) collective-permute-start(bf16[128,1024]{1,0:T(8,128)(2,1)} %refs_0_), channel_id=1, source_target_pairs={{0,3},{4,1},{8,5},{12,9},{14,13},{10,15},{6,11},{2,7},{1,4},{5,8},... | collective-permute-start | bytes 786440 | tf_op jit(solution)/shard_map/ppermute | solution.py:76
  4.4 22.4 %collective-permute-start.10 = (bf16[128,1024]{1,0:T(8,128)(2,1)}, bf16[128,1024]{1,0:T(8,128)(2,1)S(1)}, u32[]{:S(2)}, u32[]{:S(2)}) collective-permute-start(bf16[128,1024]{1,0:T(8,128)(2,1)} %refs_0_), channel_id=1, source_target_pairs={{0,1},{1,0},{2,3},{3,2},{4,5},{5,4},{6,7},{7,6},{8,9},{9,8},{10,11... | collective-permute-start | bytes 786440 | tf_op jit(solution)/shard_map/ppermute | solution.py:76
  12.4 6.4 %collective-permute-start.4 = (bf16[128,1024]{1,0:T(8,128)(2,1)S(1)}, bf16[128,1024]{1,0:T(8,128)(2,1)S(1)}, u32[]{:S(2)}, u32[]{:S(2)}) collective-permute-start(bf16[128,1024]{1,0:T(8,128)(2,1)S(1)} %collective-permute-done.2.refs_1_), channel_id=1, source_target_pairs={{0,4},{4,8},{8,12},{12,14},{14,10},{10,6},{6,2},{2,0},{1,3},{5,1},... | collective-permute-start | bytes 786440 | tf_op jit(solution)/shard_map/ppermute | solution.py:76
  14.1 6.8 %collective-permute-start = (bf16[2,64,1024]{2,1,0:T(8,128)(2,1)S(1)}, bf16[2,64,1024]{2,1,0:T(8,128)(2,1)S(1)}, u32[]{:S(2)}, u32[]{:S(2)}) collective-permute-start(bf16[2,64,1024]{2,1,0:T(8,128)(2,1)S(1)} %pad_maximum_fusion), channel_id=1, source_target_pairs={{0,1},{1,0},{2,3},{3,2},{4,5},{5,4},{6,7},{7,6},{8,9},{9,8},{10,11... | collective-permute-start | bytes 786440 | tf_op jit(solution)/shard_map/ppermute | solution.py:76
  14.2 8.2 %collective-permute-start.5 = (bf16[128,1024]{1,0:T(8,128)(2,1)S(1)}, bf16[128,1024]{1,0:T(8,128)(2,1)S(1)}, u32[]{:S(2)}, u32[]{:S(2)}) collective-permute-start(bf16[128,1024]{1,0:T(8,128)(2,1)S(1)} %collective-permute-done.3.refs_2_), channel_id=1, source_target_pairs={{0,4},{4,8},{8,12},{12,14},{14,10},{10,6},{6,2},{2,0},{1,3},{5,1},... | collective-permute-start | bytes 786440 | tf_op jit(solution)/shard_map/ppermute | solution.py:76
  18.8 7.9 %collective-permute-start.6 = (bf16[128,1024]{1,0:T(8,128)(2,1)S(1)}, bf16[128,1024]{1,0:T(8,128)(2,1)S(1)}, u32[]{:S(2)}, u32[]{:S(2)}) collective-permute-start(bf16[128,1024]{1,0:T(8,128)(2,1)S(1)} %collective-permute-done.4.refs_3_), channel_id=1, source_target_pairs={{0,4},{4,8},{8,12},{12,14},{14,10},{10,6},{6,2},{2,0},{1,3},{5,1},... | collective-permute-start | bytes 786440 | tf_op jit(solution)/shard_map/ppermute | solution.py:76
  22.0 8.9 %collective-permute-start.1 = (bf16[4,2,2,64,128]{4,3,2,1,0:T(8,128)(2,1)S(1)}, bf16[4,2,2,64,128]{4,3,2,1,0:T(8,128)(2,1)S(1)}, u32[]{:S(2)}, u32[]{:S(2)}) collective-permute-start(bf16[4,2,2,64,128]{4,3,2,1,0:T(8,128)(2,1)S(1)} %get-tuple-element.23), channel_id=1, source_target_pairs={{0,2},{1,3},{2,0},{3,1},{4,6},{5,7},{6,4},{7,5},{8,10},{9,11},{10,... | collective-permute-start | bytes 786440 | tf_op jit(solution)/shard_map/ppermute | solution.py:76
  22.5 8.4 %collective-permute-start.11 = (bf16[128,1024]{1,0:T(8,128)(2,1)S(1)}, bf16[128,1024]{1,0:T(8,128)(2,1)S(1)}, u32[]{:S(2)}, u32[]{:S(2)}) collective-permute-start(bf16[128,1024]{1,0:T(8,128)(2,1)S(1)} %collective-permute-done.2.refs_1_), channel_id=1, source_target_pairs={{0,1},{1,0},{2,3},{3,2},{4,5},{5,4},{6,7},{7,6},{8,9},{9,8},{10,11... | collective-permute-start | bytes 786440 | tf_op jit(solution)/shard_map/ppermute | solution.py:76
  26.8 7.0 %collective-permute-start.7 = (bf16[128,1024]{1,0:T(8,128)(2,1)S(1)}, bf16[128,1024]{1,0:T(8,128)(2,1)}, u32[]{:S(2)}, u32[]{:S(2)}) collective-permute-start(bf16[128,1024]{1,0:T(8,128)(2,1)S(1)} %collective-permute-done.5.refs_4_), channel_id=1, source_target_pairs={{0,4},{4,8},{8,12},{12,14},{14,10},{10,6},{6,2},{2,0},{1,3},{5,1},... | collective-permute-start | bytes 786440 | tf_op jit(solution)/shard_map/ppermute | solution.py:76
  26.8 9.8 %collective-permute-start.9 = (bf16[128,1024]{1,0:T(8,128)(2,1)S(1)}, bf16[128,1024]{1,0:T(8,128)(2,1)}, u32[]{:S(2)}, u32[]{:S(2)}) collective-permute-start(bf16[128,1024]{1,0:T(8,128)(2,1)S(1)} %collective-permute-done.6.refs_5_), channel_id=1, source_target_pairs={{0,4},{4,8},{8,12},{12,14},{14,10},{10,6},{6,2},{2,0},{1,3},{5,1},... | collective-permute-start | bytes 786440 | tf_op jit(solution)/shard_map/ppermute | solution.py:76
  30.8 7.1 %collective-permute-start.13 = (bf16[128,1024]{1,0:T(8,128)(2,1)S(1)}, bf16[128,1024]{1,0:T(8,128)(2,1)S(1)}, u32[]{:S(2)}, u32[]{:S(2)}) collective-permute-start(bf16[128,1024]{1,0:T(8,128)(2,1)S(1)} %collective-permute-done.4.refs_3_), channel_id=1, source_target_pairs={{0,1},{1,0},{2,3},{3,2},{4,5},{5,4},{6,7},{7,6},{8,9},{9,8},{10,11... | collective-permute-start | bytes 786440 | tf_op jit(solution)/shard_map/ppermute | solution.py:76
  30.8 7.1 %collective-permute-start.14 = (bf16[128,1024]{1,0:T(8,128)(2,1)S(1)}, bf16[128,1024]{1,0:T(8,128)(2,1)S(1)}, u32[]{:S(2)}, u32[]{:S(2)}) collective-permute-start(bf16[128,1024]{1,0:T(8,128)(2,1)S(1)} %collective-permute-done.5.refs_4_), channel_id=1, source_target_pairs={{0,1},{1,0},{2,3},{3,2},{4,5},{5,4},{6,7},{7,6},{8,9},{9,8},{10,11... | collective-permute-start | bytes 786440 | tf_op jit(solution)/shard_map/ppermute | solution.py:76
  31.3 8.4 %collective-permute-start.15 = (bf16[128,1024]{1,0:T(8,128)(2,1)S(1)}, bf16[128,1024]{1,0:T(8,128)(2,1)S(1)}, u32[]{:S(2)}, u32[]{:S(2)}) collective-permute-start(bf16[128,1024]{1,0:T(8,128)(2,1)S(1)} %collective-permute-done.6.refs_5_), channel_id=1, source_target_pairs={{0,1},{1,0},{2,3},{3,2},{4,5},{5,4},{6,7},{7,6},{8,9},{9,8},{10,11... | collective-permute-start | bytes 786440 | tf_op jit(solution)/shard_map/ppermute | solution.py:76
  37.9 14.9 %collective-permute-start.21 = (bf16[2,2,2,64,128]{4,3,2,1,0:T(8,128)(2,1)}, bf16[2,2,2,64,128]{4,3,2,1,0:T(8,128)(2,1)S(1)}, u32[]{:S(2)}, u32[]{:S(2)}) collective-permute-start(bf16[2,2,2,64,128]{4,3,2,1,0:T(8,128)(2,1)} %pad_maximum_fusion.1), channel_id=1, source_target_pairs={{0,4},{1,5},{2,6},{3,7},{4,0},{5,1},{6,2},{7,3},{8,12},{9,13},{10,... | collective-permute-start | bytes 393224 | tf_op jit(solution)/shard_map/ppermute | solution.py:76
  37.9 14.9 %collective-permute-start.22 = (bf16[2,2,2,64,128]{4,3,2,1,0:T(8,128)(2,1)}, bf16[2,2,2,64,128]{4,3,2,1,0:T(8,128)(2,1)S(1)}, u32[]{:S(2)}, u32[]{:S(2)}) collective-permute-start(bf16[2,2,2,64,128]{4,3,2,1,0:T(8,128)(2,1)} %pad_maximum_fusion.2), channel_id=1, source_target_pairs={{0,8},{1,9},{2,10},{3,11},{4,12},{5,13},{6,14},{7,15},{8,0},{9,1},... | collective-permute-start | bytes 393224 | tf_op jit(solution)/shard_map/ppermute | solution.py:76
  47.3 7.5 %collective-permute-start.23 = (bf16[2,2,2,64,128]{4,3,2,1,0:T(8,128)(2,1)S(1)}, bf16[2,2,2,64,128]{4,3,2,1,0:T(8,128)(2,1)S(1)}, u32[]{:S(2)}, u32[]{:S(2)}) collective-permute-start(bf16[2,2,2,64,128]{4,3,2,1,0:T(8,128)(2,1)S(1)} %pad_maximum_fusion.3), channel_id=1, source_target_pairs={{0,12},{1,13},{2,14},{3,15},{4,8},{5,9},{6,10},{7,11},{8,4},{9,5},... | collective-permute-start | bytes 393224 | tf_op jit(solution)/shard_map/ppermute | solution.py:76
  61.0 6.9 %collective-permute-start.25 = (bf16[128,1024]{1,0:T(8,128)(2,1)S(1)}, bf16[128,1024]{1,0:T(8,128)(2,1)S(1)}, u32[]{:S(2)}, u32[]{:S(2)}) collective-permute-start(bf16[128,1024]{1,0:T(8,128)(2,1)S(1)} %get-tuple-element.34), channel_id=1, source_target_pairs={{0,4},{4,8},{8,12},{12,14},{14,10},{10,6},{6,2},{2,0},{1,3},{5,1},... | collective-permute-start | bytes 786440 | tf_op jit(solution)/shard_map/ppermute | solution.py:76
  64.0 9.1 %collective-permute-start.29 = (bf16[128,1024]{1,0:T(8,128)(2,1)S(1)}, bf16[128,1024]{1,0:T(8,128)(2,1)S(1)}, u32[]{:S(2)}, u32[]{:S(2)}) collective-permute-start(bf16[128,1024]{1,0:T(8,128)(2,1)S(1)} %get-tuple-element.38), channel_id=1, source_target_pairs={{0,4},{4,8},{8,12},{12,14},{14,10},{10,6},{6,2},{2,0},{1,3},{5,1},... | collective-permute-start | bytes 786440 | tf_op jit(solution)/shard_map/ppermute | solution.py:76
  67.9 6.4 %collective-permute-start.26 = (bf16[128,1024]{1,0:T(8,128)(2,1)S(1)}, bf16[128,1024]{1,0:T(8,128)(2,1)S(1)}, u32[]{:S(2)}, u32[]{:S(2)}) collective-permute-start(bf16[128,1024]{1,0:T(8,128)(2,1)S(1)} %add_convert_fusion.5), channel_id=1, source_target_pairs={{0,4},{4,8},{8,12},{12,14},{14,10},{10,6},{6,2},{2,0},{1,3},{5,1},... | collective-permute-start | bytes 786440 | tf_op jit(solution)/shard_map/ppermute | solution.py:76
  74.4 8.0 %collective-permute-start.27 = (bf16[128,1024]{1,0:T(8,128)(2,1)S(1)}, bf16[128,1024]{1,0:T(8,128)(2,1)S(1)}, u32[]{:S(2)}, u32[]{:S(2)}) collective-permute-start(bf16[128,1024]{1,0:T(8,128)(2,1)S(1)} %add_convert_fusion.4), channel_id=1, source_target_pairs={{0,4},{4,8},{8,12},{12,14},{14,10},{10,6},{6,2},{2,0},{1,3},{5,1},... | collective-permute-start | bytes 786440 | tf_op jit(solution)/shard_map/ppermute | solution.py:76
  90.6 7.7 %collective-permute-start.34 = (bf16[128,1024]{1,0:T(8,128)(2,1)S(1)}, bf16[128,1024]{1,0:T(8,128)(2,1)S(1)}, u32[]{:S(2)}, u32[]{:S(2)}) collective-permute-start(bf16[128,1024]{1,0:T(8,128)(2,1)S(1)} %collective-permute-done.33.refs_8_), channel_id=1, source_target_pairs={{0,4},{4,8},{8,12},{12,14},{14,10},{10,6},{6,2},{2,0},{1,3},{5,1},... | collective-permute-start | bytes 786440 | tf_op jit(solution)/shard_map/ppermute | solution.py:76
  102.9 6.9 %collective-permute-start.41 = (bf16[128,1024]{1,0:T(8,128)(2,1)S(1)}, bf16[128,1024]{1,0:T(8,128)(2,1)S(1)}, u32[]{:S(2)}, u32[]{:S(2)}) collective-permute-start(bf16[128,1024]{1,0:T(8,128)(2,1)S(1)} %collective-permute-done.34.refs_2_), channel_id=1, source_target_pairs={{0,1},{1,0},{2,3},{3,2},{4,5},{5,4},{6,7},{7,6},{8,9},{9,8},{10,11... | collective-permute-start | bytes 786440 | tf_op jit(solution)/shard_map/ppermute | solution.py:76
  (31 other events, 247.4 us)

commit v11 on v8

--- a/solution.py
+++ b/solution.py
@@ -252,10 +252,11 @@
     return row_factors(total, 16 * blocks[0].shape[1])
 
 
-def project_kernel(ids, *refs):
+def project_kernel(ids, to, *refs):
     blocks, refs = refs[:16], refs[16:]
-    gain, weights, cosine, sine, kv_cos, kv_sin = refs[:6]
-    q_keep, q_send, fresh = refs[6:]
+    gain, weights, cosine, sine, kv_cos, kv_sin, wo, wo_other = refs[:8]
+    q_keep, q_send, fresh, first_weights, sems = refs[8:]
+    copies = share_copies(to, 0, wo, wo_other, first_weights, sems)
     factors = all_factors(blocks)
     total = jnp.zeros((TOKENS, 2 * HD), jnp.float32)
     for i in range(16):
@@ -268,21 +269,29 @@
     q_keep[...] = jnp.where(core_one, q[SPAN:], q[:SPAN])
     q_send[...] = jnp.where(core_one, q[:SPAN], q[SPAN:])
     fresh[...] = kv
-
-
-def project(ids, arrays, gain, weights, tables):
+    for pair in copies:
+        for copy in pair:
+            copy.wait()
+
+
+def project(ids, to, arrays, gain, weights, tables, wo, wo_other, ahead):
+    width = arrays[0].shape[1]
     return pl.pallas_call(
         project_kernel,
         out_shape=[jax.ShapeDtypeStruct((SPAN, HD), jnp.bfloat16)] * 2
-        + [jax.ShapeDtypeStruct((TOKENS, HD), jnp.bfloat16)],
-        in_specs=[SMEM] + [VMEM] * (len(arrays) + 6),
-        out_specs=[VMEM] * 3,
+        + [
+            jax.ShapeDtypeStruct((TOKENS, HD), jnp.bfloat16),
+            jax.ShapeDtypeStruct((ahead, 2 * HD, width), jnp.bfloat16),
+        ],
+        in_specs=[SMEM] * 2 + [VMEM] * (len(arrays) + 6) + [HBM] * 2,
+        out_specs=[VMEM] * 4,
+        scratch_shapes=[pltpu.SemaphoreType.DMA((2, ahead))],
         compiler_params=pltpu.CompilerParams(vmem_limit_bytes=24 * MIB),
         cost_estimate=pl.CostEstimate(
             flops=2 * TOKENS * weights.size, bytes_accessed=12 * MIB, transcendentals=0
         ),
         name="norm_project",
-    )(ids, *arrays, gain, weights, *tables)
+    )(ids, to, *arrays, gain, weights, *tables, in_hbm(wo), wo_other)
 
 
 def share_copies(to, first, weight, weight_other, out, sems):
@@ -310,9 +319,8 @@
 CONTRACT = (((1,), (1,)), ((), ()))
 
 
-def scores_kernel(info, to, q, q_other, *refs):
-    cache, weight, weight_other, scores, weights, sems = refs[:5], *refs[5:]
-    copies = share_copies(to, 0, weight, weight_other, weights, sems)
+def scores_kernel(info, q, q_other, *refs):
+    cache, scores = refs[:5], refs[5]
     core, rank = info[SEQS], info[SEQS + 1]
     queries = jnp.concatenate([q[...], q_other[...]], axis=0)
     old = lax.dot_general(
@@ -321,28 +329,18 @@
     lane = lax.broadcasted_iota(jnp.int32, old.shape, 1)
     position = (rank ^ (lane // CTX_DEV)) * CTX_DEV + lane % CTX_DEV
     scores[...] = jnp.where(position < info[core], old * HD ** (-0.5), -1e30)
-    for pair in copies:
-        for copy in pair:
-            copy.wait()
-
-
-def cache_scores(info, to, q, q_other, cache, weight, weight_other, ahead):
-    width = weight.shape[1] // 16
+
+
+def cache_scores(info, q, q_other, cache):
     return pl.pallas_call(
         scores_kernel,
-        out_shape=[
-            jax.ShapeDtypeStruct((TOKENS, 16 * CTX_DEV), jnp.float32),
-            jax.ShapeDtypeStruct((ahead, 2 * HD, width), jnp.bfloat16),
-        ],
-        in_specs=[SMEM] * 2 + [VMEM] * 7 + [HBM] * 2,
-        out_specs=[VMEM] * 2,
-        scratch_shapes=[pltpu.SemaphoreType.DMA((2, ahead))],
+        out_shape=jax.ShapeDtypeStruct((TOKENS, 16 * CTX_DEV), jnp.float32),
+        in_specs=[SMEM] + [VMEM] * 7,
+        out_specs=VMEM,
         compiler_params=pltpu.CompilerParams(vmem_limit_bytes=16 * MIB),
-        cost_estimate=pl.CostEstimate(
-            flops=32 * MIB, bytes_accessed=3 * MIB, transcendentals=0
-        ),
+        cost_estimate=pl.CostEstimate(flops=32 * MIB, bytes_accessed=MIB, transcendentals=0),
         name="cache_scores",
-    )(info, to, q, q_other, *cache, in_hbm(weight), weight_other)
+    )(info, q, q_other, *cache)
 
 
 def attend_kernel(info, q, q_other, fresh_own, fresh_other, scores, *refs):
@@ -519,20 +517,20 @@
 
     gain = attn_gain.reshape(16, 1, width).astype(jnp.float32)
     mine[0] = after(mine[0], cache[1])
-    q_keep, q_send, fresh = project(ids, mine + theirs, gain, weights, tables)
+    q_keep, q_send, fresh, first_weights = project(
+        ids, to, mine + theirs, gain, weights, tables, o_weight, weight_other, 2
+    )
     q_other = send(q_send, SWAP)
     fresh_own = send(fresh, FRESH)
     fresh_other = send(jnp.where(core == 0, fresh_own[SPAN:], fresh_own[:SPAN]), SWAP)
-    scores, first_weights = cache_scores(
-        info, to, q_keep, q_other, cache, o_weight, weight_other, 2
-    )
+    scores = cache_scores(info, q_keep, q_other, cache)
     attn = attend(info, q_keep, q_other, fresh_own, fresh_other, scores, cache)
     attn_other = send(attn, SWAP)
 
     shares = first_shares(SHARES[:2], core_id, attn, attn_other, first_weights)
-    inputs = (attn, attn_other, o_weight, weight_other)
-    for first, last in ((2, 4), (4, len(SHARES))):
-        shares.update(more_shares(core_id, to, *inputs, first, last))
+    shares.update(
+        more_shares(core_id, to, attn, attn_other, o_weight, weight_other, 2, len(SHARES))
+    )
     one_way, other_way = ring_sum(shares)
     projected = shares[0, 0] + one_way.astype(jnp.float32) + other_way.astype(jnp.float32)
     hidden = (residual.astype(jnp.float32) + projected).astype(jnp.bfloat16)

time: 116 us -> 124 us (1.069)
  local copies, waits for them, and re-layouts: 1.29 us -> 10.5 us
  starting transfers between devices: 49.3 us -> 57.4 us
  waiting for transfers between devices: 40.5 us -> 33.5 us
  Pallas kernels: 20.3 us -> 19 us
    unnamed x6 -> x16, local copies, waits for them, and re-layouts: 0.02 us -> 9.21 us
    ppermute x47, starting transfers between devices: 49.3 us -> 57.4 us  [send(): return lax.ppermute(array, 'tp', pairs)]
    ppermute x47, waiting for transfers between devices: 40.5 us -> 33.5 us  [send(): return lax.ppermute(array, 'tp', pairs)]
    pallas_call x2 -> x1, Pallas kernels: 4.67 us -> 3.1 us  [more_shares(): pl.pallas_call(functools.partial(more_shares_kernel, first), out_shape=ou...]
    another operation x3, other arithmetic: 1.35 us -> 0.05 us  [move_cache(): pieces = [jnp.stack([keep[m], came[m]]) for m in range(1, 4)]]
  transfers between devices with their start and end apart: 47 -> 47, of which waited for: 19 -> 18; matrix products, arithmetic and copies ran while one was open for 4% -> 4% of each run, Pallas kernels for 13% -> 11%
where the time goes in v11:
time: 124 us
  starting transfers between devices  57.4 us (46%)
  waiting for transfers between devices  33.5 us (27%)
  Pallas kernels  19 us (15%)
  local copies, waits for them, and re-layouts  10.5 us (8%)
  other arithmetic  3.26 us (3%)
    ppermute x47, starting transfers between devices, send(): return lax.ppermute(array, 'tp', pairs)  57.4 us
    ppermute x47, waiting for transfers between devices, send(): return lax.ppermute(array, 'tp', pairs)  33.5 us
    unnamed x16, local copies, waits for them, and re-layouts  9.21 us
    pallas_call x1, Pallas kernels, load_weights(): pl.pallas_call(load_kernel, out_shape=jax.ShapeDtypeStruct((16, width, 2...  4.19 us
    pallas_call x1, Pallas kernels, project(): pl.pallas_call(project_kernel, out_shape=[jax.ShapeDtypeStruct((SPAN, HD)...  4.06 us
    pallas_call x1, Pallas kernels, final_norm(): pl.pallas_call(final_kernel, out_shape=jax.ShapeDtypeStruct((TOKENS, 16 *...  3.65 us
    pallas_call x1, Pallas kernels, more_shares(): pl.pallas_call(functools.partial(more_shares_kernel, first), out_shape=ou...  3.1 us
  transfers between devices with their start and end apart: 47, of which 18 were waited for; matrix products, arithmetic and copies ran while one was open for 4% of the time, Pallas kernels for 11%

profile of v11, /device:TPU:0, one launch (start us, length us, event | category | flops | bytes accessed | tf_op | source)
XLA Modules:
  0.0 124.0 jit_solution(5139765806055536383)
XLA Ops:
  0.5 2.6 %collective-permute-start.2 = (bf16[128,1024]{1,0:T(8,128)(2,1)}, bf16[128,1024]{1,0:T(8,128)(2,1)S(1)}, u32[]{:S(2)}, u32[]{:S(2)}) collective-permute-start(bf16[128,1024]{1,0:T(8,128)(2,1)} %refs_0_), channel_id=1, source_target_pairs={{0,4},{4,8},{8,12},{12,14},{14,10},{10,6},{6,2},{2,0},{1,3},{5,1},... | collective-permute-start | bytes 786440 | tf_op jit(solution)/shard_map/ppermute | solution.py:76
  5.7 3.3 %collective-permute-done.2.refs_1_ = bf16[128,1024]{1,0:T(8,128)(2,1)S(1)} collective-permute-done((bf16[128,1024]{1,0:T(8,128)(2,1)}, bf16[128,1024]{1,0:T(8,128)(2,1)S(1)}, u32[]{:S(2)}, u32[]{:S(2)}) %collective-permute-start.2) | collective-permute-done | bytes 262176 | tf_op jit(solution)/shard_map/ppermute | solution.py:76
  9.0 2.4 %collective-permute-start.4 = (bf16[128,1024]{1,0:T(8,128)(2,1)S(1)}, bf16[128,1024]{1,0:T(8,128)(2,1)S(1)}, u32[]{:S(2)}, u32[]{:S(2)}) collective-permute-start(bf16[128,1024]{1,0:T(8,128)(2,1)S(1)} %collective-permute-done.2.refs_1_), channel_id=1, source_target_pairs={{0,4},{4,8},{8,12},{12,14},{14,10},{10,6},{6,2},{2,0},{1,3},{5,1},... | collective-permute-start | bytes 786440 | tf_op jit(solution)/shard_map/ppermute | solution.py:76
  20.4 4.1 %collective-permute-done.6.refs_5_ = bf16[128,1024]{1,0:T(8,128)(2,1)S(1)} collective-permute-done((bf16[128,1024]{1,0:T(8,128)(2,1)S(1)}, bf16[128,1024]{1,0:T(8,128)(2,1)S(1)}, u32[]{:S(2)}, u32[]{:S(2)}) %collective-permute-start.6) | collective-permute-done | bytes 262176 | tf_op jit(solution)/shard_map/ppermute | solution.py:76
  27.4 4.2 %load_weights.1.refs_17_ = bf16[16,1024,256]{2,1,0:T(8,128)(2,1)S(1)} custom-call(s32[16]{0:T(128)S(1)} %stack.108.ids, bf16[16384,128]{1,0:T(8,128)(2,1)} %wq.1, bf16[16384,128]{1,0:T(8,128)(2,1)} %wkv.1), custom_call_target="tpu_custom_call" | custom-call | bytes 16777216 | tf_op jit(solution)/shard_map/load_weights/pallas_call | solution.py:238
  31.6 3.3 %copy-done = bf16[16,1024,256]{2,1,0:T(8,128)(2,1)} copy-done((bf16[16,1024,256]{2,1,0:T(8,128)(2,1)}, bf16[16,1024,256]{2,1,0:T(8,128)(2,1)S(1)}, u32[]{:S(2)}) %copy-start) | copy-done | bytes 8388632
  36.6 4.3 %collective-permute-start.21 = (bf16[2,2,2,64,128]{4,3,2,1,0:T(8,128)(2,1)S(1)}, bf16[2,2,2,64,128]{4,3,2,1,0:T(8,128)(2,1)S(1)}, u32[]{:S(2)}, u32[]{:S(2)}) collective-permute-start(bf16[2,2,2,64,128]{4,3,2,1,0:T(8,128)(2,1)S(1)} %pad_maximum_fusion.1), channel_id=1, source_target_pairs={{0,4},{1,5},{2,6},{3,7},{4,0},{5,1},{6,2},{7,3},{8,12},{9,13},{10,... | collective-permute-start | bytes 393224 | tf_op jit(solution)/shard_map/ppermute | solution.py:76
  43.2 3.4 %copy-done.1 = bf16[16,1024,256]{2,1,0:T(8,128)(2,1)S(1)} copy-done((bf16[16,1024,256]{2,1,0:T(8,128)(2,1)S(1)}, bf16[16,1024,256]{2,1,0:T(8,128)(2,1)}, u32[]{:S(2)}) %copy-start.1) | copy-done | bytes 8388632
  49.1 4.1 %norm_project.1 = (bf16[64,128]{1,0:T(8,128)(2,1)S(1)}, bf16[64,128]{1,0:T(8,128)(2,1)S(1)}, bf16[128,128]{1,0:T(8,128)(2,1)S(1)}, bf16[2,256,1024]{2,1,0:T(8,128)(2,1)S(1)}) custom-call(s32[16]{0:T(128)S(1)} %stack.108.ids, s32[8]{0:T(128)S(1)} %stack.117.to, bf16[128,1024]{1,0:T(8,128)(2,1)S(1)} %copy-done.2, ...), custom_call_target="tpu_custom_call" | custom-call | flops 1073741824 | bytes 12582912 | tf_op jit(solution)/shard_map/norm_project/pallas_call | solution.py:279
  53.8 3.6 %collective-permute-start.23 = (bf16[2,2,2,64,128]{4,3,2,1,0:T(8,128)(2,1)S(1)}, bf16[2,2,2,64,128]{4,3,2,1,0:T(8,128)(2,1)S(1)}, u32[]{:S(2)}, u32[]{:S(2)}) collective-permute-start(bf16[2,2,2,64,128]{4,3,2,1,0:T(8,128)(2,1)S(1)} %pad_maximum_fusion.3), channel_id=1, source_target_pairs={{0,12},{1,13},{2,14},{3,15},{4,8},{5,9},{6,10},{7,11},{8,4},{9,5},... | collective-permute-start | bytes 393224 | tf_op jit(solution)/shard_map/ppermute | solution.py:76
  59.2 3.2 %collective-permute-done.23.refs_4_ = bf16[2,2,2,64,128]{4,3,2,1,0:T(8,128)(2,1)S(1)} collective-permute-done((bf16[2,2,2,64,128]{4,3,2,1,0:T(8,128)(2,1)S(1)}, bf16[2,2,2,64,128]{4,3,2,1,0:T(8,128)(2,1)S(1)}, u32[]{:S(2)}, u32[]{:S(2)}) %collective-permute-start.23) | collective-permute-done | bytes 131104 | tf_op jit(solution)/shard_map/ppermute | solution.py:76
  65.9 3.4 %collective-permute-start.25 = (bf16[128,1024]{1,0:T(8,128)(2,1)S(1)}, bf16[128,1024]{1,0:T(8,128)(2,1)S(1)}, u32[]{:S(2)}, u32[]{:S(2)}) collective-permute-start(bf16[128,1024]{1,0:T(8,128)(2,1)S(1)} %get-tuple-element.30), channel_id=1, source_target_pairs={{0,4},{4,8},{8,12},{12,14},{14,10},{10,6},{6,2},{2,0},{1,3},{5,1},... | collective-permute-start | bytes 786440 | tf_op jit(solution)/shard_map/ppermute | solution.py:76
  70.2 3.1 %shares_2.1 = (f32[128,1024]{1,0:T(8,128)S(1)}, f32[128,1024]{1,0:T(8,128)S(1)}, f32[128,1024]{1,0:T(8,128)S(1)}, f32[128,1024]{1,0:T(8,128)S(1)}, f32[128,1024]{1,0:T(8,128)S(1)}, /*index=5*/f32[128,1024]{1,0:T(8,128)S(1)}) custom-call(s32[1]{0:T(128)} %bitcast.16.core, s32[8]{0:T(128)S(1)} %stack.117.to, bf16[64,256]{1,0:T(8,128)(2,1)S(1)} %attend.1.attn, ...), custom_call_target="tpu_custom_call" | custom-call | flops 402653184 | bytes 6291456 | tf_op jit(solution)/shard_map/shares_2/pallas_call | solution.py:436
  73.5 2.3 %collective-permute-start.26 = (bf16[128,1024]{1,0:T(8,128)(2,1)S(1)}, bf16[128,1024]{1,0:T(8,128)(2,1)S(1)}, u32[]{:S(2)}, u32[]{:S(2)}) collective-permute-start(bf16[128,1024]{1,0:T(8,128)(2,1)S(1)} %add_convert_fusion.5), channel_id=1, source_target_pairs={{0,4},{4,8},{8,12},{12,14},{14,10},{10,6},{6,2},{2,0},{1,3},{5,1},... | collective-permute-start | bytes 786440 | tf_op jit(solution)/shard_map/ppermute | solution.py:76
  76.1 2.5 %collective-permute-start.30 = (bf16[128,1024]{1,0:T(8,128)(2,1)S(1)}, bf16[128,1024]{1,0:T(8,128)(2,1)S(1)}, u32[]{:S(2)}, u32[]{:S(2)}) collective-permute-start(bf16[128,1024]{1,0:T(8,128)(2,1)S(1)} %add_convert_fusion.2), channel_id=1, source_target_pairs={{0,4},{4,8},{8,12},{12,14},{14,10},{10,6},{6,2},{2,0},{1,3},{5,1},... | collective-permute-start | bytes 786440 | tf_op jit(solution)/shard_map/ppermute | solution.py:76
  80.0 2.3 %collective-permute-start.27 = (bf16[128,1024]{1,0:T(8,128)(2,1)S(1)}, bf16[128,1024]{1,0:T(8,128)(2,1)S(1)}, u32[]{:S(2)}, u32[]{:S(2)}) collective-permute-start(bf16[128,1024]{1,0:T(8,128)(2,1)S(1)} %add_convert_fusion.4), channel_id=1, source_target_pairs={{0,4},{4,8},{8,12},{12,14},{14,10},{10,6},{6,2},{2,0},{1,3},{5,1},... | collective-permute-start | bytes 786440 | tf_op jit(solution)/shard_map/ppermute | solution.py:76
  83.2 3.2 %collective-permute-done.27 = bf16[128,1024]{1,0:T(8,128)(2,1)S(1)} collective-permute-done((bf16[128,1024]{1,0:T(8,128)(2,1)S(1)}, bf16[128,1024]{1,0:T(8,128)(2,1)S(1)}, u32[]{:S(2)}, u32[]{:S(2)}) %collective-permute-start.27) | collective-permute-done | bytes 262176 | tf_op jit(solution)/shard_map/ppermute | solution.py:76
  86.5 2.3 %collective-permute-start.28 = (bf16[128,1024]{1,0:T(8,128)(2,1)S(1)}, bf16[128,1024]{1,0:T(8,128)(2,1)S(1)}, u32[]{:S(2)}, u32[]{:S(2)}) collective-permute-start(bf16[128,1024]{1,0:T(8,128)(2,1)S(1)} %add_convert_fusion.3), channel_id=1, source_target_pairs={{0,4},{4,8},{8,12},{12,14},{14,10},{10,6},{6,2},{2,0},{1,3},{5,1},... | collective-permute-start | bytes 786440 | tf_op jit(solution)/shard_map/ppermute | solution.py:76
  89.0 3.9 %collective-permute-done.28 = bf16[128,1024]{1,0:T(8,128)(2,1)S(1)} collective-permute-done((bf16[128,1024]{1,0:T(8,128)(2,1)S(1)}, bf16[128,1024]{1,0:T(8,128)(2,1)S(1)}, u32[]{:S(2)}, u32[]{:S(2)}) %collective-permute-start.28) | collective-permute-done | bytes 262176 | tf_op jit(solution)/shard_map/ppermute | solution.py:76
  93.1 2.3 %collective-permute-start.32 = (bf16[128,1024]{1,0:T(8,128)(2,1)S(1)}, bf16[128,1024]{1,0:T(8,128)(2,1)S(1)}, u32[]{:S(2)}, u32[]{:S(2)}) collective-permute-start(bf16[128,1024]{1,0:T(8,128)(2,1)S(1)} %add_convert_fusion.refs_0_), channel_id=1, source_target_pairs={{0,4},{4,8},{8,12},{12,14},{14,10},{10,6},{6,2},{2,0},{1,3},{5,1},... | collective-permute-start | bytes 786440 | tf_op jit(solution)/shard_map/ppermute | solution.py:76
  96.9 2.6 %collective-permute-done.32.refs_1_ = bf16[128,1024]{1,0:T(8,128)(2,1)S(1)} collective-permute-done((bf16[128,1024]{1,0:T(8,128)(2,1)S(1)}, bf16[128,1024]{1,0:T(8,128)(2,1)S(1)}, u32[]{:S(2)}, u32[]{:S(2)}) %collective-permute-start.32) | collective-permute-done | bytes 262176 | tf_op jit(solution)/shard_map/ppermute | solution.py:76
  112.3 2.3 %collective-permute-start.39 = (bf16[128,1024]{1,0:T(8,128)(2,1)S(1)}, bf16[128,1024]{1,0:T(8,128)(2,1)S(1)}, u32[]{:S(2)}, u32[]{:S(2)}) collective-permute-start(bf16[128,1024]{1,0:T(8,128)(2,1)S(1)} %collective-permute-done.37.refs_5_), channel_id=1, source_target_pairs={{0,4},{4,8},{8,12},{12,14},{14,10},{10,6},{6,2},{2,0},{1,3},{5,1},... | collective-permute-start | bytes 786440 | tf_op jit(solution)/shard_map/ppermute | solution.py:76
  115.6 3.0 %collective-permute-done.39.refs_7_ = bf16[128,1024]{1,0:T(8,128)(2,1)S(1)} collective-permute-done((bf16[128,1024]{1,0:T(8,128)(2,1)S(1)}, bf16[128,1024]{1,0:T(8,128)(2,1)S(1)}, u32[]{:S(2)}, u32[]{:S(2)}) %collective-permute-start.39) | collective-permute-done | bytes 262176 | tf_op jit(solution)/shard_map/ppermute | solution.py:76
  120.2 3.6 %final_norm.1 = bf16[128,16384]{1,0:T(8,128)(2,1)} custom-call(s32[16]{0:T(128)S(1)} %stack.108.ids, bf16[128,1024]{1,0:T(8,128)(2,1)S(1)} %add_convert_fusion.refs_0_, bf16[128,1024]{1,0:T(8,128)(2,1)S(1)} %collective-permute-done.32.refs_1_, bf16[128,1024]{1,0:T(8,128)(2,1)S(1)} %collective-permute-done.34.refs_2_, ...), custom_call_target="tpu_custom_call" | custom-call | flops 16777216 | bytes 12582912 | tf_op jit(solution)/shard_map/final_norm/pallas_call | solution.py:477
  (118 shorter events, 48.1 us)
Async XLA Ops:
  0.0 24.4 %collective-permute-start.8 = (bf16[128,16384]{1,0:T(8,128)(2,1)}, bf16[128,16384]{1,0:T(8,128)(2,1)}, u32[]{:S(2)}, u32[]{:S(2)}) collective-permute-start(bf16[128,16384]{1,0:T(8,128)(2,1)} %weight.1), channel_id=1, source_target_pairs={{0,1},{1,0},{2,3},{3,2},{4,5},{5,4},{6,7},{7,6},{8,9},{9,8},{10,11... | collective-permute-start | bytes 12582920 | tf_op jit(solution)/shard_map/ppermute | solution.py:76
  0.5 8.6 %collective-permute-start.2 = (bf16[128,1024]{1,0:T(8,128)(2,1)}, bf16[128,1024]{1,0:T(8,128)(2,1)S(1)}, u32[]{:S(2)}, u32[]{:S(2)}) collective-permute-start(bf16[128,1024]{1,0:T(8,128)(2,1)} %refs_0_), channel_id=1, source_target_pairs={{0,4},{4,8},{8,12},{12,14},{14,10},{10,6},{6,2},{2,0},{1,3},{5,1},... | collective-permute-start | bytes 786440 | tf_op jit(solution)/shard_map/ppermute | solution.py:76
  3.0 9.2 %collective-permute-start.3 = (bf16[128,1024]{1,0:T(8,128)(2,1)}, bf16[128,1024]{1,0:T(8,128)(2,1)S(1)}, u32[]{:S(2)}, u32[]{:S(2)}) collective-permute-start(bf16[128,1024]{1,0:T(8,128)(2,1)} %refs_0_), channel_id=1, source_target_pairs={{0,3},{4,1},{8,5},{12,9},{14,13},{10,15},{6,11},{2,7},{1,4},{5,8},... | collective-permute-start | bytes 786440 | tf_op jit(solution)/shard_map/ppermute | solution.py:76
  4.4 20.1 %collective-permute-start.10 = (bf16[128,1024]{1,0:T(8,128)(2,1)}, bf16[128,1024]{1,0:T(8,128)(2,1)S(1)}, u32[]{:S(2)}, u32[]{:S(2)}) collective-permute-start(bf16[128,1024]{1,0:T(8,128)(2,1)} %refs_0_), channel_id=1, source_target_pairs={{0,1},{1,0},{2,3},{3,2},{4,5},{5,4},{6,7},{7,6},{8,9},{9,8},{10,11... | collective-permute-start | bytes 786440 | tf_op jit(solution)/shard_map/ppermute | solution.py:76
  9.0 7.0 %collective-permute-start.4 = (bf16[128,1024]{1,0:T(8,128)(2,1)S(1)}, bf16[128,1024]{1,0:T(8,128)(2,1)S(1)}, u32[]{:S(2)}, u32[]{:S(2)}) collective-permute-start(bf16[128,1024]{1,0:T(8,128)(2,1)S(1)} %collective-permute-done.2.refs_1_), channel_id=1, source_target_pairs={{0,4},{4,8},{8,12},{12,14},{14,10},{10,6},{6,2},{2,0},{1,3},{5,1},... | collective-permute-start | bytes 786440 | tf_op jit(solution)/shard_map/ppermute | solution.py:76
  11.4 6.8 %collective-permute-start = (bf16[2,64,1024]{2,1,0:T(8,128)(2,1)S(1)}, bf16[2,64,1024]{2,1,0:T(8,128)(2,1)S(1)}, u32[]{:S(2)}, u32[]{:S(2)}) collective-permute-start(bf16[2,64,1024]{2,1,0:T(8,128)(2,1)S(1)} %pad_maximum_fusion), channel_id=1, source_target_pairs={{0,1},{1,0},{2,3},{3,2},{4,5},{5,4},{6,7},{7,6},{8,9},{9,8},{10,11... | collective-permute-start | bytes 786440 | tf_op jit(solution)/shard_map/ppermute | solution.py:76
  12.3 8.1 %collective-permute-start.5 = (bf16[128,1024]{1,0:T(8,128)(2,1)S(1)}, bf16[128,1024]{1,0:T(8,128)(2,1)S(1)}, u32[]{:S(2)}, u32[]{:S(2)}) collective-permute-start(bf16[128,1024]{1,0:T(8,128)(2,1)S(1)} %collective-permute-done.3.refs_2_), channel_id=1, source_target_pairs={{0,4},{4,8},{8,12},{12,14},{14,10},{10,6},{6,2},{2,0},{1,3},{5,1},... | collective-permute-start | bytes 786440 | tf_op jit(solution)/shard_map/ppermute | solution.py:76
  16.0 8.4 %collective-permute-start.6 = (bf16[128,1024]{1,0:T(8,128)(2,1)S(1)}, bf16[128,1024]{1,0:T(8,128)(2,1)S(1)}, u32[]{:S(2)}, u32[]{:S(2)}) collective-permute-start(bf16[128,1024]{1,0:T(8,128)(2,1)S(1)} %collective-permute-done.4.refs_3_), channel_id=1, source_target_pairs={{0,4},{4,8},{8,12},{12,14},{14,10},{10,6},{6,2},{2,0},{1,3},{5,1},... | collective-permute-start | bytes 786440 | tf_op jit(solution)/shard_map/ppermute | solution.py:76
  20.0 15.0 %collective-permute-start.1 = (bf16[4,2,2,64,128]{4,3,2,1,0:T(8,128)(2,1)}, bf16[4,2,2,64,128]{4,3,2,1,0:T(8,128)(2,1)S(1)}, u32[]{:S(2)}, u32[]{:S(2)}) collective-permute-start(bf16[4,2,2,64,128]{4,3,2,1,0:T(8,128)(2,1)} %get-tuple-element.21), channel_id=1, source_target_pairs={{0,2},{1,3},{2,0},{3,1},{4,6},{5,7},{6,4},{7,5},{8,10},{9,11},{10,... | collective-permute-start | bytes 786440 | tf_op jit(solution)/shard_map/ppermute | solution.py:76
  20.4 15.0 %collective-permute-start.11 = (bf16[128,1024]{1,0:T(8,128)(2,1)S(1)}, bf16[128,1024]{1,0:T(8,128)(2,1)S(1)}, u32[]{:S(2)}, u32[]{:S(2)}) collective-permute-start(bf16[128,1024]{1,0:T(8,128)(2,1)S(1)} %collective-permute-done.2.refs_1_), channel_id=1, source_target_pairs={{0,1},{1,0},{2,3},{3,2},{4,5},{5,4},{6,7},{7,6},{8,9},{9,8},{10,11... | collective-permute-start | bytes 786440 | tf_op jit(solution)/shard_map/ppermute | solution.py:76
  24.4 11.2 %collective-permute-start.12 = (bf16[128,1024]{1,0:T(8,128)(2,1)S(1)}, bf16[128,1024]{1,0:T(8,128)(2,1)S(1)}, u32[]{:S(2)}, u32[]{:S(2)}) collective-permute-start(bf16[128,1024]{1,0:T(8,128)(2,1)S(1)} %collective-permute-done.3.refs_2_), channel_id=1, source_target_pairs={{0,1},{1,0},{2,3},{3,2},{4,5},{5,4},{6,7},{7,6},{8,9},{9,8},{10,11... | collective-permute-start | bytes 786440 | tf_op jit(solution)/shard_map/ppermute | solution.py:76
  24.4 11.5 %collective-permute-start.7 = (bf16[128,1024]{1,0:T(8,128)(2,1)S(1)}, bf16[128,1024]{1,0:T(8,128)(2,1)S(1)}, u32[]{:S(2)}, u32[]{:S(2)}) collective-permute-start(bf16[128,1024]{1,0:T(8,128)(2,1)S(1)} %collective-permute-done.5.refs_4_), channel_id=1, source_target_pairs={{0,4},{4,8},{8,12},{12,14},{14,10},{10,6},{6,2},{2,0},{1,3},{5,1},... | collective-permute-start | bytes 786440 | tf_op jit(solution)/shard_map/ppermute | solution.py:76
  24.4 11.7 %collective-permute-start.9 = (bf16[128,1024]{1,0:T(8,128)(2,1)S(1)}, bf16[128,1024]{1,0:T(8,128)(2,1)S(1)}, u32[]{:S(2)}, u32[]{:S(2)}) collective-permute-start(bf16[128,1024]{1,0:T(8,128)(2,1)S(1)} %collective-permute-done.6.refs_5_), channel_id=1, source_target_pairs={{0,4},{4,8},{8,12},{12,14},{14,10},{10,6},{6,2},{2,0},{1,3},{5,1},... | collective-permute-start | bytes 786440 | tf_op jit(solution)/shard_map/ppermute | solution.py:76
  35.6 7.6 %collective-permute-start.15 = (bf16[128,1024]{1,0:T(8,128)(2,1)S(1)}, bf16[128,1024]{1,0:T(8,128)(2,1)S(1)}, u32[]{:S(2)}, u32[]{:S(2)}) collective-permute-start(bf16[128,1024]{1,0:T(8,128)(2,1)S(1)} %collective-permute-done.6.refs_5_), channel_id=1, source_target_pairs={{0,1},{1,0},{2,3},{3,2},{4,5},{5,4},{6,7},{7,6},{8,9},{9,8},{10,11... | collective-permute-start | bytes 786440 | tf_op jit(solution)/shard_map/ppermute | solution.py:76
  35.9 7.3 %collective-permute-start.16 = (bf16[128,1024]{1,0:T(8,128)(2,1)S(1)}, bf16[128,1024]{1,0:T(8,128)(2,1)S(1)}, u32[]{:S(2)}, u32[]{:S(2)}) collective-permute-start(bf16[128,1024]{1,0:T(8,128)(2,1)S(1)} %collective-permute-done.7.refs_6_), channel_id=1, source_target_pairs={{0,1},{1,0},{2,3},{3,2},{4,5},{5,4},{6,7},{7,6},{8,9},{9,8},{10,11... | collective-permute-start | bytes 786440 | tf_op jit(solution)/shard_map/ppermute | solution.py:76
  36.1 7.1 %collective-permute-start.17 = (bf16[128,1024]{1,0:T(8,128)(2,1)S(1)}, bf16[128,1024]{1,0:T(8,128)(2,1)S(1)}, u32[]{:S(2)}, u32[]{:S(2)}) collective-permute-start(bf16[128,1024]{1,0:T(8,128)(2,1)S(1)} %collective-permute-done.9.refs_7_), channel_id=1, source_target_pairs={{0,1},{1,0},{2,3},{3,2},{4,5},{5,4},{6,7},{7,6},{8,9},{9,8},{10,11... | collective-permute-start | bytes 786440 | tf_op jit(solution)/shard_map/ppermute | solution.py:76
  36.6 22.6 %collective-permute-start.21 = (bf16[2,2,2,64,128]{4,3,2,1,0:T(8,128)(2,1)S(1)}, bf16[2,2,2,64,128]{4,3,2,1,0:T(8,128)(2,1)S(1)}, u32[]{:S(2)}, u32[]{:S(2)}) collective-permute-start(bf16[2,2,2,64,128]{4,3,2,1,0:T(8,128)(2,1)S(1)} %pad_maximum_fusion.1), channel_id=1, source_target_pairs={{0,4},{1,5},{2,6},{3,7},{4,0},{5,1},{6,2},{7,3},{8,12},{9,13},{10,... | collective-permute-start | bytes 393224 | tf_op jit(solution)/shard_map/ppermute | solution.py:76
  40.9 18.4 %collective-permute-start.22 = (bf16[2,2,2,64,128]{4,3,2,1,0:T(8,128)(2,1)S(1)}, bf16[2,2,2,64,128]{4,3,2,1,0:T(8,128)(2,1)S(1)}, u32[]{:S(2)}, u32[]{:S(2)}) collective-permute-start(bf16[2,2,2,64,128]{4,3,2,1,0:T(8,128)(2,1)S(1)} %pad_maximum_fusion.2), channel_id=1, source_target_pairs={{0,8},{1,9},{2,10},{3,11},{4,12},{5,13},{6,14},{7,15},{8,0},{9,1},... | collective-permute-start | bytes 393224 | tf_op jit(solution)/shard_map/ppermute | solution.py:76
  53.8 8.6 %collective-permute-start.23 = (bf16[2,2,2,64,128]{4,3,2,1,0:T(8,128)(2,1)S(1)}, bf16[2,2,2,64,128]{4,3,2,1,0:T(8,128)(2,1)S(1)}, u32[]{:S(2)}, u32[]{:S(2)}) collective-permute-start(bf16[2,2,2,64,128]{4,3,2,1,0:T(8,128)(2,1)S(1)} %pad_maximum_fusion.3), channel_id=1, source_target_pairs={{0,12},{1,13},{2,14},{3,15},{4,8},{5,9},{6,10},{7,11},{8,4},{9,5},... | collective-permute-start | bytes 393224 | tf_op jit(solution)/shard_map/ppermute | solution.py:76
  65.9 7.5 %collective-permute-start.25 = (bf16[128,1024]{1,0:T(8,128)(2,1)S(1)}, bf16[128,1024]{1,0:T(8,128)(2,1)S(1)}, u32[]{:S(2)}, u32[]{:S(2)}) collective-permute-start(bf16[128,1024]{1,0:T(8,128)(2,1)S(1)} %get-tuple-element.30), channel_id=1, source_target_pairs={{0,4},{4,8},{8,12},{12,14},{14,10},{10,6},{6,2},{2,0},{1,3},{5,1},... | collective-permute-start | bytes 786440 | tf_op jit(solution)/shard_map/ppermute | solution.py:76
  69.3 6.7 %collective-permute-start.29 = (bf16[128,1024]{1,0:T(8,128)(2,1)S(1)}, bf16[128,1024]{1,0:T(8,128)(2,1)S(1)}, u32[]{:S(2)}, u32[]{:S(2)}) collective-permute-start(bf16[128,1024]{1,0:T(8,128)(2,1)S(1)} %get-tuple-element.34), channel_id=1, source_target_pairs={{0,4},{4,8},{8,12},{12,14},{14,10},{10,6},{6,2},{2,0},{1,3},{5,1},... | collective-permute-start | bytes 786440 | tf_op jit(solution)/shard_map/ppermute | solution.py:76
  76.1 6.6 %collective-permute-start.30 = (bf16[128,1024]{1,0:T(8,128)(2,1)S(1)}, bf16[128,1024]{1,0:T(8,128)(2,1)S(1)}, u32[]{:S(2)}, u32[]{:S(2)}) collective-permute-start(bf16[128,1024]{1,0:T(8,128)(2,1)S(1)} %add_convert_fusion.2), channel_id=1, source_target_pairs={{0,4},{4,8},{8,12},{12,14},{14,10},{10,6},{6,2},{2,0},{1,3},{5,1},... | collective-permute-start | bytes 786440 | tf_op jit(solution)/shard_map/ppermute | solution.py:76
  95.5 6.9 %collective-permute-start.34 = (bf16[128,1024]{1,0:T(8,128)(2,1)S(1)}, bf16[128,1024]{1,0:T(8,128)(2,1)S(1)}, u32[]{:S(2)}, u32[]{:S(2)}) collective-permute-start(bf16[128,1024]{1,0:T(8,128)(2,1)S(1)} %collective-permute-done.33.refs_8_), channel_id=1, source_target_pairs={{0,4},{4,8},{8,12},{12,14},{14,10},{10,6},{6,2},{2,0},{1,3},{5,1},... | collective-permute-start | bytes 786440 | tf_op jit(solution)/shard_map/ppermute | solution.py:76
  108.2 6.9 %collective-permute-start.41 = (bf16[128,1024]{1,0:T(8,128)(2,1)S(1)}, bf16[128,1024]{1,0:T(8,128)(2,1)S(1)}, u32[]{:S(2)}, u32[]{:S(2)}) collective-permute-start(bf16[128,1024]{1,0:T(8,128)(2,1)S(1)} %collective-permute-done.34.refs_2_), channel_id=1, source_target_pairs={{0,1},{1,0},{2,3},{3,2},{4,5},{5,4},{6,7},{7,6},{8,9},{9,8},{10,11... | collective-permute-start | bytes 786440 | tf_op jit(solution)/shard_map/ppermute | solution.py:76
  (31 other events, 193.3 us)

commit v12 on v11

--- a/solution.py
+++ b/solution.py
@@ -286,7 +286,7 @@
         in_specs=[SMEM] * 2 + [VMEM] * (len(arrays) + 6) + [HBM] * 2,
         out_specs=[VMEM] * 4,
         scratch_shapes=[pltpu.SemaphoreType.DMA((2, ahead))],
-        compiler_params=pltpu.CompilerParams(vmem_limit_bytes=24 * MIB),
+        compiler_params=pltpu.CompilerParams(vmem_limit_bytes=15 * MIB),
         cost_estimate=pl.CostEstimate(
             flops=2 * TOKENS * weights.size, bytes_accessed=12 * MIB, transcendentals=0
         ),
@@ -483,7 +483,7 @@
             pltpu.VMEM((16, TOKENS, width), jnp.bfloat16),
             pltpu.SemaphoreType.DMA((16,)),
         ],
-        compiler_params=pltpu.CompilerParams(vmem_limit_bytes=24 * MIB),
+        compiler_params=pltpu.CompilerParams(vmem_limit_bytes=15 * MIB),
         cost_estimate=pl.CostEstimate(
             flops=16 * MIB, bytes_accessed=12 * MIB, transcendentals=0
         ),

time: 124 us -> 124 us (level)
  no operation moved by 1% of the time
where the time goes in v12:
time: 124 us
  starting transfers between devices  57.4 us (46%)
  waiting for transfers between devices  33.5 us (27%)
  Pallas kernels  19 us (15%)
  local copies, waits for them, and re-layouts  10.5 us (8%)
  other arithmetic  3.26 us (3%)
    ppermute x47, starting transfers between devices, send(): return lax.ppermute(array, 'tp', pairs)  57.4 us
    ppermute x47, waiting for transfers between devices, send(): return lax.ppermute(array, 'tp', pairs)  33.5 us
    unnamed x16, local copies, waits for them, and re-layouts  9.21 us
    pallas_call x1, Pallas kernels, load_weights(): pl.pallas_call(load_kernel, out_shape=jax.ShapeDtypeStruct((16, width, 2...  4.19 us
    pallas_call x1, Pallas kernels, project(): pl.pallas_call(project_kernel, out_shape=[jax.ShapeDtypeStruct((SPAN, HD)...  4.06 us
    pallas_call x1, Pallas kernels, final_norm(): pl.pallas_call(final_kernel, out_shape=jax.ShapeDtypeStruct((TOKENS, 16 *...  3.65 us
    pallas_call x1, Pallas kernels, more_shares(): pl.pallas_call(functools.partial(more_shares_kernel, first), out_shape=ou...  3.1 us
  transfers between devices with their start and end apart: 47, of which 18 were waited for; matrix products, arithmetic and copies ran while one was open for 4% of the time, Pallas kernels for 11%

profile of v12, /device:TPU:0, one launch (start us, length us, event | category | flops | bytes accessed | tf_op | source)
XLA Modules:
  0.0 124.0 jit_solution(2694203324486169704)
XLA Ops:
  0.5 2.6 %collective-permute-start.2 = (bf16[128,1024]{1,0:T(8,128)(2,1)}, bf16[128,1024]{1,0:T(8,128)(2,1)S(1)}, u32[]{:S(2)}, u32[]{:S(2)}) collective-permute-start(bf16[128,1024]{1,0:T(8,128)(2,1)} %refs_0_), channel_id=1, source_target_pairs={{0,4},{4,8},{8,12},{12,14},{14,10},{10,6},{6,2},{2,0},{1,3},{5,1},... | collective-permute-start | bytes 786440 | tf_op jit(solution)/shard_map/ppermute | solution.py:76
  5.7 3.3 %collective-permute-done.2.refs_1_ = bf16[128,1024]{1,0:T(8,128)(2,1)S(1)} collective-permute-done((bf16[128,1024]{1,0:T(8,128)(2,1)}, bf16[128,1024]{1,0:T(8,128)(2,1)S(1)}, u32[]{:S(2)}, u32[]{:S(2)}) %collective-permute-start.2) | collective-permute-done | bytes 262176 | tf_op jit(solution)/shard_map/ppermute | solution.py:76
  9.0 2.4 %collective-permute-start.4 = (bf16[128,1024]{1,0:T(8,128)(2,1)S(1)}, bf16[128,1024]{1,0:T(8,128)(2,1)S(1)}, u32[]{:S(2)}, u32[]{:S(2)}) collective-permute-start(bf16[128,1024]{1,0:T(8,128)(2,1)S(1)} %collective-permute-done.2.refs_1_), channel_id=1, source_target_pairs={{0,4},{4,8},{8,12},{12,14},{14,10},{10,6},{6,2},{2,0},{1,3},{5,1},... | collective-permute-start | bytes 786440 | tf_op jit(solution)/shard_map/ppermute | solution.py:76
  20.4 4.1 %collective-permute-done.6.refs_5_ = bf16[128,1024]{1,0:T(8,128)(2,1)S(1)} collective-permute-done((bf16[128,1024]{1,0:T(8,128)(2,1)S(1)}, bf16[128,1024]{1,0:T(8,128)(2,1)S(1)}, u32[]{:S(2)}, u32[]{:S(2)}) %collective-permute-start.6) | collective-permute-done | bytes 262176 | tf_op jit(solution)/shard_map/ppermute | solution.py:76
  27.4 4.2 %load_weights.1.refs_17_ = bf16[16,1024,256]{2,1,0:T(8,128)(2,1)S(1)} custom-call(s32[16]{0:T(128)S(1)} %stack.108.ids, bf16[16384,128]{1,0:T(8,128)(2,1)} %wq.1, bf16[16384,128]{1,0:T(8,128)(2,1)} %wkv.1), custom_call_target="tpu_custom_call" | custom-call | bytes 16777216 | tf_op jit(solution)/shard_map/load_weights/pallas_call | solution.py:238
  31.6 3.3 %copy-done = bf16[16,1024,256]{2,1,0:T(8,128)(2,1)} copy-done((bf16[16,1024,256]{2,1,0:T(8,128)(2,1)}, bf16[16,1024,256]{2,1,0:T(8,128)(2,1)S(1)}, u32[]{:S(2)}) %copy-start) | copy-done | bytes 8388632
  36.6 4.3 %collective-permute-start.21 = (bf16[2,2,2,64,128]{4,3,2,1,0:T(8,128)(2,1)S(1)}, bf16[2,2,2,64,128]{4,3,2,1,0:T(8,128)(2,1)S(1)}, u32[]{:S(2)}, u32[]{:S(2)}) collective-permute-start(bf16[2,2,2,64,128]{4,3,2,1,0:T(8,128)(2,1)S(1)} %pad_maximum_fusion.1), channel_id=1, source_target_pairs={{0,4},{1,5},{2,6},{3,7},{4,0},{5,1},{6,2},{7,3},{8,12},{9,13},{10,... | collective-permute-start | bytes 393224 | tf_op jit(solution)/shard_map/ppermute | solution.py:76
  43.2 3.4 %copy-done.1 = bf16[16,1024,256]{2,1,0:T(8,128)(2,1)S(1)} copy-done((bf16[16,1024,256]{2,1,0:T(8,128)(2,1)S(1)}, bf16[16,1024,256]{2,1,0:T(8,128)(2,1)}, u32[]{:S(2)}) %copy-start.1) | copy-done | bytes 8388632
  49.1 4.1 %norm_project.1 = (bf16[64,128]{1,0:T(8,128)(2,1)S(1)}, bf16[64,128]{1,0:T(8,128)(2,1)S(1)}, bf16[128,128]{1,0:T(8,128)(2,1)S(1)}, bf16[2,256,1024]{2,1,0:T(8,128)(2,1)S(1)}) custom-call(s32[16]{0:T(128)S(1)} %stack.108.ids, s32[8]{0:T(128)S(1)} %stack.117.to, bf16[128,1024]{1,0:T(8,128)(2,1)S(1)} %copy-done.2, ...), custom_call_target="tpu_custom_call" | custom-call | flops 1073741824 | bytes 12582912 | tf_op jit(solution)/shard_map/norm_project/pallas_call | solution.py:279
  53.8 3.6 %collective-permute-start.23 = (bf16[2,2,2,64,128]{4,3,2,1,0:T(8,128)(2,1)S(1)}, bf16[2,2,2,64,128]{4,3,2,1,0:T(8,128)(2,1)S(1)}, u32[]{:S(2)}, u32[]{:S(2)}) collective-permute-start(bf16[2,2,2,64,128]{4,3,2,1,0:T(8,128)(2,1)S(1)} %pad_maximum_fusion.3), channel_id=1, source_target_pairs={{0,12},{1,13},{2,14},{3,15},{4,8},{5,9},{6,10},{7,11},{8,4},{9,5},... | collective-permute-start | bytes 393224 | tf_op jit(solution)/shard_map/ppermute | solution.py:76
  59.2 3.2 %collective-permute-done.23.refs_4_ = bf16[2,2,2,64,128]{4,3,2,1,0:T(8,128)(2,1)S(1)} collective-permute-done((bf16[2,2,2,64,128]{4,3,2,1,0:T(8,128)(2,1)S(1)}, bf16[2,2,2,64,128]{4,3,2,1,0:T(8,128)(2,1)S(1)}, u32[]{:S(2)}, u32[]{:S(2)}) %collective-permute-start.23) | collective-permute-done | bytes 131104 | tf_op jit(solution)/shard_map/ppermute | solution.py:76
  65.9 3.4 %collective-permute-start.25 = (bf16[128,1024]{1,0:T(8,128)(2,1)S(1)}, bf16[128,1024]{1,0:T(8,128)(2,1)S(1)}, u32[]{:S(2)}, u32[]{:S(2)}) collective-permute-start(bf16[128,1024]{1,0:T(8,128)(2,1)S(1)} %get-tuple-element.30), channel_id=1, source_target_pairs={{0,4},{4,8},{8,12},{12,14},{14,10},{10,6},{6,2},{2,0},{1,3},{5,1},... | collective-permute-start | bytes 786440 | tf_op jit(solution)/shard_map/ppermute | solution.py:76
  70.2 3.1 %shares_2.1 = (f32[128,1024]{1,0:T(8,128)S(1)}, f32[128,1024]{1,0:T(8,128)S(1)}, f32[128,1024]{1,0:T(8,128)S(1)}, f32[128,1024]{1,0:T(8,128)S(1)}, f32[128,1024]{1,0:T(8,128)S(1)}, /*index=5*/f32[128,1024]{1,0:T(8,128)S(1)}) custom-call(s32[1]{0:T(128)} %bitcast.16.core, s32[8]{0:T(128)S(1)} %stack.117.to, bf16[64,256]{1,0:T(8,128)(2,1)S(1)} %attend.1.attn, ...), custom_call_target="tpu_custom_call" | custom-call | flops 402653184 | bytes 6291456 | tf_op jit(solution)/shard_map/shares_2/pallas_call | solution.py:436
  73.5 2.3 %collective-permute-start.26 = (bf16[128,1024]{1,0:T(8,128)(2,1)S(1)}, bf16[128,1024]{1,0:T(8,128)(2,1)S(1)}, u32[]{:S(2)}, u32[]{:S(2)}) collective-permute-start(bf16[128,1024]{1,0:T(8,128)(2,1)S(1)} %add_convert_fusion.5), channel_id=1, source_target_pairs={{0,4},{4,8},{8,12},{12,14},{14,10},{10,6},{6,2},{2,0},{1,3},{5,1},... | collective-permute-start | bytes 786440 | tf_op jit(solution)/shard_map/ppermute | solution.py:76
  76.1 2.5 %collective-permute-start.30 = (bf16[128,1024]{1,0:T(8,128)(2,1)S(1)}, bf16[128,1024]{1,0:T(8,128)(2,1)S(1)}, u32[]{:S(2)}, u32[]{:S(2)}) collective-permute-start(bf16[128,1024]{1,0:T(8,128)(2,1)S(1)} %add_convert_fusion.2), channel_id=1, source_target_pairs={{0,4},{4,8},{8,12},{12,14},{14,10},{10,6},{6,2},{2,0},{1,3},{5,1},... | collective-permute-start | bytes 786440 | tf_op jit(solution)/shard_map/ppermute | solution.py:76
  80.0 2.3 %collective-permute-start.27 = (bf16[128,1024]{1,0:T(8,128)(2,1)S(1)}, bf16[128,1024]{1,0:T(8,128)(2,1)S(1)}, u32[]{:S(2)}, u32[]{:S(2)}) collective-permute-start(bf16[128,1024]{1,0:T(8,128)(2,1)S(1)} %add_convert_fusion.4), channel_id=1, source_target_pairs={{0,4},{4,8},{8,12},{12,14},{14,10},{10,6},{6,2},{2,0},{1,3},{5,1},... | collective-permute-start | bytes 786440 | tf_op jit(solution)/shard_map/ppermute | solution.py:76
  83.2 3.2 %collective-permute-done.27 = bf16[128,1024]{1,0:T(8,128)(2,1)S(1)} collective-permute-done((bf16[128,1024]{1,0:T(8,128)(2,1)S(1)}, bf16[128,1024]{1,0:T(8,128)(2,1)S(1)}, u32[]{:S(2)}, u32[]{:S(2)}) %collective-permute-start.27) | collective-permute-done | bytes 262176 | tf_op jit(solution)/shard_map/ppermute | solution.py:76
  86.5 2.3 %collective-permute-start.28 = (bf16[128,1024]{1,0:T(8,128)(2,1)S(1)}, bf16[128,1024]{1,0:T(8,128)(2,1)S(1)}, u32[]{:S(2)}, u32[]{:S(2)}) collective-permute-start(bf16[128,1024]{1,0:T(8,128)(2,1)S(1)} %add_convert_fusion.3), channel_id=1, source_target_pairs={{0,4},{4,8},{8,12},{12,14},{14,10},{10,6},{6,2},{2,0},{1,3},{5,1},... | collective-permute-start | bytes 786440 | tf_op jit(solution)/shard_map/ppermute | solution.py:76
  89.0 3.9 %collective-permute-done.28 = bf16[128,1024]{1,0:T(8,128)(2,1)S(1)} collective-permute-done((bf16[128,1024]{1,0:T(8,128)(2,1)S(1)}, bf16[128,1024]{1,0:T(8,128)(2,1)S(1)}, u32[]{:S(2)}, u32[]{:S(2)}) %collective-permute-start.28) | collective-permute-done | bytes 262176 | tf_op jit(solution)/shard_map/ppermute | solution.py:76
  93.1 2.3 %collective-permute-start.32 = (bf16[128,1024]{1,0:T(8,128)(2,1)S(1)}, bf16[128,1024]{1,0:T(8,128)(2,1)S(1)}, u32[]{:S(2)}, u32[]{:S(2)}) collective-permute-start(bf16[128,1024]{1,0:T(8,128)(2,1)S(1)} %add_convert_fusion.refs_0_), channel_id=1, source_target_pairs={{0,4},{4,8},{8,12},{12,14},{14,10},{10,6},{6,2},{2,0},{1,3},{5,1},... | collective-permute-start | bytes 786440 | tf_op jit(solution)/shard_map/ppermute | solution.py:76
  96.9 2.6 %collective-permute-done.32.refs_1_ = bf16[128,1024]{1,0:T(8,128)(2,1)S(1)} collective-permute-done((bf16[128,1024]{1,0:T(8,128)(2,1)S(1)}, bf16[128,1024]{1,0:T(8,128)(2,1)S(1)}, u32[]{:S(2)}, u32[]{:S(2)}) %collective-permute-start.32) | collective-permute-done | bytes 262176 | tf_op jit(solution)/shard_map/ppermute | solution.py:76
  112.3 2.3 %collective-permute-start.39 = (bf16[128,1024]{1,0:T(8,128)(2,1)S(1)}, bf16[128,1024]{1,0:T(8,128)(2,1)S(1)}, u32[]{:S(2)}, u32[]{:S(2)}) collective-permute-start(bf16[128,1024]{1,0:T(8,128)(2,1)S(1)} %collective-permute-done.37.refs_5_), channel_id=1, source_target_pairs={{0,4},{4,8},{8,12},{12,14},{14,10},{10,6},{6,2},{2,0},{1,3},{5,1},... | collective-permute-start | bytes 786440 | tf_op jit(solution)/shard_map/ppermute | solution.py:76
  115.6 3.0 %collective-permute-done.39.refs_7_ = bf16[128,1024]{1,0:T(8,128)(2,1)S(1)} collective-permute-done((bf16[128,1024]{1,0:T(8,128)(2,1)S(1)}, bf16[128,1024]{1,0:T(8,128)(2,1)S(1)}, u32[]{:S(2)}, u32[]{:S(2)}) %collective-permute-start.39) | collective-permute-done | bytes 262176 | tf_op jit(solution)/shard_map/ppermute | solution.py:76
  120.2 3.6 %final_norm.1 = bf16[128,16384]{1,0:T(8,128)(2,1)} custom-call(s32[16]{0:T(128)S(1)} %stack.108.ids, bf16[128,1024]{1,0:T(8,128)(2,1)S(1)} %add_convert_fusion.refs_0_, bf16[128,1024]{1,0:T(8,128)(2,1)S(1)} %collective-permute-done.32.refs_1_, bf16[128,1024]{1,0:T(8,128)(2,1)S(1)} %collective-permute-done.34.refs_2_, ...), custom_call_target="tpu_custom_call" | custom-call | flops 16777216 | bytes 12582912 | tf_op jit(solution)/shard_map/final_norm/pallas_call | solution.py:477
  (118 shorter events, 48.1 us)
Async XLA Ops:
  0.0 24.4 %collective-permute-start.8 = (bf16[128,16384]{1,0:T(8,128)(2,1)}, bf16[128,16384]{1,0:T(8,128)(2,1)}, u32[]{:S(2)}, u32[]{:S(2)}) collective-permute-start(bf16[128,16384]{1,0:T(8,128)(2,1)} %weight.1), channel_id=1, source_target_pairs={{0,1},{1,0},{2,3},{3,2},{4,5},{5,4},{6,7},{7,6},{8,9},{9,8},{10,11... | collective-permute-start | bytes 12582920 | tf_op jit(solution)/shard_map/ppermute | solution.py:76
  0.5 8.6 %collective-permute-start.2 = (bf16[128,1024]{1,0:T(8,128)(2,1)}, bf16[128,1024]{1,0:T(8,128)(2,1)S(1)}, u32[]{:S(2)}, u32[]{:S(2)}) collective-permute-start(bf16[128,1024]{1,0:T(8,128)(2,1)} %refs_0_), channel_id=1, source_target_pairs={{0,4},{4,8},{8,12},{12,14},{14,10},{10,6},{6,2},{2,0},{1,3},{5,1},... | collective-permute-start | bytes 786440 | tf_op jit(solution)/shard_map/ppermute | solution.py:76
  3.0 9.2 %collective-permute-start.3 = (bf16[128,1024]{1,0:T(8,128)(2,1)}, bf16[128,1024]{1,0:T(8,128)(2,1)S(1)}, u32[]{:S(2)}, u32[]{:S(2)}) collective-permute-start(bf16[128,1024]{1,0:T(8,128)(2,1)} %refs_0_), channel_id=1, source_target_pairs={{0,3},{4,1},{8,5},{12,9},{14,13},{10,15},{6,11},{2,7},{1,4},{5,8},... | collective-permute-start | bytes 786440 | tf_op jit(solution)/shard_map/ppermute | solution.py:76
  4.4 20.1 %collective-permute-start.10 = (bf16[128,1024]{1,0:T(8,128)(2,1)}, bf16[128,1024]{1,0:T(8,128)(2,1)S(1)}, u32[]{:S(2)}, u32[]{:S(2)}) collective-permute-start(bf16[128,1024]{1,0:T(8,128)(2,1)} %refs_0_), channel_id=1, source_target_pairs={{0,1},{1,0},{2,3},{3,2},{4,5},{5,4},{6,7},{7,6},{8,9},{9,8},{10,11... | collective-permute-start | bytes 786440 | tf_op jit(solution)/shard_map/ppermute | solution.py:76
  9.0 7.0 %collective-permute-start.4 = (bf16[128,1024]{1,0:T(8,128)(2,1)S(1)}, bf16[128,1024]{1,0:T(8,128)(2,1)S(1)}, u32[]{:S(2)}, u32[]{:S(2)}) collective-permute-start(bf16[128,1024]{1,0:T(8,128)(2,1)S(1)} %collective-permute-done.2.refs_1_), channel_id=1, source_target_pairs={{0,4},{4,8},{8,12},{12,14},{14,10},{10,6},{6,2},{2,0},{1,3},{5,1},... | collective-permute-start | bytes 786440 | tf_op jit(solution)/shard_map/ppermute | solution.py:76
  11.4 6.8 %collective-permute-start = (bf16[2,64,1024]{2,1,0:T(8,128)(2,1)S(1)}, bf16[2,64,1024]{2,1,0:T(8,128)(2,1)S(1)}, u32[]{:S(2)}, u32[]{:S(2)}) collective-permute-start(bf16[2,64,1024]{2,1,0:T(8,128)(2,1)S(1)} %pad_maximum_fusion), channel_id=1, source_target_pairs={{0,1},{1,0},{2,3},{3,2},{4,5},{5,4},{6,7},{7,6},{8,9},{9,8},{10,11... | collective-permute-start | bytes 786440 | tf_op jit(solution)/shard_map/ppermute | solution.py:76
  12.3 8.1 %collective-permute-start.5 = (bf16[128,1024]{1,0:T(8,128)(2,1)S(1)}, bf16[128,1024]{1,0:T(8,128)(2,1)S(1)}, u32[]{:S(2)}, u32[]{:S(2)}) collective-permute-start(bf16[128,1024]{1,0:T(8,128)(2,1)S(1)} %collective-permute-done.3.refs_2_), channel_id=1, source_target_pairs={{0,4},{4,8},{8,12},{12,14},{14,10},{10,6},{6,2},{2,0},{1,3},{5,1},... | collective-permute-start | bytes 786440 | tf_op jit(solution)/shard_map/ppermute | solution.py:76
  16.0 8.4 %collective-permute-start.6 = (bf16[128,1024]{1,0:T(8,128)(2,1)S(1)}, bf16[128,1024]{1,0:T(8,128)(2,1)S(1)}, u32[]{:S(2)}, u32[]{:S(2)}) collective-permute-start(bf16[128,1024]{1,0:T(8,128)(2,1)S(1)} %collective-permute-done.4.refs_3_), channel_id=1, source_target_pairs={{0,4},{4,8},{8,12},{12,14},{14,10},{10,6},{6,2},{2,0},{1,3},{5,1},... | collective-permute-start | bytes 786440 | tf_op jit(solution)/shard_map/ppermute | solution.py:76
  20.0 15.0 %collective-permute-start.1 = (bf16[4,2,2,64,128]{4,3,2,1,0:T(8,128)(2,1)}, bf16[4,2,2,64,128]{4,3,2,1,0:T(8,128)(2,1)S(1)}, u32[]{:S(2)}, u32[]{:S(2)}) collective-permute-start(bf16[4,2,2,64,128]{4,3,2,1,0:T(8,128)(2,1)} %get-tuple-element.21), channel_id=1, source_target_pairs={{0,2},{1,3},{2,0},{3,1},{4,6},{5,7},{6,4},{7,5},{8,10},{9,11},{10,... | collective-permute-start | bytes 786440 | tf_op jit(solution)/shard_map/ppermute | solution.py:76
  20.4 15.0 %collective-permute-start.11 = (bf16[128,1024]{1,0:T(8,128)(2,1)S(1)}, bf16[128,1024]{1,0:T(8,128)(2,1)S(1)}, u32[]{:S(2)}, u32[]{:S(2)}) collective-permute-start(bf16[128,1024]{1,0:T(8,128)(2,1)S(1)} %collective-permute-done.2.refs_1_), channel_id=1, source_target_pairs={{0,1},{1,0},{2,3},{3,2},{4,5},{5,4},{6,7},{7,6},{8,9},{9,8},{10,11... | collective-permute-start | bytes 786440 | tf_op jit(solution)/shard_map/ppermute | solution.py:76
  24.4 11.2 %collective-permute-start.12 = (bf16[128,1024]{1,0:T(8,128)(2,1)S(1)}, bf16[128,1024]{1,0:T(8,128)(2,1)S(1)}, u32[]{:S(2)}, u32[]{:S(2)}) collective-permute-start(bf16[128,1024]{1,0:T(8,128)(2,1)S(1)} %collective-permute-done.3.refs_2_), channel_id=1, source_target_pairs={{0,1},{1,0},{2,3},{3,2},{4,5},{5,4},{6,7},{7,6},{8,9},{9,8},{10,11... | collective-permute-start | bytes 786440 | tf_op jit(solution)/shard_map/ppermute | solution.py:76
  24.4 11.5 %collective-permute-start.7 = (bf16[128,1024]{1,0:T(8,128)(2,1)S(1)}, bf16[128,1024]{1,0:T(8,128)(2,1)S(1)}, u32[]{:S(2)}, u32[]{:S(2)}) collective-permute-start(bf16[128,1024]{1,0:T(8,128)(2,1)S(1)} %collective-permute-done.5.refs_4_), channel_id=1, source_target_pairs={{0,4},{4,8},{8,12},{12,14},{14,10},{10,6},{6,2},{2,0},{1,3},{5,1},... | collective-permute-start | bytes 786440 | tf_op jit(solution)/shard_map/ppermute | solution.py:76
  24.4 11.7 %collective-permute-start.9 = (bf16[128,1024]{1,0:T(8,128)(2,1)S(1)}, bf16[128,1024]{1,0:T(8,128)(2,1)S(1)}, u32[]{:S(2)}, u32[]{:S(2)}) collective-permute-start(bf16[128,1024]{1,0:T(8,128)(2,1)S(1)} %collective-permute-done.6.refs_5_), channel_id=1, source_target_pairs={{0,4},{4,8},{8,12},{12,14},{14,10},{10,6},{6,2},{2,0},{1,3},{5,1},... | collective-permute-start | bytes 786440 | tf_op jit(solution)/shard_map/ppermute | solution.py:76
  35.6 7.6 %collective-permute-start.15 = (bf16[128,1024]{1,0:T(8,128)(2,1)S(1)}, bf16[128,1024]{1,0:T(8,128)(2,1)S(1)}, u32[]{:S(2)}, u32[]{:S(2)}) collective-permute-start(bf16[128,1024]{1,0:T(8,128)(2,1)S(1)} %collective-permute-done.6.refs_5_), channel_id=1, source_target_pairs={{0,1},{1,0},{2,3},{3,2},{4,5},{5,4},{6,7},{7,6},{8,9},{9,8},{10,11... | collective-permute-start | bytes 786440 | tf_op jit(solution)/shard_map/ppermute | solution.py:76
  35.9 7.3 %collective-permute-start.16 = (bf16[128,1024]{1,0:T(8,128)(2,1)S(1)}, bf16[128,1024]{1,0:T(8,128)(2,1)S(1)}, u32[]{:S(2)}, u32[]{:S(2)}) collective-permute-start(bf16[128,1024]{1,0:T(8,128)(2,1)S(1)} %collective-permute-done.7.refs_6_), channel_id=1, source_target_pairs={{0,1},{1,0},{2,3},{3,2},{4,5},{5,4},{6,7},{7,6},{8,9},{9,8},{10,11... | collective-permute-start | bytes 786440 | tf_op jit(solution)/shard_map/ppermute | solution.py:76
  36.1 7.1 %collective-permute-start.17 = (bf16[128,1024]{1,0:T(8,128)(2,1)S(1)}, bf16[128,1024]{1,0:T(8,128)(2,1)S(1)}, u32[]{:S(2)}, u32[]{:S(2)}) collective-permute-start(bf16[128,1024]{1,0:T(8,128)(2,1)S(1)} %collective-permute-done.9.refs_7_), channel_id=1, source_target_pairs={{0,1},{1,0},{2,3},{3,2},{4,5},{5,4},{6,7},{7,6},{8,9},{9,8},{10,11... | collective-permute-start | bytes 786440 | tf_op jit(solution)/shard_map/ppermute | solution.py:76
  36.6 22.6 %collective-permute-start.21 = (bf16[2,2,2,64,128]{4,3,2,1,0:T(8,128)(2,1)S(1)}, bf16[2,2,2,64,128]{4,3,2,1,0:T(8,128)(2,1)S(1)}, u32[]{:S(2)}, u32[]{:S(2)}) collective-permute-start(bf16[2,2,2,64,128]{4,3,2,1,0:T(8,128)(2,1)S(1)} %pad_maximum_fusion.1), channel_id=1, source_target_pairs={{0,4},{1,5},{2,6},{3,7},{4,0},{5,1},{6,2},{7,3},{8,12},{9,13},{10,... | collective-permute-start | bytes 393224 | tf_op jit(solution)/shard_map/ppermute | solution.py:76
  40.9 18.4 %collective-permute-start.22 = (bf16[2,2,2,64,128]{4,3,2,1,0:T(8,128)(2,1)S(1)}, bf16[2,2,2,64,128]{4,3,2,1,0:T(8,128)(2,1)S(1)}, u32[]{:S(2)}, u32[]{:S(2)}) collective-permute-start(bf16[2,2,2,64,128]{4,3,2,1,0:T(8,128)(2,1)S(1)} %pad_maximum_fusion.2), channel_id=1, source_target_pairs={{0,8},{1,9},{2,10},{3,11},{4,12},{5,13},{6,14},{7,15},{8,0},{9,1},... | collective-permute-start | bytes 393224 | tf_op jit(solution)/shard_map/ppermute | solution.py:76
  53.8 8.6 %collective-permute-start.23 = (bf16[2,2,2,64,128]{4,3,2,1,0:T(8,128)(2,1)S(1)}, bf16[2,2,2,64,128]{4,3,2,1,0:T(8,128)(2,1)S(1)}, u32[]{:S(2)}, u32[]{:S(2)}) collective-permute-start(bf16[2,2,2,64,128]{4,3,2,1,0:T(8,128)(2,1)S(1)} %pad_maximum_fusion.3), channel_id=1, source_target_pairs={{0,12},{1,13},{2,14},{3,15},{4,8},{5,9},{6,10},{7,11},{8,4},{9,5},... | collective-permute-start | bytes 393224 | tf_op jit(solution)/shard_map/ppermute | solution.py:76
  65.9 7.5 %collective-permute-start.25 = (bf16[128,1024]{1,0:T(8,128)(2,1)S(1)}, bf16[128,1024]{1,0:T(8,128)(2,1)S(1)}, u32[]{:S(2)}, u32[]{:S(2)}) collective-permute-start(bf16[128,1024]{1,0:T(8,128)(2,1)S(1)} %get-tuple-element.30), channel_id=1, source_target_pairs={{0,4},{4,8},{8,12},{12,14},{14,10},{10,6},{6,2},{2,0},{1,3},{5,1},... | collective-permute-start | bytes 786440 | tf_op jit(solution)/shard_map/ppermute | solution.py:76
  69.3 6.7 %collective-permute-start.29 = (bf16[128,1024]{1,0:T(8,128)(2,1)S(1)}, bf16[128,1024]{1,0:T(8,128)(2,1)S(1)}, u32[]{:S(2)}, u32[]{:S(2)}) collective-permute-start(bf16[128,1024]{1,0:T(8,128)(2,1)S(1)} %get-tuple-element.34), channel_id=1, source_target_pairs={{0,4},{4,8},{8,12},{12,14},{14,10},{10,6},{6,2},{2,0},{1,3},{5,1},... | collective-permute-start | bytes 786440 | tf_op jit(solution)/shard_map/ppermute | solution.py:76
  76.1 6.6 %collective-permute-start.30 = (bf16[128,1024]{1,0:T(8,128)(2,1)S(1)}, bf16[128,1024]{1,0:T(8,128)(2,1)S(1)}, u32[]{:S(2)}, u32[]{:S(2)}) collective-permute-start(bf16[128,1024]{1,0:T(8,128)(2,1)S(1)} %add_convert_fusion.2), channel_id=1, source_target_pairs={{0,4},{4,8},{8,12},{12,14},{14,10},{10,6},{6,2},{2,0},{1,3},{5,1},... | collective-permute-start | bytes 786440 | tf_op jit(solution)/shard_map/ppermute | solution.py:76
  95.5 6.9 %collective-permute-start.34 = (bf16[128,1024]{1,0:T(8,128)(2,1)S(1)}, bf16[128,1024]{1,0:T(8,128)(2,1)S(1)}, u32[]{:S(2)}, u32[]{:S(2)}) collective-permute-start(bf16[128,1024]{1,0:T(8,128)(2,1)S(1)} %collective-permute-done.33.refs_8_), channel_id=1, source_target_pairs={{0,4},{4,8},{8,12},{12,14},{14,10},{10,6},{6,2},{2,0},{1,3},{5,1},... | collective-permute-start | bytes 786440 | tf_op jit(solution)/shard_map/ppermute | solution.py:76
  108.2 6.9 %collective-permute-start.41 = (bf16[128,1024]{1,0:T(8,128)(2,1)S(1)}, bf16[128,1024]{1,0:T(8,128)(2,1)S(1)}, u32[]{:S(2)}, u32[]{:S(2)}) collective-permute-start(bf16[128,1024]{1,0:T(8,128)(2,1)S(1)} %collective-permute-done.34.refs_2_), channel_id=1, source_target_pairs={{0,1},{1,0},{2,3},{3,2},{4,5},{5,4},{6,7},{7,6},{8,9},{9,8},{10,11... | collective-permute-start | bytes 786440 | tf_op jit(solution)/shard_map/ppermute | solution.py:76
  (31 other events, 193.3 us)

commit v13 on v8

--- a/solution.py
+++ b/solution.py
@@ -455,11 +455,29 @@
     return dict(zip(SHARES[first:last], arrays))
 
 
+def squares_kernel(*refs):
+    refs[-1][...] = square_sums(refs[:-1], jnp.zeros((TOKENS, 128), jnp.float32))
+
+
+def squares_of(blocks):
+    return pl.pallas_call(
+        squares_kernel,
+        out_shape=jax.ShapeDtypeStruct((TOKENS, 128), jnp.float32),
+        in_specs=[VMEM] * len(blocks),
+        out_specs=VMEM,
+        compiler_params=pltpu.CompilerParams(vmem_limit_bytes=16 * MIB),
+        cost_estimate=pl.CostEstimate(
+            flops=4 * MIB, bytes_accessed=len(blocks) * MIB // 4, transcendentals=0
+        ),
+        name="squares",
+    )(*blocks)
+
+
 def final_kernel(ids, *refs):
     blocks, refs = refs[:16], refs[16:]
-    gain, out, staged, sems = refs
+    squares, gain, out, staged, sems = refs
     width = staged.shape[2]
-    factors = all_factors(blocks)
+    factors = row_factors(square_sums(blocks[15:], squares[...]), 16 * width)
     copies = []
     for i in range(16):
         staged[i] = normed_block(blocks[i], factors, gain[ids[i]])
@@ -474,12 +492,12 @@
         copy.wait()
 
 
-def final_norm(ids, arrays, gain):
+def final_norm(ids, arrays, squares, gain):
     width = arrays[0].shape[1]
     return pl.pallas_call(
         final_kernel,
         out_shape=jax.ShapeDtypeStruct((TOKENS, 16 * width), jnp.bfloat16),
-        in_specs=[SMEM] + [VMEM] * (len(arrays) + 1),
+        in_specs=[SMEM] + [VMEM] * (len(arrays) + 2),
         out_specs=HBM,
         scratch_shapes=[
             pltpu.VMEM((16, TOKENS, width), jnp.bfloat16),
@@ -490,7 +508,7 @@
             flops=16 * MIB, bytes_accessed=12 * MIB, transcendentals=0
         ),
         name="final_norm",
-    )(ids, *arrays, gain)
+    )(ids, *arrays, squares, gain)
 
 
 def per_device_ring(
@@ -530,16 +548,16 @@
     attn_other = send(attn, SWAP)
 
     shares = first_shares(SHARES[:2], core_id, attn, attn_other, first_weights)
-    inputs = (attn, attn_other, o_weight, weight_other)
-    for first, last in ((2, 4), (4, len(SHARES))):
-        shares.update(more_shares(core_id, to, *inputs, first, last))
+    shares.update(
+        more_shares(core_id, to, attn, attn_other, o_weight, weight_other, 2, len(SHARES))
+    )
     one_way, other_way = ring_sum(shares)
     projected = shares[0, 0] + one_way.astype(jnp.float32) + other_way.astype(jnp.float32)
     hidden = (residual.astype(jnp.float32) + projected).astype(jnp.bfloat16)
 
     mine, theirs = ring_gather(hidden)
     gain = ffn_gain.reshape(16, 1, width).astype(jnp.float32)
-    return final_norm(ids, mine + theirs, gain)
+    return final_norm(ids, mine + theirs, squares_of((mine + theirs)[:15]), gain)
 
 
 def per_device(

time: 116 us -> 115 us (level)
  Pallas kernels: 20.3 us -> 18.8 us
    pallas_call x2 -> x1, Pallas kernels: 4.67 us -> 3.1 us  [more_shares(): pl.pallas_call(functools.partial(more_shares_kernel, first), out_shape=ou...]
  transfers between devices with their start and end apart: 47 -> 47, of which waited for: 19 -> 20; matrix products, arithmetic and copies ran while one was open for 4% -> 4% of each run, Pallas kernels for 13% -> 13%
where the time goes in v13:
time: 115 us; the launch traced here: 114 us
  starting transfers between devices  50.2 us (44%)
  waiting for transfers between devices  39.6 us (34%)
  Pallas kernels  18.8 us (16%)
  other arithmetic  3.87 us (3%)
  local copies, waits for them, and re-layouts  1.29 us (1%)
    ppermute x47, starting transfers between devices, send(): return lax.ppermute(array, 'tp', pairs)  50.2 us
    ppermute x47, waiting for transfers between devices, send(): return lax.ppermute(array, 'tp', pairs)  39.6 us
    pallas_call x1, Pallas kernels, load_weights(): pl.pallas_call(load_kernel, out_shape=jax.ShapeDtypeStruct((16, width, 2...  4.19 us
    pallas_call x1, Pallas kernels, project(): pl.pallas_call(project_kernel, out_shape=[jax.ShapeDtypeStruct((SPAN, HD)...  3.52 us
    pallas_call x1, Pallas kernels, more_shares(): pl.pallas_call(functools.partial(more_shares_kernel, first), out_shape=ou...  3.1 us
    pallas_call x1, Pallas kernels, final_norm(): pl.pallas_call(final_kernel, out_shape=jax.ShapeDtypeStruct((TOKENS, 16 *...  2.83 us
  transfers between devices with their start and end apart: 47, of which 20 were waited for; matrix products, arithmetic and copies ran while one was open for 4% of the time, Pallas kernels for 13%

profile of v13, /device:TPU:0, one launch (start us, length us, event | category | flops | bytes accessed | tf_op | source)
XLA Modules:
  0.0 114.4 jit_solution(15701068304652531752)
XLA Ops:
  0.5 2.6 %collective-permute-start.2 = (bf16[128,1024]{1,0:T(8,128)(2,1)}, bf16[128,1024]{1,0:T(8,128)(2,1)S(1)}, u32[]{:S(2)}, u32[]{:S(2)}) collective-permute-start(bf16[128,1024]{1,0:T(8,128)(2,1)} %refs_0_), channel_id=1, source_target_pairs={{0,4},{4,8},{8,12},{12,14},{14,10},{10,6},{6,2},{2,0},{1,3},{5,1},... | collective-permute-start | bytes 786440 | tf_op jit(solution)/shard_map/ppermute | solution.py:76
  5.7 3.3 %collective-permute-done.2.refs_1_ = bf16[128,1024]{1,0:T(8,128)(2,1)S(1)} collective-permute-done((bf16[128,1024]{1,0:T(8,128)(2,1)}, bf16[128,1024]{1,0:T(8,128)(2,1)S(1)}, u32[]{:S(2)}, u32[]{:S(2)}) %collective-permute-start.2) | collective-permute-done | bytes 262176 | tf_op jit(solution)/shard_map/ppermute | solution.py:76
  9.0 2.4 %collective-permute-start.4 = (bf16[128,1024]{1,0:T(8,128)(2,1)S(1)}, bf16[128,1024]{1,0:T(8,128)(2,1)S(1)}, u32[]{:S(2)}, u32[]{:S(2)}) collective-permute-start(bf16[128,1024]{1,0:T(8,128)(2,1)S(1)} %collective-permute-done.2.refs_1_), channel_id=1, source_target_pairs={{0,4},{4,8},{8,12},{12,14},{14,10},{10,6},{6,2},{2,0},{1,3},{5,1},... | collective-permute-start | bytes 786440 | tf_op jit(solution)/shard_map/ppermute | solution.py:76
  13.8 2.2 %collective-permute-done.4.refs_3_ = bf16[128,1024]{1,0:T(8,128)(2,1)S(1)} collective-permute-done((bf16[128,1024]{1,0:T(8,128)(2,1)S(1)}, bf16[128,1024]{1,0:T(8,128)(2,1)S(1)}, u32[]{:S(2)}, u32[]{:S(2)}) %collective-permute-start.4) | collective-permute-done | bytes 262176 | tf_op jit(solution)/shard_map/ppermute | solution.py:76
  16.0 1.8 %collective-permute-start.6 = (bf16[128,1024]{1,0:T(8,128)(2,1)S(1)}, bf16[128,1024]{1,0:T(8,128)(2,1)S(1)}, u32[]{:S(2)}, u32[]{:S(2)}) collective-permute-start(bf16[128,1024]{1,0:T(8,128)(2,1)S(1)} %collective-permute-done.4.refs_3_), channel_id=1, source_target_pairs={{0,4},{4,8},{8,12},{12,14},{14,10},{10,6},{6,2},{2,0},{1,3},{5,1},... | collective-permute-start | bytes 786440 | tf_op jit(solution)/shard_map/ppermute | solution.py:76
  19.7 5.4 %collective-permute-done.6.refs_5_ = bf16[128,1024]{1,0:T(8,128)(2,1)S(1)} collective-permute-done((bf16[128,1024]{1,0:T(8,128)(2,1)S(1)}, bf16[128,1024]{1,0:T(8,128)(2,1)S(1)}, u32[]{:S(2)}, u32[]{:S(2)}) %collective-permute-start.6) | collective-permute-done | bytes 262176 | tf_op jit(solution)/shard_map/ppermute | solution.py:76
  27.0 4.2 %load_weights.1.refs_17_ = bf16[16,1024,256]{2,1,0:T(8,128)(2,1)S(1)} custom-call(s32[16]{0:T(128)S(1)} %stack.108.ids, bf16[16384,128]{1,0:T(8,128)(2,1)} %wq.1, bf16[16384,128]{1,0:T(8,128)(2,1)} %wkv.1), custom_call_target="tpu_custom_call" | custom-call | bytes 16777216 | tf_op jit(solution)/shard_map/load_weights/pallas_call | solution.py:238
  32.3 2.1 %collective-permute-done.9.refs_7_ = bf16[128,1024]{1,0:T(8,128)(2,1)} collective-permute-done((bf16[128,1024]{1,0:T(8,128)(2,1)S(1)}, bf16[128,1024]{1,0:T(8,128)(2,1)}, u32[]{:S(2)}, u32[]{:S(2)}) %collective-permute-start.9) | collective-permute-done | bytes 262176 | tf_op jit(solution)/shard_map/ppermute | solution.py:76
  37.3 2.2 %collective-permute-start.22 = (bf16[2,2,2,64,128]{4,3,2,1,0:T(8,128)(2,1)}, bf16[2,2,2,64,128]{4,3,2,1,0:T(8,128)(2,1)S(1)}, u32[]{:S(2)}, u32[]{:S(2)}) collective-permute-start(bf16[2,2,2,64,128]{4,3,2,1,0:T(8,128)(2,1)} %pad_maximum_fusion.2), channel_id=1, source_target_pairs={{0,8},{1,9},{2,10},{3,11},{4,12},{5,13},{6,14},{7,15},{8,0},{9,1},... | collective-permute-start | bytes 393224 | tf_op jit(solution)/shard_map/ppermute | solution.py:76
  39.5 3.5 %norm_project.1 = (bf16[64,128]{1,0:T(8,128)(2,1)S(1)}, bf16[64,128]{1,0:T(8,128)(2,1)S(1)}, bf16[128,128]{1,0:T(8,128)(2,1)S(1)}) custom-call(s32[16]{0:T(128)S(1)} %stack.108.ids, bf16[128,1024]{1,0:T(8,128)(2,1)S(1)} %copy-done, bf16[128,1024]{1,0:T(8,128)(2,1)S(1)} %collective-permute-done.2.refs_1_, ...), custom_call_target="tpu_custom_call" | custom-call | flops 1073741824 | bytes 12582912 | tf_op jit(solution)/shard_map/norm_project/pallas_call | solution.py:274
  43.7 3.0 %collective-permute-start.23 = (bf16[2,2,2,64,128]{4,3,2,1,0:T(8,128)(2,1)S(1)}, bf16[2,2,2,64,128]{4,3,2,1,0:T(8,128)(2,1)S(1)}, u32[]{:S(2)}, u32[]{:S(2)}) collective-permute-start(bf16[2,2,2,64,128]{4,3,2,1,0:T(8,128)(2,1)S(1)} %pad_maximum_fusion.3), channel_id=1, source_target_pairs={{0,12},{1,13},{2,14},{3,15},{4,8},{5,9},{6,10},{7,11},{8,4},{9,5},... | collective-permute-start | bytes 393224 | tf_op jit(solution)/shard_map/ppermute | solution.py:76
  50.9 1.8 %cache_scores.1 = (f32[128,1024]{1,0:T(8,128)S(1)}, bf16[2,256,1024]{2,1,0:T(8,128)(2,1)S(1)}) custom-call(s32[4]{0:T(128)S(1)} %pad_add_fusion.info, s32[8]{0:T(128)S(1)} %stack.117.to, bf16[64,128]{1,0:T(8,128)(2,1)S(1)} %get-tuple-element.25.q, bf16[64,128]{1,0:T(8,128)(2,1)S(1)} %collective-permute-done.18.q_other, ...), custom_call_target="tpu_custom_call" | custom-call | flops 33554432 | bytes 3145728 | tf_op jit(solution)/shard_map/cache_scores/pallas_call | solution.py:331
  53.8 2.4 %collective-permute-start.24 = (bf16[64,256]{1,0:T(8,128)(2,1)S(1)}, bf16[64,256]{1,0:T(8,128)(2,1)S(1)}, u32[]{:S(2)}, u32[]{:S(2)}) collective-permute-start(bf16[64,256]{1,0:T(8,128)(2,1)S(1)} %attend.1.attn), channel_id=1, source_target_pairs={{0,1},{1,0},{2,3},{3,2},{4,5},{5,4},{6,7},{7,6},{8,9},{9,8},{10,11... | collective-permute-start | bytes 98312 | tf_op jit(solution)/shard_map/ppermute | solution.py:76
  57.4 2.7 %collective-permute-start.25 = (bf16[128,1024]{1,0:T(8,128)(2,1)S(1)}, bf16[128,1024]{1,0:T(8,128)(2,1)S(1)}, u32[]{:S(2)}, u32[]{:S(2)}) collective-permute-start(bf16[128,1024]{1,0:T(8,128)(2,1)S(1)} %get-tuple-element.32), channel_id=1, source_target_pairs={{0,4},{4,8},{8,12},{12,14},{14,10},{10,6},{6,2},{2,0},{1,3},{5,1},... | collective-permute-start | bytes 786440 | tf_op jit(solution)/shard_map/ppermute | solution.py:76
  61.6 3.1 %shares_2.1 = (f32[128,1024]{1,0:T(8,128)S(1)}, f32[128,1024]{1,0:T(8,128)S(1)}, f32[128,1024]{1,0:T(8,128)S(1)}, f32[128,1024]{1,0:T(8,128)S(1)}, f32[128,1024]{1,0:T(8,128)S(1)}, /*index=5*/f32[128,1024]{1,0:T(8,128)S(1)}) custom-call(s32[1]{0:T(128)} %bitcast.16.core, s32[8]{0:T(128)S(1)} %stack.117.to, bf16[64,256]{1,0:T(8,128)(2,1)S(1)} %attend.1.attn, ...), custom_call_target="tpu_custom_call" | custom-call | flops 402653184 | bytes 6291456 | tf_op jit(solution)/shard_map/shares_2/pallas_call | solution.py:438
  66.9 2.5 %collective-permute-start.30 = (bf16[128,1024]{1,0:T(8,128)(2,1)S(1)}, bf16[128,1024]{1,0:T(8,128)(2,1)S(1)}, u32[]{:S(2)}, u32[]{:S(2)}) collective-permute-start(bf16[128,1024]{1,0:T(8,128)(2,1)S(1)} %add_convert_fusion.2), channel_id=1, source_target_pairs={{0,4},{4,8},{8,12},{12,14},{14,10},{10,6},{6,2},{2,0},{1,3},{5,1},... | collective-permute-start | bytes 786440 | tf_op jit(solution)/shard_map/ppermute | solution.py:76
  69.4 1.9 %collective-permute-done.26 = bf16[128,1024]{1,0:T(8,128)(2,1)S(1)} collective-permute-done((bf16[128,1024]{1,0:T(8,128)(2,1)S(1)}, bf16[128,1024]{1,0:T(8,128)(2,1)S(1)}, u32[]{:S(2)}, u32[]{:S(2)}) %collective-permute-start.26) | collective-permute-done | bytes 262176 | tf_op jit(solution)/shard_map/ppermute | solution.py:76
  74.2 3.5 %collective-permute-done.27 = bf16[128,1024]{1,0:T(8,128)(2,1)S(1)} collective-permute-done((bf16[128,1024]{1,0:T(8,128)(2,1)S(1)}, bf16[128,1024]{1,0:T(8,128)(2,1)S(1)}, u32[]{:S(2)}, u32[]{:S(2)}) %collective-permute-start.27) | collective-permute-done | bytes 262176 | tf_op jit(solution)/shard_map/ppermute | solution.py:76
  80.0 4.2 %collective-permute-done.28 = bf16[128,1024]{1,0:T(8,128)(2,1)S(1)} collective-permute-done((bf16[128,1024]{1,0:T(8,128)(2,1)S(1)}, bf16[128,1024]{1,0:T(8,128)(2,1)S(1)}, u32[]{:S(2)}, u32[]{:S(2)}) %collective-permute-start.28) | collective-permute-done | bytes 262176 | tf_op jit(solution)/shard_map/ppermute | solution.py:76
  87.7 3.1 %collective-permute-done.32.refs_1_ = bf16[128,1024]{1,0:T(8,128)(2,1)S(1)} collective-permute-done((bf16[128,1024]{1,0:T(8,128)(2,1)S(1)}, bf16[128,1024]{1,0:T(8,128)(2,1)S(1)}, u32[]{:S(2)}, u32[]{:S(2)}) %collective-permute-start.32) | collective-permute-done | bytes 262176 | tf_op jit(solution)/shard_map/ppermute | solution.py:76
  95.4 1.9 %collective-permute-done.35.refs_3_ = bf16[128,1024]{1,0:T(8,128)(2,1)S(1)} collective-permute-done((bf16[128,1024]{1,0:T(8,128)(2,1)S(1)}, bf16[128,1024]{1,0:T(8,128)(2,1)S(1)}, u32[]{:S(2)}, u32[]{:S(2)}) %collective-permute-start.35) | collective-permute-done | bytes 262176 | tf_op jit(solution)/shard_map/ppermute | solution.py:76
  101.8 1.9 %collective-permute-done.37.refs_5_ = bf16[128,1024]{1,0:T(8,128)(2,1)S(1)} collective-permute-done((bf16[128,1024]{1,0:T(8,128)(2,1)S(1)}, bf16[128,1024]{1,0:T(8,128)(2,1)S(1)}, u32[]{:S(2)}, u32[]{:S(2)}) %collective-permute-start.37) | collective-permute-done | bytes 262176 | tf_op jit(solution)/shard_map/ppermute | solution.py:76
  106.4 3.6 %collective-permute-done.39.refs_7_ = bf16[128,1024]{1,0:T(8,128)(2,1)S(1)} collective-permute-done((bf16[128,1024]{1,0:T(8,128)(2,1)S(1)}, bf16[128,1024]{1,0:T(8,128)(2,1)S(1)}, u32[]{:S(2)}, u32[]{:S(2)}) %collective-permute-start.39) | collective-permute-done | bytes 262176 | tf_op jit(solution)/shard_map/ppermute | solution.py:76
  111.5 2.8 %final_norm.1 = bf16[128,16384]{1,0:T(8,128)(2,1)} custom-call(s32[16]{0:T(128)S(1)} %stack.108.ids, bf16[128,1024]{1,0:T(8,128)(2,1)S(1)} %add_convert_fusion.refs_0_, bf16[128,1024]{1,0:T(8,128)(2,1)S(1)} %collective-permute-done.32.refs_1_, bf16[128,1024]{1,0:T(8,128)(2,1)S(1)} %collective-permute-done.34.refs_2_, ...), custom_call_target="tpu_custom_call" | custom-call | flops 16777216 | bytes 12582912 | tf_op jit(solution)/shard_map/final_norm/pallas_call | solution.py:497
  (109 shorter events, 45.7 us)
Async XLA Ops:
  0.0 25.1 %collective-permute-start.8 = (bf16[128,16384]{1,0:T(8,128)(2,1)}, bf16[128,16384]{1,0:T(8,128)(2,1)}, u32[]{:S(2)}, u32[]{:S(2)}) collective-permute-start(bf16[128,16384]{1,0:T(8,128)(2,1)} %weight.1), channel_id=1, source_target_pairs={{0,1},{1,0},{2,3},{3,2},{4,5},{5,4},{6,7},{7,6},{8,9},{9,8},{10,11... | collective-permute-start | bytes 12582920 | tf_op jit(solution)/shard_map/ppermute | solution.py:76
  0.5 8.6 %collective-permute-start.2 = (bf16[128,1024]{1,0:T(8,128)(2,1)}, bf16[128,1024]{1,0:T(8,128)(2,1)S(1)}, u32[]{:S(2)}, u32[]{:S(2)}) collective-permute-start(bf16[128,1024]{1,0:T(8,128)(2,1)} %refs_0_), channel_id=1, source_target_pairs={{0,4},{4,8},{8,12},{12,14},{14,10},{10,6},{6,2},{2,0},{1,3},{5,1},... | collective-permute-start | bytes 786440 | tf_op jit(solution)/shard_map/ppermute | solution.py:76
  3.0 9.2 %collective-permute-start.3 = (bf16[128,1024]{1,0:T(8,128)(2,1)}, bf16[128,1024]{1,0:T(8,128)(2,1)S(1)}, u32[]{:S(2)}, u32[]{:S(2)}) collective-permute-start(bf16[128,1024]{1,0:T(8,128)(2,1)} %refs_0_), channel_id=1, source_target_pairs={{0,3},{4,1},{8,5},{12,9},{14,13},{10,15},{6,11},{2,7},{1,4},{5,8},... | collective-permute-start | bytes 786440 | tf_op jit(solution)/shard_map/ppermute | solution.py:76
  4.4 20.8 %collective-permute-start.10 = (bf16[128,1024]{1,0:T(8,128)(2,1)}, bf16[128,1024]{1,0:T(8,128)(2,1)S(1)}, u32[]{:S(2)}, u32[]{:S(2)}) collective-permute-start(bf16[128,1024]{1,0:T(8,128)(2,1)} %refs_0_), channel_id=1, source_target_pairs={{0,1},{1,0},{2,3},{3,2},{4,5},{5,4},{6,7},{7,6},{8,9},{9,8},{10,11... | collective-permute-start | bytes 786440 | tf_op jit(solution)/shard_map/ppermute | solution.py:76
  9.0 7.0 %collective-permute-start.4 = (bf16[128,1024]{1,0:T(8,128)(2,1)S(1)}, bf16[128,1024]{1,0:T(8,128)(2,1)S(1)}, u32[]{:S(2)}, u32[]{:S(2)}) collective-permute-start(bf16[128,1024]{1,0:T(8,128)(2,1)S(1)} %collective-permute-done.2.refs_1_), channel_id=1, source_target_pairs={{0,4},{4,8},{8,12},{12,14},{14,10},{10,6},{6,2},{2,0},{1,3},{5,1},... | collective-permute-start | bytes 786440 | tf_op jit(solution)/shard_map/ppermute | solution.py:76
  11.4 6.8 %collective-permute-start = (bf16[2,64,1024]{2,1,0:T(8,128)(2,1)S(1)}, bf16[2,64,1024]{2,1,0:T(8,128)(2,1)S(1)}, u32[]{:S(2)}, u32[]{:S(2)}) collective-permute-start(bf16[2,64,1024]{2,1,0:T(8,128)(2,1)S(1)} %pad_maximum_fusion), channel_id=1, source_target_pairs={{0,1},{1,0},{2,3},{3,2},{4,5},{5,4},{6,7},{7,6},{8,9},{9,8},{10,11... | collective-permute-start | bytes 786440 | tf_op jit(solution)/shard_map/ppermute | solution.py:76
  12.3 7.4 %collective-permute-start.5 = (bf16[128,1024]{1,0:T(8,128)(2,1)S(1)}, bf16[128,1024]{1,0:T(8,128)(2,1)S(1)}, u32[]{:S(2)}, u32[]{:S(2)}) collective-permute-start(bf16[128,1024]{1,0:T(8,128)(2,1)S(1)} %collective-permute-done.3.refs_2_), channel_id=1, source_target_pairs={{0,4},{4,8},{8,12},{12,14},{14,10},{10,6},{6,2},{2,0},{1,3},{5,1},... | collective-permute-start | bytes 786440 | tf_op jit(solution)/shard_map/ppermute | solution.py:76
  16.0 9.1 %collective-permute-start.6 = (bf16[128,1024]{1,0:T(8,128)(2,1)S(1)}, bf16[128,1024]{1,0:T(8,128)(2,1)S(1)}, u32[]{:S(2)}, u32[]{:S(2)}) collective-permute-start(bf16[128,1024]{1,0:T(8,128)(2,1)S(1)} %collective-permute-done.4.refs_3_), channel_id=1, source_target_pairs={{0,4},{4,8},{8,12},{12,14},{14,10},{10,6},{6,2},{2,0},{1,3},{5,1},... | collective-permute-start | bytes 786440 | tf_op jit(solution)/shard_map/ppermute | solution.py:76
  19.3 11.9 %collective-permute-start.1 = (bf16[4,2,2,64,128]{4,3,2,1,0:T(8,128)(2,1)S(1)}, bf16[4,2,2,64,128]{4,3,2,1,0:T(8,128)(2,1)S(1)}, u32[]{:S(2)}, u32[]{:S(2)}) collective-permute-start(bf16[4,2,2,64,128]{4,3,2,1,0:T(8,128)(2,1)S(1)} %get-tuple-element.22), channel_id=1, source_target_pairs={{0,2},{1,3},{2,0},{3,1},{4,6},{5,7},{6,4},{7,5},{8,10},{9,11},{10,... | collective-permute-start | bytes 786440 | tf_op jit(solution)/shard_map/ppermute | solution.py:76
  19.7 11.9 %collective-permute-start.11 = (bf16[128,1024]{1,0:T(8,128)(2,1)S(1)}, bf16[128,1024]{1,0:T(8,128)(2,1)S(1)}, u32[]{:S(2)}, u32[]{:S(2)}) collective-permute-start(bf16[128,1024]{1,0:T(8,128)(2,1)S(1)} %collective-permute-done.2.refs_1_), channel_id=1, source_target_pairs={{0,1},{1,0},{2,3},{3,2},{4,5},{5,4},{6,7},{7,6},{8,9},{9,8},{10,11... | collective-permute-start | bytes 786440 | tf_op jit(solution)/shard_map/ppermute | solution.py:76
  25.1 6.7 %collective-permute-start.12 = (bf16[128,1024]{1,0:T(8,128)(2,1)S(1)}, bf16[128,1024]{1,0:T(8,128)(2,1)S(1)}, u32[]{:S(2)}, u32[]{:S(2)}) collective-permute-start(bf16[128,1024]{1,0:T(8,128)(2,1)S(1)} %collective-permute-done.3.refs_2_), channel_id=1, source_target_pairs={{0,1},{1,0},{2,3},{3,2},{4,5},{5,4},{6,7},{7,6},{8,9},{9,8},{10,11... | collective-permute-start | bytes 786440 | tf_op jit(solution)/shard_map/ppermute | solution.py:76
  25.1 7.0 %collective-permute-start.7 = (bf16[128,1024]{1,0:T(8,128)(2,1)S(1)}, bf16[128,1024]{1,0:T(8,128)(2,1)}, u32[]{:S(2)}, u32[]{:S(2)}) collective-permute-start(bf16[128,1024]{1,0:T(8,128)(2,1)S(1)} %collective-permute-done.5.refs_4_), channel_id=1, source_target_pairs={{0,4},{4,8},{8,12},{12,14},{14,10},{10,6},{6,2},{2,0},{1,3},{5,1},... | collective-permute-start | bytes 786440 | tf_op jit(solution)/shard_map/ppermute | solution.py:76
  25.1 9.3 %collective-permute-start.9 = (bf16[128,1024]{1,0:T(8,128)(2,1)S(1)}, bf16[128,1024]{1,0:T(8,128)(2,1)}, u32[]{:S(2)}, u32[]{:S(2)}) collective-permute-start(bf16[128,1024]{1,0:T(8,128)(2,1)S(1)} %collective-permute-done.6.refs_5_), channel_id=1, source_target_pairs={{0,4},{4,8},{8,12},{12,14},{14,10},{10,6},{6,2},{2,0},{1,3},{5,1},... | collective-permute-start | bytes 786440 | tf_op jit(solution)/shard_map/ppermute | solution.py:76
  31.8 7.7 %collective-permute-start.15 = (bf16[128,1024]{1,0:T(8,128)(2,1)S(1)}, bf16[128,1024]{1,0:T(8,128)(2,1)S(1)}, u32[]{:S(2)}, u32[]{:S(2)}) collective-permute-start(bf16[128,1024]{1,0:T(8,128)(2,1)S(1)} %collective-permute-done.6.refs_5_), channel_id=1, source_target_pairs={{0,1},{1,0},{2,3},{3,2},{4,5},{5,4},{6,7},{7,6},{8,9},{9,8},{10,11... | collective-permute-start | bytes 786440 | tf_op jit(solution)/shard_map/ppermute | solution.py:76
  32.1 7.4 %collective-permute-start.16 = (bf16[128,1024]{1,0:T(8,128)(2,1)}, bf16[128,1024]{1,0:T(8,128)(2,1)S(1)}, u32[]{:S(2)}, u32[]{:S(2)}) collective-permute-start(bf16[128,1024]{1,0:T(8,128)(2,1)} %collective-permute-done.7.refs_6_), channel_id=1, source_target_pairs={{0,1},{1,0},{2,3},{3,2},{4,5},{5,4},{6,7},{7,6},{8,9},{9,8},{10,11... | collective-permute-start | bytes 786440 | tf_op jit(solution)/shard_map/ppermute | solution.py:76
  35.8 14.0 %collective-permute-start.21 = (bf16[2,2,2,64,128]{4,3,2,1,0:T(8,128)(2,1)}, bf16[2,2,2,64,128]{4,3,2,1,0:T(8,128)(2,1)S(1)}, u32[]{:S(2)}, u32[]{:S(2)}) collective-permute-start(bf16[2,2,2,64,128]{4,3,2,1,0:T(8,128)(2,1)} %pad_maximum_fusion.1), channel_id=1, source_target_pairs={{0,4},{1,5},{2,6},{3,7},{4,0},{5,1},{6,2},{7,3},{8,12},{9,13},{10,... | collective-permute-start | bytes 393224 | tf_op jit(solution)/shard_map/ppermute | solution.py:76
  37.3 12.5 %collective-permute-start.22 = (bf16[2,2,2,64,128]{4,3,2,1,0:T(8,128)(2,1)}, bf16[2,2,2,64,128]{4,3,2,1,0:T(8,128)(2,1)S(1)}, u32[]{:S(2)}, u32[]{:S(2)}) collective-permute-start(bf16[2,2,2,64,128]{4,3,2,1,0:T(8,128)(2,1)} %pad_maximum_fusion.2), channel_id=1, source_target_pairs={{0,8},{1,9},{2,10},{3,11},{4,12},{5,13},{6,14},{7,15},{8,0},{9,1},... | collective-permute-start | bytes 393224 | tf_op jit(solution)/shard_map/ppermute | solution.py:76
  43.7 7.1 %collective-permute-start.23 = (bf16[2,2,2,64,128]{4,3,2,1,0:T(8,128)(2,1)S(1)}, bf16[2,2,2,64,128]{4,3,2,1,0:T(8,128)(2,1)S(1)}, u32[]{:S(2)}, u32[]{:S(2)}) collective-permute-start(bf16[2,2,2,64,128]{4,3,2,1,0:T(8,128)(2,1)S(1)} %pad_maximum_fusion.3), channel_id=1, source_target_pairs={{0,12},{1,13},{2,14},{3,15},{4,8},{5,9},{6,10},{7,11},{8,4},{9,5},... | collective-permute-start | bytes 393224 | tf_op jit(solution)/shard_map/ppermute | solution.py:76
  57.4 7.3 %collective-permute-start.25 = (bf16[128,1024]{1,0:T(8,128)(2,1)S(1)}, bf16[128,1024]{1,0:T(8,128)(2,1)S(1)}, u32[]{:S(2)}, u32[]{:S(2)}) collective-permute-start(bf16[128,1024]{1,0:T(8,128)(2,1)S(1)} %get-tuple-element.32), channel_id=1, source_target_pairs={{0,4},{4,8},{8,12},{12,14},{14,10},{10,6},{6,2},{2,0},{1,3},{5,1},... | collective-permute-start | bytes 786440 | tf_op jit(solution)/shard_map/ppermute | solution.py:76
  60.1 6.7 %collective-permute-start.29 = (bf16[128,1024]{1,0:T(8,128)(2,1)S(1)}, bf16[128,1024]{1,0:T(8,128)(2,1)S(1)}, u32[]{:S(2)}, u32[]{:S(2)}) collective-permute-start(bf16[128,1024]{1,0:T(8,128)(2,1)S(1)} %get-tuple-element.36), channel_id=1, source_target_pairs={{0,4},{4,8},{8,12},{12,14},{14,10},{10,6},{6,2},{2,0},{1,3},{5,1},... | collective-permute-start | bytes 786440 | tf_op jit(solution)/shard_map/ppermute | solution.py:76
  64.8 6.4 %collective-permute-start.26 = (bf16[128,1024]{1,0:T(8,128)(2,1)S(1)}, bf16[128,1024]{1,0:T(8,128)(2,1)S(1)}, u32[]{:S(2)}, u32[]{:S(2)}) collective-permute-start(bf16[128,1024]{1,0:T(8,128)(2,1)S(1)} %add_convert_fusion.5), channel_id=1, source_target_pairs={{0,4},{4,8},{8,12},{12,14},{14,10},{10,6},{6,2},{2,0},{1,3},{5,1},... | collective-permute-start | bytes 786440 | tf_op jit(solution)/shard_map/ppermute | solution.py:76
  66.9 7.2 %collective-permute-start.30 = (bf16[128,1024]{1,0:T(8,128)(2,1)S(1)}, bf16[128,1024]{1,0:T(8,128)(2,1)S(1)}, u32[]{:S(2)}, u32[]{:S(2)}) collective-permute-start(bf16[128,1024]{1,0:T(8,128)(2,1)S(1)} %add_convert_fusion.2), channel_id=1, source_target_pairs={{0,4},{4,8},{8,12},{12,14},{14,10},{10,6},{6,2},{2,0},{1,3},{5,1},... | collective-permute-start | bytes 786440 | tf_op jit(solution)/shard_map/ppermute | solution.py:76
  86.2 7.5 %collective-permute-start.34 = (bf16[128,1024]{1,0:T(8,128)(2,1)S(1)}, bf16[128,1024]{1,0:T(8,128)(2,1)S(1)}, u32[]{:S(2)}, u32[]{:S(2)}) collective-permute-start(bf16[128,1024]{1,0:T(8,128)(2,1)S(1)} %collective-permute-done.33.refs_8_), channel_id=1, source_target_pairs={{0,4},{4,8},{8,12},{12,14},{14,10},{10,6},{6,2},{2,0},{1,3},{5,1},... | collective-permute-start | bytes 786440 | tf_op jit(solution)/shard_map/ppermute | solution.py:76
  99.0 6.9 %collective-permute-start.41 = (bf16[128,1024]{1,0:T(8,128)(2,1)S(1)}, bf16[128,1024]{1,0:T(8,128)(2,1)S(1)}, u32[]{:S(2)}, u32[]{:S(2)}) collective-permute-start(bf16[128,1024]{1,0:T(8,128)(2,1)S(1)} %collective-permute-done.34.refs_2_), channel_id=1, source_target_pairs={{0,1},{1,0},{2,3},{3,2},{4,5},{5,4},{6,7},{7,6},{8,9},{9,8},{10,11... | collective-permute-start | bytes 786440 | tf_op jit(solution)/shard_map/ppermute | solution.py:76
  (26 other events, 184.1 us)

commit v14 on v13

--- a/solution.py
+++ b/solution.py
@@ -310,9 +310,27 @@
 CONTRACT = (((1,), (1,)), ((), ()))
 
 
-def scores_kernel(info, to, q, q_other, *refs):
-    cache, weight, weight_other, scores, weights, sems = refs[:5], *refs[5:]
-    copies = share_copies(to, 0, weight, weight_other, weights, sems)
+def first_weights_kernel(to, weight, weight_other, out, sems):
+    for pair in share_copies(to, 0, weight, weight_other, out, sems):
+        for copy in pair:
+            copy.wait()
+
+
+def load_first(to, weight, weight_other, count):
+    return pl.pallas_call(
+        first_weights_kernel,
+        out_shape=jax.ShapeDtypeStruct((count, 2 * HD, weight.shape[1] // 16), jnp.bfloat16),
+        in_specs=[SMEM] + [HBM] * 2,
+        out_specs=VMEM,
+        scratch_shapes=[pltpu.SemaphoreType.DMA((2, count))],
+        compiler_params=pltpu.CompilerParams(vmem_limit_bytes=8 * MIB),
+        cost_estimate=pl.CostEstimate(flops=0, bytes_accessed=2 * MIB, transcendentals=0),
+        name="load_first",
+    )(to, in_hbm(weight), weight_other)
+
+
+def scores_kernel(info, q, q_other, *refs):
+    cache, scores = refs[:5], refs[5]
     core, rank = info[SEQS], info[SEQS + 1]
     queries = jnp.concatenate([q[...], q_other[...]], axis=0)
     old = lax.dot_general(
@@ -321,28 +339,18 @@
     lane = lax.broadcasted_iota(jnp.int32, old.shape, 1)
     position = (rank ^ (lane // CTX_DEV)) * CTX_DEV + lane % CTX_DEV
     scores[...] = jnp.where(position < info[core], old * HD ** (-0.5), -1e30)
-    for pair in copies:
-        for copy in pair:
-            copy.wait()
-
-
-def cache_scores(info, to, q, q_other, cache, weight, weight_other, ahead):
-    width = weight.shape[1] // 16
+
+
+def cache_scores(info, q, q_other, cache):
     return pl.pallas_call(
         scores_kernel,
-        out_shape=[
-            jax.ShapeDtypeStruct((TOKENS, 16 * CTX_DEV), jnp.float32),
-            jax.ShapeDtypeStruct((ahead, 2 * HD, width), jnp.bfloat16),
-        ],
-        in_specs=[SMEM] * 2 + [VMEM] * 7 + [HBM] * 2,
-        out_specs=[VMEM] * 2,
-        scratch_shapes=[pltpu.SemaphoreType.DMA((2, ahead))],
+        out_shape=jax.ShapeDtypeStruct((TOKENS, 16 * CTX_DEV), jnp.float32),
+        in_specs=[SMEM] + [VMEM] * 7,
+        out_specs=VMEM,
         compiler_params=pltpu.CompilerParams(vmem_limit_bytes=16 * MIB),
-        cost_estimate=pl.CostEstimate(
-            flops=32 * MIB, bytes_accessed=3 * MIB, transcendentals=0
-        ),
+        cost_estimate=pl.CostEstimate(flops=32 * MIB, bytes_accessed=MIB, transcendentals=0),
         name="cache_scores",
-    )(info, to, q, q_other, *cache, in_hbm(weight), weight_other)
+    )(info, q, q_other, *cache)
 
 
 def attend_kernel(info, q, q_other, fresh_own, fresh_other, scores, *refs):
@@ -541,9 +549,8 @@
     q_other = send(q_send, SWAP)
     fresh_own = send(fresh, FRESH)
     fresh_other = send(jnp.where(core == 0, fresh_own[SPAN:], fresh_own[:SPAN]), SWAP)
-    scores, first_weights = cache_scores(
-        info, to, q_keep, q_other, cache, o_weight, weight_other, 2
-    )
+    first_weights = load_first(after(to, fresh), o_weight, weight_other, 2)
+    scores = cache_scores(info, after(q_keep, first_weights), q_other, cache)
     attn = attend(info, q_keep, q_other, fresh_own, fresh_other, scores, cache)
     attn_other = send(attn, SWAP)
 

time: 115 us -> 114 us (level)
    pallas_call x1 -> x2, Pallas kernels: 1.78 us -> 2.54 us  [the longest x1 1.77 us: load_first(): pl.pallas_call(first_weights_kernel, out_shape=jax.ShapeDtypeStruct((coun...]
  transfers between devices with their start and end apart: 47 -> 47, of which waited for: 20 -> 19; matrix products, arithmetic and copies ran while one was open for 4% -> 4% of each run, Pallas kernels for 13% -> 13%
where the time goes in v14:
time: 114 us; the launch traced here: 113 us
  starting transfers between devices  49.3 us (43%)
  waiting for transfers between devices  38.7 us (34%)
  Pallas kernels  19.5 us (17%)
  other arithmetic  3.89 us (3%)
  local copies, waits for them, and re-layouts  1.29 us (1%)
    ppermute x47, starting transfers between devices, send(): return lax.ppermute(array, 'tp', pairs)  49.3 us
    ppermute x47, waiting for transfers between devices, send(): return lax.ppermute(array, 'tp', pairs)  38.7 us
    pallas_call x1, Pallas kernels, load_weights(): pl.pallas_call(load_kernel, out_shape=jax.ShapeDtypeStruct((16, width, 2...  4.19 us
    pallas_call x1, Pallas kernels, project(): pl.pallas_call(project_kernel, out_shape=[jax.ShapeDtypeStruct((SPAN, HD)...  3.52 us
    pallas_call x1, Pallas kernels, more_shares(): pl.pallas_call(functools.partial(more_shares_kernel, first), out_shape=ou...  3.11 us
    pallas_call x1, Pallas kernels, final_norm(): pl.pallas_call(final_kernel, out_shape=jax.ShapeDtypeStruct((TOKENS, 16 *...  2.83 us
  transfers between devices with their start and end apart: 47, of which 19 were waited for; matrix products, arithmetic and copies ran while one was open for 4% of the time, Pallas kernels for 13%

profile of v14, /device:TPU:0, one launch (start us, length us, event | category | flops | bytes accessed | tf_op | source)
XLA Modules:
  0.0 113.4 jit_solution(5059205068081176977)
XLA Ops:
  0.5 2.6 %collective-permute-start.2 = (bf16[128,1024]{1,0:T(8,128)(2,1)}, bf16[128,1024]{1,0:T(8,128)(2,1)S(1)}, u32[]{:S(2)}, u32[]{:S(2)}) collective-permute-start(bf16[128,1024]{1,0:T(8,128)(2,1)} %refs_0_), channel_id=1, source_target_pairs={{0,4},{4,8},{8,12},{12,14},{14,10},{10,6},{6,2},{2,0},{1,3},{5,1},... | collective-permute-start | bytes 786440 | tf_op jit(solution)/shard_map/ppermute | solution.py:76
  5.7 3.3 %collective-permute-done.2.refs_1_ = bf16[128,1024]{1,0:T(8,128)(2,1)S(1)} collective-permute-done((bf16[128,1024]{1,0:T(8,128)(2,1)}, bf16[128,1024]{1,0:T(8,128)(2,1)S(1)}, u32[]{:S(2)}, u32[]{:S(2)}) %collective-permute-start.2) | collective-permute-done | bytes 262176 | tf_op jit(solution)/shard_map/ppermute | solution.py:76
  9.0 2.4 %collective-permute-start.4 = (bf16[128,1024]{1,0:T(8,128)(2,1)S(1)}, bf16[128,1024]{1,0:T(8,128)(2,1)S(1)}, u32[]{:S(2)}, u32[]{:S(2)}) collective-permute-start(bf16[128,1024]{1,0:T(8,128)(2,1)S(1)} %collective-permute-done.2.refs_1_), channel_id=1, source_target_pairs={{0,4},{4,8},{8,12},{12,14},{14,10},{10,6},{6,2},{2,0},{1,3},{5,1},... | collective-permute-start | bytes 786440 | tf_op jit(solution)/shard_map/ppermute | solution.py:76
  13.8 2.2 %collective-permute-done.4.refs_3_ = bf16[128,1024]{1,0:T(8,128)(2,1)S(1)} collective-permute-done((bf16[128,1024]{1,0:T(8,128)(2,1)S(1)}, bf16[128,1024]{1,0:T(8,128)(2,1)S(1)}, u32[]{:S(2)}, u32[]{:S(2)}) %collective-permute-start.4) | collective-permute-done | bytes 262176 | tf_op jit(solution)/shard_map/ppermute | solution.py:76
  16.0 1.8 %collective-permute-start.6 = (bf16[128,1024]{1,0:T(8,128)(2,1)S(1)}, bf16[128,1024]{1,0:T(8,128)(2,1)S(1)}, u32[]{:S(2)}, u32[]{:S(2)}) collective-permute-start(bf16[128,1024]{1,0:T(8,128)(2,1)S(1)} %collective-permute-done.4.refs_3_), channel_id=1, source_target_pairs={{0,4},{4,8},{8,12},{12,14},{14,10},{10,6},{6,2},{2,0},{1,3},{5,1},... | collective-permute-start | bytes 786440 | tf_op jit(solution)/shard_map/ppermute | solution.py:76
  19.7 5.4 %collective-permute-done.6.refs_5_ = bf16[128,1024]{1,0:T(8,128)(2,1)S(1)} collective-permute-done((bf16[128,1024]{1,0:T(8,128)(2,1)S(1)}, bf16[128,1024]{1,0:T(8,128)(2,1)S(1)}, u32[]{:S(2)}, u32[]{:S(2)}) %collective-permute-start.6) | collective-permute-done | bytes 262176 | tf_op jit(solution)/shard_map/ppermute | solution.py:76
  27.0 4.2 %load_weights.1.refs_17_ = bf16[16,1024,256]{2,1,0:T(8,128)(2,1)S(1)} custom-call(s32[16]{0:T(128)S(1)} %stack.108.ids, bf16[16384,128]{1,0:T(8,128)(2,1)} %wq.1, bf16[16384,128]{1,0:T(8,128)(2,1)} %wkv.1), custom_call_target="tpu_custom_call" | custom-call | bytes 16777216 | tf_op jit(solution)/shard_map/load_weights/pallas_call | solution.py:238
  32.3 2.1 %collective-permute-done.9.refs_7_ = bf16[128,1024]{1,0:T(8,128)(2,1)} collective-permute-done((bf16[128,1024]{1,0:T(8,128)(2,1)S(1)}, bf16[128,1024]{1,0:T(8,128)(2,1)}, u32[]{:S(2)}, u32[]{:S(2)}) %collective-permute-start.9) | collective-permute-done | bytes 262176 | tf_op jit(solution)/shard_map/ppermute | solution.py:76
  37.3 2.2 %collective-permute-start.22 = (bf16[2,2,2,64,128]{4,3,2,1,0:T(8,128)(2,1)}, bf16[2,2,2,64,128]{4,3,2,1,0:T(8,128)(2,1)S(1)}, u32[]{:S(2)}, u32[]{:S(2)}) collective-permute-start(bf16[2,2,2,64,128]{4,3,2,1,0:T(8,128)(2,1)} %pad_maximum_fusion.2), channel_id=1, source_target_pairs={{0,8},{1,9},{2,10},{3,11},{4,12},{5,13},{6,14},{7,15},{8,0},{9,1},... | collective-permute-start | bytes 393224 | tf_op jit(solution)/shard_map/ppermute | solution.py:76
  39.5 3.5 %norm_project.1 = (bf16[64,128]{1,0:T(8,128)(2,1)S(1)}, bf16[64,128]{1,0:T(8,128)(2,1)S(1)}, bf16[128,128]{1,0:T(8,128)(2,1)S(1)}) custom-call(s32[16]{0:T(128)S(1)} %stack.108.ids, bf16[128,1024]{1,0:T(8,128)(2,1)S(1)} %copy-done, bf16[128,1024]{1,0:T(8,128)(2,1)S(1)} %collective-permute-done.2.refs_1_, ...), custom_call_target="tpu_custom_call" | custom-call | flops 1073741824 | bytes 12582912 | tf_op jit(solution)/shard_map/norm_project/pallas_call | solution.py:274
  43.8 3.0 %collective-permute-start.23 = (bf16[2,2,2,64,128]{4,3,2,1,0:T(8,128)(2,1)S(1)}, bf16[2,2,2,64,128]{4,3,2,1,0:T(8,128)(2,1)S(1)}, u32[]{:S(2)}, u32[]{:S(2)}) collective-permute-start(bf16[2,2,2,64,128]{4,3,2,1,0:T(8,128)(2,1)S(1)} %pad_maximum_fusion.3), channel_id=1, source_target_pairs={{0,12},{1,13},{2,14},{3,15},{4,8},{5,9},{6,10},{7,11},{8,4},{9,5},... | collective-permute-start | bytes 393224 | tf_op jit(solution)/shard_map/ppermute | solution.py:76
  49.8 1.8 %load_first.1.weights = bf16[2,256,1024]{2,1,0:T(8,128)(2,1)S(1)} custom-call(s32[8]{0:T(128)S(1)} %stack.117.to, bf16[128,16384]{1,0:T(8,128)(2,1)} %weight.3, bf16[128,16384]{1,0:T(8,128)(2,1)} %collective-permute-done.8.weight_other), custom_call_target="tpu_custom_call" | custom-call | bytes 2097152 | tf_op jit(solution)/shard_map/load_first/pallas_call | solution.py:320
  56.4 2.7 %collective-permute-start.25 = (bf16[128,1024]{1,0:T(8,128)(2,1)S(1)}, bf16[128,1024]{1,0:T(8,128)(2,1)S(1)}, u32[]{:S(2)}, u32[]{:S(2)}) collective-permute-start(bf16[128,1024]{1,0:T(8,128)(2,1)S(1)} %get-tuple-element.32), channel_id=1, source_target_pairs={{0,4},{4,8},{8,12},{12,14},{14,10},{10,6},{6,2},{2,0},{1,3},{5,1},... | collective-permute-start | bytes 786440 | tf_op jit(solution)/shard_map/ppermute | solution.py:76
  60.6 3.1 %shares_2.1 = (f32[128,1024]{1,0:T(8,128)S(1)}, f32[128,1024]{1,0:T(8,128)S(1)}, f32[128,1024]{1,0:T(8,128)S(1)}, f32[128,1024]{1,0:T(8,128)S(1)}, f32[128,1024]{1,0:T(8,128)S(1)}, /*index=5*/f32[128,1024]{1,0:T(8,128)S(1)}) custom-call(s32[1]{0:T(128)} %bitcast.16.core, s32[8]{0:T(128)S(1)} %stack.117.to, bf16[64,256]{1,0:T(8,128)(2,1)S(1)} %attend.1.attn, ...), custom_call_target="tpu_custom_call" | custom-call | flops 402653184 | bytes 6291456 | tf_op jit(solution)/shard_map/shares_2/pallas_call | solution.py:446
  63.8 1.7 %collective-permute-start.26 = (bf16[128,1024]{1,0:T(8,128)(2,1)S(1)}, bf16[128,1024]{1,0:T(8,128)(2,1)S(1)}, u32[]{:S(2)}, u32[]{:S(2)}) collective-permute-start(bf16[128,1024]{1,0:T(8,128)(2,1)S(1)} %add_convert_fusion.5), channel_id=1, source_target_pairs={{0,4},{4,8},{8,12},{12,14},{14,10},{10,6},{6,2},{2,0},{1,3},{5,1},... | collective-permute-start | bytes 786440 | tf_op jit(solution)/shard_map/ppermute | solution.py:76
  65.9 2.5 %collective-permute-start.30 = (bf16[128,1024]{1,0:T(8,128)(2,1)S(1)}, bf16[128,1024]{1,0:T(8,128)(2,1)S(1)}, u32[]{:S(2)}, u32[]{:S(2)}) collective-permute-start(bf16[128,1024]{1,0:T(8,128)(2,1)S(1)} %add_convert_fusion.2), channel_id=1, source_target_pairs={{0,4},{4,8},{8,12},{12,14},{14,10},{10,6},{6,2},{2,0},{1,3},{5,1},... | collective-permute-start | bytes 786440 | tf_op jit(solution)/shard_map/ppermute | solution.py:76
  68.4 1.9 %collective-permute-done.26 = bf16[128,1024]{1,0:T(8,128)(2,1)S(1)} collective-permute-done((bf16[128,1024]{1,0:T(8,128)(2,1)S(1)}, bf16[128,1024]{1,0:T(8,128)(2,1)S(1)}, u32[]{:S(2)}, u32[]{:S(2)}) %collective-permute-start.26) | collective-permute-done | bytes 262176 | tf_op jit(solution)/shard_map/ppermute | solution.py:76
  73.2 3.5 %collective-permute-done.27 = bf16[128,1024]{1,0:T(8,128)(2,1)S(1)} collective-permute-done((bf16[128,1024]{1,0:T(8,128)(2,1)S(1)}, bf16[128,1024]{1,0:T(8,128)(2,1)S(1)}, u32[]{:S(2)}, u32[]{:S(2)}) %collective-permute-start.27) | collective-permute-done | bytes 262176 | tf_op jit(solution)/shard_map/ppermute | solution.py:76
  79.0 4.2 %collective-permute-done.28 = bf16[128,1024]{1,0:T(8,128)(2,1)S(1)} collective-permute-done((bf16[128,1024]{1,0:T(8,128)(2,1)S(1)}, bf16[128,1024]{1,0:T(8,128)(2,1)S(1)}, u32[]{:S(2)}, u32[]{:S(2)}) %collective-permute-start.28) | collective-permute-done | bytes 262176 | tf_op jit(solution)/shard_map/ppermute | solution.py:76
  86.8 3.1 %collective-permute-done.32.refs_1_ = bf16[128,1024]{1,0:T(8,128)(2,1)S(1)} collective-permute-done((bf16[128,1024]{1,0:T(8,128)(2,1)S(1)}, bf16[128,1024]{1,0:T(8,128)(2,1)S(1)}, u32[]{:S(2)}, u32[]{:S(2)}) %collective-permute-start.32) | collective-permute-done | bytes 262176 | tf_op jit(solution)/shard_map/ppermute | solution.py:76
  94.4 1.9 %collective-permute-done.35.refs_3_ = bf16[128,1024]{1,0:T(8,128)(2,1)S(1)} collective-permute-done((bf16[128,1024]{1,0:T(8,128)(2,1)S(1)}, bf16[128,1024]{1,0:T(8,128)(2,1)S(1)}, u32[]{:S(2)}, u32[]{:S(2)}) %collective-permute-start.35) | collective-permute-done | bytes 262176 | tf_op jit(solution)/shard_map/ppermute | solution.py:76
  100.8 1.9 %collective-permute-done.37.refs_5_ = bf16[128,1024]{1,0:T(8,128)(2,1)S(1)} collective-permute-done((bf16[128,1024]{1,0:T(8,128)(2,1)S(1)}, bf16[128,1024]{1,0:T(8,128)(2,1)S(1)}, u32[]{:S(2)}, u32[]{:S(2)}) %collective-permute-start.37) | collective-permute-done | bytes 262176 | tf_op jit(solution)/shard_map/ppermute | solution.py:76
  105.5 3.6 %collective-permute-done.39.refs_7_ = bf16[128,1024]{1,0:T(8,128)(2,1)S(1)} collective-permute-done((bf16[128,1024]{1,0:T(8,128)(2,1)S(1)}, bf16[128,1024]{1,0:T(8,128)(2,1)S(1)}, u32[]{:S(2)}, u32[]{:S(2)}) %collective-permute-start.39) | collective-permute-done | bytes 262176 | tf_op jit(solution)/shard_map/ppermute | solution.py:76
  110.6 2.8 %final_norm.1 = bf16[128,16384]{1,0:T(8,128)(2,1)} custom-call(s32[16]{0:T(128)S(1)} %stack.108.ids, bf16[128,1024]{1,0:T(8,128)(2,1)S(1)} %add_convert_fusion.refs_0_, bf16[128,1024]{1,0:T(8,128)(2,1)S(1)} %collective-permute-done.32.refs_1_, bf16[128,1024]{1,0:T(8,128)(2,1)S(1)} %collective-permute-done.34.refs_2_, ...), custom_call_target="tpu_custom_call" | custom-call | flops 16777216 | bytes 12582912 | tf_op jit(solution)/shard_map/final_norm/pallas_call | solution.py:505
  (110 shorter events, 45.3 us)
Async XLA Ops:
  0.0 25.1 %collective-permute-start.8 = (bf16[128,16384]{1,0:T(8,128)(2,1)}, bf16[128,16384]{1,0:T(8,128)(2,1)}, u32[]{:S(2)}, u32[]{:S(2)}) collective-permute-start(bf16[128,16384]{1,0:T(8,128)(2,1)} %weight.3), channel_id=1, source_target_pairs={{0,1},{1,0},{2,3},{3,2},{4,5},{5,4},{6,7},{7,6},{8,9},{9,8},{10,11... | collective-permute-start | bytes 12582920 | tf_op jit(solution)/shard_map/ppermute | solution.py:76
  0.5 8.6 %collective-permute-start.2 = (bf16[128,1024]{1,0:T(8,128)(2,1)}, bf16[128,1024]{1,0:T(8,128)(2,1)S(1)}, u32[]{:S(2)}, u32[]{:S(2)}) collective-permute-start(bf16[128,1024]{1,0:T(8,128)(2,1)} %refs_0_), channel_id=1, source_target_pairs={{0,4},{4,8},{8,12},{12,14},{14,10},{10,6},{6,2},{2,0},{1,3},{5,1},... | collective-permute-start | bytes 786440 | tf_op jit(solution)/shard_map/ppermute | solution.py:76
  3.0 9.2 %collective-permute-start.3 = (bf16[128,1024]{1,0:T(8,128)(2,1)}, bf16[128,1024]{1,0:T(8,128)(2,1)S(1)}, u32[]{:S(2)}, u32[]{:S(2)}) collective-permute-start(bf16[128,1024]{1,0:T(8,128)(2,1)} %refs_0_), channel_id=1, source_target_pairs={{0,3},{4,1},{8,5},{12,9},{14,13},{10,15},{6,11},{2,7},{1,4},{5,8},... | collective-permute-start | bytes 786440 | tf_op jit(solution)/shard_map/ppermute | solution.py:76
  4.4 20.8 %collective-permute-start.10 = (bf16[128,1024]{1,0:T(8,128)(2,1)}, bf16[128,1024]{1,0:T(8,128)(2,1)S(1)}, u32[]{:S(2)}, u32[]{:S(2)}) collective-permute-start(bf16[128,1024]{1,0:T(8,128)(2,1)} %refs_0_), channel_id=1, source_target_pairs={{0,1},{1,0},{2,3},{3,2},{4,5},{5,4},{6,7},{7,6},{8,9},{9,8},{10,11... | collective-permute-start | bytes 786440 | tf_op jit(solution)/shard_map/ppermute | solution.py:76
  9.0 7.0 %collective-permute-start.4 = (bf16[128,1024]{1,0:T(8,128)(2,1)S(1)}, bf16[128,1024]{1,0:T(8,128)(2,1)S(1)}, u32[]{:S(2)}, u32[]{:S(2)}) collective-permute-start(bf16[128,1024]{1,0:T(8,128)(2,1)S(1)} %collective-permute-done.2.refs_1_), channel_id=1, source_target_pairs={{0,4},{4,8},{8,12},{12,14},{14,10},{10,6},{6,2},{2,0},{1,3},{5,1},... | collective-permute-start | bytes 786440 | tf_op jit(solution)/shard_map/ppermute | solution.py:76
  11.4 6.8 %collective-permute-start = (bf16[2,64,1024]{2,1,0:T(8,128)(2,1)S(1)}, bf16[2,64,1024]{2,1,0:T(8,128)(2,1)S(1)}, u32[]{:S(2)}, u32[]{:S(2)}) collective-permute-start(bf16[2,64,1024]{2,1,0:T(8,128)(2,1)S(1)} %pad_maximum_fusion), channel_id=1, source_target_pairs={{0,1},{1,0},{2,3},{3,2},{4,5},{5,4},{6,7},{7,6},{8,9},{9,8},{10,11... | collective-permute-start | bytes 786440 | tf_op jit(solution)/shard_map/ppermute | solution.py:76
  12.3 7.4 %collective-permute-start.5 = (bf16[128,1024]{1,0:T(8,128)(2,1)S(1)}, bf16[128,1024]{1,0:T(8,128)(2,1)S(1)}, u32[]{:S(2)}, u32[]{:S(2)}) collective-permute-start(bf16[128,1024]{1,0:T(8,128)(2,1)S(1)} %collective-permute-done.3.refs_2_), channel_id=1, source_target_pairs={{0,4},{4,8},{8,12},{12,14},{14,10},{10,6},{6,2},{2,0},{1,3},{5,1},... | collective-permute-start | bytes 786440 | tf_op jit(solution)/shard_map/ppermute | solution.py:76
  16.0 9.1 %collective-permute-start.6 = (bf16[128,1024]{1,0:T(8,128)(2,1)S(1)}, bf16[128,1024]{1,0:T(8,128)(2,1)S(1)}, u32[]{:S(2)}, u32[]{:S(2)}) collective-permute-start(bf16[128,1024]{1,0:T(8,128)(2,1)S(1)} %collective-permute-done.4.refs_3_), channel_id=1, source_target_pairs={{0,4},{4,8},{8,12},{12,14},{14,10},{10,6},{6,2},{2,0},{1,3},{5,1},... | collective-permute-start | bytes 786440 | tf_op jit(solution)/shard_map/ppermute | solution.py:76
  19.3 11.9 %collective-permute-start.1 = (bf16[4,2,2,64,128]{4,3,2,1,0:T(8,128)(2,1)S(1)}, bf16[4,2,2,64,128]{4,3,2,1,0:T(8,128)(2,1)S(1)}, u32[]{:S(2)}, u32[]{:S(2)}) collective-permute-start(bf16[4,2,2,64,128]{4,3,2,1,0:T(8,128)(2,1)S(1)} %get-tuple-element.22), channel_id=1, source_target_pairs={{0,2},{1,3},{2,0},{3,1},{4,6},{5,7},{6,4},{7,5},{8,10},{9,11},{10,... | collective-permute-start | bytes 786440 | tf_op jit(solution)/shard_map/ppermute | solution.py:76
  19.7 11.9 %collective-permute-start.11 = (bf16[128,1024]{1,0:T(8,128)(2,1)S(1)}, bf16[128,1024]{1,0:T(8,128)(2,1)S(1)}, u32[]{:S(2)}, u32[]{:S(2)}) collective-permute-start(bf16[128,1024]{1,0:T(8,128)(2,1)S(1)} %collective-permute-done.2.refs_1_), channel_id=1, source_target_pairs={{0,1},{1,0},{2,3},{3,2},{4,5},{5,4},{6,7},{7,6},{8,9},{9,8},{10,11... | collective-permute-start | bytes 786440 | tf_op jit(solution)/shard_map/ppermute | solution.py:76
  25.1 6.7 %collective-permute-start.12 = (bf16[128,1024]{1,0:T(8,128)(2,1)S(1)}, bf16[128,1024]{1,0:T(8,128)(2,1)S(1)}, u32[]{:S(2)}, u32[]{:S(2)}) collective-permute-start(bf16[128,1024]{1,0:T(8,128)(2,1)S(1)} %collective-permute-done.3.refs_2_), channel_id=1, source_target_pairs={{0,1},{1,0},{2,3},{3,2},{4,5},{5,4},{6,7},{7,6},{8,9},{9,8},{10,11... | collective-permute-start | bytes 786440 | tf_op jit(solution)/shard_map/ppermute | solution.py:76
  25.1 7.0 %collective-permute-start.7 = (bf16[128,1024]{1,0:T(8,128)(2,1)S(1)}, bf16[128,1024]{1,0:T(8,128)(2,1)}, u32[]{:S(2)}, u32[]{:S(2)}) collective-permute-start(bf16[128,1024]{1,0:T(8,128)(2,1)S(1)} %collective-permute-done.5.refs_4_), channel_id=1, source_target_pairs={{0,4},{4,8},{8,12},{12,14},{14,10},{10,6},{6,2},{2,0},{1,3},{5,1},... | collective-permute-start | bytes 786440 | tf_op jit(solution)/shard_map/ppermute | solution.py:76
  25.1 9.3 %collective-permute-start.9 = (bf16[128,1024]{1,0:T(8,128)(2,1)S(1)}, bf16[128,1024]{1,0:T(8,128)(2,1)}, u32[]{:S(2)}, u32[]{:S(2)}) collective-permute-start(bf16[128,1024]{1,0:T(8,128)(2,1)S(1)} %collective-permute-done.6.refs_5_), channel_id=1, source_target_pairs={{0,4},{4,8},{8,12},{12,14},{14,10},{10,6},{6,2},{2,0},{1,3},{5,1},... | collective-permute-start | bytes 786440 | tf_op jit(solution)/shard_map/ppermute | solution.py:76
  31.8 7.7 %collective-permute-start.15 = (bf16[128,1024]{1,0:T(8,128)(2,1)S(1)}, bf16[128,1024]{1,0:T(8,128)(2,1)S(1)}, u32[]{:S(2)}, u32[]{:S(2)}) collective-permute-start(bf16[128,1024]{1,0:T(8,128)(2,1)S(1)} %collective-permute-done.6.refs_5_), channel_id=1, source_target_pairs={{0,1},{1,0},{2,3},{3,2},{4,5},{5,4},{6,7},{7,6},{8,9},{9,8},{10,11... | collective-permute-start | bytes 786440 | tf_op jit(solution)/shard_map/ppermute | solution.py:76
  32.1 7.4 %collective-permute-start.16 = (bf16[128,1024]{1,0:T(8,128)(2,1)}, bf16[128,1024]{1,0:T(8,128)(2,1)S(1)}, u32[]{:S(2)}, u32[]{:S(2)}) collective-permute-start(bf16[128,1024]{1,0:T(8,128)(2,1)} %collective-permute-done.7.refs_6_), channel_id=1, source_target_pairs={{0,1},{1,0},{2,3},{3,2},{4,5},{5,4},{6,7},{7,6},{8,9},{9,8},{10,11... | collective-permute-start | bytes 786440 | tf_op jit(solution)/shard_map/ppermute | solution.py:76
  35.8 15.8 %collective-permute-start.21 = (bf16[2,2,2,64,128]{4,3,2,1,0:T(8,128)(2,1)}, bf16[2,2,2,64,128]{4,3,2,1,0:T(8,128)(2,1)S(1)}, u32[]{:S(2)}, u32[]{:S(2)}) collective-permute-start(bf16[2,2,2,64,128]{4,3,2,1,0:T(8,128)(2,1)} %pad_maximum_fusion.1), channel_id=1, source_target_pairs={{0,4},{1,5},{2,6},{3,7},{4,0},{5,1},{6,2},{7,3},{8,12},{9,13},{10,... | collective-permute-start | bytes 393224 | tf_op jit(solution)/shard_map/ppermute | solution.py:76
  37.3 14.3 %collective-permute-start.22 = (bf16[2,2,2,64,128]{4,3,2,1,0:T(8,128)(2,1)}, bf16[2,2,2,64,128]{4,3,2,1,0:T(8,128)(2,1)S(1)}, u32[]{:S(2)}, u32[]{:S(2)}) collective-permute-start(bf16[2,2,2,64,128]{4,3,2,1,0:T(8,128)(2,1)} %pad_maximum_fusion.2), channel_id=1, source_target_pairs={{0,8},{1,9},{2,10},{3,11},{4,12},{5,13},{6,14},{7,15},{8,0},{9,1},... | collective-permute-start | bytes 393224 | tf_op jit(solution)/shard_map/ppermute | solution.py:76
  43.8 7.9 %collective-permute-start.23 = (bf16[2,2,2,64,128]{4,3,2,1,0:T(8,128)(2,1)S(1)}, bf16[2,2,2,64,128]{4,3,2,1,0:T(8,128)(2,1)S(1)}, u32[]{:S(2)}, u32[]{:S(2)}) collective-permute-start(bf16[2,2,2,64,128]{4,3,2,1,0:T(8,128)(2,1)S(1)} %pad_maximum_fusion.3), channel_id=1, source_target_pairs={{0,12},{1,13},{2,14},{3,15},{4,8},{5,9},{6,10},{7,11},{8,4},{9,5},... | collective-permute-start | bytes 393224 | tf_op jit(solution)/shard_map/ppermute | solution.py:76
  56.4 7.4 %collective-permute-start.25 = (bf16[128,1024]{1,0:T(8,128)(2,1)S(1)}, bf16[128,1024]{1,0:T(8,128)(2,1)S(1)}, u32[]{:S(2)}, u32[]{:S(2)}) collective-permute-start(bf16[128,1024]{1,0:T(8,128)(2,1)S(1)} %get-tuple-element.32), channel_id=1, source_target_pairs={{0,4},{4,8},{8,12},{12,14},{14,10},{10,6},{6,2},{2,0},{1,3},{5,1},... | collective-permute-start | bytes 786440 | tf_op jit(solution)/shard_map/ppermute | solution.py:76
  59.1 6.7 %collective-permute-start.29 = (bf16[128,1024]{1,0:T(8,128)(2,1)S(1)}, bf16[128,1024]{1,0:T(8,128)(2,1)S(1)}, u32[]{:S(2)}, u32[]{:S(2)}) collective-permute-start(bf16[128,1024]{1,0:T(8,128)(2,1)S(1)} %get-tuple-element.36), channel_id=1, source_target_pairs={{0,4},{4,8},{8,12},{12,14},{14,10},{10,6},{6,2},{2,0},{1,3},{5,1},... | collective-permute-start | bytes 786440 | tf_op jit(solution)/shard_map/ppermute | solution.py:76
  63.8 6.4 %collective-permute-start.26 = (bf16[128,1024]{1,0:T(8,128)(2,1)S(1)}, bf16[128,1024]{1,0:T(8,128)(2,1)S(1)}, u32[]{:S(2)}, u32[]{:S(2)}) collective-permute-start(bf16[128,1024]{1,0:T(8,128)(2,1)S(1)} %add_convert_fusion.5), channel_id=1, source_target_pairs={{0,4},{4,8},{8,12},{12,14},{14,10},{10,6},{6,2},{2,0},{1,3},{5,1},... | collective-permute-start | bytes 786440 | tf_op jit(solution)/shard_map/ppermute | solution.py:76
  65.9 7.2 %collective-permute-start.30 = (bf16[128,1024]{1,0:T(8,128)(2,1)S(1)}, bf16[128,1024]{1,0:T(8,128)(2,1)S(1)}, u32[]{:S(2)}, u32[]{:S(2)}) collective-permute-start(bf16[128,1024]{1,0:T(8,128)(2,1)S(1)} %add_convert_fusion.2), channel_id=1, source_target_pairs={{0,4},{4,8},{8,12},{12,14},{14,10},{10,6},{6,2},{2,0},{1,3},{5,1},... | collective-permute-start | bytes 786440 | tf_op jit(solution)/shard_map/ppermute | solution.py:76
  85.2 7.5 %collective-permute-start.34 = (bf16[128,1024]{1,0:T(8,128)(2,1)S(1)}, bf16[128,1024]{1,0:T(8,128)(2,1)S(1)}, u32[]{:S(2)}, u32[]{:S(2)}) collective-permute-start(bf16[128,1024]{1,0:T(8,128)(2,1)S(1)} %collective-permute-done.33.refs_8_), channel_id=1, source_target_pairs={{0,4},{4,8},{8,12},{12,14},{14,10},{10,6},{6,2},{2,0},{1,3},{5,1},... | collective-permute-start | bytes 786440 | tf_op jit(solution)/shard_map/ppermute | solution.py:76
  98.0 6.9 %collective-permute-start.41 = (bf16[128,1024]{1,0:T(8,128)(2,1)S(1)}, bf16[128,1024]{1,0:T(8,128)(2,1)S(1)}, u32[]{:S(2)}, u32[]{:S(2)}) collective-permute-start(bf16[128,1024]{1,0:T(8,128)(2,1)S(1)} %collective-permute-done.34.refs_2_), channel_id=1, source_target_pairs={{0,1},{1,0},{2,3},{3,2},{4,5},{5,4},{6,7},{7,6},{8,9},{9,8},{10,11... | collective-permute-start | bytes 786440 | tf_op jit(solution)/shard_map/ppermute | solution.py:76
  (26 other events, 184.0 us)
